TPU v7x, 512 devices: a whole 4x4x16 slice. The times are simulated.
512 devices in a mesh: dp: 32 (over y, x, core), ctx: 16 (over z).
Axes of the slice: x: 4, y: 4, z: 16, core: 2. Of those that a mesh axis runs over, the one named last changes fastest.
Arguments:
- queries: bfloat16 [65536, 2048], P(('dp', 'ctx')), parts along dimension 0, may hold values from -6 to 6
- keys: bfloat16 [65536, 512], P(('dp', 'ctx')), parts along dimension 0, may hold values from -6 to 6
- values: bfloat16 [65536, 512], P(('dp', 'ctx')), parts along dimension 0, may hold values from -6 to 6
- out_grad: bfloat16 [65536, 2048], P(('dp', 'ctx')), parts along dimension 0, may hold values from -6 to 6
- segment_ids: int32 [65536], P('dp'), parts along dimension 0, may hold values from 0 to 5, never falling along the last dimension, each value on 1 to 1536 neighbouring positions
Outputs:
- attended: bfloat16 [65536, 2048], P(('dp', 'ctx')), parts along dimension 0
- grad_query: bfloat16 [65536, 2048], P(('dp', 'ctx')), parts along dimension 0
- grad_key: float32 [65536, 512], P(('dp', 'ctx')), parts along dimension 0
- grad_value: float32 [65536, 512], P(('dp', 'ctx')), parts along dimension 0
There are 32 independent parts, one for each index of `dp`. A program takes and returns all parts, laid end to end along the dimension named above; each array names one. Nothing has to cross between parts.
Inputs may be any that keep to these rules, and one draw needn't show every extreme that they name: `segment_ids`: ids never fall along the window.
All inputs are finite; a program needn't handle non-finite values.
Results may differ from a plain program's by a relative error of at most 0.025.
Values may be sent and summed in bfloat16 or wider, within the bound.
No kernel may reach another device: no remote copies, remote signals or barrier semaphores. Data moves between devices by JAX's collectives and lax.ppermute only.
A program may use at most 128 MiB of HBM per device.

v0:
```python
import math

import jax
import jax.numpy as jnp
from jax import lax
from jax.sharding import PartitionSpec as P

H = 16
KVH = 4
HD = 128
GROUP = 4


neg_big = -1e30


def from_behind(x, axis, by):
    peers = lax.axis_size(axis)
    return lax.ppermute(x, axis, [(i, (i + by) % peers) for i in range(peers)])


def block_scores(q_group, key_all, seg_ids, q_places, q_seg, k_start, key_block):
    k_block = lax.dynamic_slice_in_dim(key_all, k_start, key_block, 0).reshape(key_block, KVH, HD)
    k_seg = lax.dynamic_slice_in_dim(seg_ids, k_start, key_block, 0)
    k_places = k_start + jnp.arange(key_block, dtype=jnp.int32)
    allowed = (k_places[None, :] <= q_places[:, None]) & (k_seg[None, :] == q_seg[:, None])
    scores = jnp.einsum("qgrd,kgd->grqk", q_group, k_block, preferred_element_type=jnp.float32) * (
        1.0 / math.sqrt(HD)
    )
    return (jnp.where(allowed, scores, neg_big), allowed, k_block)


def attend_rows(q_rows, g_rows, q_start, key_all, value_all, seg_ids, grads_in):
    n_rows = q_rows.shape[0]
    all_rows = key_all.shape[0]
    key_block = min(all_rows, 512)
    scale = 1.0 / math.sqrt(HD)
    q_places = q_start + jnp.arange(n_rows, dtype=jnp.int32)
    q_seg = lax.dynamic_slice_in_dim(seg_ids, q_start, n_rows, 0)
    first_key = jnp.sum((seg_ids < q_seg[0]).astype(jnp.int32))
    low_block = first_key // key_block
    high_block = jnp.where(True, (q_start + n_rows - 1) // key_block + 1, low_block)
    q_group = q_rows.reshape(n_rows, KVH, GROUP, HD)
    g_group = g_rows.reshape(n_rows, KVH, GROUP, HD)

    def stats_step(step_idx, state_now):
        run_max, run_sum = state_now
        k_start = step_idx * key_block
        scores, allowed, k_block = block_scores(
            q_group, key_all, seg_ids, q_places, q_seg, k_start, key_block
        )
        new_max = jnp.maximum(run_max, jnp.max(scores, axis=3))
        weights = jnp.where(allowed, jnp.exp(scores - new_max[..., None]), 0.0)
        run_sum = run_sum * jnp.exp(run_max - new_max) + jnp.sum(weights, axis=3)
        return (new_max, run_sum)

    start_state = (
        jnp.full((KVH, GROUP, n_rows), neg_big, jnp.float32),
        jnp.zeros((KVH, GROUP, n_rows), jnp.float32),
    )
    run_max, run_sum = lax.fori_loop(low_block, high_block, stats_step, start_state)
    safe_sum = jnp.where(run_sum > 0, run_sum, 1.0)
    log_total = run_max + jnp.log(safe_sum)

    def value_step(step_idx, partial_value):
        k_start = step_idx * key_block
        scores, allowed, k_block = block_scores(
            q_group, key_all, seg_ids, q_places, q_seg, k_start, key_block
        )
        v_block = lax.dynamic_slice_in_dim(value_all, k_start, key_block, 0).reshape(
            key_block, KVH, HD
        )
        probs = jnp.where(allowed, jnp.exp(scores - log_total[..., None]), 0.0)
        return partial_value + jnp.einsum(
            "grqk,kgd->qgrd",
            probs.astype(jnp.bfloat16),
            v_block,
            preferred_element_type=jnp.float32,
        )

    partial_value = lax.fori_loop(
        low_block, high_block, value_step, jnp.zeros((n_rows, KVH, GROUP, HD), jnp.float32)
    )
    attended = partial_value.astype(jnp.bfloat16)
    inner = jnp.sum(g_group.astype(jnp.float32) * attended.astype(jnp.float32), axis=3).transpose(
        1, 2, 0
    )

    def backward_step(step_idx, state_now):
        grad_q, grad_k, grad_v = state_now
        k_start = step_idx * key_block
        scores, allowed, k_block = block_scores(
            q_group, key_all, seg_ids, q_places, q_seg, k_start, key_block
        )
        v_block = lax.dynamic_slice_in_dim(value_all, k_start, key_block, 0).reshape(
            key_block, KVH, HD
        )
        probs = jnp.where(allowed, jnp.exp(scores - log_total[..., None]), 0.0)
        grad_probs = jnp.einsum(
            "qgrd,kgd->grqk", g_group, v_block, preferred_element_type=jnp.float32
        )
        grad_scores = (probs * (grad_probs - inner[..., None]) * scale).astype(jnp.bfloat16)
        grad_q = grad_q + jnp.einsum(
            "grqk,kgd->qgrd", grad_scores, k_block, preferred_element_type=jnp.float32
        )
        key_part = jnp.einsum(
            "grqk,qgrd->kgd", grad_scores, q_group, preferred_element_type=jnp.float32
        ).reshape(key_block, KVH * HD)
        value_part = jnp.einsum(
            "grqk,qgrd->kgd",
            probs.astype(jnp.bfloat16),
            g_group,
            preferred_element_type=jnp.float32,
        ).reshape(key_block, KVH * HD)
        grad_k = lax.dynamic_update_slice_in_dim(
            grad_k, lax.dynamic_slice_in_dim(grad_k, k_start, key_block, 0) + key_part, k_start, 0
        )
        grad_v = lax.dynamic_update_slice_in_dim(
            grad_v, lax.dynamic_slice_in_dim(grad_v, k_start, key_block, 0) + value_part, k_start, 0
        )
        return (grad_q, grad_k, grad_v)

    back_state = (jnp.zeros((n_rows, KVH, GROUP, HD), jnp.float32), grads_in[0], grads_in[1])
    grad_q, grad_k, grad_v = lax.fori_loop(low_block, high_block, backward_step, back_state)
    return (
        attended.reshape(n_rows, H * HD),
        grad_q.reshape(n_rows, H * HD).astype(jnp.bfloat16),
        (grad_k, grad_v),
    )


def local(queries, keys, values, out_grad, segment_ids):
    tok_rows = queries.shape[0]
    axis_count = lax.axis_size("ctx")
    my_index = lax.axis_index("ctx")
    key_all, value_all = (
        lax.all_gather(keys, "ctx", axis=0, tiled=True),
        lax.all_gather(values, "ctx", axis=0, tiled=True),
    )
    all_rows = key_all.shape[0]
    empty_grads = (
        jnp.zeros((all_rows, KVH * HD), jnp.float32),
        jnp.zeros((all_rows, KVH * HD), jnp.float32),
    )
    own_start = my_index * tok_rows
    attended, grad_query, grads_now = attend_rows(
        queries, out_grad, own_start, key_all, value_all, segment_ids, empty_grads
    )
    key_terms, value_terms = grads_now

    def pick_block(buffer, block_id):
        return lax.dynamic_slice_in_dim(buffer, block_id * tok_rows, tok_rows, 0)

    first_id = (my_index - 1) % axis_count
    running = (pick_block(key_terms, first_id), pick_block(value_terms, first_id))

    def chain_step(step_idx, running_now):
        arrived = (
            from_behind(running_now[0].astype(jnp.bfloat16), "ctx", 1).astype(jnp.float32),
            from_behind(running_now[1].astype(jnp.bfloat16), "ctx", 1).astype(jnp.float32),
        )
        block_id = (my_index - step_idx - 1) % axis_count
        return (
            arrived[0] + pick_block(key_terms, block_id),
            arrived[1] + pick_block(value_terms, block_id),
        )

    key_sum, value_sum = lax.fori_loop(1, axis_count, chain_step, running)
    return (attended, grad_query, key_sum, value_sum)


def solution(mesh):
    placed = (
        P(("dp", "ctx"), None),
        P(("dp", "ctx"), None),
        P(("dp", "ctx"), None),
        P(("dp", "ctx"), None),
        P("dp"),
    )
    return jax.shard_map(
        local,
        mesh=mesh,
        in_specs=placed,
        out_specs=(
            P(("dp", "ctx"), None),
            P(("dp", "ctx"), None),
            P(("dp", "ctx"), None),
            P(("dp", "ctx"), None),
        ),
        check_vma=False,
    )
```

profile of v0, /device:TPU:24, one launch (start us, length us, event | category | flops | bytes accessed | tf_op | source)
XLA Modules:
  0.0 409.1 jit_solution(5293943969455945906)
XLA Ops:
  7.2 1.7 copy.35
  9.0 1.7 copy.34
  18.6 75.0 %all-gather.5.cloned.1.call-done = bf16[2048,512]{0,1:T(8,128)(2,1)} async-done(((bf16[128,512]{0,1:T(8,128)(2,1)}), bf16[2048,512]{0,1:T(8,128)(2,1)}) %all-gather.5.cloned.1.call-update) | async-done | bytes 2097168 | tf_op jit(solution)/shard_map/all_gather | solution.py:137
  93.6 3.3 while.57
  96.9 74.4 %all-gather.3.cloned.1.call-done = bf16[2048,512]{0,1:T(8,128)(2,1)} async-done(((bf16[128,512]{0,1:T(8,128)(2,1)}), bf16[2048,512]{0,1:T(8,128)(2,1)}) %all-gather.3.cloned.1.call-update) | async-done | bytes 2097168 | tf_op jit(solution)/shard_map/all_gather | solution.py:138
  171.4 4.5 %while.58 = (s32[]{:T(128)}, f32[128,4,4,128]{0,3,2,1:T(8,128)S(1)}, s32[]{:T(128)}, bf16[2048,512]{0,1:T(8,128)(2,1)}, s32[2048]{0:T(1024)S(1)}, /*index=5*/s32...) while((s32[]{:T(128)}, ...), condition=%wide.region_6.7_spmd.clone, body=%wide.region_5.6_spmd.clone.sunk | while | flops 542573184 | bytes 5918411 | solution.py:81
  172.9 3.0 fusion.78
  177.2 2.5 broadcast.57
  179.6 2.5 broadcast.57.clone
  182.1 10.8 %while.59 = (s32[]{:T(128)}, f32[128,4,4,128]{0,3,2,1:T(8,128)S(1)}, f32[2048,512]{0,1:T(8,128)}, f32[2048,512]{0,1:T(8,128)}, s32[]{:T(128)}, /*index=5*/bf16[2...) while((s32[]{:T(128)}, ...), condition=%wide.region_9.10_spmd.clone, body=%wide.region_8.9_spmd.clone.sunk | while | flops 1356792448 | bytes 35360496 | solution.py:124
  185.4 1.7 fusion.90
  189.7 3.2 constant_dynamic-update-slice_fusion.3
  195.3 206.1 %while.56 = (s32[]{:T(128)}, f32[128,512]{1,0:T(8,128)S(1)}, f32[128,512]{1,0:T(8,128)S(1)}, s32[]{:T(128)}, f32[2048,512]{0,1:T(8,128)}, /*index=5*/f32[2048,51...) while((s32[]{:T(128)}, f32[128,512]{1,0:T(8,128)S(1)}, ...), condition=%wide.region_11.12_spmd, body=%wide.region_10.11_spmd.sunk | while | flops 393235 | bytes 5243268 | solution.py:168
  195.4 3.9 collective-permute-start
  199.3 2.8 collective-permute-start.1
  204.8 2.6 collective-permute-done.1
  207.5 1.9 collective-permute-start
  209.4 16.5 %collective-permute-start.1 = (bf16[128,512]{1,0:T(8,128)(2,1)S(1)}, bf16[128,512]{1,0:T(8,128)(2,1)S(1)}, u32[]{:S(2)}, u32[]{:S(2)}) collective-permute-start(bf16[128,512]{1,0:T(8,128)(2,1)S(1)} %convert_element_type.102), channel_id=1, source_target_pairs={{0,1},{1,2},{2,3},{3,4},{4,5},{5,6},{6,7},{7,8},{8,9},{9,10},{10,1... | collective-permute-start | bytes 393224 | tf_op jit(solution)/shard_map/while/body/eval_jaxpr/ppermute | solution.py:19
  227.3 28.6 %collective-permute-done = bf16[128,512]{1,0:T(8,128)(2,1)S(1)} collective-permute-done((bf16[128,512]{1,0:T(8,128)(2,1)S(1)}, bf16[128,512]{1,0:T(8,128)(2,1)S(1)}, u32[]{:S(2)}, u32[]{:S(2)}) %collective-permute-start) | collective-permute-done | bytes 131104 | tf_op jit(solution)/shard_map/while/body/eval_jaxpr/ppermute | solution.py:19
  255.9 1.9 collective-permute-done.1
  257.9 1.9 collective-permute-start
  259.8 1.9 collective-permute-start.1
  263.2 2.8 collective-permute-done
  266.0 1.9 collective-permute-done.1
  268.0 1.9 collective-permute-start
  269.9 1.9 collective-permute-start.1
  273.3 2.8 collective-permute-done
  276.1 1.9 collective-permute-done.1
  278.1 1.9 collective-permute-start
  280.1 1.9 collective-permute-start.1
  283.4 2.8 collective-permute-done
  286.2 1.9 collective-permute-done.1
  288.2 1.9 collective-permute-start
  290.2 1.9 collective-permute-start.1
  293.5 2.8 collective-permute-done
  296.3 1.9 collective-permute-done.1
  298.3 1.9 collective-permute-start
  300.3 3.3 collective-permute-start.1
  304.9 1.5 collective-permute-done
  306.4 1.9 collective-permute-done.1
  308.4 2.1 collective-permute-start
  310.5 6.8 %collective-permute-start.1 = (bf16[128,512]{1,0:T(8,128)(2,1)S(1)}, bf16[128,512]{1,0:T(8,128)(2,1)S(1)}, u32[]{:S(2)}, u32[]{:S(2)}) collective-permute-start(bf16[128,512]{1,0:T(8,128)(2,1)S(1)} %convert_element_type.102), channel_id=1, source_target_pairs={{0,1},{1,2},{2,3},{3,4},{4,5},{5,6},{6,7},{7,8},{8,9},{9,10},{10,1... | collective-permute-start | bytes 393224 | tf_op jit(solution)/shard_map/while/body/eval_jaxpr/ppermute | solution.py:19
  319.9 4.4 %collective-permute-start = (bf16[128,512]{1,0:T(8,128)(2,1)S(1)}, bf16[128,512]{1,0:T(8,128)(2,1)S(1)}, u32[]{:S(2)}, u32[]{:S(2)}) collective-permute-start(bf16[128,512]{1,0:T(8,128)(2,1)S(1)} %convert_element_type.101), channel_id=1, source_target_pairs={{0,1},{1,2},{2,3},{3,4},{4,5},{5,6},{6,7},{7,8},{8,9},{9,10},{10,1... | collective-permute-start | bytes 393224 | tf_op jit(solution)/shard_map/while/body/eval_jaxpr/ppermute | solution.py:19
  324.3 4.4 %collective-permute-start.1 = (bf16[128,512]{1,0:T(8,128)(2,1)S(1)}, bf16[128,512]{1,0:T(8,128)(2,1)S(1)}, u32[]{:S(2)}, u32[]{:S(2)}) collective-permute-start(bf16[128,512]{1,0:T(8,128)(2,1)S(1)} %convert_element_type.102), channel_id=1, source_target_pairs={{0,1},{1,2},{2,3},{3,4},{4,5},{5,6},{6,7},{7,8},{8,9},{9,10},{10,1... | collective-permute-start | bytes 393224 | tf_op jit(solution)/shard_map/while/body/eval_jaxpr/ppermute | solution.py:19
  330.1 3.0 collective-permute-done.1
  333.2 2.4 collective-permute-start
  335.6 3.5 collective-permute-start.1
  340.6 1.6 collective-permute-done
  342.2 2.7 collective-permute-done.1
  345.0 1.9 collective-permute-start
  347.0 4.9 %collective-permute-start.1 = (bf16[128,512]{1,0:T(8,128)(2,1)S(1)}, bf16[128,512]{1,0:T(8,128)(2,1)S(1)}, u32[]{:S(2)}, u32[]{:S(2)}) collective-permute-start(bf16[128,512]{1,0:T(8,128)(2,1)S(1)} %convert_element_type.102), channel_id=1, source_target_pairs={{0,1},{1,2},{2,3},{3,4},{4,5},{5,6},{6,7},{7,8},{8,9},{9,10},{10,1... | collective-permute-start | bytes 393224 | tf_op jit(solution)/shard_map/while/body/eval_jaxpr/ppermute | solution.py:19
  354.4 2.0 collective-permute-done.1
  356.5 3.4 collective-permute-start
  360.0 4.1 %collective-permute-start.1 = (bf16[128,512]{1,0:T(8,128)(2,1)S(1)}, bf16[128,512]{1,0:T(8,128)(2,1)S(1)}, u32[]{:S(2)}, u32[]{:S(2)}) collective-permute-start(bf16[128,512]{1,0:T(8,128)(2,1)S(1)} %convert_element_type.102), channel_id=1, source_target_pairs={{0,1},{1,2},{2,3},{3,4},{4,5},{5,6},{6,7},{7,8},{8,9},{9,10},{10,1... | collective-permute-start | bytes 393224 | tf_op jit(solution)/shard_map/while/body/eval_jaxpr/ppermute | solution.py:19
  365.6 2.5 collective-permute-done.1
  368.1 2.9 collective-permute-start
  371.1 3.9 collective-permute-start.1
  376.5 2.7 collective-permute-done.1
  379.2 2.9 collective-permute-start
  382.2 4.2 %collective-permute-start.1 = (bf16[128,512]{1,0:T(8,128)(2,1)S(1)}, bf16[128,512]{1,0:T(8,128)(2,1)S(1)}, u32[]{:S(2)}, u32[]{:S(2)}) collective-permute-start(bf16[128,512]{1,0:T(8,128)(2,1)S(1)} %convert_element_type.102), channel_id=1, source_target_pairs={{0,1},{1,2},{2,3},{3,4},{4,5},{5,6},{6,7},{7,8},{8,9},{9,10},{10,1... | collective-permute-start | bytes 393224 | tf_op jit(solution)/shard_map/while/body/eval_jaxpr/ppermute | solution.py:19
  387.8 2.5 collective-permute-done.1
  390.3 3.0 collective-permute-start
  393.3 3.8 collective-permute-start.1
  398.6 2.8 collective-permute-done.1
  (169 shorter events, 45.4 us)
Async XLA Ops:
  7.2 86.4 %copy-start.3 = (s32[2048]{0:T(1024)S(1)}, s32[2048]{0:T(1024)}, u32[]{:S(2)}) copy-start(s32[2048]{0:T(1024)} %param.17) | copy-start | bytes 24580
  7.2 11.1 %copy-start.2 = (bf16[128,2048]{1,0:T(8,128)(2,1)S(1)}, bf16[128,2048]{1,0:T(8,128)(2,1)}, u32[]{:S(2)}) copy-start(bf16[128,2048]{1,0:T(8,128)(2,1)} %param.16) | copy-start | bytes 1572868
  7.2 86.4 %all-gather.5.cloned.1.call-start = ((), (), s32[]{:S(2)}) async-start(), calls=%async_computation.1 | async-start | bytes 2228224 | tf_op jit(solution)/shard_map/all_gather | solution.py:137
  9.0 162.3 %all-gather.3.cloned.1.call-start = ((), (), s32[]{:S(2)}) async-start(), calls=%async_computation | async-start | bytes 2228224 | tf_op jit(solution)/shard_map/all_gather | solution.py:138
  195.4 9.4 %collective-permute-start = (bf16[128,512]{1,0:T(8,128)(2,1)S(1)}, bf16[128,512]{1,0:T(8,128)(2,1)S(1)}, u32[]{:S(2)}, u32[]{:S(2)}) collective-permute-start(bf16[128,512]{1,0:T(8,128)(2,1)S(1)} %convert_element_type.101), channel_id=1, source_target_pairs={{0,1},{1,2},{2,3},{3,4},{4,5},{5,6},{6,7},{7,8},{8,9},{9,10},{10,1... | collective-permute-start | bytes 393224 | tf_op jit(solution)/shard_map/while/body/eval_jaxpr/ppermute | solution.py:19
  199.3 8.1 %collective-permute-start.1 = (bf16[128,512]{1,0:T(8,128)(2,1)S(1)}, bf16[128,512]{1,0:T(8,128)(2,1)S(1)}, u32[]{:S(2)}, u32[]{:S(2)}) collective-permute-start(bf16[128,512]{1,0:T(8,128)(2,1)S(1)} %convert_element_type.102), channel_id=1, source_target_pairs={{0,1},{1,2},{2,3},{3,4},{4,5},{5,6},{6,7},{7,8},{8,9},{9,10},{10,1... | collective-permute-start | bytes 393224 | tf_op jit(solution)/shard_map/while/body/eval_jaxpr/ppermute | solution.py:19
  207.5 48.4 %collective-permute-start = (bf16[128,512]{1,0:T(8,128)(2,1)S(1)}, bf16[128,512]{1,0:T(8,128)(2,1)S(1)}, u32[]{:S(2)}, u32[]{:S(2)}) collective-permute-start(bf16[128,512]{1,0:T(8,128)(2,1)S(1)} %convert_element_type.101), channel_id=1, source_target_pairs={{0,1},{1,2},{2,3},{3,4},{4,5},{5,6},{6,7},{7,8},{8,9},{9,10},{10,1... | collective-permute-start | bytes 393224 | tf_op jit(solution)/shard_map/while/body/eval_jaxpr/ppermute | solution.py:19
  209.4 48.4 %collective-permute-start.1 = (bf16[128,512]{1,0:T(8,128)(2,1)S(1)}, bf16[128,512]{1,0:T(8,128)(2,1)S(1)}, u32[]{:S(2)}, u32[]{:S(2)}) collective-permute-start(bf16[128,512]{1,0:T(8,128)(2,1)S(1)} %convert_element_type.102), channel_id=1, source_target_pairs={{0,1},{1,2},{2,3},{3,4},{4,5},{5,6},{6,7},{7,8},{8,9},{9,10},{10,1... | collective-permute-start | bytes 393224 | tf_op jit(solution)/shard_map/while/body/eval_jaxpr/ppermute | solution.py:19
  257.9 8.1 %collective-permute-start = (bf16[128,512]{1,0:T(8,128)(2,1)S(1)}, bf16[128,512]{1,0:T(8,128)(2,1)S(1)}, u32[]{:S(2)}, u32[]{:S(2)}) collective-permute-start(bf16[128,512]{1,0:T(8,128)(2,1)S(1)} %convert_element_type.101), channel_id=1, source_target_pairs={{0,1},{1,2},{2,3},{3,4},{4,5},{5,6},{6,7},{7,8},{8,9},{9,10},{10,1... | collective-permute-start | bytes 393224 | tf_op jit(solution)/shard_map/while/body/eval_jaxpr/ppermute | solution.py:19
  259.8 8.1 %collective-permute-start.1 = (bf16[128,512]{1,0:T(8,128)(2,1)S(1)}, bf16[128,512]{1,0:T(8,128)(2,1)S(1)}, u32[]{:S(2)}, u32[]{:S(2)}) collective-permute-start(bf16[128,512]{1,0:T(8,128)(2,1)S(1)} %convert_element_type.102), channel_id=1, source_target_pairs={{0,1},{1,2},{2,3},{3,4},{4,5},{5,6},{6,7},{7,8},{8,9},{9,10},{10,1... | collective-permute-start | bytes 393224 | tf_op jit(solution)/shard_map/while/body/eval_jaxpr/ppermute | solution.py:19
  268.0 8.1 %collective-permute-start = (bf16[128,512]{1,0:T(8,128)(2,1)S(1)}, bf16[128,512]{1,0:T(8,128)(2,1)S(1)}, u32[]{:S(2)}, u32[]{:S(2)}) collective-permute-start(bf16[128,512]{1,0:T(8,128)(2,1)S(1)} %convert_element_type.101), channel_id=1, source_target_pairs={{0,1},{1,2},{2,3},{3,4},{4,5},{5,6},{6,7},{7,8},{8,9},{9,10},{10,1... | collective-permute-start | bytes 393224 | tf_op jit(solution)/shard_map/while/body/eval_jaxpr/ppermute | solution.py:19
  269.9 8.1 %collective-permute-start.1 = (bf16[128,512]{1,0:T(8,128)(2,1)S(1)}, bf16[128,512]{1,0:T(8,128)(2,1)S(1)}, u32[]{:S(2)}, u32[]{:S(2)}) collective-permute-start(bf16[128,512]{1,0:T(8,128)(2,1)S(1)} %convert_element_type.102), channel_id=1, source_target_pairs={{0,1},{1,2},{2,3},{3,4},{4,5},{5,6},{6,7},{7,8},{8,9},{9,10},{10,1... | collective-permute-start | bytes 393224 | tf_op jit(solution)/shard_map/while/body/eval_jaxpr/ppermute | solution.py:19
  278.1 8.1 %collective-permute-start = (bf16[128,512]{1,0:T(8,128)(2,1)S(1)}, bf16[128,512]{1,0:T(8,128)(2,1)S(1)}, u32[]{:S(2)}, u32[]{:S(2)}) collective-permute-start(bf16[128,512]{1,0:T(8,128)(2,1)S(1)} %convert_element_type.101), channel_id=1, source_target_pairs={{0,1},{1,2},{2,3},{3,4},{4,5},{5,6},{6,7},{7,8},{8,9},{9,10},{10,1... | collective-permute-start | bytes 393224 | tf_op jit(solution)/shard_map/while/body/eval_jaxpr/ppermute | solution.py:19
  280.1 8.1 %collective-permute-start.1 = (bf16[128,512]{1,0:T(8,128)(2,1)S(1)}, bf16[128,512]{1,0:T(8,128)(2,1)S(1)}, u32[]{:S(2)}, u32[]{:S(2)}) collective-permute-start(bf16[128,512]{1,0:T(8,128)(2,1)S(1)} %convert_element_type.102), channel_id=1, source_target_pairs={{0,1},{1,2},{2,3},{3,4},{4,5},{5,6},{6,7},{7,8},{8,9},{9,10},{10,1... | collective-permute-start | bytes 393224 | tf_op jit(solution)/shard_map/while/body/eval_jaxpr/ppermute | solution.py:19
  288.2 8.1 %collective-permute-start = (bf16[128,512]{1,0:T(8,128)(2,1)S(1)}, bf16[128,512]{1,0:T(8,128)(2,1)S(1)}, u32[]{:S(2)}, u32[]{:S(2)}) collective-permute-start(bf16[128,512]{1,0:T(8,128)(2,1)S(1)} %convert_element_type.101), channel_id=1, source_target_pairs={{0,1},{1,2},{2,3},{3,4},{4,5},{5,6},{6,7},{7,8},{8,9},{9,10},{10,1... | collective-permute-start | bytes 393224 | tf_op jit(solution)/shard_map/while/body/eval_jaxpr/ppermute | solution.py:19
  290.2 8.1 %collective-permute-start.1 = (bf16[128,512]{1,0:T(8,128)(2,1)S(1)}, bf16[128,512]{1,0:T(8,128)(2,1)S(1)}, u32[]{:S(2)}, u32[]{:S(2)}) collective-permute-start(bf16[128,512]{1,0:T(8,128)(2,1)S(1)} %convert_element_type.102), channel_id=1, source_target_pairs={{0,1},{1,2},{2,3},{3,4},{4,5},{5,6},{6,7},{7,8},{8,9},{9,10},{10,1... | collective-permute-start | bytes 393224 | tf_op jit(solution)/shard_map/while/body/eval_jaxpr/ppermute | solution.py:19
  298.3 8.1 %collective-permute-start = (bf16[128,512]{1,0:T(8,128)(2,1)S(1)}, bf16[128,512]{1,0:T(8,128)(2,1)S(1)}, u32[]{:S(2)}, u32[]{:S(2)}) collective-permute-start(bf16[128,512]{1,0:T(8,128)(2,1)S(1)} %convert_element_type.101), channel_id=1, source_target_pairs={{0,1},{1,2},{2,3},{3,4},{4,5},{5,6},{6,7},{7,8},{8,9},{9,10},{10,1... | collective-permute-start | bytes 393224 | tf_op jit(solution)/shard_map/while/body/eval_jaxpr/ppermute | solution.py:19
  300.3 8.1 %collective-permute-start.1 = (bf16[128,512]{1,0:T(8,128)(2,1)S(1)}, bf16[128,512]{1,0:T(8,128)(2,1)S(1)}, u32[]{:S(2)}, u32[]{:S(2)}) collective-permute-start(bf16[128,512]{1,0:T(8,128)(2,1)S(1)} %convert_element_type.102), channel_id=1, source_target_pairs={{0,1},{1,2},{2,3},{3,4},{4,5},{5,6},{6,7},{7,8},{8,9},{9,10},{10,1... | collective-permute-start | bytes 393224 | tf_op jit(solution)/shard_map/while/body/eval_jaxpr/ppermute | solution.py:19
  308.4 10.3 %collective-permute-start = (bf16[128,512]{1,0:T(8,128)(2,1)S(1)}, bf16[128,512]{1,0:T(8,128)(2,1)S(1)}, u32[]{:S(2)}, u32[]{:S(2)}) collective-permute-start(bf16[128,512]{1,0:T(8,128)(2,1)S(1)} %convert_element_type.101), channel_id=1, source_target_pairs={{0,1},{1,2},{2,3},{3,4},{4,5},{5,6},{6,7},{7,8},{8,9},{9,10},{10,1... | collective-permute-start | bytes 393224 | tf_op jit(solution)/shard_map/while/body/eval_jaxpr/ppermute | solution.py:19
  310.5 9.3 %collective-permute-start.1 = (bf16[128,512]{1,0:T(8,128)(2,1)S(1)}, bf16[128,512]{1,0:T(8,128)(2,1)S(1)}, u32[]{:S(2)}, u32[]{:S(2)}) collective-permute-start(bf16[128,512]{1,0:T(8,128)(2,1)S(1)} %convert_element_type.102), channel_id=1, source_target_pairs={{0,1},{1,2},{2,3},{3,4},{4,5},{5,6},{6,7},{7,8},{8,9},{9,10},{10,1... | collective-permute-start | bytes 393224 | tf_op jit(solution)/shard_map/while/body/eval_jaxpr/ppermute | solution.py:19
  319.9 10.2 %collective-permute-start = (bf16[128,512]{1,0:T(8,128)(2,1)S(1)}, bf16[128,512]{1,0:T(8,128)(2,1)S(1)}, u32[]{:S(2)}, u32[]{:S(2)}) collective-permute-start(bf16[128,512]{1,0:T(8,128)(2,1)S(1)} %convert_element_type.101), channel_id=1, source_target_pairs={{0,1},{1,2},{2,3},{3,4},{4,5},{5,6},{6,7},{7,8},{8,9},{9,10},{10,1... | collective-permute-start | bytes 393224 | tf_op jit(solution)/shard_map/while/body/eval_jaxpr/ppermute | solution.py:19
  324.3 8.8 %collective-permute-start.1 = (bf16[128,512]{1,0:T(8,128)(2,1)S(1)}, bf16[128,512]{1,0:T(8,128)(2,1)S(1)}, u32[]{:S(2)}, u32[]{:S(2)}) collective-permute-start(bf16[128,512]{1,0:T(8,128)(2,1)S(1)} %convert_element_type.102), channel_id=1, source_target_pairs={{0,1},{1,2},{2,3},{3,4},{4,5},{5,6},{6,7},{7,8},{8,9},{9,10},{10,1... | collective-permute-start | bytes 393224 | tf_op jit(solution)/shard_map/while/body/eval_jaxpr/ppermute | solution.py:19
  333.2 9.0 %collective-permute-start = (bf16[128,512]{1,0:T(8,128)(2,1)S(1)}, bf16[128,512]{1,0:T(8,128)(2,1)S(1)}, u32[]{:S(2)}, u32[]{:S(2)}) collective-permute-start(bf16[128,512]{1,0:T(8,128)(2,1)S(1)} %convert_element_type.101), channel_id=1, source_target_pairs={{0,1},{1,2},{2,3},{3,4},{4,5},{5,6},{6,7},{7,8},{8,9},{9,10},{10,1... | collective-permute-start | bytes 393224 | tf_op jit(solution)/shard_map/while/body/eval_jaxpr/ppermute | solution.py:19
  335.6 9.3 %collective-permute-start.1 = (bf16[128,512]{1,0:T(8,128)(2,1)S(1)}, bf16[128,512]{1,0:T(8,128)(2,1)S(1)}, u32[]{:S(2)}, u32[]{:S(2)}) collective-permute-start(bf16[128,512]{1,0:T(8,128)(2,1)S(1)} %convert_element_type.102), channel_id=1, source_target_pairs={{0,1},{1,2},{2,3},{3,4},{4,5},{5,6},{6,7},{7,8},{8,9},{9,10},{10,1... | collective-permute-start | bytes 393224 | tf_op jit(solution)/shard_map/while/body/eval_jaxpr/ppermute | solution.py:19
  345.0 9.4 %collective-permute-start = (bf16[128,512]{1,0:T(8,128)(2,1)S(1)}, bf16[128,512]{1,0:T(8,128)(2,1)S(1)}, u32[]{:S(2)}, u32[]{:S(2)}) collective-permute-start(bf16[128,512]{1,0:T(8,128)(2,1)S(1)} %convert_element_type.101), channel_id=1, source_target_pairs={{0,1},{1,2},{2,3},{3,4},{4,5},{5,6},{6,7},{7,8},{8,9},{9,10},{10,1... | collective-permute-start | bytes 393224 | tf_op jit(solution)/shard_map/while/body/eval_jaxpr/ppermute | solution.py:19
  347.0 9.5 %collective-permute-start.1 = (bf16[128,512]{1,0:T(8,128)(2,1)S(1)}, bf16[128,512]{1,0:T(8,128)(2,1)S(1)}, u32[]{:S(2)}, u32[]{:S(2)}) collective-permute-start(bf16[128,512]{1,0:T(8,128)(2,1)S(1)} %convert_element_type.102), channel_id=1, source_target_pairs={{0,1},{1,2},{2,3},{3,4},{4,5},{5,6},{6,7},{7,8},{8,9},{9,10},{10,1... | collective-permute-start | bytes 393224 | tf_op jit(solution)/shard_map/while/body/eval_jaxpr/ppermute | solution.py:19
  356.5 9.0 %collective-permute-start = (bf16[128,512]{1,0:T(8,128)(2,1)S(1)}, bf16[128,512]{1,0:T(8,128)(2,1)S(1)}, u32[]{:S(2)}, u32[]{:S(2)}) collective-permute-start(bf16[128,512]{1,0:T(8,128)(2,1)S(1)} %convert_element_type.101), channel_id=1, source_target_pairs={{0,1},{1,2},{2,3},{3,4},{4,5},{5,6},{6,7},{7,8},{8,9},{9,10},{10,1... | collective-permute-start | bytes 393224 | tf_op jit(solution)/shard_map/while/body/eval_jaxpr/ppermute | solution.py:19
  360.0 8.1 %collective-permute-start.1 = (bf16[128,512]{1,0:T(8,128)(2,1)S(1)}, bf16[128,512]{1,0:T(8,128)(2,1)S(1)}, u32[]{:S(2)}, u32[]{:S(2)}) collective-permute-start(bf16[128,512]{1,0:T(8,128)(2,1)S(1)} %convert_element_type.102), channel_id=1, source_target_pairs={{0,1},{1,2},{2,3},{3,4},{4,5},{5,6},{6,7},{7,8},{8,9},{9,10},{10,1... | collective-permute-start | bytes 393224 | tf_op jit(solution)/shard_map/while/body/eval_jaxpr/ppermute | solution.py:19
  368.1 8.3 %collective-permute-start = (bf16[128,512]{1,0:T(8,128)(2,1)S(1)}, bf16[128,512]{1,0:T(8,128)(2,1)S(1)}, u32[]{:S(2)}, u32[]{:S(2)}) collective-permute-start(bf16[128,512]{1,0:T(8,128)(2,1)S(1)} %convert_element_type.101), channel_id=1, source_target_pairs={{0,1},{1,2},{2,3},{3,4},{4,5},{5,6},{6,7},{7,8},{8,9},{9,10},{10,1... | collective-permute-start | bytes 393224 | tf_op jit(solution)/shard_map/while/body/eval_jaxpr/ppermute | solution.py:19
  371.1 8.1 %collective-permute-start.1 = (bf16[128,512]{1,0:T(8,128)(2,1)S(1)}, bf16[128,512]{1,0:T(8,128)(2,1)S(1)}, u32[]{:S(2)}, u32[]{:S(2)}) collective-permute-start(bf16[128,512]{1,0:T(8,128)(2,1)S(1)} %convert_element_type.102), channel_id=1, source_target_pairs={{0,1},{1,2},{2,3},{3,4},{4,5},{5,6},{6,7},{7,8},{8,9},{9,10},{10,1... | collective-permute-start | bytes 393224 | tf_op jit(solution)/shard_map/while/body/eval_jaxpr/ppermute | solution.py:19
  379.2 8.5 %collective-permute-start = (bf16[128,512]{1,0:T(8,128)(2,1)S(1)}, bf16[128,512]{1,0:T(8,128)(2,1)S(1)}, u32[]{:S(2)}, u32[]{:S(2)}) collective-permute-start(bf16[128,512]{1,0:T(8,128)(2,1)S(1)} %convert_element_type.101), channel_id=1, source_target_pairs={{0,1},{1,2},{2,3},{3,4},{4,5},{5,6},{6,7},{7,8},{8,9},{9,10},{10,1... | collective-permute-start | bytes 393224 | tf_op jit(solution)/shard_map/while/body/eval_jaxpr/ppermute | solution.py:19
  382.2 8.1 %collective-permute-start.1 = (bf16[128,512]{1,0:T(8,128)(2,1)S(1)}, bf16[128,512]{1,0:T(8,128)(2,1)S(1)}, u32[]{:S(2)}, u32[]{:S(2)}) collective-permute-start(bf16[128,512]{1,0:T(8,128)(2,1)S(1)} %convert_element_type.102), channel_id=1, source_target_pairs={{0,1},{1,2},{2,3},{3,4},{4,5},{5,6},{6,7},{7,8},{8,9},{9,10},{10,1... | collective-permute-start | bytes 393224 | tf_op jit(solution)/shard_map/while/body/eval_jaxpr/ppermute | solution.py:19
  390.3 8.2 %collective-permute-start = (bf16[128,512]{1,0:T(8,128)(2,1)S(1)}, bf16[128,512]{1,0:T(8,128)(2,1)S(1)}, u32[]{:S(2)}, u32[]{:S(2)}) collective-permute-start(bf16[128,512]{1,0:T(8,128)(2,1)S(1)} %convert_element_type.101), channel_id=1, source_target_pairs={{0,1},{1,2},{2,3},{3,4},{4,5},{5,6},{6,7},{7,8},{8,9},{9,10},{10,1... | collective-permute-start | bytes 393224 | tf_op jit(solution)/shard_map/while/body/eval_jaxpr/ppermute | solution.py:19
  393.3 8.1 %collective-permute-start.1 = (bf16[128,512]{1,0:T(8,128)(2,1)S(1)}, bf16[128,512]{1,0:T(8,128)(2,1)S(1)}, u32[]{:S(2)}, u32[]{:S(2)}) collective-permute-start(bf16[128,512]{1,0:T(8,128)(2,1)S(1)} %convert_element_type.102), channel_id=1, source_target_pairs={{0,1},{1,2},{2,3},{3,4},{4,5},{5,6},{6,7},{7,8},{8,9},{9,10},{10,1... | collective-permute-start | bytes 393224 | tf_op jit(solution)/shard_map/while/body/eval_jaxpr/ppermute | solution.py:19
  401.4 0.7 copy-start
  401.4 0.8 copy-start.1
Sparse Core Ops, SparseCore 0:
  10.6 82.9 all-gather.4
  96.1 75.1 all-gather.2
where the time goes:
time: 412 us; the launch traced here: 409 us
  waiting for transfers between devices  228 us (55%)
  starting transfers between devices  104 us (25%)
  local copies, waits for them, and re-layouts  41.2 us (10%)
  between operations  16.8 us (4%)
  matrix products  8.91 us (2%)
  other arithmetic  7.82 us (2%)
    ppermute x30, starting transfers between devices, from_behind(): return lax.ppermute(x, axis, [(i, (i + by) % peers) for i in range(peers)])  104 us
    ppermute x30, waiting for transfers between devices, from_behind(): return lax.ppermute(x, axis, [(i, (i + by) % peers) for i in range(peers)])  78.8 us
    all_gather x1, waiting for transfers between devices, local(): lax.all_gather(keys, 'ctx', axis=0, tiled=True)  75 us
    all_gather x1, waiting for transfers between devices, local(): lax.all_gather(values, 'ctx', axis=0, tiled=True)  74.4 us
    dynamic_slice x46, local copies, waits for them, and re-layouts, pick_block(): return lax.dynamic_slice_in_dim(buffer, block_id * tok_rows, tok_rows, 0)  21 us
  transfers between devices with their start and end apart: 32, of which 26 were waited for; matrix products, arithmetic and copies ran while one was open for 8% of the time, Pallas kernels for 0%

commit v1 on v0

v1 whole, which is shorter than its diff:
```python
import math

import jax
import jax.numpy as jnp
from jax import lax
from jax.experimental import pallas as pl
from jax.experimental.pallas import tpu as pltpu
from jax.sharding import PartitionSpec as P

KVH = 4
HD = 128
GROUP = 4
CHUNK = 256

neg_big = -1e30


def dot_nt(a, b):
    return lax.dot_general(a, b, (((1,), (1,)), ((), ())), preferred_element_type=jnp.float32)


def dot_nn(a, b):
    return lax.dot_general(a, b, (((1,), (0,)), ((), ())), preferred_element_type=jnp.float32)


def dot_tn(a, b):
    return lax.dot_general(a, b, (((0,), (0,)), ((), ())), preferred_element_type=jnp.float32)


def heads_of(ref, g):
    base = g * GROUP * HD
    return jnp.concatenate(
        [ref[:, base + r * HD : base + (r + 1) * HD] for r in range(GROUP)], axis=0
    )


def attend_kernel(
    bounds, first_ref, q_ref, g_ref, kv_ref, out_ref, gq_ref, gkv_ref,
    s_ref, e_ref, acc_ref, stat_ref, low_ref,
):
    rows = q_ref.shape[0]
    stacked = rows * GROUP
    wide = KVH * HD
    scale = 1.0 / math.sqrt(HD)
    to_two = scale / math.log(2.0)
    q_start, low, high, clear_from = bounds[0], bounds[1], bounds[2], bounds[3]
    first = jnp.concatenate([first_ref[...]] * GROUP, axis=0)
    q_place = q_start + jnp.bitwise_and(
        lax.broadcasted_iota(jnp.int32, (stacked, CHUNK), 0), rows - 1
    )
    lanes = lax.broadcasted_iota(jnp.int32, (stacked, CHUNK), 1)

    gkv_ref[...] = jnp.zeros_like(gkv_ref)
    stat_ref[...] = jnp.full(stat_ref.shape, neg_big, jnp.float32)

    def scores_step(c, carry):
        at = pl.multiple_of(c * CHUNK, CHUNK)
        for g in range(KVH):
            k_block = kv_ref[pl.ds(at, CHUNK), g * HD : (g + 1) * HD]
            s_ref[g, c] = dot_nt(heads_of(q_ref, g), k_block)

        @pl.when((at < clear_from) | (at + CHUNK > q_start))
        def _():
            k_place = at + lanes
            allowed = (k_place >= first) & (k_place <= q_place)
            for g in range(KVH):
                s_ref[g, c] = jnp.where(allowed, s_ref[g, c], neg_big)

        for g in range(KVH):
            s = s_ref[g, c]
            stat_ref[g] = jnp.maximum(stat_ref[g], jnp.maximum(s[:, :HD], s[:, HD:]))
        return carry

    lax.fori_loop(low, high, scores_step, 0)

    tops = []
    for g in range(KVH):
        tops.append(jnp.max(stat_ref[g], axis=1, keepdims=True) * to_two)
        stat_ref[g] = jnp.broadcast_to(tops[g], (stacked, HD))
        acc_ref[g] = jnp.zeros((stacked, HD), jnp.float32)
        low_ref[g] = jnp.zeros((stacked, HD), jnp.float32)

    def value_step(c, carry):
        at = pl.multiple_of(c * CHUNK, CHUNK)
        for g in range(KVH):
            v_block = kv_ref[pl.ds(at, CHUNK), wide + g * HD : wide + (g + 1) * HD]
            top = stat_ref[g]
            e = jnp.exp2(s_ref[g, c] * to_two - jnp.concatenate([top, top], axis=1))
            low_ref[g] = low_ref[g] + (e[:, :HD] + e[:, HD:])
            e_low = e.astype(jnp.bfloat16)
            e_ref[g, c] = e_low
            acc_ref[g] = acc_ref[g] + dot_nn(e_low, v_block)
        return carry

    lax.fori_loop(low, high, value_step, 0)

    for g in range(KVH):
        inverse = 1.0 / jnp.sum(low_ref[g], axis=1, keepdims=True)
        attended = acc_ref[g] * inverse
        grads = (heads_of(g_ref, g).astype(jnp.float32) * inverse).astype(jnp.bfloat16)
        inner = jnp.sum(grads.astype(jnp.float32) * attended, axis=1, keepdims=True)
        stat_ref[g] = jnp.broadcast_to(inner, (stacked, HD))
        acc_ref[g] = jnp.zeros((stacked, HD), jnp.float32)
        for r in range(GROUP):
            cols = slice((g * GROUP + r) * HD, (g * GROUP + r + 1) * HD)
            out_ref[:, cols] = attended[r * rows : (r + 1) * rows].astype(jnp.bfloat16)
            gq_ref[:, cols] = grads[r * rows : (r + 1) * rows]

    def backward_step(c, carry):
        at = pl.multiple_of(c * CHUNK, CHUNK)
        for g in range(KVH):
            keys_at, values_at = slice(g * HD, (g + 1) * HD), slice(wide + g * HD, wide + (g + 1) * HD)
            k_block = kv_ref[pl.ds(at, CHUNK), keys_at]
            v_block = kv_ref[pl.ds(at, CHUNK), values_at]
            grads = heads_of(gq_ref, g)
            inner = stat_ref[g]
            e_low = e_ref[g, c]
            grad_probs = dot_nt(grads, v_block) - jnp.concatenate([inner, inner], axis=1)
            grad_scores = (e_low.astype(jnp.float32) * grad_probs).astype(jnp.bfloat16)
            acc_ref[g] = acc_ref[g] + dot_nn(grad_scores, k_block)
            grad_k = dot_tn(grad_scores, heads_of(q_ref, g)) * scale
            grad_v = dot_tn(e_low, grads)
            gkv_ref[pl.ds(at, CHUNK), keys_at] = grad_k.astype(gkv_ref.dtype)
            gkv_ref[pl.ds(at, CHUNK), values_at] = grad_v.astype(gkv_ref.dtype)
        return carry

    lax.fori_loop(low, high, backward_step, 0)

    for g in range(KVH):
        for r in range(GROUP):
            cols = slice((g * GROUP + r) * HD, (g * GROUP + r + 1) * HD)
            gq_ref[:, cols] = (acc_ref[g, r * rows : (r + 1) * rows] * scale).astype(jnp.bfloat16)


def attend(bounds, first, queries, out_grad, kv_all):
    rows = queries.shape[0]
    all_rows = kv_all.shape[0]
    stacked = rows * GROUP
    chunks = all_rows // CHUNK
    in_vmem = pl.BlockSpec(memory_space=pltpu.VMEM)
    return pl.pallas_call(
        attend_kernel,
        out_shape=(
            jax.ShapeDtypeStruct(queries.shape, jnp.bfloat16),
            jax.ShapeDtypeStruct(queries.shape, jnp.bfloat16),
            jax.ShapeDtypeStruct(kv_all.shape, jnp.bfloat16),
        ),
        in_specs=[pl.BlockSpec(memory_space=pltpu.SMEM)] + [in_vmem] * 4,
        out_specs=(in_vmem, in_vmem, in_vmem),
        scratch_shapes=[
            pltpu.VMEM((KVH, chunks, stacked, CHUNK), jnp.float32),
            pltpu.VMEM((KVH, chunks, stacked, CHUNK), jnp.bfloat16),
            pltpu.VMEM((KVH, stacked, HD), jnp.float32),
            pltpu.VMEM((KVH, stacked, HD), jnp.float32),
            pltpu.VMEM((KVH, stacked, HD), jnp.float32),
        ],
        compiler_params=pltpu.CompilerParams(vmem_limit_bytes=56 * 1024 * 1024),
        cost_estimate=pl.CostEstimate(
            flops=6 * 2 * rows * all_rows * KVH * GROUP * HD,
            bytes_accessed=12 * 1024 * 1024,
            transcendentals=rows * all_rows * KVH * GROUP,
        ),
    )(bounds, first, queries, out_grad, kv_all)


def local(queries, keys, values, out_grad, segment_ids):
    rows = queries.shape[0]
    my_index = lax.axis_index("ctx")
    kv_all = lax.all_gather(jnp.concatenate([keys, values], axis=1), "ctx", axis=0, tiled=True)
    q_start = my_index * rows
    q_seg = lax.dynamic_slice_in_dim(segment_ids, q_start, rows, 0)
    first = jnp.sum((segment_ids[None, :] < q_seg[:, None]).astype(jnp.int32), axis=1, keepdims=True)
    bounds = jnp.stack(
        [q_start, first[0, 0] // CHUNK, (q_start + rows - 1) // CHUNK + 1, first[rows - 1, 0]]
    ).astype(jnp.int32)
    attended, grad_query, grad_kv = attend(bounds, first, queries, out_grad, kv_all)
    summed = lax.psum_scatter(grad_kv, "ctx", scatter_dimension=0, tiled=True).astype(jnp.float32)
    half = KVH * HD
    return (attended, grad_query, summed[:, :half], summed[:, half:])


def solution(mesh):
    placed = P(("dp", "ctx"), None)
    return jax.shard_map(
        local,
        mesh=mesh,
        in_specs=(placed, placed, placed, placed, P("dp")),
        out_specs=(placed, placed, placed, placed),
        check_vma=False,
    )
```

time: 412 us -> 204 us (0.50)
  starting transfers between devices: 104 us -> 0.08 us
  waiting for transfers between devices: 228 us -> 168 us
  local copies, waits for them, and re-layouts: 41.2 us -> 3.91 us
  Pallas kernels: 0 us -> 9.6 us
  matrix products: 8.91 us -> 0 us
    ppermute x30 -> x0, starting transfers between devices: 104 us -> none  [from_behind(): return lax.ppermute(x, axis, [(i, (i + by) % peers) for i in range(peers)])]
    reduce_scatter x0 -> x1, waiting for transfers between devices: none -> 90.6 us  [local(): lax.psum_scatter(grad_kv, 'ctx', scatter_dimension=0, tiled=True)]
    ppermute x30 -> x0, waiting for transfers between devices: 78.8 us -> none  [from_behind(): return lax.ppermute(x, axis, [(i, (i + by) % peers) for i in range(peers)])]
    all_gather x2 -> x1, waiting for transfers between devices: 149 us -> 77.9 us  [local(): lax.all_gather(jnp.concatenate([keys, values], axis=1), 'ctx', axis=0, ti...]
    dynamic_slice x54 -> x1, local copies, waits for them, and re-layouts: 26.6 us -> 0.76 us  [local(): q_seg = lax.dynamic_slice_in_dim(segment_ids, q_start, rows, 0)]
    pallas_call x0 -> x1, Pallas kernels: none -> 9.6 us  [attend(): pl.pallas_call(attend_kernel, out_shape=(jax.ShapeDtypeStruct(queries.sha...]
    dot_general x7 -> x0, matrix products: 8.91 us -> none  [the longest x1 2.96 us: value_step(): jnp.einsum('grqk,kgd->qgrd', probs.astype(jnp.bfloat16), v_block, preferr...]
    unnamed x14 -> x0, local copies, waits for them, and re-layouts: 7.22 us -> none
  transfers between devices with their start and end apart: 32 -> 2, of which waited for: 26 -> 2; matrix products, arithmetic and copies ran while one was open for 8% -> 2% of each run, Pallas kernels for 0% -> 0%
where the time goes in v1:
time: 204 us; the launch traced here: 203 us
  waiting for transfers between devices  168 us (82%)
  between operations  16.7 us (8%)
  Pallas kernels  9.6 us (5%)
  local copies, waits for them, and re-layouts  3.91 us (2%)
  other arithmetic  3.84 us (2%)
    reduce_scatter x1, waiting for transfers between devices, local(): lax.psum_scatter(grad_kv, 'ctx', scatter_dimension=0, tiled=True)  90.6 us
    all_gather x1, waiting for transfers between devices, local(): lax.all_gather(jnp.concatenate([keys, values], axis=1), 'ctx', axis=0, ti...  77.9 us
    pallas_call x1, Pallas kernels, attend(): pl.pallas_call(attend_kernel, out_shape=(jax.ShapeDtypeStruct(queries.sha...  9.6 us
  transfers between devices with their start and end apart: 2, of which 2 were waited for; matrix products, arithmetic and copies ran while one was open for 2% of the time, Pallas kernels for 0%

profile of v1, /device:TPU:24, one launch (start us, length us, event | category | flops | bytes accessed | tf_op | source)
XLA Modules:
  0.0 202.6 jit_solution(13012076410955503667)
XLA Ops:
  7.2 0.0 all-gather.2.cloned.1.call-start
  7.2 1.7 pad_maximum_fusion
  8.9 0.0 all-gather.2.cloned.1.call-update
  8.9 0.0 reduce-scatter.2.cloned.1.call-start
  9.0 0.8 dynamic_slice.3
  9.7 0.9 convert_reduce_fusion
  10.7 0.6 fusion.1
  13.9 0.7 copy.10.first_ref
  14.6 1.2 pad_add_fusion.bounds
  15.8 77.9 %all-gather.2.cloned.1.call-done.kv_ref = bf16[2048,1024]{1,0:T(8,128)(2,1)} async-done(((bf16[128,1024]{1,0:T(8,128)(2,1)}), bf16[2048,1024]{1,0:T(8,128)(2,1)}) %all-gather.2.cloned.1.call-update) | async-done | bytes 4194320 | tf_op jit(solution)/shard_map/all_gather | solution.py:169
  93.7 9.6 %shard_map.84 = (bf16[128,2048]{1,0:T(8,128)(2,1)}, bf16[128,2048]{1,0:T(8,128)(2,1)}, bf16[2048,1024]{1,0:T(8,128)(2,1)}) custom-call(s32[4]{0:T(128)} %pad_add_fusion.bounds, s32[128,1]{1,0:T(8,128)} %copy.10.first_ref, bf16[128,2048]{1,0:T(8,128)(2,1)} %q_ref.1, bf16[128,2048]{1,0:T(8,128)(2,1)} %g_ref.1, ...), custom_call_target="tpu_custom_call" | custom-call | flops 6442450944 | bytes 12582912 | tf_op jit(solution)/shard_map/pallas_call | solution.py:141
  103.3 0.0 reduce-scatter.2.cloned.1.call-update
  103.3 90.6 %reduce-scatter.2.cloned.1.call-done = bf16[128,1024]{1,0:T(8,128)(2,1)} async-done(((bf16[2048,1024]{1,0:T(8,128)(2,1)}), bf16[128,1024]{1,0:T(8,128)(2,1)}) %reduce-scatter.2.cloned.1.call-update) | async-done | bytes 262160 | tf_op jit(solution)/shard_map/reduce_scatter | solution.py:177
  193.9 1.8 fusion
Async XLA Ops:
  7.2 86.5 %all-gather.2.cloned.1.call-start = ((), (), s32[]{:S(2)}) async-start(), calls=%async_computation.1 | async-start | bytes 4456448 | tf_op jit(solution)/shard_map/all_gather | solution.py:169
  8.9 185.0 %reduce-scatter.2.cloned.1.call-start = ((), (), s32[]{:S(2)}) async-start(), calls=%async_computation.2 | async-start | bytes 4456448 | tf_op jit(solution)/shard_map/reduce_scatter | solution.py:177
Sparse Core Ops, SparseCore 0:
  10.7 82.9 all-gather.1
  103.4 90.4 reduce-scatter.1

commit v2 on v1

v2 whole, which is shorter than its diff:
```python
import math

import jax
import jax.numpy as jnp
from jax import lax
from jax.experimental import pallas as pl
from jax.experimental.pallas import tpu as pltpu
from jax.sharding import PartitionSpec as P

KVH = 4
HD = 128
GROUP = 4
WIDE = KVH * HD
CHUNK = 256
FAR = 12
NEAR = 7
SLOTS = 14

neg_big = -1e30


def dot_nt(a, b):
    return lax.dot_general(a, b, (((1,), (1,)), ((), ())), preferred_element_type=jnp.float32)


def dot_nn(a, b):
    return lax.dot_general(a, b, (((1,), (0,)), ((), ())), preferred_element_type=jnp.float32)


def dot_tn(a, b):
    return lax.dot_general(a, b, (((0,), (0,)), ((), ())), preferred_element_type=jnp.float32)


def heads_of(ref, g):
    base = g * GROUP * HD
    return jnp.concatenate(
        [ref[:, base + r * HD : base + (r + 1) * HD] for r in range(GROUP)], axis=0
    )


def attend_kernel(bounds, first_ref, q_ref, g_ref, *rest):
    blocks = rest[: FAR + 1]
    out_ref, gq_ref = rest[FAR + 1 : FAR + 3]
    grads_out = rest[FAR + 3 : 2 * FAR + 4]
    kv_ref, gkv_ref, s_ref, e_ref, acc_ref, stat_ref, low_ref, in_sem, out_sem = rest[2 * FAR + 4 :]
    rows = q_ref.shape[0]
    stacked = rows * GROUP
    scale = 1.0 / math.sqrt(HD)
    to_two = scale / math.log(2.0)
    q_start, high, clear_from = bounds[0], bounds[1], bounds[2]

    copies = [
        pltpu.make_async_copy(block, kv_ref.at[pl.ds(r * rows, rows)], in_sem.at[r])
        for r, block in enumerate(blocks)
    ]
    for copy in copies:
        copy.start()
    kv_ref[(FAR + 1) * rows :, :] = jnp.zeros(((SLOTS - FAR - 1) * rows, 2 * WIDE), jnp.bfloat16)
    gkv_ref[...] = jnp.zeros_like(gkv_ref)
    stat_ref[...] = jnp.full(stat_ref.shape, neg_big, jnp.float32)
    first = jnp.concatenate([first_ref[...]] * GROUP, axis=0)
    q_place = q_start + jnp.bitwise_and(
        lax.broadcasted_iota(jnp.int32, (stacked, CHUNK), 0), rows - 1
    )
    lanes = lax.broadcasted_iota(jnp.int32, (stacked, CHUNK), 1)
    lanes = jnp.where(lanes < rows, lanes, lanes - 2 * rows)
    for copy in copies:
        copy.wait()

    def scores_step(c, carry):
        at = pl.multiple_of(c * CHUNK, CHUNK)
        for g in range(KVH):
            k_block = kv_ref[pl.ds(at, CHUNK), g * HD : (g + 1) * HD]
            s_ref[g, c] = dot_nt(heads_of(q_ref, g), k_block)

        @pl.when((q_start - at - rows < clear_from) | (c == 0))
        def _():
            k_place = (q_start - at) + lanes
            allowed = (k_place >= first) & (k_place <= q_place)
            for g in range(KVH):
                s_ref[g, c] = jnp.where(allowed, s_ref[g, c], neg_big)

        for g in range(KVH):
            s = s_ref[g, c]
            stat_ref[g] = jnp.maximum(stat_ref[g], jnp.maximum(s[:, :HD], s[:, HD:]))
        return carry

    lax.fori_loop(0, high, scores_step, 0)

    for g in range(KVH):
        top = jnp.max(stat_ref[g], axis=1, keepdims=True) * to_two
        stat_ref[g] = jnp.broadcast_to(top, (stacked, HD))
        acc_ref[g] = jnp.zeros((stacked, HD), jnp.float32)
        low_ref[g] = jnp.zeros((stacked, HD), jnp.float32)

    def value_step(c, carry):
        at = pl.multiple_of(c * CHUNK, CHUNK)
        for g in range(KVH):
            v_block = kv_ref[pl.ds(at, CHUNK), WIDE + g * HD : WIDE + (g + 1) * HD]
            top = stat_ref[g]
            e = jnp.exp2(s_ref[g, c] * to_two - jnp.concatenate([top, top], axis=1))
            low_ref[g] = low_ref[g] + (e[:, :HD] + e[:, HD:])
            e_low = e.astype(jnp.bfloat16)
            e_ref[g, c] = e_low
            acc_ref[g] = acc_ref[g] + dot_nn(e_low, v_block)
        return carry

    lax.fori_loop(0, high, value_step, 0)

    for g in range(KVH):
        inverse = 1.0 / jnp.sum(low_ref[g], axis=1, keepdims=True)
        attended = acc_ref[g] * inverse
        grads = (heads_of(g_ref, g).astype(jnp.float32) * inverse).astype(jnp.bfloat16)
        inner = jnp.sum(grads.astype(jnp.float32) * attended, axis=1, keepdims=True)
        stat_ref[g] = jnp.broadcast_to(inner, (stacked, HD))
        acc_ref[g] = jnp.zeros((stacked, HD), jnp.float32)
        for r in range(GROUP):
            cols = slice((g * GROUP + r) * HD, (g * GROUP + r + 1) * HD)
            out_ref[:, cols] = attended[r * rows : (r + 1) * rows].astype(jnp.bfloat16)
            gq_ref[:, cols] = grads[r * rows : (r + 1) * rows]

    def backward_step(c, carry):
        at = pl.multiple_of(c * CHUNK, CHUNK)
        for g in range(KVH):
            keys_at, values_at = slice(g * HD, (g + 1) * HD), slice(WIDE + g * HD, WIDE + (g + 1) * HD)
            k_block = kv_ref[pl.ds(at, CHUNK), keys_at]
            v_block = kv_ref[pl.ds(at, CHUNK), values_at]
            grads = heads_of(gq_ref, g)
            inner = stat_ref[g]
            e_low = e_ref[g, c]
            grad_probs = dot_nt(grads, v_block) - jnp.concatenate([inner, inner], axis=1)
            grad_scores = (e_low.astype(jnp.float32) * grad_probs).astype(jnp.bfloat16)
            acc_ref[g] = acc_ref[g] + dot_nn(grad_scores, k_block)
            grad_k = dot_tn(grad_scores, heads_of(q_ref, g)) * scale
            grad_v = dot_tn(e_low, grads)
            gkv_ref[pl.ds(at, CHUNK), keys_at] = grad_k.astype(gkv_ref.dtype)
            gkv_ref[pl.ds(at, CHUNK), values_at] = grad_v.astype(gkv_ref.dtype)
        return carry

    lax.fori_loop(0, high, backward_step, 0)

    copies = [
        pltpu.make_async_copy(gkv_ref.at[pl.ds(r * rows, rows)], grad, out_sem.at[r])
        for r, grad in enumerate(grads_out)
    ]
    for copy in copies:
        copy.start()
    for g in range(KVH):
        for r in range(GROUP):
            cols = slice((g * GROUP + r) * HD, (g * GROUP + r + 1) * HD)
            gq_ref[:, cols] = (acc_ref[g, r * rows : (r + 1) * rows] * scale).astype(jnp.bfloat16)
    for copy in copies:
        copy.wait()


def attend(bounds, first, queries, out_grad, blocks):
    rows = queries.shape[0]
    stacked = rows * GROUP
    chunks = SLOTS * rows // CHUNK
    in_vmem = pl.BlockSpec(memory_space=pltpu.VMEM)
    anywhere = pl.BlockSpec(memory_space=pl.ANY)
    results = pl.pallas_call(
        attend_kernel,
        out_shape=[jax.ShapeDtypeStruct(queries.shape, jnp.bfloat16)] * 2
        + [jax.ShapeDtypeStruct(blocks[0].shape, jnp.bfloat16)] * (FAR + 1),
        in_specs=[pl.BlockSpec(memory_space=pltpu.SMEM)] + [in_vmem] * 3 + [anywhere] * (FAR + 1),
        out_specs=[in_vmem] * 2 + [anywhere] * (FAR + 1),
        scratch_shapes=[
            pltpu.VMEM((SLOTS * rows, 2 * WIDE), jnp.bfloat16),
            pltpu.VMEM((SLOTS * rows, 2 * WIDE), jnp.bfloat16),
            pltpu.VMEM((KVH, chunks, stacked, CHUNK), jnp.float32),
            pltpu.VMEM((KVH, chunks, stacked, CHUNK), jnp.bfloat16),
            pltpu.VMEM((KVH, stacked, HD), jnp.float32),
            pltpu.VMEM((KVH, stacked, HD), jnp.float32),
            pltpu.VMEM((KVH, stacked, HD), jnp.float32),
            pltpu.SemaphoreType.DMA((FAR + 1,)),
            pltpu.SemaphoreType.DMA((FAR + 1,)),
        ],
        compiler_params=pltpu.CompilerParams(vmem_limit_bytes=56 * 1024 * 1024),
        cost_estimate=pl.CostEstimate(
            flops=6 * 2 * rows * SLOTS * rows * KVH * GROUP * HD,
            bytes_accessed=12 * 1024 * 1024,
            transcendentals=rows * SLOTS * rows * KVH * GROUP,
        ),
    )(bounds, first, queries, out_grad, *blocks)
    return results[0], results[1], results[2:]


def send(x, pairs):
    return lax.ppermute(x, "ctx", pairs)


def gather_blocks(own, count):
    back = {0: own}
    wrapped = range(count - NEAR - 1)
    for step in range(1, max(NEAR, FAR - NEAR) + 1):
        if step <= NEAR:
            back[step] = send(back[step - 1], [(j, j + 1) for j in range(step - 1, count - 1)])
        r = FAR + 1 - step
        if r > NEAR:
            by = count - FAR if step == 1 else 1
            back[r] = send(
                own if step == 1 else back[r + 1],
                [((b + r + by) % count, (b + r) % count) for b in wrapped],
            )
    return [back[r] for r in range(FAR + 1)]


def add_low(a, b):
    return (a.astype(jnp.float32) + b.astype(jnp.float32)).astype(jnp.bfloat16)


def return_sums(terms, count):
    wrapped = range(count - NEAR - 1)
    near, far = terms[NEAR], terms[NEAR + 1]
    for step in range(1, max(NEAR, FAR - NEAR) + 1):
        r = NEAR + step
        if r <= FAR:
            by = count - FAR if r == FAR else 1
            far = send(far, [((b + r) % count, (b + r + by) % count) for b in wrapped])
            if r < FAR:
                far = add_low(far, terms[r + 1])
        if step <= NEAR:
            r = NEAR + 1 - step
            near = send(near, [(j, j - 1) for j in range(r, count)])
            if r > 1:
                near = add_low(near, terms[r - 1])
    return near, far


def local(queries, keys, values, out_grad, segment_ids):
    rows = queries.shape[0]
    count = lax.axis_size("ctx")
    q_start = lax.axis_index("ctx") * rows
    blocks = gather_blocks(jnp.concatenate([keys, values], axis=1), count)
    q_seg = lax.dynamic_slice_in_dim(segment_ids, q_start, rows, 0)
    first = jnp.sum((segment_ids[None, :] < q_seg[:, None]).astype(jnp.int32), axis=1, keepdims=True)
    high = (q_start + rows - first[0, 0] + CHUNK - 1) // CHUNK
    bounds = jnp.stack([q_start, high, first[rows - 1, 0]]).astype(jnp.int32)
    attended, grad_query, terms = attend(bounds, first, queries, out_grad, blocks)
    near, far = return_sums(terms, count)
    summed = near.astype(jnp.float32) + far.astype(jnp.float32) + terms[0].astype(jnp.float32)
    return (attended, grad_query, summed[:, :WIDE], summed[:, WIDE:])


def solution(mesh):
    placed = P(("dp", "ctx"), None)
    return jax.shard_map(
        local,
        mesh=mesh,
        in_specs=(placed, placed, placed, placed, P("dp")),
        out_specs=(placed, placed, placed, placed),
        check_vma=False,
    )
```

time: 204 us -> 202 us (level)
  starting transfers between devices: 0.08 us -> 53.9 us
  waiting for transfers between devices: 168 us -> 127 us
  between operations: 16.7 us -> 1.96 us
    ppermute x0 -> x24, waiting for transfers between devices: none -> 127 us  [send(): return lax.ppermute(x, 'ctx', pairs)]
    reduce_scatter x1 -> x0, waiting for transfers between devices: 90.6 us -> none  [local(): lax.psum_scatter(grad_kv, 'ctx', scatter_dimension=0, tiled=True)]
    all_gather x1 -> x0, waiting for transfers between devices: 77.9 us -> none  [local(): lax.all_gather(jnp.concatenate([keys, values], axis=1), 'ctx', axis=0, ti...]
    ppermute x0 -> x24, starting transfers between devices: none -> 53.9 us  [send(): return lax.ppermute(x, 'ctx', pairs)]
    unnamed x0 -> x53, local copies, waits for them, and re-layouts: none -> 2.35 us
  transfers between devices with their start and end apart: 2 -> 24, of which waited for: 2 -> 10; matrix products, arithmetic and copies ran while one was open for 2% -> 2% of each run, Pallas kernels for 0% -> 0%
where the time goes in v2:
time: 202 us; the launch traced here: 201 us
  waiting for transfers between devices  127 us (63%)
  starting transfers between devices  53.9 us (27%)
  Pallas kernels  10.3 us (5%)
  local copies, waits for them, and re-layouts  4.61 us (2%)
  other arithmetic  3.25 us (2%)
    ppermute x24, waiting for transfers between devices, send(): return lax.ppermute(x, 'ctx', pairs)  127 us
    ppermute x24, starting transfers between devices, send(): return lax.ppermute(x, 'ctx', pairs)  53.9 us
    pallas_call x1, Pallas kernels, attend(): pl.pallas_call(attend_kernel, out_shape=[jax.ShapeDtypeStruct(queries.sha...  10.3 us
  transfers between devices with their start and end apart: 24, of which 10 were waited for; matrix products, arithmetic and copies ran while one was open for 2% of the time, Pallas kernels for 0%

profile of v2, /device:TPU:24, one launch (start us, length us, event | category | flops | bytes accessed | tf_op | source)
XLA Modules:
  0.0 200.7 jit_solution(2165811571547560948)
XLA Ops:
  0.6 0.9 constant_dynamic-update-slice_fusion.1
  1.6 0.0 copy-done.10
  1.6 0.0 copy-start.11
  1.6 0.0 copy-start.12
  1.6 4.0 %collective-permute-start = (bf16[128,1024]{1,0:T(8,128)(2,1)S(1)}, bf16[128,1024]{1,0:T(8,128)(2,1)S(1)}, u32[]{:S(2)}, u32[]{:S(2)}) collective-permute-start(bf16[128,1024]{1,0:T(8,128)(2,1)S(1)} %constant_dynamic-update-slice_fusion.rest_0_), channel_id=1, source_target_pairs={{0,1},{1,2},{2,3},{3,4},{4,5},{5,6},{6,7},{7,8},{8,9},{9,10},{10,1... | collective-permute-start | bytes 786440 | tf_op jit(solution)/shard_map/ppermute | solution.py:190
  5.6 5.5 %collective-permute-done.rest_1_ = bf16[128,1024]{1,0:T(8,128)(2,1)S(1)} collective-permute-done((bf16[128,1024]{1,0:T(8,128)(2,1)S(1)}, bf16[128,1024]{1,0:T(8,128)(2,1)S(1)}, u32[]{:S(2)}, u32[]{:S(2)}) %collective-permute-start) | collective-permute-done | bytes 262176 | tf_op jit(solution)/shard_map/ppermute | solution.py:190
  11.2 0.7 collective-permute-start.1
  11.8 15.8 %collective-permute-start.7 = (bf16[128,1024]{1,0:T(8,128)(2,1)S(1)}, bf16[128,1024]{1,0:T(8,128)(2,1)S(1)}, u32[]{:S(2)}, u32[]{:S(2)}) collective-permute-start(bf16[128,1024]{1,0:T(8,128)(2,1)S(1)} %constant_dynamic-update-slice_fusion.rest_0_), channel_id=1, source_target_pairs={{0,12},{1,13},{2,14},{3,15},{4,0},{5,1},{6,2},{7,3},{16,28},{17,29... | collective-permute-start | bytes 786440 | tf_op jit(solution)/shard_map/ppermute | solution.py:190
  27.6 0.0 collective-permute-done.1.rest_2_
  27.6 0.7 collective-permute-start.2
  28.3 20.8 %collective-permute-done.7.rest_12_ = bf16[128,1024]{1,0:T(8,128)(2,1)S(1)} collective-permute-done((bf16[128,1024]{1,0:T(8,128)(2,1)S(1)}, bf16[128,1024]{1,0:T(8,128)(2,1)S(1)}, u32[]{:S(2)}, u32[]{:S(2)}) %collective-permute-start.7) | collective-permute-done | bytes 262176 | tf_op jit(solution)/shard_map/ppermute | solution.py:190
  49.1 1.9 collective-permute-start.8
  51.0 0.0 collective-permute-done.2.rest_3_
  51.0 0.7 collective-permute-start.3
  51.7 7.3 %collective-permute-done.8.rest_11_ = bf16[128,1024]{1,0:T(8,128)(2,1)S(1)} collective-permute-done((bf16[128,1024]{1,0:T(8,128)(2,1)S(1)}, bf16[128,1024]{1,0:T(8,128)(2,1)S(1)}, u32[]{:S(2)}, u32[]{:S(2)}) %collective-permute-start.8) | collective-permute-done | bytes 262176 | tf_op jit(solution)/shard_map/ppermute | solution.py:190
  59.1 3.4 %collective-permute-start.9 = (bf16[128,1024]{1,0:T(8,128)(2,1)S(1)}, bf16[128,1024]{1,0:T(8,128)(2,1)S(1)}, u32[]{:S(2)}, u32[]{:S(2)}) collective-permute-start(bf16[128,1024]{1,0:T(8,128)(2,1)S(1)} %collective-permute-done.8.rest_11_), channel_id=1, source_target_pairs={{11,10},{12,11},{13,12},{14,13},{15,14},{0,15},{1,0},{2,1},{27,26}... | collective-permute-start | bytes 786440 | tf_op jit(solution)/shard_map/ppermute | solution.py:190
  62.5 0.7 collective-permute-start.4
  63.2 5.0 %collective-permute-done.9.rest_10_ = bf16[128,1024]{1,0:T(8,128)(2,1)S(1)} collective-permute-done((bf16[128,1024]{1,0:T(8,128)(2,1)S(1)}, bf16[128,1024]{1,0:T(8,128)(2,1)S(1)}, u32[]{:S(2)}, u32[]{:S(2)}) %collective-permute-start.9) | collective-permute-done | bytes 262176 | tf_op jit(solution)/shard_map/ppermute | solution.py:190
  68.2 4.9 %collective-permute-start.10 = (bf16[128,1024]{1,0:T(8,128)(2,1)S(1)}, bf16[128,1024]{1,0:T(8,128)(2,1)S(1)}, u32[]{:S(2)}, u32[]{:S(2)}) collective-permute-start(bf16[128,1024]{1,0:T(8,128)(2,1)S(1)} %collective-permute-done.9.rest_10_), channel_id=1, source_target_pairs={{10,9},{11,10},{12,11},{13,12},{14,13},{15,14},{0,15},{1,0},{26,25... | collective-permute-start | bytes 786440 | tf_op jit(solution)/shard_map/ppermute | solution.py:190
  73.1 0.7 collective-permute-start.5
  73.8 0.1 dynamic_slice.3
  73.9 3.3 %collective-permute-done.10.rest_9_ = bf16[128,1024]{1,0:T(8,128)(2,1)S(1)} collective-permute-done((bf16[128,1024]{1,0:T(8,128)(2,1)S(1)}, bf16[128,1024]{1,0:T(8,128)(2,1)S(1)}, u32[]{:S(2)}, u32[]{:S(2)}) %collective-permute-start.10) | collective-permute-done | bytes 262176 | tf_op jit(solution)/shard_map/ppermute | solution.py:190
  77.2 5.6 %collective-permute-start.11 = (bf16[128,1024]{1,0:T(8,128)(2,1)S(1)}, bf16[128,1024]{1,0:T(8,128)(2,1)S(1)}, u32[]{:S(2)}, u32[]{:S(2)}) collective-permute-start(bf16[128,1024]{1,0:T(8,128)(2,1)S(1)} %collective-permute-done.10.rest_9_), channel_id=1, source_target_pairs={{9,8},{10,9},{11,10},{12,11},{13,12},{14,13},{15,14},{0,15},{25,24... | collective-permute-start | bytes 786440 | tf_op jit(solution)/shard_map/ppermute | solution.py:190
  82.8 0.7 collective-permute-start.6
  83.5 0.2 convert_reduce_fusion
  83.8 0.6 fusion.1
  85.0 0.7 copy.10.first_ref
  85.8 1.2 pad_add_fusion.bounds
  87.0 0.0 collective-permute-done.6.rest_7_
  87.1 0.6 copy-done.23
  87.7 0.7 copy-done.24
  88.4 10.3 %shard_map.84 = (bf16[128,2048]{1,0:T(8,128)(2,1)}, bf16[128,2048]{1,0:T(8,128)(2,1)}, bf16[128,1024]{1,0:T(8,128)(2,1)}, bf16[128,1024]{1,0:T(8,128)(2,1)}, bf1...) custom-call(s32[3]{0:T(128)} %pad_add_fusion.bounds, ...), custom_call_target="tpu_custom_call" | custom-call | flops 5637144576 | bytes 12582912 | tf_op jit(solution)/shard_map/pallas_call | solution.py:162
  98.7 0.7 collective-permute-start.12
  99.4 0.0 collective-permute-done.12
  99.4 1.1 add_convert_fusion.9
  100.5 0.7 collective-permute-start.13
  101.2 1.3 collective-permute-start.19
  102.5 0.0 collective-permute-done.13
  102.5 0.1 add_convert_fusion.8
  102.6 0.7 collective-permute-start.14
  103.3 38.9 %collective-permute-done.19 = bf16[128,1024]{1,0:T(8,128)(2,1)S(1)} collective-permute-done((bf16[128,1024]{1,0:T(8,128)(2,1)S(1)}, bf16[128,1024]{1,0:T(8,128)(2,1)S(1)}, u32[]{:S(2)}, u32[]{:S(2)}) %collective-permute-start.19) | collective-permute-done | bytes 262176 | tf_op jit(solution)/shard_map/ppermute | solution.py:190
  142.2 0.1 add_convert_fusion.3
  142.2 1.9 collective-permute-start.20
  144.2 0.1 add_convert_fusion.7
  144.3 0.7 collective-permute-start.15
  145.0 7.4 %collective-permute-done.20 = bf16[128,1024]{1,0:T(8,128)(2,1)S(1)} collective-permute-done((bf16[128,1024]{1,0:T(8,128)(2,1)S(1)}, bf16[128,1024]{1,0:T(8,128)(2,1)S(1)}, u32[]{:S(2)}, u32[]{:S(2)}) %collective-permute-start.20) | collective-permute-done | bytes 262176 | tf_op jit(solution)/shard_map/ppermute | solution.py:190
  152.4 0.1 add_convert_fusion.2
  152.5 1.9 collective-permute-start.21
  154.4 0.1 add_convert_fusion.6
  154.5 0.7 collective-permute-start.16
  155.2 6.8 %collective-permute-done.21 = bf16[128,1024]{1,0:T(8,128)(2,1)S(1)} collective-permute-done((bf16[128,1024]{1,0:T(8,128)(2,1)S(1)}, bf16[128,1024]{1,0:T(8,128)(2,1)S(1)}, u32[]{:S(2)}, u32[]{:S(2)}) %collective-permute-start.21) | collective-permute-done | bytes 262176 | tf_op jit(solution)/shard_map/ppermute | solution.py:190
  161.9 0.1 add_convert_fusion.1
  162.0 1.9 collective-permute-start.22
  163.9 0.0 collective-permute-done.16
  164.0 0.1 add_convert_fusion.5
  164.0 0.7 collective-permute-start.17
  164.7 22.8 %collective-permute-done.22 = bf16[128,1024]{1,0:T(8,128)(2,1)S(1)} collective-permute-done((bf16[128,1024]{1,0:T(8,128)(2,1)S(1)}, bf16[128,1024]{1,0:T(8,128)(2,1)S(1)}, u32[]{:S(2)}, u32[]{:S(2)}) %collective-permute-start.22) | collective-permute-done | bytes 262176 | tf_op jit(solution)/shard_map/ppermute | solution.py:190
  187.5 0.1 add_convert_fusion
  187.6 1.9 collective-permute-start.23
  189.6 0.1 add_convert_fusion.4
  189.6 1.3 collective-permute-start.18
  190.9 8.8 %collective-permute-done.23 = bf16[128,1024]{1,0:T(8,128)(2,1)S(1)} collective-permute-done((bf16[128,1024]{1,0:T(8,128)(2,1)S(1)}, bf16[128,1024]{1,0:T(8,128)(2,1)S(1)}, u32[]{:S(2)}, u32[]{:S(2)}) %collective-permute-start.23) | collective-permute-done | bytes 262176 | tf_op jit(solution)/shard_map/ppermute | solution.py:190
  199.8 0.1 convert_add_fusion
  199.9 0.8 fusion
  (56 shorter events, 0.1 us)
Async XLA Ops:
  0.6 1.0 copy-start.10
  1.6 85.4 %copy-start.11 = (bf16[128,1024]{1,0:T(8,128)(2,1)}, bf16[128,1024]{1,0:T(8,128)(2,1)S(1)}, u32[]{:S(2)}) copy-start(bf16[128,1024]{1,0:T(8,128)(2,1)S(1)} %constant_dynamic-update-slice_fusion.rest_0_) | copy-start | bytes 786436
  1.6 72.2 %copy-start.12 = (s32[2048]{0:T(1024)S(1)}, s32[2048]{0:T(1024)}, u32[]{:S(2)}) copy-start(s32[2048]{0:T(1024)} %param.9) | copy-start | bytes 24580
  1.6 9.5 %collective-permute-start = (bf16[128,1024]{1,0:T(8,128)(2,1)S(1)}, bf16[128,1024]{1,0:T(8,128)(2,1)S(1)}, u32[]{:S(2)}, u32[]{:S(2)}) collective-permute-start(bf16[128,1024]{1,0:T(8,128)(2,1)S(1)} %constant_dynamic-update-slice_fusion.rest_0_), channel_id=1, source_target_pairs={{0,1},{1,2},{2,3},{3,4},{4,5},{5,6},{6,7},{7,8},{8,9},{9,10},{10,1... | collective-permute-start | bytes 786440 | tf_op jit(solution)/shard_map/ppermute | solution.py:190
  11.2 75.9 %copy-start.13 = (bf16[128,1024]{1,0:T(8,128)(2,1)}, bf16[128,1024]{1,0:T(8,128)(2,1)S(1)}, u32[]{:S(2)}) copy-start(bf16[128,1024]{1,0:T(8,128)(2,1)S(1)} %collective-permute-done.rest_1_) | copy-start | bytes 786436
  11.2 16.4 %collective-permute-start.1 = (bf16[128,1024]{1,0:T(8,128)(2,1)S(1)}, bf16[128,1024]{1,0:T(8,128)(2,1)S(1)}, u32[]{:S(2)}, u32[]{:S(2)}) collective-permute-start(bf16[128,1024]{1,0:T(8,128)(2,1)S(1)} %collective-permute-done.rest_1_), channel_id=1, source_target_pairs={{1,2},{2,3},{3,4},{4,5},{5,6},{6,7},{7,8},{8,9},{9,10},{10,11},{11... | collective-permute-start | bytes 786440 | tf_op jit(solution)/shard_map/ppermute | solution.py:190
  11.8 37.3 %collective-permute-start.7 = (bf16[128,1024]{1,0:T(8,128)(2,1)S(1)}, bf16[128,1024]{1,0:T(8,128)(2,1)S(1)}, u32[]{:S(2)}, u32[]{:S(2)}) collective-permute-start(bf16[128,1024]{1,0:T(8,128)(2,1)S(1)} %constant_dynamic-update-slice_fusion.rest_0_), channel_id=1, source_target_pairs={{0,12},{1,13},{2,14},{3,15},{4,0},{5,1},{6,2},{7,3},{16,28},{17,29... | collective-permute-start | bytes 786440 | tf_op jit(solution)/shard_map/ppermute | solution.py:190
  27.6 59.4 %copy-start.14 = (bf16[128,1024]{1,0:T(8,128)(2,1)}, bf16[128,1024]{1,0:T(8,128)(2,1)S(1)}, u32[]{:S(2)}) copy-start(bf16[128,1024]{1,0:T(8,128)(2,1)S(1)} %collective-permute-done.1.rest_2_) | copy-start | bytes 786436
  27.6 23.4 %collective-permute-start.2 = (bf16[128,1024]{1,0:T(8,128)(2,1)S(1)}, bf16[128,1024]{1,0:T(8,128)(2,1)S(1)}, u32[]{:S(2)}, u32[]{:S(2)}) collective-permute-start(bf16[128,1024]{1,0:T(8,128)(2,1)S(1)} %collective-permute-done.1.rest_2_), channel_id=1, source_target_pairs={{2,3},{3,4},{4,5},{5,6},{6,7},{7,8},{8,9},{9,10},{10,11},{11,12},{... | collective-permute-start | bytes 786440 | tf_op jit(solution)/shard_map/ppermute | solution.py:190
  49.1 38.0 %copy-start.15 = (bf16[128,1024]{1,0:T(8,128)(2,1)}, bf16[128,1024]{1,0:T(8,128)(2,1)S(1)}, u32[]{:S(2)}) copy-start(bf16[128,1024]{1,0:T(8,128)(2,1)S(1)} %collective-permute-done.7.rest_12_) | copy-start | bytes 786436
  49.1 10.0 %collective-permute-start.8 = (bf16[128,1024]{1,0:T(8,128)(2,1)S(1)}, bf16[128,1024]{1,0:T(8,128)(2,1)S(1)}, u32[]{:S(2)}, u32[]{:S(2)}) collective-permute-start(bf16[128,1024]{1,0:T(8,128)(2,1)S(1)} %collective-permute-done.7.rest_12_), channel_id=1, source_target_pairs={{12,11},{13,12},{14,13},{15,14},{0,15},{1,0},{2,1},{3,2},{28,27},{... | collective-permute-start | bytes 786440 | tf_op jit(solution)/shard_map/ppermute | solution.py:190
  51.0 36.0 %copy-start.16 = (bf16[128,1024]{1,0:T(8,128)(2,1)}, bf16[128,1024]{1,0:T(8,128)(2,1)S(1)}, u32[]{:S(2)}) copy-start(bf16[128,1024]{1,0:T(8,128)(2,1)S(1)} %collective-permute-done.2.rest_3_) | copy-start | bytes 786436
  51.0 11.4 %collective-permute-start.3 = (bf16[128,1024]{1,0:T(8,128)(2,1)S(1)}, bf16[128,1024]{1,0:T(8,128)(2,1)S(1)}, u32[]{:S(2)}, u32[]{:S(2)}) collective-permute-start(bf16[128,1024]{1,0:T(8,128)(2,1)S(1)} %collective-permute-done.2.rest_3_), channel_id=1, source_target_pairs={{3,4},{4,5},{5,6},{6,7},{7,8},{8,9},{9,10},{10,11},{11,12},{12,13}... | collective-permute-start | bytes 786440 | tf_op jit(solution)/shard_map/ppermute | solution.py:190
  59.1 28.0 %copy-start.17 = (bf16[128,1024]{1,0:T(8,128)(2,1)}, bf16[128,1024]{1,0:T(8,128)(2,1)S(1)}, u32[]{:S(2)}) copy-start(bf16[128,1024]{1,0:T(8,128)(2,1)S(1)} %collective-permute-done.8.rest_11_) | copy-start | bytes 786436
  59.1 9.1 %collective-permute-start.9 = (bf16[128,1024]{1,0:T(8,128)(2,1)S(1)}, bf16[128,1024]{1,0:T(8,128)(2,1)S(1)}, u32[]{:S(2)}, u32[]{:S(2)}) collective-permute-start(bf16[128,1024]{1,0:T(8,128)(2,1)S(1)} %collective-permute-done.8.rest_11_), channel_id=1, source_target_pairs={{11,10},{12,11},{13,12},{14,13},{15,14},{0,15},{1,0},{2,1},{27,26}... | collective-permute-start | bytes 786440 | tf_op jit(solution)/shard_map/ppermute | solution.py:190
  62.5 24.6 %copy-start.18 = (bf16[128,1024]{1,0:T(8,128)(2,1)}, bf16[128,1024]{1,0:T(8,128)(2,1)S(1)}, u32[]{:S(2)}) copy-start(bf16[128,1024]{1,0:T(8,128)(2,1)S(1)} %collective-permute-done.3.rest_4_) | copy-start | bytes 786436
  62.5 10.6 %collective-permute-start.4 = (bf16[128,1024]{1,0:T(8,128)(2,1)S(1)}, bf16[128,1024]{1,0:T(8,128)(2,1)S(1)}, u32[]{:S(2)}, u32[]{:S(2)}) collective-permute-start(bf16[128,1024]{1,0:T(8,128)(2,1)S(1)} %collective-permute-done.3.rest_4_), channel_id=1, source_target_pairs={{4,5},{5,6},{6,7},{7,8},{8,9},{9,10},{10,11},{11,12},{12,13},{13,1... | collective-permute-start | bytes 786440 | tf_op jit(solution)/shard_map/ppermute | solution.py:190
  68.2 18.9 %copy-start.19 = (bf16[128,1024]{1,0:T(8,128)(2,1)}, bf16[128,1024]{1,0:T(8,128)(2,1)S(1)}, u32[]{:S(2)}) copy-start(bf16[128,1024]{1,0:T(8,128)(2,1)S(1)} %collective-permute-done.9.rest_10_) | copy-start | bytes 786436
  68.2 9.0 %collective-permute-start.10 = (bf16[128,1024]{1,0:T(8,128)(2,1)S(1)}, bf16[128,1024]{1,0:T(8,128)(2,1)S(1)}, u32[]{:S(2)}, u32[]{:S(2)}) collective-permute-start(bf16[128,1024]{1,0:T(8,128)(2,1)S(1)} %collective-permute-done.9.rest_10_), channel_id=1, source_target_pairs={{10,9},{11,10},{12,11},{13,12},{14,13},{15,14},{0,15},{1,0},{26,25... | collective-permute-start | bytes 786440 | tf_op jit(solution)/shard_map/ppermute | solution.py:190
  73.1 14.0 %copy-start.20 = (bf16[128,1024]{1,0:T(8,128)(2,1)}, bf16[128,1024]{1,0:T(8,128)(2,1)S(1)}, u32[]{:S(2)}) copy-start(bf16[128,1024]{1,0:T(8,128)(2,1)S(1)} %collective-permute-done.4.rest_5_) | copy-start | bytes 786436
  73.1 9.7 %collective-permute-start.5 = (bf16[128,1024]{1,0:T(8,128)(2,1)S(1)}, bf16[128,1024]{1,0:T(8,128)(2,1)S(1)}, u32[]{:S(2)}, u32[]{:S(2)}) collective-permute-start(bf16[128,1024]{1,0:T(8,128)(2,1)S(1)} %collective-permute-done.4.rest_5_), channel_id=1, source_target_pairs={{5,6},{6,7},{7,8},{8,9},{9,10},{10,11},{11,12},{12,13},{13,14},{14... | collective-permute-start | bytes 786440 | tf_op jit(solution)/shard_map/ppermute | solution.py:190
  77.2 9.9 %copy-start.21 = (bf16[128,1024]{1,0:T(8,128)(2,1)}, bf16[128,1024]{1,0:T(8,128)(2,1)S(1)}, u32[]{:S(2)}) copy-start(bf16[128,1024]{1,0:T(8,128)(2,1)S(1)} %collective-permute-done.10.rest_9_) | copy-start | bytes 786436
  77.2 9.8 %collective-permute-start.11 = (bf16[128,1024]{1,0:T(8,128)(2,1)S(1)}, bf16[128,1024]{1,0:T(8,128)(2,1)S(1)}, u32[]{:S(2)}, u32[]{:S(2)}) collective-permute-start(bf16[128,1024]{1,0:T(8,128)(2,1)S(1)} %collective-permute-done.10.rest_9_), channel_id=1, source_target_pairs={{9,8},{10,9},{11,10},{12,11},{13,12},{14,13},{15,14},{0,15},{25,24... | collective-permute-start | bytes 786440 | tf_op jit(solution)/shard_map/ppermute | solution.py:190
  82.8 4.3 %copy-start.22 = (bf16[128,1024]{1,0:T(8,128)(2,1)}, bf16[128,1024]{1,0:T(8,128)(2,1)S(1)}, u32[]{:S(2)}) copy-start(bf16[128,1024]{1,0:T(8,128)(2,1)S(1)} %collective-permute-done.5.rest_6_) | copy-start | bytes 786436
  82.8 4.2 %collective-permute-start.6 = (bf16[128,1024]{1,0:T(8,128)(2,1)S(1)}, bf16[128,1024]{1,0:T(8,128)(2,1)S(1)}, u32[]{:S(2)}, u32[]{:S(2)}) collective-permute-start(bf16[128,1024]{1,0:T(8,128)(2,1)S(1)} %collective-permute-done.5.rest_6_), channel_id=1, source_target_pairs={{6,7},{7,8},{8,9},{9,10},{10,11},{11,12},{12,13},{13,14},{14,15},{... | collective-permute-start | bytes 786440 | tf_op jit(solution)/shard_map/ppermute | solution.py:190
  87.0 0.7 copy-start.23
  87.7 0.7 copy-start.24
  98.7 0.7 collective-permute-start.12
  99.4 1.8 copy-start.25
  99.4 3.1 %copy-start.9 = (bf16[128,1024]{1,0:T(8,128)(2,1)S(1)}, bf16[128,1024]{1,0:T(8,128)(2,1)}, u32[]{:S(2)}) copy-start(bf16[128,1024]{1,0:T(8,128)(2,1)} %get-tuple-element.23) | copy-start | bytes 786436
  100.5 2.0 collective-permute-start.13
  101.2 41.0 %collective-permute-start.19 = (bf16[128,1024]{1,0:T(8,128)(2,1)S(1)}, bf16[128,1024]{1,0:T(8,128)(2,1)S(1)}, u32[]{:S(2)}, u32[]{:S(2)}) collective-permute-start(bf16[128,1024]{1,0:T(8,128)(2,1)S(1)} %copy-done.25), channel_id=1, source_target_pairs={{8,9},{9,10},{10,11},{11,12},{12,13},{13,14},{14,15},{15,0},{24,25... | collective-permute-start | bytes 786440 | tf_op jit(solution)/shard_map/ppermute | solution.py:190
  102.5 39.6 %copy-start.8 = (bf16[128,1024]{1,0:T(8,128)(2,1)S(1)}, bf16[128,1024]{1,0:T(8,128)(2,1)}, u32[]{:S(2)}) copy-start(bf16[128,1024]{1,0:T(8,128)(2,1)} %get-tuple-element.29) | copy-start | bytes 786436
  102.6 41.6 %collective-permute-start.14 = (bf16[128,1024]{1,0:T(8,128)(2,1)S(1)}, bf16[128,1024]{1,0:T(8,128)(2,1)S(1)}, u32[]{:S(2)}, u32[]{:S(2)}) collective-permute-start(bf16[128,1024]{1,0:T(8,128)(2,1)S(1)} %add_convert_fusion.8), channel_id=1, source_target_pairs={{5,4},{6,5},{7,6},{8,7},{9,8},{10,9},{11,10},{12,11},{13,12},{14,1... | collective-permute-start | bytes 786440 | tf_op jit(solution)/shard_map/ppermute | solution.py:190
  142.2 2.0 %copy-start.7 = (bf16[128,1024]{1,0:T(8,128)(2,1)S(1)}, bf16[128,1024]{1,0:T(8,128)(2,1)}, u32[]{:S(2)}) copy-start(bf16[128,1024]{1,0:T(8,128)(2,1)} %get-tuple-element.24) | copy-start | bytes 786436
  142.2 10.1 %collective-permute-start.20 = (bf16[128,1024]{1,0:T(8,128)(2,1)S(1)}, bf16[128,1024]{1,0:T(8,128)(2,1)S(1)}, u32[]{:S(2)}, u32[]{:S(2)}) collective-permute-start(bf16[128,1024]{1,0:T(8,128)(2,1)S(1)} %add_convert_fusion.3), channel_id=1, source_target_pairs={{9,10},{10,11},{11,12},{12,13},{13,14},{14,15},{15,0},{0,1},{25,26... | collective-permute-start | bytes 786440 | tf_op jit(solution)/shard_map/ppermute | solution.py:190
  144.2 8.2 %copy-start.6 = (bf16[128,1024]{1,0:T(8,128)(2,1)S(1)}, bf16[128,1024]{1,0:T(8,128)(2,1)}, u32[]{:S(2)}) copy-start(bf16[128,1024]{1,0:T(8,128)(2,1)} %get-tuple-element.30) | copy-start | bytes 786436
  144.3 10.1 %collective-permute-start.15 = (bf16[128,1024]{1,0:T(8,128)(2,1)S(1)}, bf16[128,1024]{1,0:T(8,128)(2,1)S(1)}, u32[]{:S(2)}, u32[]{:S(2)}) collective-permute-start(bf16[128,1024]{1,0:T(8,128)(2,1)S(1)} %add_convert_fusion.7), channel_id=1, source_target_pairs={{4,3},{5,4},{6,5},{7,6},{8,7},{9,8},{10,9},{11,10},{12,11},{13,12}... | collective-permute-start | bytes 786440 | tf_op jit(solution)/shard_map/ppermute | solution.py:190
  152.4 2.0 %copy-start.5 = (bf16[128,1024]{1,0:T(8,128)(2,1)S(1)}, bf16[128,1024]{1,0:T(8,128)(2,1)}, u32[]{:S(2)}) copy-start(bf16[128,1024]{1,0:T(8,128)(2,1)} %get-tuple-element.25) | copy-start | bytes 786436
  152.5 9.5 %collective-permute-start.21 = (bf16[128,1024]{1,0:T(8,128)(2,1)S(1)}, bf16[128,1024]{1,0:T(8,128)(2,1)S(1)}, u32[]{:S(2)}, u32[]{:S(2)}) collective-permute-start(bf16[128,1024]{1,0:T(8,128)(2,1)S(1)} %add_convert_fusion.2), channel_id=1, source_target_pairs={{10,11},{11,12},{12,13},{13,14},{14,15},{15,0},{0,1},{1,2},{26,27}... | collective-permute-start | bytes 786440 | tf_op jit(solution)/shard_map/ppermute | solution.py:190
  154.4 7.5 %copy-start.4 = (bf16[128,1024]{1,0:T(8,128)(2,1)S(1)}, bf16[128,1024]{1,0:T(8,128)(2,1)}, u32[]{:S(2)}) copy-start(bf16[128,1024]{1,0:T(8,128)(2,1)} %get-tuple-element.31) | copy-start | bytes 786436
  154.5 9.4 %collective-permute-start.16 = (bf16[128,1024]{1,0:T(8,128)(2,1)S(1)}, bf16[128,1024]{1,0:T(8,128)(2,1)S(1)}, u32[]{:S(2)}, u32[]{:S(2)}) collective-permute-start(bf16[128,1024]{1,0:T(8,128)(2,1)S(1)} %add_convert_fusion.6), channel_id=1, source_target_pairs={{3,2},{4,3},{5,4},{6,5},{7,6},{8,7},{9,8},{10,9},{11,10},{12,11},{... | collective-permute-start | bytes 786440 | tf_op jit(solution)/shard_map/ppermute | solution.py:190
  161.9 2.0 %copy-start.3 = (bf16[128,1024]{1,0:T(8,128)(2,1)S(1)}, bf16[128,1024]{1,0:T(8,128)(2,1)}, u32[]{:S(2)}) copy-start(bf16[128,1024]{1,0:T(8,128)(2,1)} %get-tuple-element.26) | copy-start | bytes 786436
  162.0 25.5 %collective-permute-start.22 = (bf16[128,1024]{1,0:T(8,128)(2,1)S(1)}, bf16[128,1024]{1,0:T(8,128)(2,1)S(1)}, u32[]{:S(2)}, u32[]{:S(2)}) collective-permute-start(bf16[128,1024]{1,0:T(8,128)(2,1)S(1)} %add_convert_fusion.1), channel_id=1, source_target_pairs={{11,12},{12,13},{13,14},{14,15},{15,0},{0,1},{1,2},{2,3},{27,28},{... | collective-permute-start | bytes 786440 | tf_op jit(solution)/shard_map/ppermute | solution.py:190
  164.0 23.6 %copy-start.2 = (bf16[128,1024]{1,0:T(8,128)(2,1)S(1)}, bf16[128,1024]{1,0:T(8,128)(2,1)}, u32[]{:S(2)}) copy-start(bf16[128,1024]{1,0:T(8,128)(2,1)} %get-tuple-element.32) | copy-start | bytes 786436
  164.0 25.5 %collective-permute-start.17 = (bf16[128,1024]{1,0:T(8,128)(2,1)S(1)}, bf16[128,1024]{1,0:T(8,128)(2,1)S(1)}, u32[]{:S(2)}, u32[]{:S(2)}) collective-permute-start(bf16[128,1024]{1,0:T(8,128)(2,1)S(1)} %add_convert_fusion.5), channel_id=1, source_target_pairs={{2,1},{3,2},{4,3},{5,4},{6,5},{7,6},{8,7},{9,8},{10,9},{11,10},{12... | collective-permute-start | bytes 786440 | tf_op jit(solution)/shard_map/ppermute | solution.py:190
  187.5 2.0 %copy-start.1 = (bf16[128,1024]{1,0:T(8,128)(2,1)S(1)}, bf16[128,1024]{1,0:T(8,128)(2,1)}, u32[]{:S(2)}) copy-start(bf16[128,1024]{1,0:T(8,128)(2,1)} %get-tuple-element.27) | copy-start | bytes 786436
  187.6 12.2 %collective-permute-start.23 = (bf16[128,1024]{1,0:T(8,128)(2,1)S(1)}, bf16[128,1024]{1,0:T(8,128)(2,1)S(1)}, u32[]{:S(2)}, u32[]{:S(2)}) collective-permute-start(bf16[128,1024]{1,0:T(8,128)(2,1)S(1)} %add_convert_fusion), channel_id=1, source_target_pairs={{12,0},{13,1},{14,2},{15,3},{0,4},{1,5},{2,6},{3,7},{28,16},{29,17... | collective-permute-start | bytes 786440 | tf_op jit(solution)/shard_map/ppermute | solution.py:190
  189.6 10.2 %copy-start = (bf16[128,1024]{1,0:T(8,128)(2,1)S(1)}, bf16[128,1024]{1,0:T(8,128)(2,1)}, u32[]{:S(2)}) copy-start(bf16[128,1024]{1,0:T(8,128)(2,1)} %get-tuple-element.33) | copy-start | bytes 786436
  189.6 10.1 %collective-permute-start.18 = (bf16[128,1024]{1,0:T(8,128)(2,1)S(1)}, bf16[128,1024]{1,0:T(8,128)(2,1)S(1)}, u32[]{:S(2)}, u32[]{:S(2)}) collective-permute-start(bf16[128,1024]{1,0:T(8,128)(2,1)S(1)} %add_convert_fusion.4), channel_id=1, source_target_pairs={{1,0},{2,1},{3,2},{4,3},{5,4},{6,5},{7,6},{8,7},{9,8},{10,9},{11,1... | collective-permute-start | bytes 786440 | tf_op jit(solution)/shard_map/ppermute | solution.py:190

commit v3 on v1

v3 whole, which is shorter than its diff:
```python
import functools
import math

import jax
import jax.numpy as jnp
from jax import lax
from jax.experimental import pallas as pl
from jax.experimental.pallas import tpu as pltpu
from jax.sharding import PartitionSpec as P

KVH = 4
HD = 128
GROUP = 4
WIDE = KVH * HD
FAR = 12
STEPS = 7
LANES = GROUP * 128
SCALE = 1.0 / math.sqrt(HD)
TO_TWO = SCALE / math.log(2.0)

neg_big = -1e30


def dot_nt(a, b):
    return lax.dot_general(a, b, (((1,), (1,)), ((), ())), preferred_element_type=jnp.float32)


def dot_nn(a, b):
    return lax.dot_general(a, b, (((1,), (0,)), ((), ())), preferred_element_type=jnp.float32)


def dot_tn(a, b):
    return lax.dot_general(a, b, (((0,), (0,)), ((), ())), preferred_element_type=jnp.float32)


def heads_of(ref, g):
    base = g * GROUP * HD
    return jnp.concatenate(
        [ref[:, base + r * HD : base + (r + 1) * HD] for r in range(GROUP)], axis=0
    )


def put_heads(ref, g, turned):
    flat = turned.T
    rows = ref.shape[0]
    for r in range(GROUP):
        cols = slice((g * GROUP + r) * HD, (g * GROUP + r + 1) * HD)
        ref[:, cols] = flat[r * rows : (r + 1) * rows].astype(ref.dtype)


def keys_of(blocks, g):
    return jnp.concatenate([b[:, g * HD : (g + 1) * HD] for b in blocks], axis=0)


def values_of(blocks, g):
    return jnp.concatenate([b[:, WIDE + g * HD : WIDE + (g + 1) * HD] for b in blocks], axis=0)


def allowed_keys(scal, first_ref, backs, rows):
    q_start = scal[0]
    first = jnp.concatenate([first_ref[...]] * GROUP, axis=1)
    within = lax.broadcasted_iota(jnp.int32, (rows, LANES), 0)
    parts = []
    for back in backs:
        place = (q_start - back * rows) + within
        seen = place >= first
        if isinstance(back, int) and back == 0:
            lanes = lax.broadcasted_iota(jnp.int32, (rows, LANES), 1)
            seen = seen & (within <= jnp.bitwise_and(lanes, rows - 1))
        parts.append(seen)
    return jnp.concatenate(parts, axis=0)


def forward_part(scal, first_ref, q_ref, blocks, backs, top_ref, sum_ref, acc_ref):
    allowed = allowed_keys(scal, first_ref, backs, q_ref.shape[0])
    for g in range(KVH):
        s = dot_nt(keys_of(blocks, g), heads_of(q_ref, g)) * TO_TWO
        s = jnp.where(allowed, s, neg_big)
        top = top_ref[g]
        new_top = jnp.maximum(top, jnp.max(s, axis=0, keepdims=True))
        e = jnp.exp2(s - new_top)
        shrink = jnp.exp2(top - new_top)
        top_ref[g] = new_top
        sum_ref[g] = sum_ref[g] * shrink + jnp.sum(e, axis=0, keepdims=True)
        acc_ref[g] = acc_ref[g] * shrink + dot_tn(values_of(blocks, g), e.astype(jnp.bfloat16))


def backward_part(scal, first_ref, q_ref, g_ref, blocks, backs, log_ref, inner_ref, acc_ref, outs):
    rows = q_ref.shape[0]
    allowed = allowed_keys(scal, first_ref, backs, rows)
    for g in range(KVH):
        k, v = keys_of(blocks, g), values_of(blocks, g)
        q, grads = heads_of(q_ref, g), heads_of(g_ref, g)
        s = dot_nt(k, q) * TO_TWO - log_ref[g]
        probs = jnp.exp2(jnp.where(allowed, s, neg_big))
        grad_probs = dot_nt(v, grads)
        grad_scores = (probs * (grad_probs - inner_ref[g])).astype(jnp.bfloat16)
        acc_ref[g] = acc_ref[g] + dot_tn(k, grad_scores)
        grad_k = dot_nn(grad_scores, q) * SCALE
        grad_v = dot_nn(probs.astype(jnp.bfloat16), grads)
        for i, out in enumerate(outs):
            part = slice(i * rows, (i + 1) * rows)
            out[:, g * HD : (g + 1) * HD] = grad_k[part].astype(out.dtype)
            out[:, WIDE + g * HD : WIDE + (g + 1) * HD] = grad_v[part].astype(out.dtype)


def backs_of(scal, step):
    near, far = step, 15 - step
    odd = scal[2] == 1
    return [jnp.where(odd, far, near), jnp.where(odd, near, far)]


class Near:
    def __init__(self, scal, a, b):
        self.even, self.a, self.b = scal[2] == 0, a, b

    def __getitem__(self, at):
        return jnp.where(self.even, self.a[at], self.b[at])


def first_kernel(scal, first_ref, q_ref, g_ref, own, a1, b1, a2, b2, top, total, acc, turned):
    rows = q_ref.shape[0]
    top[...] = jnp.full(top.shape, neg_big, jnp.float32)
    total[...] = jnp.zeros(total.shape, jnp.float32)
    acc[...] = jnp.zeros(acc.shape, jnp.float32)
    forward_part(scal, first_ref, q_ref, [own], [0], top, total, acc)

    @pl.when(scal[1] >= 1)
    def _():
        near = [Near(scal, a1, b1), Near(scal, a2, b2)]
        forward_part(scal, first_ref, q_ref, near, [1, 2], top, total, acc)

    for g in range(KVH):
        turned[g] = heads_of(g_ref, g).astype(jnp.float32).T


def more_kernel(steps, scal, first_ref, q_ref, top_in, total_in, acc_in, *rest):
    blocks, (top, total, acc) = rest[: 2 * len(steps)], rest[2 * len(steps) :]
    top[...] = top_in[...]
    total[...] = total_in[...]
    acc[...] = acc_in[...]
    for i, step in enumerate(steps):

        @pl.when(scal[1] >= step)
        def _(i=i, step=step):
            pair = blocks[2 * i : 2 * i + 2]
            forward_part(scal, first_ref, q_ref, pair, backs_of(scal, step), top, total, acc)


def middle_kernel(
    scal, first_ref, q_ref, g_ref, turned, top_in, total_in, acc_in, a, b,
    out_ref, log_ref, inner_ref, gq_acc, term_a, term_b, acc,
):
    log_ref[...] = top_in[...]
    inner_ref[...] = total_in[...]
    acc[...] = acc_in[...]

    @pl.when(scal[1] >= STEPS)
    def _():
        backs = backs_of(scal, STEPS)
        forward_part(scal, first_ref, q_ref, [a, b], backs, log_ref, inner_ref, acc)

    for g in range(KVH):
        total = inner_ref[g]
        attended = acc[g] * (1.0 / total)
        log_ref[g] = log_ref[g] + jnp.log2(total)
        inner_ref[g] = jnp.sum(attended * turned[g], axis=0, keepdims=True)
        put_heads(out_ref, g, attended)
    gq_acc[...] = jnp.zeros(gq_acc.shape, jnp.float32)
    back_step(STEPS, scal, first_ref, q_ref, g_ref, a, b, log_ref, inner_ref, gq_acc, term_a, term_b)


def back_step(step, scal, first_ref, q_ref, g_ref, a, b, log_ref, inner_ref, acc, term_a, term_b):
    @pl.when(scal[1] >= step)
    def _():
        backs = backs_of(scal, step)
        backward_part(
            scal, first_ref, q_ref, g_ref, [a, b], backs, log_ref, inner_ref, acc, [term_a, term_b]
        )

    @pl.when(scal[1] < step)
    def _():
        term_a[...] = jnp.zeros(term_a.shape, term_a.dtype)
        term_b[...] = jnp.zeros(term_b.shape, term_b.dtype)


def back_kernel(
    step, scal, first_ref, q_ref, g_ref, log_ref, inner_ref, acc_in, a, b, acc, term_a, term_b
):
    acc[...] = acc_in[...]
    back_step(step, scal, first_ref, q_ref, g_ref, a, b, log_ref, inner_ref, acc, term_a, term_b)


def last_kernel(
    scal, first_ref, q_ref, g_ref, log_ref, inner_ref, acc_in, own, a1, b1, a2, b2,
    gq_ref, term_0, term_1, term_2, acc,
):
    acc[...] = acc_in[...]
    backward_part(
        scal, first_ref, q_ref, g_ref, [own], [0], log_ref, inner_ref, acc, [term_0]
    )

    @pl.when(scal[1] >= 1)
    def _():
        near = [Near(scal, a1, b1), Near(scal, a2, b2)]
        backward_part(
            scal, first_ref, q_ref, g_ref, near, [1, 2], log_ref, inner_ref, acc, [term_1, term_2]
        )

    @pl.when(scal[1] < 1)
    def _():
        term_1[...] = jnp.zeros(term_1.shape, term_1.dtype)
        term_2[...] = jnp.zeros(term_2.shape, term_2.dtype)

    for g in range(KVH):
        put_heads(gq_ref, g, acc[g] * SCALE)


ROW = jax.ShapeDtypeStruct((KVH, 1, LANES), jnp.float32)
TURNED = jax.ShapeDtypeStruct((KVH, HD, LANES), jnp.float32)


def call(kernel, outs, work, scal, *operands, scratch=()):
    in_vmem = pl.BlockSpec(memory_space=pltpu.VMEM)
    return pl.pallas_call(
        kernel,
        out_shape=outs,
        in_specs=[pl.BlockSpec(memory_space=pltpu.SMEM)] + [in_vmem] * len(operands),
        out_specs=[in_vmem] * len(outs),
        scratch_shapes=list(scratch),
        compiler_params=pltpu.CompilerParams(vmem_limit_bytes=24 * 1024 * 1024),
        cost_estimate=pl.CostEstimate(
            flops=int(work * 1.0e9), bytes_accessed=4 * 1024 * 1024, transcendentals=1 << 20
        ),
    )(scal, *operands)


def both_ways(x, near_pairs, far_pairs, flip):
    windows, count = lax.axis_size("dp"), lax.axis_size("ctx")
    pairs = []
    for window in range(windows):
        chosen = near_pairs if (window + flip) % 2 == 0 else far_pairs
        pairs += [(window * count + i, window * count + j) for i, j in chosen]
    return lax.ppermute(x, ("dp", "ctx"), pairs)


def gather_pairs(step, count):
    near = [(j, j + 1) for j in range(step - 1, count - 1)]
    blocks = range(count - STEPS - 1)
    start = 0 if step == 1 else step
    far = [((b - start) % count, (b - step - 1) % count) for b in blocks]
    return near, far


def return_pairs(step, count):
    near = [(j, j - 1) for j in range(STEPS + 1 - step, count)]
    blocks = range(count - STEPS - 1)
    end = STEPS + 1 + step if step < STEPS else count
    far = [((b + STEPS + step) % count, (b + end) % count) for b in blocks]
    return near, far


def add_low(a, b):
    return (a.astype(jnp.float32) + b.astype(jnp.float32)).astype(jnp.bfloat16)


def local(queries, keys, values, out_grad, segment_ids):
    rows = queries.shape[0]
    count = lax.axis_size("ctx")
    odd = lax.rem(lax.axis_index("dp"), 2)
    q_start = lax.axis_index("ctx") * rows
    own = jnp.concatenate([keys, values], axis=1)
    q_seg = lax.dynamic_slice_in_dim(segment_ids, q_start, rows, 0)
    first = jnp.sum((segment_ids[:, None] < q_seg[None, :]).astype(jnp.int32), axis=0, keepdims=True)
    scal = jnp.stack([q_start, (q_start - first[0, 0] + rows - 1) // rows, odd]).astype(jnp.int32)

    block = jax.ShapeDtypeStruct(own.shape, jnp.bfloat16)
    wide = jax.ShapeDtypeStruct(queries.shape, jnp.bfloat16)
    a, b, tops = [own], [own], {}
    for step in range(1, STEPS + 1):
        pairs = gather_pairs(step, count)
        to_a = a[-1]
        if step in (5, 7):
            to_a, _ = lax.optimization_barrier((to_a, tops[step - 3]))
        a.append(both_ways(to_a, *pairs, 0))
        b.append(both_ways(b[-1], *pairs, 1))
        if step == 2:
            top, total, acc, turned = call(
                first_kernel, [ROW, ROW, TURNED, TURNED], 0.8,
                scal, first, queries, out_grad, own, a[1], b[1], a[2], b[2],
            )
        elif step in (4, 6):
            pairs = [x for i in (step - 1, step) for x in (a[i], b[i])]
            top, total, acc = call(
                functools.partial(more_kernel, (step - 1, step)), [ROW, ROW, TURNED], 1.0,
                scal, first, queries, top, total, acc, *pairs,
            )
        tops[step] = top if step > 1 else None
    attended, log_total, inner, acc, term_a, term_b = call(
        middle_kernel, [wide, ROW, ROW, TURNED, block, block], 1.5,
        scal, first, queries, out_grad, turned, top, total, acc, a[STEPS], b[STEPS],
        scratch=[pltpu.VMEM((KVH, HD, LANES), jnp.float32)],
    )

    sum_a, sum_b = term_a, term_b
    for step in range(1, STEPS + 1):
        pairs = return_pairs(step, count)
        sum_a = both_ways(sum_a, *pairs, 0)
        sum_b = both_ways(sum_b, *pairs, 1)
        back = STEPS - step
        if back >= 3:
            acc, term_a, term_b = call(
                functools.partial(back_kernel, back), [TURNED, block, block], 1.2,
                scal, first, queries, out_grad, log_total, inner, acc, a[back], b[back],
            )
            sum_a, sum_b = add_low(sum_a, term_a), add_low(sum_b, term_b)
        elif back >= 1:
            if back == 2:
                grad_query, term_0, term_1, term_2 = call(
                    last_kernel, [wide, jax.ShapeDtypeStruct(own.shape, jnp.float32), block, block], 2.0,
                    scal, first, queries, out_grad, log_total, inner, acc, own, a[1], b[1], a[2], b[2],
                    scratch=[pltpu.VMEM((KVH, HD, LANES), jnp.float32)],
                )
            term = term_2 if back == 2 else term_1
            nothing = jnp.zeros_like(term)
            sum_a = add_low(sum_a, jnp.where(odd == 0, term, nothing))
            sum_b = add_low(sum_b, jnp.where(odd == 1, term, nothing))
    summed = sum_a.astype(jnp.float32) + sum_b.astype(jnp.float32) + term_0
    return (attended, grad_query, summed[:, :WIDE], summed[:, WIDE:])


def solution(mesh):
    placed = P(("dp", "ctx"), None)
    return jax.shard_map(
        local,
        mesh=mesh,
        in_specs=(placed, placed, placed, placed, P("dp")),
        out_specs=(placed, placed, placed, placed),
        check_vma=False,
    )
```

time: 204 us -> 180 us (0.88)
  the two profiles are of different devices: /device:TPU:24 before, /device:TPU:60 now
where the time goes in v3:
time: 180 us; the launch traced here: 179 us
  starting transfers between devices  79 us (44%)
  waiting for transfers between devices  77.5 us (43%)
  Pallas kernels  14.1 us (8%)
  local copies, waits for them, and re-layouts  3.85 us (2%)
  other arithmetic  3.81 us (2%)
    ppermute x28, starting transfers between devices, both_ways(): return lax.ppermute(x, ('dp', 'ctx'), pairs)  79 us
    ppermute x28, waiting for transfers between devices, both_ways(): return lax.ppermute(x, ('dp', 'ctx'), pairs)  77.5 us
    pallas_call x9, Pallas kernels, call(): pl.pallas_call(kernel, out_shape=outs, in_specs=[pl.BlockSpec(memory_spac...  14.1 us
  transfers between devices with their start and end apart: 28, of which 12 were waited for; matrix products, arithmetic and copies ran while one was open for 1% of the time, Pallas kernels for 7%

profile of v3, /device:TPU:60, one launch (start us, length us, event | category | flops | bytes accessed | tf_op | source)
XLA Modules:
  0.0 179.5 jit_solution(5448174750134596997)
XLA Ops:
  0.6 1.0 constant_dynamic-update-slice_fusion.1
  1.6 0.9 constant_dynamic-update-slice_fusion.own
  2.5 3.8 %collective-permute-start = (bf16[128,1024]{1,0:T(8,128)(2,1)S(1)}, bf16[128,1024]{1,0:T(8,128)(2,1)S(1)}, u32[]{:S(2)}, u32[]{:S(2)}) collective-permute-start(bf16[128,1024]{1,0:T(8,128)(2,1)S(1)} %constant_dynamic-update-slice_fusion.own), channel_id=1, source_target_pairs={{0,1},{1,2},{2,3},{3,4},{4,5},{5,6},{6,7},{7,8},{8,9},{9,10},{10,1... | collective-permute-start | bytes 786440 | tf_op jit(solution)/shard_map/ppermute | solution.py:244
  6.4 8.4 %collective-permute-start.1 = (bf16[128,1024]{1,0:T(8,128)(2,1)S(1)}, bf16[128,1024]{1,0:T(8,128)(2,1)S(1)}, u32[]{:S(2)}, u32[]{:S(2)}) collective-permute-start(bf16[128,1024]{1,0:T(8,128)(2,1)S(1)} %constant_dynamic-update-slice_fusion.own), channel_id=1, source_target_pairs={{0,14},{1,15},{2,0},{3,1},{4,2},{5,3},{6,4},{7,5},{16,17},{17,18},... | collective-permute-start | bytes 786440 | tf_op jit(solution)/shard_map/ppermute | solution.py:244
  14.8 1.3 collective-permute-start.2
  16.1 4.6 %collective-permute-done.1.b1 = bf16[128,1024]{1,0:T(8,128)(2,1)S(1)} collective-permute-done((bf16[128,1024]{1,0:T(8,128)(2,1)S(1)}, bf16[128,1024]{1,0:T(8,128)(2,1)S(1)}, u32[]{:S(2)}, u32[]{:S(2)}) %collective-permute-start.1) | collective-permute-done | bytes 262176 | tf_op jit(solution)/shard_map/ppermute | solution.py:244
  20.7 6.9 %collective-permute-start.3 = (bf16[128,1024]{1,0:T(8,128)(2,1)S(1)}, bf16[128,1024]{1,0:T(8,128)(2,1)S(1)}, u32[]{:S(2)}, u32[]{:S(2)}) collective-permute-start(bf16[128,1024]{1,0:T(8,128)(2,1)S(1)} %collective-permute-done.1.b1), channel_id=1, source_target_pairs={{14,13},{15,14},{0,15},{1,0},{2,1},{3,2},{4,3},{5,4},{17,18},{18,1... | collective-permute-start | bytes 786440 | tf_op jit(solution)/shard_map/ppermute | solution.py:244
  27.6 0.7 collective-permute-start.4
  28.3 3.6 %collective-permute-done.3.b2 = bf16[128,1024]{1,0:T(8,128)(2,1)S(1)} collective-permute-done((bf16[128,1024]{1,0:T(8,128)(2,1)S(1)}, bf16[128,1024]{1,0:T(8,128)(2,1)S(1)}, u32[]{:S(2)}, u32[]{:S(2)}) %collective-permute-start.3) | collective-permute-done | bytes 262176 | tf_op jit(solution)/shard_map/ppermute | solution.py:244
  31.8 4.4 %collective-permute-start.5 = (bf16[128,1024]{1,0:T(8,128)(2,1)S(1)}, bf16[128,1024]{1,0:T(8,128)(2,1)S(1)}, u32[]{:S(2)}, u32[]{:S(2)}) collective-permute-start(bf16[128,1024]{1,0:T(8,128)(2,1)S(1)} %collective-permute-done.3.b2), channel_id=1, source_target_pairs={{13,12},{14,13},{15,14},{0,15},{1,0},{2,1},{3,2},{4,3},{18,19},{19... | collective-permute-start | bytes 786440 | tf_op jit(solution)/shard_map/ppermute | solution.py:244
  36.2 0.1 dynamic_slice.3
  36.3 0.7 collective-permute-start.6
  37.0 3.1 %collective-permute-done.5.rest_1_.b = bf16[128,1024]{1,0:T(8,128)(2,1)S(1)} collective-permute-done((bf16[128,1024]{1,0:T(8,128)(2,1)S(1)}, bf16[128,1024]{1,0:T(8,128)(2,1)S(1)}, u32[]{:S(2)}, u32[]{:S(2)}) %collective-permute-start.5) | collective-permute-done | bytes 262176 | tf_op jit(solution)/shard_map/ppermute | solution.py:244
  40.1 4.6 %collective-permute-start.7 = (bf16[128,1024]{1,0:T(8,128)(2,1)S(1)}, bf16[128,1024]{1,0:T(8,128)(2,1)S(1)}, u32[]{:S(2)}, u32[]{:S(2)}) collective-permute-start(bf16[128,1024]{1,0:T(8,128)(2,1)S(1)} %collective-permute-done.5.rest_1_.b), channel_id=1, source_target_pairs={{12,11},{13,12},{14,13},{15,14},{0,15},{1,0},{2,1},{3,2},{19,20},{... | collective-permute-start | bytes 786440 | tf_op jit(solution)/shard_map/ppermute | solution.py:244
  44.7 0.4 convert_reduce_fusion
  45.1 0.1 pad_add_fusion.scal
  45.2 1.0 copy-done.1
  46.2 3.5 %shard_map.84 = (f32[4,1,512]{2,1,0:T(1,128)S(1)}, f32[4,1,512]{2,1,0:T(1,128)S(1)}, f32[4,128,512]{2,1,0:T(8,128)S(1)}, f32[4,128,512]{2,1,0:T(8,128)S(1)}) custom-call(s32[3]{0:T(128)S(1)} %pad_add_fusion.scal, s32[1,128]{1,0:T(1,128)S(1)} %bitcast.7, bf16[128,2048]{1,0:T(8,128)(2,1)S(1)} %copy-done, bf16[128,2048]{1,0:T(8,128)(2,1)S(1)} %copy-done.1, ...), custom_call_target="tpu_custom_call" | custom-call | flops 800000000 | bytes 4194304 | tf_op jit(solution)/shard_map/pallas_call | solution.py:225
  49.8 0.7 collective-permute-start.8
  50.5 4.1 %collective-permute-start.9 = (bf16[128,1024]{1,0:T(8,128)(2,1)S(1)}, bf16[128,1024]{1,0:T(8,128)(2,1)S(1)}, u32[]{:S(2)}, u32[]{:S(2)}) collective-permute-start(bf16[128,1024]{1,0:T(8,128)(2,1)S(1)} %collective-permute-done.7.rest_3_.b), channel_id=1, source_target_pairs={{11,10},{12,11},{13,12},{14,13},{15,14},{0,15},{1,0},{2,1},{20,21}... | collective-permute-start | bytes 786440 | tf_op jit(solution)/shard_map/ppermute | solution.py:244
  54.5 0.7 collective-permute-start.10
  55.2 3.5 %collective-permute-done.9.rest_1_.b = bf16[128,1024]{1,0:T(8,128)(2,1)S(1)} collective-permute-done((bf16[128,1024]{1,0:T(8,128)(2,1)S(1)}, bf16[128,1024]{1,0:T(8,128)(2,1)S(1)}, u32[]{:S(2)}, u32[]{:S(2)}) %collective-permute-start.9) | collective-permute-done | bytes 262176 | tf_op jit(solution)/shard_map/ppermute | solution.py:244
  58.7 5.0 %collective-permute-start.11 = (bf16[128,1024]{1,0:T(8,128)(2,1)S(1)}, bf16[128,1024]{1,0:T(8,128)(2,1)S(1)}, u32[]{:S(2)}, u32[]{:S(2)}) collective-permute-start(bf16[128,1024]{1,0:T(8,128)(2,1)S(1)} %collective-permute-done.9.rest_1_.b), channel_id=1, source_target_pairs={{10,9},{11,10},{12,11},{13,12},{14,13},{15,14},{0,15},{1,0},{21,22... | collective-permute-start | bytes 786440 | tf_op jit(solution)/shard_map/ppermute | solution.py:244
  63.7 0.6 shard_map.85
  64.4 0.7 collective-permute-start.12
  65.1 2.5 %collective-permute-done.11.rest_3_.b = bf16[128,1024]{1,0:T(8,128)(2,1)S(1)} collective-permute-done((bf16[128,1024]{1,0:T(8,128)(2,1)S(1)}, bf16[128,1024]{1,0:T(8,128)(2,1)S(1)}, u32[]{:S(2)}, u32[]{:S(2)}) %collective-permute-start.11) | collective-permute-done | bytes 262176 | tf_op jit(solution)/shard_map/ppermute | solution.py:244
  67.6 0.7 collective-permute-start.13
  68.3 0.6 shard_map.86
  68.9 1.8 shard_map.87
  70.7 0.8 collective-permute-start.21
  71.5 0.7 collective-permute-start.14
  72.2 0.6 shard_map.88
  72.9 0.1 add_convert_fusion.5
  73.0 1.3 collective-permute-start.22
  74.3 0.1 add_convert_fusion.11
  74.3 0.7 collective-permute-start.15
  75.0 0.6 shard_map.89
  75.7 25.4 %collective-permute-done.22 = bf16[128,1024]{1,0:T(8,128)(2,1)S(1)} collective-permute-done((bf16[128,1024]{1,0:T(8,128)(2,1)S(1)}, bf16[128,1024]{1,0:T(8,128)(2,1)S(1)}, u32[]{:S(2)}, u32[]{:S(2)}) %collective-permute-start.22) | collective-permute-done | bytes 262176 | tf_op jit(solution)/shard_map/ppermute | solution.py:244
  101.2 1.9 %collective-permute-start.23 = (bf16[128,1024]{1,0:T(8,128)(2,1)S(1)}, bf16[128,1024]{1,0:T(8,128)(2,1)S(1)}, u32[]{:S(2)}, u32[]{:S(2)}) collective-permute-start(bf16[128,1024]{1,0:T(8,128)(2,1)S(1)} %add_convert_fusion.4), channel_id=1, source_target_pairs={{10,11},{11,12},{12,13},{13,14},{14,15},{15,0},{0,1},{1,2},{21,20}... | collective-permute-start | bytes 786440 | tf_op jit(solution)/shard_map/ppermute | solution.py:244
  103.1 0.1 add_convert_fusion.10
  103.2 0.7 collective-permute-start.16
  103.9 0.6 shard_map.90
  104.5 7.8 %collective-permute-done.23 = bf16[128,1024]{1,0:T(8,128)(2,1)S(1)} collective-permute-done((bf16[128,1024]{1,0:T(8,128)(2,1)S(1)}, bf16[128,1024]{1,0:T(8,128)(2,1)S(1)}, u32[]{:S(2)}, u32[]{:S(2)}) %collective-permute-start.23) | collective-permute-done | bytes 262176 | tf_op jit(solution)/shard_map/ppermute | solution.py:244
  112.3 1.9 %collective-permute-start.24 = (bf16[128,1024]{1,0:T(8,128)(2,1)S(1)}, bf16[128,1024]{1,0:T(8,128)(2,1)S(1)}, u32[]{:S(2)}, u32[]{:S(2)}) collective-permute-start(bf16[128,1024]{1,0:T(8,128)(2,1)S(1)} %add_convert_fusion.3), channel_id=1, source_target_pairs={{11,12},{12,13},{13,14},{14,15},{15,0},{0,1},{1,2},{2,3},{20,19},{... | collective-permute-start | bytes 786440 | tf_op jit(solution)/shard_map/ppermute | solution.py:244
  114.4 0.7 collective-permute-start.17
  115.0 0.6 shard_map.91
  115.7 9.0 %collective-permute-done.24 = bf16[128,1024]{1,0:T(8,128)(2,1)S(1)} collective-permute-done((bf16[128,1024]{1,0:T(8,128)(2,1)S(1)}, bf16[128,1024]{1,0:T(8,128)(2,1)S(1)}, u32[]{:S(2)}, u32[]{:S(2)}) %collective-permute-start.24) | collective-permute-done | bytes 262176 | tf_op jit(solution)/shard_map/ppermute | solution.py:244
  124.7 0.8 add_convert_fusion.2
  125.5 2.0 %collective-permute-start.25 = (bf16[128,1024]{1,0:T(8,128)(2,1)}, bf16[128,1024]{1,0:T(8,128)(2,1)}, u32[]{:S(2)}, u32[]{:S(2)}) collective-permute-start(bf16[128,1024]{1,0:T(8,128)(2,1)} %add_convert_fusion.2), channel_id=1, source_target_pairs={{12,13},{13,14},{14,15},{15,0},{0,1},{1,2},{2,3},{3,4},{19,18},{20... | collective-permute-start | bytes 786440 | tf_op jit(solution)/shard_map/ppermute | solution.py:244
  127.5 0.8 add_convert_fusion.8
  128.3 1.4 collective-permute-start.18
  129.7 5.0 %shard_map.92 = (bf16[128,2048]{1,0:T(8,128)(2,1)}, f32[128,1024]{1,0:T(8,128)S(1)}, bf16[128,1024]{1,0:T(8,128)(2,1)S(1)}, bf16[128,1024]{1,0:T(8,128)(2,1)S(1)}) custom-call(s32[3]{0:T(128)S(1)} %pad_add_fusion.scal, s32[1,128]{1,0:T(1,128)S(1)} %bitcast.15, bf16[128,2048]{1,0:T(8,128)(2,1)S(1)} %copy-done, bf16[128,2048]{1,0:T(8,128)(2,1)S(1)} %copy-done.2, ...), custom_call_target="tpu_custom_call" | custom-call | flops 2000000000 | bytes 4194304 | tf_op jit(solution)/shard_map/pallas_call | solution.py:225
  134.6 3.1 %collective-permute-done.25 = bf16[128,1024]{1,0:T(8,128)(2,1)} collective-permute-done((bf16[128,1024]{1,0:T(8,128)(2,1)}, bf16[128,1024]{1,0:T(8,128)(2,1)}, u32[]{:S(2)}, u32[]{:S(2)}) %collective-permute-start.25) | collective-permute-done | bytes 262176 | tf_op jit(solution)/shard_map/ppermute | solution.py:244
  137.7 1.2 add_convert_fusion.7
  138.9 1.3 collective-permute-start.19
  140.2 4.6 %collective-permute-start.26 = (bf16[128,1024]{1,0:T(8,128)(2,1)S(1)}, bf16[128,1024]{1,0:T(8,128)(2,1)S(1)}, u32[]{:S(2)}, u32[]{:S(2)}) collective-permute-start(bf16[128,1024]{1,0:T(8,128)(2,1)S(1)} %get-tuple-element.77), channel_id=1, source_target_pairs={{13,14},{14,15},{15,0},{0,1},{1,2},{2,3},{3,4},{4,5},{18,17},{19,1... | collective-permute-start | bytes 786440 | tf_op jit(solution)/shard_map/ppermute | solution.py:244
  144.7 4.9 %collective-permute-done.19 = bf16[128,1024]{1,0:T(8,128)(2,1)S(1)} collective-permute-done((bf16[128,1024]{1,0:T(8,128)(2,1)S(1)}, bf16[128,1024]{1,0:T(8,128)(2,1)S(1)}, u32[]{:S(2)}, u32[]{:S(2)}) %collective-permute-start.19) | collective-permute-done | bytes 262176 | tf_op jit(solution)/shard_map/ppermute | solution.py:244
  149.7 0.2 add_convert_fusion.6
  149.9 16.7 %collective-permute-start.20 = (bf16[128,1024]{1,0:T(8,128)(2,1)S(1)}, bf16[128,1024]{1,0:T(8,128)(2,1)S(1)}, u32[]{:S(2)}, u32[]{:S(2)}) collective-permute-start(bf16[128,1024]{1,0:T(8,128)(2,1)S(1)} %get-tuple-element.74), channel_id=1, source_target_pairs={{1,0},{2,1},{3,2},{4,3},{5,4},{6,5},{7,6},{8,7},{9,8},{10,9},{11,1... | collective-permute-start | bytes 786440 | tf_op jit(solution)/shard_map/ppermute | solution.py:244
  166.5 1.9 %collective-permute-start.27 = (bf16[128,1024]{1,0:T(8,128)(2,1)S(1)}, bf16[128,1024]{1,0:T(8,128)(2,1)S(1)}, u32[]{:S(2)}, u32[]{:S(2)}) collective-permute-start(bf16[128,1024]{1,0:T(8,128)(2,1)S(1)} %get-tuple-element.75), channel_id=1, source_target_pairs={{14,0},{15,1},{0,2},{1,3},{2,4},{3,5},{4,6},{5,7},{17,16},{18,17},... | collective-permute-start | bytes 786440 | tf_op jit(solution)/shard_map/ppermute | solution.py:244
  168.4 1.9 %collective-permute-done.20 = bf16[128,1024]{1,0:T(8,128)(2,1)S(1)} collective-permute-done((bf16[128,1024]{1,0:T(8,128)(2,1)S(1)}, bf16[128,1024]{1,0:T(8,128)(2,1)S(1)}, u32[]{:S(2)}, u32[]{:S(2)}) %collective-permute-start.20) | collective-permute-done | bytes 262176 | tf_op jit(solution)/shard_map/ppermute | solution.py:244
  170.4 8.1 %collective-permute-done.27 = bf16[128,1024]{1,0:T(8,128)(2,1)S(1)} collective-permute-done((bf16[128,1024]{1,0:T(8,128)(2,1)S(1)}, bf16[128,1024]{1,0:T(8,128)(2,1)S(1)}, u32[]{:S(2)}, u32[]{:S(2)}) %collective-permute-start.27) | collective-permute-done | bytes 262176 | tf_op jit(solution)/shard_map/ppermute | solution.py:244
  178.5 0.1 add_add_fusion
  178.6 0.8 fusion
  (26 shorter events, 0.3 us)
Async XLA Ops:
  0.6 44.5 %copy-start = (bf16[128,2048]{1,0:T(8,128)(2,1)S(1)}, bf16[128,2048]{1,0:T(8,128)(2,1)}, u32[]{:S(2)}) copy-start(bf16[128,2048]{1,0:T(8,128)(2,1)} %q_ref.17) | copy-start | bytes 1572868
  2.5 33.7 %copy-start.3 = (s32[2048]{0:T(1024)S(1)}, s32[2048]{0:T(1024)}, u32[]{:S(2)}) copy-start(s32[2048]{0:T(1024)} %param.9) | copy-start | bytes 24580
  2.5 12.3 %collective-permute-start = (bf16[128,1024]{1,0:T(8,128)(2,1)S(1)}, bf16[128,1024]{1,0:T(8,128)(2,1)S(1)}, u32[]{:S(2)}, u32[]{:S(2)}) collective-permute-start(bf16[128,1024]{1,0:T(8,128)(2,1)S(1)} %constant_dynamic-update-slice_fusion.own), channel_id=1, source_target_pairs={{0,1},{1,2},{2,3},{3,4},{4,5},{5,6},{6,7},{7,8},{8,9},{9,10},{10,1... | collective-permute-start | bytes 786440 | tf_op jit(solution)/shard_map/ppermute | solution.py:244
  6.4 14.3 %collective-permute-start.1 = (bf16[128,1024]{1,0:T(8,128)(2,1)S(1)}, bf16[128,1024]{1,0:T(8,128)(2,1)S(1)}, u32[]{:S(2)}, u32[]{:S(2)}) collective-permute-start(bf16[128,1024]{1,0:T(8,128)(2,1)S(1)} %constant_dynamic-update-slice_fusion.own), channel_id=1, source_target_pairs={{0,14},{1,15},{2,0},{3,1},{4,2},{5,3},{6,4},{7,5},{16,17},{17,18},... | collective-permute-start | bytes 786440 | tf_op jit(solution)/shard_map/ppermute | solution.py:244
  14.8 12.8 %collective-permute-start.2 = (bf16[128,1024]{1,0:T(8,128)(2,1)S(1)}, bf16[128,1024]{1,0:T(8,128)(2,1)S(1)}, u32[]{:S(2)}, u32[]{:S(2)}) collective-permute-start(bf16[128,1024]{1,0:T(8,128)(2,1)S(1)} %collective-permute-done.a1), channel_id=1, source_target_pairs={{1,2},{2,3},{3,4},{4,5},{5,6},{6,7},{7,8},{8,9},{9,10},{10,11},{11... | collective-permute-start | bytes 786440 | tf_op jit(solution)/shard_map/ppermute | solution.py:244
  20.7 11.1 %collective-permute-start.3 = (bf16[128,1024]{1,0:T(8,128)(2,1)S(1)}, bf16[128,1024]{1,0:T(8,128)(2,1)S(1)}, u32[]{:S(2)}, u32[]{:S(2)}) collective-permute-start(bf16[128,1024]{1,0:T(8,128)(2,1)S(1)} %collective-permute-done.1.b1), channel_id=1, source_target_pairs={{14,13},{15,14},{0,15},{1,0},{2,1},{3,2},{4,3},{5,4},{17,18},{18,1... | collective-permute-start | bytes 786440 | tf_op jit(solution)/shard_map/ppermute | solution.py:244
  27.6 8.7 %collective-permute-start.4 = (bf16[128,1024]{1,0:T(8,128)(2,1)S(1)}, bf16[128,1024]{1,0:T(8,128)(2,1)S(1)}, u32[]{:S(2)}, u32[]{:S(2)}) collective-permute-start(bf16[128,1024]{1,0:T(8,128)(2,1)S(1)} %collective-permute-done.2.a2), channel_id=1, source_target_pairs={{2,3},{3,4},{4,5},{5,6},{6,7},{7,8},{8,9},{9,10},{10,11},{11,12},{... | collective-permute-start | bytes 786440 | tf_op jit(solution)/shard_map/ppermute | solution.py:244
  31.8 8.3 %collective-permute-start.5 = (bf16[128,1024]{1,0:T(8,128)(2,1)S(1)}, bf16[128,1024]{1,0:T(8,128)(2,1)S(1)}, u32[]{:S(2)}, u32[]{:S(2)}) collective-permute-start(bf16[128,1024]{1,0:T(8,128)(2,1)S(1)} %collective-permute-done.3.b2), channel_id=1, source_target_pairs={{13,12},{14,13},{15,14},{0,15},{1,0},{2,1},{3,2},{4,3},{18,19},{19... | collective-permute-start | bytes 786440 | tf_op jit(solution)/shard_map/ppermute | solution.py:244
  36.3 13.4 %collective-permute-start.6 = (bf16[128,1024]{1,0:T(8,128)(2,1)S(1)}, bf16[128,1024]{1,0:T(8,128)(2,1)S(1)}, u32[]{:S(2)}, u32[]{:S(2)}) collective-permute-start(bf16[128,1024]{1,0:T(8,128)(2,1)S(1)} %collective-permute-done.4.rest_0_.a), channel_id=1, source_target_pairs={{3,4},{4,5},{5,6},{6,7},{7,8},{8,9},{9,10},{10,11},{11,12},{12,13}... | collective-permute-start | bytes 786440 | tf_op jit(solution)/shard_map/ppermute | solution.py:244
  40.1 10.4 %collective-permute-start.7 = (bf16[128,1024]{1,0:T(8,128)(2,1)S(1)}, bf16[128,1024]{1,0:T(8,128)(2,1)S(1)}, u32[]{:S(2)}, u32[]{:S(2)}) collective-permute-start(bf16[128,1024]{1,0:T(8,128)(2,1)S(1)} %collective-permute-done.5.rest_1_.b), channel_id=1, source_target_pairs={{12,11},{13,12},{14,13},{15,14},{0,15},{1,0},{2,1},{3,2},{19,20},{... | collective-permute-start | bytes 786440 | tf_op jit(solution)/shard_map/ppermute | solution.py:244
  45.2 1.0 copy-start.1
  49.8 4.8 %collective-permute-start.8 = (bf16[128,1024]{1,0:T(8,128)(2,1)S(1)}, bf16[128,1024]{1,0:T(8,128)(2,1)S(1)}, u32[]{:S(2)}, u32[]{:S(2)}) collective-permute-start(bf16[128,1024]{1,0:T(8,128)(2,1)S(1)} %collective-permute-done.6.rest_2_.a), channel_id=1, source_target_pairs={{4,5},{5,6},{6,7},{7,8},{8,9},{9,10},{10,11},{11,12},{12,13},{13,1... | collective-permute-start | bytes 786440 | tf_op jit(solution)/shard_map/ppermute | solution.py:244
  50.5 8.3 %collective-permute-start.9 = (bf16[128,1024]{1,0:T(8,128)(2,1)S(1)}, bf16[128,1024]{1,0:T(8,128)(2,1)S(1)}, u32[]{:S(2)}, u32[]{:S(2)}) collective-permute-start(bf16[128,1024]{1,0:T(8,128)(2,1)S(1)} %collective-permute-done.7.rest_3_.b), channel_id=1, source_target_pairs={{11,10},{12,11},{13,12},{14,13},{15,14},{0,15},{1,0},{2,1},{20,21}... | collective-permute-start | bytes 786440 | tf_op jit(solution)/shard_map/ppermute | solution.py:244
  54.5 9.8 %collective-permute-start.10 = (bf16[128,1024]{1,0:T(8,128)(2,1)S(1)}, bf16[128,1024]{1,0:T(8,128)(2,1)S(1)}, u32[]{:S(2)}, u32[]{:S(2)}) collective-permute-start(bf16[128,1024]{1,0:T(8,128)(2,1)S(1)} %collective-permute-done.8.rest_0_.a), channel_id=1, source_target_pairs={{5,6},{6,7},{7,8},{8,9},{9,10},{10,11},{11,12},{12,13},{13,14},{14... | collective-permute-start | bytes 786440 | tf_op jit(solution)/shard_map/ppermute | solution.py:244
  58.7 8.9 %collective-permute-start.11 = (bf16[128,1024]{1,0:T(8,128)(2,1)S(1)}, bf16[128,1024]{1,0:T(8,128)(2,1)S(1)}, u32[]{:S(2)}, u32[]{:S(2)}) collective-permute-start(bf16[128,1024]{1,0:T(8,128)(2,1)S(1)} %collective-permute-done.9.rest_1_.b), channel_id=1, source_target_pairs={{10,9},{11,10},{12,11},{13,12},{14,13},{15,14},{0,15},{1,0},{21,22... | collective-permute-start | bytes 786440 | tf_op jit(solution)/shard_map/ppermute | solution.py:244
  64.4 4.5 %collective-permute-start.12 = (bf16[128,1024]{1,0:T(8,128)(2,1)S(1)}, bf16[128,1024]{1,0:T(8,128)(2,1)S(1)}, u32[]{:S(2)}, u32[]{:S(2)}) collective-permute-start(bf16[128,1024]{1,0:T(8,128)(2,1)S(1)} %collective-permute-done.10.rest_2_.a), channel_id=1, source_target_pairs={{6,7},{7,8},{8,9},{9,10},{10,11},{11,12},{12,13},{13,14},{14,15},{... | collective-permute-start | bytes 786440 | tf_op jit(solution)/shard_map/ppermute | solution.py:244
  67.6 1.3 collective-permute-start.13
  70.7 2.2 %collective-permute-start.21 = (bf16[128,1024]{1,0:T(8,128)(2,1)S(1)}, bf16[128,1024]{1,0:T(8,128)(2,1)S(1)}, u32[]{:S(2)}, u32[]{:S(2)}) collective-permute-start(bf16[128,1024]{1,0:T(8,128)(2,1)S(1)} %get-tuple-element.66), channel_id=1, source_target_pairs={{8,9},{9,10},{10,11},{11,12},{12,13},{13,14},{14,15},{15,0},{23,22... | collective-permute-start | bytes 786440 | tf_op jit(solution)/shard_map/ppermute | solution.py:244
  71.5 2.7 %collective-permute-start.14 = (bf16[128,1024]{1,0:T(8,128)(2,1)S(1)}, bf16[128,1024]{1,0:T(8,128)(2,1)S(1)}, u32[]{:S(2)}, u32[]{:S(2)}) collective-permute-start(bf16[128,1024]{1,0:T(8,128)(2,1)S(1)} %get-tuple-element.59), channel_id=1, source_target_pairs={{7,6},{8,7},{9,8},{10,9},{11,10},{12,11},{13,12},{14,13},{15,14},{... | collective-permute-start | bytes 786440 | tf_op jit(solution)/shard_map/ppermute | solution.py:244
  73.0 28.1 %collective-permute-start.22 = (bf16[128,1024]{1,0:T(8,128)(2,1)S(1)}, bf16[128,1024]{1,0:T(8,128)(2,1)S(1)}, u32[]{:S(2)}, u32[]{:S(2)}) collective-permute-start(bf16[128,1024]{1,0:T(8,128)(2,1)S(1)} %add_convert_fusion.5), channel_id=1, source_target_pairs={{9,10},{10,11},{11,12},{12,13},{13,14},{14,15},{15,0},{0,1},{22,21... | collective-permute-start | bytes 786440 | tf_op jit(solution)/shard_map/ppermute | solution.py:244
  74.3 28.7 %collective-permute-start.15 = (bf16[128,1024]{1,0:T(8,128)(2,1)S(1)}, bf16[128,1024]{1,0:T(8,128)(2,1)S(1)}, u32[]{:S(2)}, u32[]{:S(2)}) collective-permute-start(bf16[128,1024]{1,0:T(8,128)(2,1)S(1)} %add_convert_fusion.11), channel_id=1, source_target_pairs={{6,5},{7,6},{8,7},{9,8},{10,9},{11,10},{12,11},{13,12},{14,13},{15... | collective-permute-start | bytes 786440 | tf_op jit(solution)/shard_map/ppermute | solution.py:244
  101.2 11.1 %collective-permute-start.23 = (bf16[128,1024]{1,0:T(8,128)(2,1)S(1)}, bf16[128,1024]{1,0:T(8,128)(2,1)S(1)}, u32[]{:S(2)}, u32[]{:S(2)}) collective-permute-start(bf16[128,1024]{1,0:T(8,128)(2,1)S(1)} %add_convert_fusion.4), channel_id=1, source_target_pairs={{10,11},{11,12},{12,13},{13,14},{14,15},{15,0},{0,1},{1,2},{21,20}... | collective-permute-start | bytes 786440 | tf_op jit(solution)/shard_map/ppermute | solution.py:244
  103.2 11.1 %collective-permute-start.16 = (bf16[128,1024]{1,0:T(8,128)(2,1)S(1)}, bf16[128,1024]{1,0:T(8,128)(2,1)S(1)}, u32[]{:S(2)}, u32[]{:S(2)}) collective-permute-start(bf16[128,1024]{1,0:T(8,128)(2,1)S(1)} %add_convert_fusion.10), channel_id=1, source_target_pairs={{5,4},{6,5},{7,6},{8,7},{9,8},{10,9},{11,10},{12,11},{13,12},{14,1... | collective-permute-start | bytes 786440 | tf_op jit(solution)/shard_map/ppermute | solution.py:244
  112.3 12.4 %collective-permute-start.24 = (bf16[128,1024]{1,0:T(8,128)(2,1)S(1)}, bf16[128,1024]{1,0:T(8,128)(2,1)S(1)}, u32[]{:S(2)}, u32[]{:S(2)}) collective-permute-start(bf16[128,1024]{1,0:T(8,128)(2,1)S(1)} %add_convert_fusion.3), channel_id=1, source_target_pairs={{11,12},{12,13},{13,14},{14,15},{15,0},{0,1},{1,2},{2,3},{20,19},{... | collective-permute-start | bytes 786440 | tf_op jit(solution)/shard_map/ppermute | solution.py:244
  114.4 13.2 %collective-permute-start.17 = (bf16[128,1024]{1,0:T(8,128)(2,1)S(1)}, bf16[128,1024]{1,0:T(8,128)(2,1)S(1)}, u32[]{:S(2)}, u32[]{:S(2)}) collective-permute-start(bf16[128,1024]{1,0:T(8,128)(2,1)S(1)} %add_convert_fusion.9), channel_id=1, source_target_pairs={{4,3},{5,4},{6,5},{7,6},{8,7},{9,8},{10,9},{11,10},{12,11},{13,12}... | collective-permute-start | bytes 786440 | tf_op jit(solution)/shard_map/ppermute | solution.py:244
  125.5 4.2 %copy-start.2 = (bf16[128,2048]{1,0:T(8,128)(2,1)S(1)}, bf16[128,2048]{1,0:T(8,128)(2,1)}, u32[]{:S(2)}) copy-start(bf16[128,2048]{1,0:T(8,128)(2,1)} %g_ref.13) | copy-start | bytes 1572868
  125.5 12.2 %collective-permute-start.25 = (bf16[128,1024]{1,0:T(8,128)(2,1)}, bf16[128,1024]{1,0:T(8,128)(2,1)}, u32[]{:S(2)}, u32[]{:S(2)}) collective-permute-start(bf16[128,1024]{1,0:T(8,128)(2,1)} %add_convert_fusion.2), channel_id=1, source_target_pairs={{12,13},{13,14},{14,15},{15,0},{0,1},{1,2},{2,3},{3,4},{19,18},{20... | collective-permute-start | bytes 786440 | tf_op jit(solution)/shard_map/ppermute | solution.py:244
  128.3 9.4 %collective-permute-start.18 = (bf16[128,1024]{1,0:T(8,128)(2,1)}, bf16[128,1024]{1,0:T(8,128)(2,1)}, u32[]{:S(2)}, u32[]{:S(2)}) collective-permute-start(bf16[128,1024]{1,0:T(8,128)(2,1)} %add_convert_fusion.8), channel_id=1, source_target_pairs={{3,2},{4,3},{5,4},{6,5},{7,6},{8,7},{9,8},{10,9},{11,10},{12,11},{... | collective-permute-start | bytes 786440 | tf_op jit(solution)/shard_map/ppermute | solution.py:244
  138.9 10.8 %collective-permute-start.19 = (bf16[128,1024]{1,0:T(8,128)(2,1)S(1)}, bf16[128,1024]{1,0:T(8,128)(2,1)S(1)}, u32[]{:S(2)}, u32[]{:S(2)}) collective-permute-start(bf16[128,1024]{1,0:T(8,128)(2,1)S(1)} %get-tuple-element.76), channel_id=1, source_target_pairs={{2,1},{3,2},{4,3},{5,4},{6,5},{7,6},{8,7},{9,8},{10,9},{11,10},{12... | collective-permute-start | bytes 786440 | tf_op jit(solution)/shard_map/ppermute | solution.py:244
  140.2 9.5 %collective-permute-start.26 = (bf16[128,1024]{1,0:T(8,128)(2,1)S(1)}, bf16[128,1024]{1,0:T(8,128)(2,1)S(1)}, u32[]{:S(2)}, u32[]{:S(2)}) collective-permute-start(bf16[128,1024]{1,0:T(8,128)(2,1)S(1)} %get-tuple-element.77), channel_id=1, source_target_pairs={{13,14},{14,15},{15,0},{0,1},{1,2},{2,3},{3,4},{4,5},{18,17},{19,1... | collective-permute-start | bytes 786440 | tf_op jit(solution)/shard_map/ppermute | solution.py:244
  149.9 20.5 %collective-permute-start.20 = (bf16[128,1024]{1,0:T(8,128)(2,1)S(1)}, bf16[128,1024]{1,0:T(8,128)(2,1)S(1)}, u32[]{:S(2)}, u32[]{:S(2)}) collective-permute-start(bf16[128,1024]{1,0:T(8,128)(2,1)S(1)} %get-tuple-element.74), channel_id=1, source_target_pairs={{1,0},{2,1},{3,2},{4,3},{5,4},{6,5},{7,6},{8,7},{9,8},{10,9},{11,1... | collective-permute-start | bytes 786440 | tf_op jit(solution)/shard_map/ppermute | solution.py:244
  166.5 12.0 %collective-permute-start.27 = (bf16[128,1024]{1,0:T(8,128)(2,1)S(1)}, bf16[128,1024]{1,0:T(8,128)(2,1)S(1)}, u32[]{:S(2)}, u32[]{:S(2)}) collective-permute-start(bf16[128,1024]{1,0:T(8,128)(2,1)S(1)} %get-tuple-element.75), channel_id=1, source_target_pairs={{14,0},{15,1},{0,2},{1,3},{2,4},{3,5},{4,6},{5,7},{17,16},{18,17},... | collective-permute-start | bytes 786440 | tf_op jit(solution)/shard_map/ppermute | solution.py:244

commit v4 on v3

--- a/solution.py
+++ b/solution.py
@@ -49,11 +49,11 @@
 
 
 def keys_of(blocks, g):
-    return jnp.concatenate([b[:, g * HD : (g + 1) * HD] for b in blocks], axis=0)
+    return jnp.concatenate([k[:, g * HD : (g + 1) * HD] for k, _ in blocks], axis=0)
 
 
 def values_of(blocks, g):
-    return jnp.concatenate([b[:, WIDE + g * HD : WIDE + (g + 1) * HD] for b in blocks], axis=0)
+    return jnp.concatenate([v[:, g * HD : (g + 1) * HD] for _, v in blocks], axis=0)
 
 
 def allowed_keys(scal, first_ref, backs, rows):
@@ -98,10 +98,11 @@
         acc_ref[g] = acc_ref[g] + dot_tn(k, grad_scores)
         grad_k = dot_nn(grad_scores, q) * SCALE
         grad_v = dot_nn(probs.astype(jnp.bfloat16), grads)
-        for i, out in enumerate(outs):
+        cols = slice(g * HD, (g + 1) * HD)
+        for i, (out_k, out_v) in enumerate(outs):
             part = slice(i * rows, (i + 1) * rows)
-            out[:, g * HD : (g + 1) * HD] = grad_k[part].astype(out.dtype)
-            out[:, WIDE + g * HD : WIDE + (g + 1) * HD] = grad_v[part].astype(out.dtype)
+            out_k[:, cols] = grad_k[part].astype(out_k.dtype)
+            out_v[:, cols] = grad_v[part].astype(out_v.dtype)
 
 
 def backs_of(scal, step):
@@ -118,16 +119,25 @@
         return jnp.where(self.even, self.a[at], self.b[at])
 
 
-def first_kernel(scal, first_ref, q_ref, g_ref, own, a1, b1, a2, b2, top, total, acc, turned):
+def near_blocks(scal, arrays):
+    ak1, av1, bk1, bv1, ak2, av2, bk2, bv2 = arrays
+    return [
+        (Near(scal, ak1, bk1), Near(scal, av1, bv1)),
+        (Near(scal, ak2, bk2), Near(scal, av2, bv2)),
+    ]
+
+
+def first_kernel(scal, first_ref, q_ref, g_ref, own_k, own_v, *rest):
+    top, total, acc, turned = rest[8:]
     rows = q_ref.shape[0]
     top[...] = jnp.full(top.shape, neg_big, jnp.float32)
     total[...] = jnp.zeros(total.shape, jnp.float32)
     acc[...] = jnp.zeros(acc.shape, jnp.float32)
-    forward_part(scal, first_ref, q_ref, [own], [0], top, total, acc)
+    forward_part(scal, first_ref, q_ref, [(own_k, own_v)], [0], top, total, acc)
 
     @pl.when(scal[1] >= 1)
     def _():
-        near = [Near(scal, a1, b1), Near(scal, a2, b2)]
+        near = near_blocks(scal, rest[:8])
         forward_part(scal, first_ref, q_ref, near, [1, 2], top, total, acc)
 
     for g in range(KVH):
@@ -135,7 +145,7 @@
 
 
 def more_kernel(steps, scal, first_ref, q_ref, top_in, total_in, acc_in, *rest):
-    blocks, (top, total, acc) = rest[: 2 * len(steps)], rest[2 * len(steps) :]
+    blocks, (top, total, acc) = rest[: 4 * len(steps)], rest[4 * len(steps) :]
     top[...] = top_in[...]
     total[...] = total_in[...]
     acc[...] = acc_in[...]
@@ -143,13 +153,14 @@
 
         @pl.when(scal[1] >= step)
         def _(i=i, step=step):
-            pair = blocks[2 * i : 2 * i + 2]
+            ak, av, bk, bv = blocks[4 * i : 4 * i + 4]
+            pair = [(ak, av), (bk, bv)]
             forward_part(scal, first_ref, q_ref, pair, backs_of(scal, step), top, total, acc)
 
 
 def middle_kernel(
-    scal, first_ref, q_ref, g_ref, turned, top_in, total_in, acc_in, a, b,
-    out_ref, log_ref, inner_ref, gq_acc, term_a, term_b, acc,
+    scal, first_ref, q_ref, g_ref, turned, top_in, total_in, acc_in, ak, av, bk, bv,
+    out_ref, log_ref, inner_ref, gq_acc, tak, tav, tbk, tbv, acc,
 ):
     log_ref[...] = top_in[...]
     inner_ref[...] = total_in[...]
@@ -158,7 +169,7 @@
     @pl.when(scal[1] >= STEPS)
     def _():
         backs = backs_of(scal, STEPS)
-        forward_part(scal, first_ref, q_ref, [a, b], backs, log_ref, inner_ref, acc)
+        forward_part(scal, first_ref, q_ref, [(ak, av), (bk, bv)], backs, log_ref, inner_ref, acc)
 
     for g in range(KVH):
         total = inner_ref[g]
@@ -167,50 +178,56 @@
         inner_ref[g] = jnp.sum(attended * turned[g], axis=0, keepdims=True)
         put_heads(out_ref, g, attended)
     gq_acc[...] = jnp.zeros(gq_acc.shape, jnp.float32)
-    back_step(STEPS, scal, first_ref, q_ref, g_ref, a, b, log_ref, inner_ref, gq_acc, term_a, term_b)
-
-
-def back_step(step, scal, first_ref, q_ref, g_ref, a, b, log_ref, inner_ref, acc, term_a, term_b):
+    blocks, terms = [(ak, av), (bk, bv)], [(tak, tav), (tbk, tbv)]
+    back_step(STEPS, scal, first_ref, q_ref, g_ref, blocks, log_ref, inner_ref, gq_acc, terms)
+
+
+def clear(terms):
+    for pair in terms:
+        for term in pair:
+            term[...] = jnp.zeros(term.shape, term.dtype)
+
+
+def back_step(step, scal, first_ref, q_ref, g_ref, blocks, log_ref, inner_ref, acc, terms):
     @pl.when(scal[1] >= step)
     def _():
         backs = backs_of(scal, step)
         backward_part(
-            scal, first_ref, q_ref, g_ref, [a, b], backs, log_ref, inner_ref, acc, [term_a, term_b]
+            scal, first_ref, q_ref, g_ref, blocks, backs, log_ref, inner_ref, acc, terms
         )
 
     @pl.when(scal[1] < step)
     def _():
-        term_a[...] = jnp.zeros(term_a.shape, term_a.dtype)
-        term_b[...] = jnp.zeros(term_b.shape, term_b.dtype)
+        clear(terms)
 
 
 def back_kernel(
-    step, scal, first_ref, q_ref, g_ref, log_ref, inner_ref, acc_in, a, b, acc, term_a, term_b
+    step, scal, first_ref, q_ref, g_ref, log_ref, inner_ref, acc_in, ak, av, bk, bv,
+    acc, tak, tav, tbk, tbv,
 ):
     acc[...] = acc_in[...]
-    back_step(step, scal, first_ref, q_ref, g_ref, a, b, log_ref, inner_ref, acc, term_a, term_b)
-
-
-def last_kernel(
-    scal, first_ref, q_ref, g_ref, log_ref, inner_ref, acc_in, own, a1, b1, a2, b2,
-    gq_ref, term_0, term_1, term_2, acc,
-):
+    blocks, terms = [(ak, av), (bk, bv)], [(tak, tav), (tbk, tbv)]
+    back_step(step, scal, first_ref, q_ref, g_ref, blocks, log_ref, inner_ref, acc, terms)
+
+
+def last_kernel(scal, first_ref, q_ref, g_ref, log_ref, inner_ref, acc_in, own_k, own_v, *rest):
+    gq_ref, tk0, tv0, tk1, tv1, tk2, tv2, acc = rest[8:]
     acc[...] = acc_in[...]
     backward_part(
-        scal, first_ref, q_ref, g_ref, [own], [0], log_ref, inner_ref, acc, [term_0]
+        scal, first_ref, q_ref, g_ref, [(own_k, own_v)], [0], log_ref, inner_ref, acc, [(tk0, tv0)]
     )
+    terms = [(tk1, tv1), (tk2, tv2)]
 
     @pl.when(scal[1] >= 1)
     def _():
-        near = [Near(scal, a1, b1), Near(scal, a2, b2)]
+        near = near_blocks(scal, rest[:8])
         backward_part(
-            scal, first_ref, q_ref, g_ref, near, [1, 2], log_ref, inner_ref, acc, [term_1, term_2]
+            scal, first_ref, q_ref, g_ref, near, [1, 2], log_ref, inner_ref, acc, terms
         )
 
     @pl.when(scal[1] < 1)
     def _():
-        term_1[...] = jnp.zeros(term_1.shape, term_1.dtype)
-        term_2[...] = jnp.zeros(term_2.shape, term_2.dtype)
+        clear(terms)
 
     for g in range(KVH):
         put_heads(gq_ref, g, acc[g] * SCALE)
@@ -264,69 +281,72 @@
     return (a.astype(jnp.float32) + b.astype(jnp.float32)).astype(jnp.bfloat16)
 
 
+def step_all(held, pairs):
+    return [both_ways(x, *pairs, i // 2) for i, x in enumerate(held)]
+
+
 def local(queries, keys, values, out_grad, segment_ids):
     rows = queries.shape[0]
     count = lax.axis_size("ctx")
     odd = lax.rem(lax.axis_index("dp"), 2)
     q_start = lax.axis_index("ctx") * rows
-    own = jnp.concatenate([keys, values], axis=1)
     q_seg = lax.dynamic_slice_in_dim(segment_ids, q_start, rows, 0)
     first = jnp.sum((segment_ids[:, None] < q_seg[None, :]).astype(jnp.int32), axis=0, keepdims=True)
     scal = jnp.stack([q_start, (q_start - first[0, 0] + rows - 1) // rows, odd]).astype(jnp.int32)
 
-    block = jax.ShapeDtypeStruct(own.shape, jnp.bfloat16)
+    block = jax.ShapeDtypeStruct(keys.shape, jnp.bfloat16)
+    exact = jax.ShapeDtypeStruct(keys.shape, jnp.float32)
     wide = jax.ShapeDtypeStruct(queries.shape, jnp.bfloat16)
-    a, b, tops = [own], [own], {}
+    chains, tops = [[keys, values, keys, values]], {}
     for step in range(1, STEPS + 1):
-        pairs = gather_pairs(step, count)
-        to_a = a[-1]
+        held = list(chains[-1])
         if step in (5, 7):
-            to_a, _ = lax.optimization_barrier((to_a, tops[step - 3]))
-        a.append(both_ways(to_a, *pairs, 0))
-        b.append(both_ways(b[-1], *pairs, 1))
+            held[0], _ = lax.optimization_barrier((held[0], tops[step - 3]))
+        chains.append(step_all(held, gather_pairs(step, count)))
         if step == 2:
             top, total, acc, turned = call(
                 first_kernel, [ROW, ROW, TURNED, TURNED], 0.8,
-                scal, first, queries, out_grad, own, a[1], b[1], a[2], b[2],
+                scal, first, queries, out_grad, keys, values, *chains[1], *chains[2],
             )
         elif step in (4, 6):
-            pairs = [x for i in (step - 1, step) for x in (a[i], b[i])]
             top, total, acc = call(
                 functools.partial(more_kernel, (step - 1, step)), [ROW, ROW, TURNED], 1.0,
-                scal, first, queries, top, total, acc, *pairs,
+                scal, first, queries, top, total, acc, *chains[step - 1], *chains[step],
             )
         tops[step] = top if step > 1 else None
-    attended, log_total, inner, acc, term_a, term_b = call(
-        middle_kernel, [wide, ROW, ROW, TURNED, block, block], 1.5,
-        scal, first, queries, out_grad, turned, top, total, acc, a[STEPS], b[STEPS],
+    attended, log_total, inner, acc, *terms = call(
+        middle_kernel, [wide, ROW, ROW, TURNED] + [block] * 4, 1.5,
+        scal, first, queries, out_grad, turned, top, total, acc, *chains[STEPS],
         scratch=[pltpu.VMEM((KVH, HD, LANES), jnp.float32)],
     )
 
-    sum_a, sum_b = term_a, term_b
+    sums = terms
     for step in range(1, STEPS + 1):
-        pairs = return_pairs(step, count)
-        sum_a = both_ways(sum_a, *pairs, 0)
-        sum_b = both_ways(sum_b, *pairs, 1)
         back = STEPS - step
+        if step > 1 and back >= 2:
+            acc, _ = lax.optimization_barrier((acc, sums[0]))
+        sums = step_all(sums, return_pairs(step, count))
         if back >= 3:
-            acc, term_a, term_b = call(
-                functools.partial(back_kernel, back), [TURNED, block, block], 1.2,
-                scal, first, queries, out_grad, log_total, inner, acc, a[back], b[back],
+            acc, *terms = call(
+                functools.partial(back_kernel, back), [TURNED] + [block] * 4, 1.2,
+                scal, first, queries, out_grad, log_total, inner, acc, *chains[back],
             )
-            sum_a, sum_b = add_low(sum_a, term_a), add_low(sum_b, term_b)
+            sums = [add_low(x, term) for x, term in zip(sums, terms)]
         elif back >= 1:
             if back == 2:
-                grad_query, term_0, term_1, term_2 = call(
-                    last_kernel, [wide, jax.ShapeDtypeStruct(own.shape, jnp.float32), block, block], 2.0,
-                    scal, first, queries, out_grad, log_total, inner, acc, own, a[1], b[1], a[2], b[2],
+                grad_query, own_k, own_v, *terms = call(
+                    last_kernel, [wide, exact, exact] + [block] * 4, 2.0,
+                    scal, first, queries, out_grad, log_total, inner, acc,
+                    keys, values, *chains[1], *chains[2],
                     scratch=[pltpu.VMEM((KVH, HD, LANES), jnp.float32)],
                 )
-            term = term_2 if back == 2 else term_1
-            nothing = jnp.zeros_like(term)
-            sum_a = add_low(sum_a, jnp.where(odd == 0, term, nothing))
-            sum_b = add_low(sum_b, jnp.where(odd == 1, term, nothing))
-    summed = sum_a.astype(jnp.float32) + sum_b.astype(jnp.float32) + term_0
-    return (attended, grad_query, summed[:, :WIDE], summed[:, WIDE:])
+            near = terms[2 * back - 2 : 2 * back]
+            sums = [
+                add_low(x, jnp.where(odd == i // 2, near[i % 2], jnp.zeros_like(x)))
+                for i, x in enumerate(sums)
+            ]
+    a_k, a_v, b_k, b_v = [x.astype(jnp.float32) for x in sums]
+    return (attended, grad_query, a_k + b_k + own_k, a_v + b_v + own_v)
 
 
 def solution(mesh):

time: 180 us -> 549 us (3.05)
  the two profiles are of different devices: /device:TPU:60 before, /device:TPU:24 now
where the time goes in v4:
time: 549 us; the launch traced here: 547 us
  starting transfers between devices  469 us (85%)
  waiting for transfers between devices  49.1 us (9%)
  local copies, waits for them, and re-layouts  12.4 us (2%)
  Pallas kernels  10.8 us (2%)
    ppermute x56, starting transfers between devices, both_ways(): return lax.ppermute(x, ('dp', 'ctx'), pairs)  469 us
    ppermute x56, waiting for transfers between devices, both_ways(): return lax.ppermute(x, ('dp', 'ctx'), pairs)  49.1 us
    unnamed x52, local copies, waits for them, and re-layouts  12.3 us
  transfers between devices with their start and end apart: 56, of which 7 were waited for; matrix products, arithmetic and copies ran while one was open for 1% of the time, Pallas kernels for 2%

profile of v4, /device:TPU:24, one launch (start us, length us, event | category | flops | bytes accessed | tf_op | source)
XLA Modules:
  0.0 547.0 jit_solution(4411697049439349771)
XLA Ops:
  0.6 20.5 %collective-permute-start = (bf16[128,512]{1,0:T(8,128)(2,1)}, bf16[128,512]{1,0:T(8,128)(2,1)S(1)}, u32[]{:S(2)}, u32[]{:S(2)}) collective-permute-start(bf16[128,512]{1,0:T(8,128)(2,1)} %own_k.3), channel_id=1, source_target_pairs={{0,1},{1,2},{2,3},{3,4},{4,5},{5,6},{6,7},{7,8},{8,9},{9,10},{10,1... | collective-permute-start | bytes 393224 | tf_op jit(solution)/shard_map/ppermute | solution.py:261
  21.1 19.0 %collective-permute-start.1 = (bf16[128,512]{1,0:T(8,128)(2,1)}, bf16[128,512]{1,0:T(8,128)(2,1)S(1)}, u32[]{:S(2)}, u32[]{:S(2)}) collective-permute-start(bf16[128,512]{1,0:T(8,128)(2,1)} %own_v.3), channel_id=1, source_target_pairs={{0,1},{1,2},{2,3},{3,4},{4,5},{5,6},{6,7},{7,8},{8,9},{9,10},{10,1... | collective-permute-start | bytes 393224 | tf_op jit(solution)/shard_map/ppermute | solution.py:261
  40.1 19.0 %collective-permute-start.2 = (bf16[128,512]{1,0:T(8,128)(2,1)}, bf16[128,512]{1,0:T(8,128)(2,1)S(1)}, u32[]{:S(2)}, u32[]{:S(2)}) collective-permute-start(bf16[128,512]{1,0:T(8,128)(2,1)} %own_k.3), channel_id=1, source_target_pairs={{0,14},{1,15},{2,0},{3,1},{4,2},{5,3},{6,4},{7,5},{16,17},{17,18},... | collective-permute-start | bytes 393224 | tf_op jit(solution)/shard_map/ppermute | solution.py:261
  59.1 18.8 %collective-permute-start.3 = (bf16[128,512]{1,0:T(8,128)(2,1)}, bf16[128,512]{1,0:T(8,128)(2,1)S(1)}, u32[]{:S(2)}, u32[]{:S(2)}) collective-permute-start(bf16[128,512]{1,0:T(8,128)(2,1)} %own_v.3), channel_id=1, source_target_pairs={{0,14},{1,15},{2,0},{3,1},{4,2},{5,3},{6,4},{7,5},{16,17},{17,18},... | collective-permute-start | bytes 393224 | tf_op jit(solution)/shard_map/ppermute | solution.py:261
  77.9 18.1 %collective-permute-start.4 = (bf16[128,512]{1,0:T(8,128)(2,1)S(1)}, bf16[128,512]{1,0:T(8,128)(2,1)S(1)}, u32[]{:S(2)}, u32[]{:S(2)}) collective-permute-start(bf16[128,512]{1,0:T(8,128)(2,1)S(1)} %collective-permute-done.rest_0_), channel_id=1, source_target_pairs={{1,2},{2,3},{3,4},{4,5},{5,6},{6,7},{7,8},{8,9},{9,10},{10,11},{11... | collective-permute-start | bytes 393224 | tf_op jit(solution)/shard_map/ppermute | solution.py:261
  96.1 19.0 %collective-permute-start.5 = (bf16[128,512]{1,0:T(8,128)(2,1)S(1)}, bf16[128,512]{1,0:T(8,128)(2,1)S(1)}, u32[]{:S(2)}, u32[]{:S(2)}) collective-permute-start(bf16[128,512]{1,0:T(8,128)(2,1)S(1)} %collective-permute-done.1.rest_1_), channel_id=1, source_target_pairs={{1,2},{2,3},{3,4},{4,5},{5,6},{6,7},{7,8},{8,9},{9,10},{10,11},{11... | collective-permute-start | bytes 393224 | tf_op jit(solution)/shard_map/ppermute | solution.py:261
  115.1 19.6 %collective-permute-start.6 = (bf16[128,512]{1,0:T(8,128)(2,1)S(1)}, bf16[128,512]{1,0:T(8,128)(2,1)S(1)}, u32[]{:S(2)}, u32[]{:S(2)}) collective-permute-start(bf16[128,512]{1,0:T(8,128)(2,1)S(1)} %collective-permute-done.2.rest_2_), channel_id=1, source_target_pairs={{14,13},{15,14},{0,15},{1,0},{2,1},{3,2},{4,3},{5,4},{17,18},{18,1... | collective-permute-start | bytes 393224 | tf_op jit(solution)/shard_map/ppermute | solution.py:261
  134.8 18.8 %collective-permute-start.7 = (bf16[128,512]{1,0:T(8,128)(2,1)S(1)}, bf16[128,512]{1,0:T(8,128)(2,1)S(1)}, u32[]{:S(2)}, u32[]{:S(2)}) collective-permute-start(bf16[128,512]{1,0:T(8,128)(2,1)S(1)} %collective-permute-done.3.rest_3_), channel_id=1, source_target_pairs={{14,13},{15,14},{0,15},{1,0},{2,1},{3,2},{4,3},{5,4},{17,18},{18,1... | collective-permute-start | bytes 393224 | tf_op jit(solution)/shard_map/ppermute | solution.py:261
  153.5 18.1 %collective-permute-start.8 = (bf16[128,512]{1,0:T(8,128)(2,1)S(1)}, bf16[128,512]{1,0:T(8,128)(2,1)S(1)}, u32[]{:S(2)}, u32[]{:S(2)}) collective-permute-start(bf16[128,512]{1,0:T(8,128)(2,1)S(1)} %collective-permute-done.4.rest_4_), channel_id=1, source_target_pairs={{2,3},{3,4},{4,5},{5,6},{6,7},{7,8},{8,9},{9,10},{10,11},{11,12},{... | collective-permute-start | bytes 393224 | tf_op jit(solution)/shard_map/ppermute | solution.py:261
  171.7 19.0 %collective-permute-start.9 = (bf16[128,512]{1,0:T(8,128)(2,1)S(1)}, bf16[128,512]{1,0:T(8,128)(2,1)S(1)}, u32[]{:S(2)}, u32[]{:S(2)}) collective-permute-start(bf16[128,512]{1,0:T(8,128)(2,1)S(1)} %collective-permute-done.5.rest_5_), channel_id=1, source_target_pairs={{2,3},{3,4},{4,5},{5,6},{6,7},{7,8},{8,9},{9,10},{10,11},{11,12},{... | collective-permute-start | bytes 393224 | tf_op jit(solution)/shard_map/ppermute | solution.py:261
  190.7 8.6 %collective-permute-start.10 = (bf16[128,512]{1,0:T(8,128)(2,1)S(1)}, bf16[128,512]{1,0:T(8,128)(2,1)S(1)}, u32[]{:S(2)}, u32[]{:S(2)}) collective-permute-start(bf16[128,512]{1,0:T(8,128)(2,1)S(1)} %collective-permute-done.6.rest_6_), channel_id=1, source_target_pairs={{13,12},{14,13},{15,14},{0,15},{1,0},{2,1},{3,2},{4,3},{18,19},{19... | collective-permute-start | bytes 393224 | tf_op jit(solution)/shard_map/ppermute | solution.py:261
  199.3 3.8 collective-permute-start.11
  204.3 0.7 collective-permute-start.13
  205.0 4.3 collective-permute-start.14
  209.4 5.2 collective-permute-start.15
  214.6 1.0 copy-done
  215.7 1.0 copy-done.2
  216.7 0.9 copy-done.4
  217.6 0.9 copy-done.6
  218.5 2.0 shard_map.84
  221.9 5.2 collective-permute-start.18
  227.1 5.9 %collective-permute-start.19 = (bf16[128,512]{1,0:T(8,128)(2,1)S(1)}, bf16[128,512]{1,0:T(8,128)(2,1)S(1)}, u32[]{:S(2)}, u32[]{:S(2)}) collective-permute-start(bf16[128,512]{1,0:T(8,128)(2,1)S(1)} %collective-permute-done.15.rest_7_.bv), channel_id=1, source_target_pairs={{11,10},{12,11},{13,12},{14,13},{15,14},{0,15},{1,0},{2,1},{20,21}... | collective-permute-start | bytes 393224 | tf_op jit(solution)/shard_map/ppermute | solution.py:261
  234.3 5.2 collective-permute-start.22
  239.5 5.2 collective-permute-start.23
  246.8 5.6 %collective-permute-start.26 = (bf16[128,512]{1,0:T(8,128)(2,1)S(1)}, bf16[128,512]{1,0:T(8,128)(2,1)S(1)}, u32[]{:S(2)}, u32[]{:S(2)}) collective-permute-start(bf16[128,512]{1,0:T(8,128)(2,1)S(1)} %collective-permute-done.22.rest_6_.bk), channel_id=1, source_target_pairs={{9,8},{10,9},{11,10},{12,11},{13,12},{14,13},{15,14},{0,15},{22,23... | collective-permute-start | bytes 393224 | tf_op jit(solution)/shard_map/ppermute | solution.py:261
  252.4 5.2 collective-permute-start.27
  258.3 1.8 collective-permute-done.27.bv
  260.1 2.0 shard_map.87
  264.0 1.0 copy-done.21
  265.6 1.3 collective-permute-start.49
  268.2 1.3 collective-permute-start.35
  269.6 0.9 copy-done.11
  270.5 0.9 copy-done.13
  271.4 0.9 copy-done.15
  272.3 0.9 copy-done.17
  273.2 1.2 copy-done.22
  275.1 2.3 collective-permute-done.49
  277.4 0.9 add_convert_fusion.5
  278.3 1.9 collective-permute-start.50
  281.7 10.8 %collective-permute-done.35 = bf16[128,512]{1,0:T(8,128)(2,1)S(1)} collective-permute-done((bf16[128,512]{1,0:T(8,128)(2,1)}, bf16[128,512]{1,0:T(8,128)(2,1)S(1)}, u32[]{:S(2)}, u32[]{:S(2)}) %collective-permute-start.35) | collective-permute-done | bytes 131104 | tf_op jit(solution)/shard_map/ppermute | solution.py:261
  292.5 2.1 collective-permute-start.36
  295.3 5.4 collective-permute-done.50
  300.7 1.9 collective-permute-start.51
  304.1 10.1 %collective-permute-done.36 = bf16[128,512]{1,0:T(8,128)(2,1)S(1)} collective-permute-done((bf16[128,512]{1,0:T(8,128)(2,1)S(1)}, bf16[128,512]{1,0:T(8,128)(2,1)S(1)}, u32[]{:S(2)}, u32[]{:S(2)}) %collective-permute-start.36) | collective-permute-done | bytes 131104 | tf_op jit(solution)/shard_map/ppermute | solution.py:261
  314.3 1.9 collective-permute-start.37
  316.9 1.9 collective-permute-start.52
  320.3 9.0 %collective-permute-done.37 = bf16[128,512]{1,0:T(8,128)(2,1)S(1)} collective-permute-done((bf16[128,512]{1,0:T(8,128)(2,1)S(1)}, bf16[128,512]{1,0:T(8,128)(2,1)S(1)}, u32[]{:S(2)}, u32[]{:S(2)}) %collective-permute-start.37) | collective-permute-done | bytes 131104 | tf_op jit(solution)/shard_map/ppermute | solution.py:261
  329.3 1.9 collective-permute-start.38
  331.9 1.9 collective-permute-start.53
  333.9 23.7 %collective-permute-start.46 = (bf16[128,512]{1,0:T(8,128)(2,1)S(1)}, bf16[128,512]{1,0:T(8,128)(2,1)S(1)}, u32[]{:S(2)}, u32[]{:S(2)}) collective-permute-start(bf16[128,512]{1,0:T(8,128)(2,1)S(1)} %add_convert_fusion.8), channel_id=1, source_target_pairs={{3,2},{4,3},{5,4},{6,5},{7,6},{8,7},{9,8},{10,9},{11,10},{12,11},{... | collective-permute-start | bytes 393224 | tf_op jit(solution)/shard_map/ppermute | solution.py:261
  357.7 19.0 %collective-permute-start.32 = (bf16[128,512]{1,0:T(8,128)(2,1)S(1)}, bf16[128,512]{1,0:T(8,128)(2,1)S(1)}, u32[]{:S(2)}, u32[]{:S(2)}) collective-permute-start(bf16[128,512]{1,0:T(8,128)(2,1)S(1)} %add_convert_fusion.20), channel_id=1, source_target_pairs={{3,2},{4,3},{5,4},{6,5},{7,6},{8,7},{9,8},{10,9},{11,10},{12,11},{... | collective-permute-start | bytes 393224 | tf_op jit(solution)/shard_map/ppermute | solution.py:261
  376.8 4.0 collective-permute-start.39
  380.8 3.0 shard_map.92
  383.9 18.6 %collective-permute-start.47 = (bf16[128,512]{1,0:T(8,128)(2,1)S(1)}, bf16[128,512]{1,0:T(8,128)(2,1)S(1)}, u32[]{:S(2)}, u32[]{:S(2)}) collective-permute-start(bf16[128,512]{1,0:T(8,128)(2,1)S(1)} %get-tuple-element.108), channel_id=1, source_target_pairs={{2,1},{3,2},{4,3},{5,4},{6,5},{7,6},{8,7},{9,8},{10,9},{11,10},{12... | collective-permute-start | bytes 393224 | tf_op jit(solution)/shard_map/ppermute | solution.py:261
  402.6 19.6 %collective-permute-start.54 = (bf16[128,512]{1,0:T(8,128)(2,1)S(1)}, bf16[128,512]{1,0:T(8,128)(2,1)S(1)}, u32[]{:S(2)}, u32[]{:S(2)}) collective-permute-start(bf16[128,512]{1,0:T(8,128)(2,1)S(1)} %get-tuple-element.109), channel_id=1, source_target_pairs={{13,14},{14,15},{15,0},{0,1},{1,2},{2,3},{3,4},{4,5},{18,17},{19,1... | collective-permute-start | bytes 393224 | tf_op jit(solution)/shard_map/ppermute | solution.py:261
  422.3 18.1 %collective-permute-start.33 = (bf16[128,512]{1,0:T(8,128)(2,1)S(1)}, bf16[128,512]{1,0:T(8,128)(2,1)S(1)}, u32[]{:S(2)}, u32[]{:S(2)}) collective-permute-start(bf16[128,512]{1,0:T(8,128)(2,1)S(1)} %get-tuple-element.112), channel_id=1, source_target_pairs={{2,1},{3,2},{4,3},{5,4},{6,5},{7,6},{8,7},{9,8},{10,9},{11,10},{12... | collective-permute-start | bytes 393224 | tf_op jit(solution)/shard_map/ppermute | solution.py:261
  440.5 19.6 %collective-permute-start.40 = (bf16[128,512]{1,0:T(8,128)(2,1)S(1)}, bf16[128,512]{1,0:T(8,128)(2,1)S(1)}, u32[]{:S(2)}, u32[]{:S(2)}) collective-permute-start(bf16[128,512]{1,0:T(8,128)(2,1)S(1)} %get-tuple-element.113), channel_id=1, source_target_pairs={{13,14},{14,15},{15,0},{0,1},{1,2},{2,3},{3,4},{4,5},{18,17},{19,1... | collective-permute-start | bytes 393224 | tf_op jit(solution)/shard_map/ppermute | solution.py:261
  460.2 18.1 %collective-permute-start.48 = (bf16[128,512]{1,0:T(8,128)(2,1)S(1)}, bf16[128,512]{1,0:T(8,128)(2,1)S(1)}, u32[]{:S(2)}, u32[]{:S(2)}) collective-permute-start(bf16[128,512]{1,0:T(8,128)(2,1)S(1)} %get-tuple-element.106), channel_id=1, source_target_pairs={{1,0},{2,1},{3,2},{4,3},{5,4},{6,5},{7,6},{8,7},{9,8},{10,9},{11,1... | collective-permute-start | bytes 393224 | tf_op jit(solution)/shard_map/ppermute | solution.py:261
  478.3 19.7 %collective-permute-start.55 = (bf16[128,512]{1,0:T(8,128)(2,1)S(1)}, bf16[128,512]{1,0:T(8,128)(2,1)S(1)}, u32[]{:S(2)}, u32[]{:S(2)}) collective-permute-start(bf16[128,512]{1,0:T(8,128)(2,1)S(1)} %get-tuple-element.107), channel_id=1, source_target_pairs={{14,0},{15,1},{0,2},{1,3},{2,4},{3,5},{4,6},{5,7},{17,16},{18,17},... | collective-permute-start | bytes 393224 | tf_op jit(solution)/shard_map/ppermute | solution.py:261
  498.1 18.1 %collective-permute-start.34 = (bf16[128,512]{1,0:T(8,128)(2,1)S(1)}, bf16[128,512]{1,0:T(8,128)(2,1)S(1)}, u32[]{:S(2)}, u32[]{:S(2)}) collective-permute-start(bf16[128,512]{1,0:T(8,128)(2,1)S(1)} %get-tuple-element.110), channel_id=1, source_target_pairs={{1,0},{2,1},{3,2},{4,3},{5,4},{6,5},{7,6},{8,7},{9,8},{10,9},{11,1... | collective-permute-start | bytes 393224 | tf_op jit(solution)/shard_map/ppermute | solution.py:261
  516.2 19.7 %collective-permute-start.41 = (bf16[128,512]{1,0:T(8,128)(2,1)S(1)}, bf16[128,512]{1,0:T(8,128)(2,1)S(1)}, u32[]{:S(2)}, u32[]{:S(2)}) collective-permute-start(bf16[128,512]{1,0:T(8,128)(2,1)S(1)} %get-tuple-element.111), channel_id=1, source_target_pairs={{14,0},{15,1},{0,2},{1,3},{2,4},{3,5},{4,6},{5,7},{17,16},{18,17},... | collective-permute-start | bytes 393224 | tf_op jit(solution)/shard_map/ppermute | solution.py:261
  535.9 0.8 add_add_fusion
  536.6 9.6 %collective-permute-done.41 = bf16[128,512]{1,0:T(8,128)(2,1)S(1)} collective-permute-done((bf16[128,512]{1,0:T(8,128)(2,1)S(1)}, bf16[128,512]{1,0:T(8,128)(2,1)S(1)}, u32[]{:S(2)}, u32[]{:S(2)}) %collective-permute-start.41) | collective-permute-done | bytes 131104 | tf_op jit(solution)/shard_map/ppermute | solution.py:261
  546.2 0.8 add_add_fusion.1
  (134 shorter events, 18.0 us)
Async XLA Ops:
  0.6 202.5 %copy-start.25 = (s32[2048]{0:T(1024)S(1)}, s32[2048]{0:T(1024)}, u32[]{:S(2)}) copy-start(s32[2048]{0:T(1024)} %param.9) | copy-start | bytes 24580
  0.6 77.3 %collective-permute-start = (bf16[128,512]{1,0:T(8,128)(2,1)}, bf16[128,512]{1,0:T(8,128)(2,1)S(1)}, u32[]{:S(2)}, u32[]{:S(2)}) collective-permute-start(bf16[128,512]{1,0:T(8,128)(2,1)} %own_k.3), channel_id=1, source_target_pairs={{0,1},{1,2},{2,3},{3,4},{4,5},{5,6},{6,7},{7,8},{8,9},{9,10},{10,1... | collective-permute-start | bytes 393224 | tf_op jit(solution)/shard_map/ppermute | solution.py:261
  21.1 74.9 %collective-permute-start.1 = (bf16[128,512]{1,0:T(8,128)(2,1)}, bf16[128,512]{1,0:T(8,128)(2,1)S(1)}, u32[]{:S(2)}, u32[]{:S(2)}) collective-permute-start(bf16[128,512]{1,0:T(8,128)(2,1)} %own_v.3), channel_id=1, source_target_pairs={{0,1},{1,2},{2,3},{3,4},{4,5},{5,6},{6,7},{7,8},{8,9},{9,10},{10,1... | collective-permute-start | bytes 393224 | tf_op jit(solution)/shard_map/ppermute | solution.py:261
  40.1 75.0 %collective-permute-start.2 = (bf16[128,512]{1,0:T(8,128)(2,1)}, bf16[128,512]{1,0:T(8,128)(2,1)S(1)}, u32[]{:S(2)}, u32[]{:S(2)}) collective-permute-start(bf16[128,512]{1,0:T(8,128)(2,1)} %own_k.3), channel_id=1, source_target_pairs={{0,14},{1,15},{2,0},{3,1},{4,2},{5,3},{6,4},{7,5},{16,17},{17,18},... | collective-permute-start | bytes 393224 | tf_op jit(solution)/shard_map/ppermute | solution.py:261
  59.1 75.6 %collective-permute-start.3 = (bf16[128,512]{1,0:T(8,128)(2,1)}, bf16[128,512]{1,0:T(8,128)(2,1)S(1)}, u32[]{:S(2)}, u32[]{:S(2)}) collective-permute-start(bf16[128,512]{1,0:T(8,128)(2,1)} %own_v.3), channel_id=1, source_target_pairs={{0,14},{1,15},{2,0},{3,1},{4,2},{5,3},{6,4},{7,5},{16,17},{17,18},... | collective-permute-start | bytes 393224 | tf_op jit(solution)/shard_map/ppermute | solution.py:261
  77.9 75.6 %collective-permute-start.4 = (bf16[128,512]{1,0:T(8,128)(2,1)S(1)}, bf16[128,512]{1,0:T(8,128)(2,1)S(1)}, u32[]{:S(2)}, u32[]{:S(2)}) collective-permute-start(bf16[128,512]{1,0:T(8,128)(2,1)S(1)} %collective-permute-done.rest_0_), channel_id=1, source_target_pairs={{1,2},{2,3},{3,4},{4,5},{5,6},{6,7},{7,8},{8,9},{9,10},{10,11},{11... | collective-permute-start | bytes 393224 | tf_op jit(solution)/shard_map/ppermute | solution.py:261
  96.1 75.6 %collective-permute-start.5 = (bf16[128,512]{1,0:T(8,128)(2,1)S(1)}, bf16[128,512]{1,0:T(8,128)(2,1)S(1)}, u32[]{:S(2)}, u32[]{:S(2)}) collective-permute-start(bf16[128,512]{1,0:T(8,128)(2,1)S(1)} %collective-permute-done.1.rest_1_), channel_id=1, source_target_pairs={{1,2},{2,3},{3,4},{4,5},{5,6},{6,7},{7,8},{8,9},{9,10},{10,11},{11... | collective-permute-start | bytes 393224 | tf_op jit(solution)/shard_map/ppermute | solution.py:261
  115.1 75.6 %collective-permute-start.6 = (bf16[128,512]{1,0:T(8,128)(2,1)S(1)}, bf16[128,512]{1,0:T(8,128)(2,1)S(1)}, u32[]{:S(2)}, u32[]{:S(2)}) collective-permute-start(bf16[128,512]{1,0:T(8,128)(2,1)S(1)} %collective-permute-done.2.rest_2_), channel_id=1, source_target_pairs={{14,13},{15,14},{0,15},{1,0},{2,1},{3,2},{4,3},{5,4},{17,18},{18,1... | collective-permute-start | bytes 393224 | tf_op jit(solution)/shard_map/ppermute | solution.py:261
  134.8 64.5 %collective-permute-start.7 = (bf16[128,512]{1,0:T(8,128)(2,1)S(1)}, bf16[128,512]{1,0:T(8,128)(2,1)S(1)}, u32[]{:S(2)}, u32[]{:S(2)}) collective-permute-start(bf16[128,512]{1,0:T(8,128)(2,1)S(1)} %collective-permute-done.3.rest_3_), channel_id=1, source_target_pairs={{14,13},{15,14},{0,15},{1,0},{2,1},{3,2},{4,3},{5,4},{17,18},{18,1... | collective-permute-start | bytes 393224 | tf_op jit(solution)/shard_map/ppermute | solution.py:261
  153.5 50.1 %collective-permute-start.8 = (bf16[128,512]{1,0:T(8,128)(2,1)S(1)}, bf16[128,512]{1,0:T(8,128)(2,1)S(1)}, u32[]{:S(2)}, u32[]{:S(2)}) collective-permute-start(bf16[128,512]{1,0:T(8,128)(2,1)S(1)} %collective-permute-done.4.rest_4_), channel_id=1, source_target_pairs={{2,3},{3,4},{4,5},{5,6},{6,7},{7,8},{8,9},{9,10},{10,11},{11,12},{... | collective-permute-start | bytes 393224 | tf_op jit(solution)/shard_map/ppermute | solution.py:261
  171.7 32.6 %collective-permute-start.9 = (bf16[128,512]{1,0:T(8,128)(2,1)S(1)}, bf16[128,512]{1,0:T(8,128)(2,1)S(1)}, u32[]{:S(2)}, u32[]{:S(2)}) collective-permute-start(bf16[128,512]{1,0:T(8,128)(2,1)S(1)} %collective-permute-done.5.rest_5_), channel_id=1, source_target_pairs={{2,3},{3,4},{4,5},{5,6},{6,7},{7,8},{8,9},{9,10},{10,11},{11,12},{... | collective-permute-start | bytes 393224 | tf_op jit(solution)/shard_map/ppermute | solution.py:261
  190.7 14.3 %collective-permute-start.10 = (bf16[128,512]{1,0:T(8,128)(2,1)S(1)}, bf16[128,512]{1,0:T(8,128)(2,1)S(1)}, u32[]{:S(2)}, u32[]{:S(2)}) collective-permute-start(bf16[128,512]{1,0:T(8,128)(2,1)S(1)} %collective-permute-done.6.rest_6_), channel_id=1, source_target_pairs={{13,12},{14,13},{15,14},{0,15},{1,0},{2,1},{3,2},{4,3},{18,19},{19... | collective-permute-start | bytes 393224 | tf_op jit(solution)/shard_map/ppermute | solution.py:261
  199.3 10.0 %collective-permute-start.11 = (bf16[128,512]{1,0:T(8,128)(2,1)S(1)}, bf16[128,512]{1,0:T(8,128)(2,1)S(1)}, u32[]{:S(2)}, u32[]{:S(2)}) collective-permute-start(bf16[128,512]{1,0:T(8,128)(2,1)S(1)} %collective-permute-done.7.rest_7_), channel_id=1, source_target_pairs={{13,12},{14,13},{15,14},{0,15},{1,0},{2,1},{3,2},{4,3},{18,19},{19... | collective-permute-start | bytes 393224 | tf_op jit(solution)/shard_map/ppermute | solution.py:261
  203.6 16.9 %collective-permute-start.12 = (bf16[128,512]{1,0:T(8,128)(2,1)S(1)}, bf16[128,512]{1,0:T(8,128)(2,1)S(1)}, u32[]{:S(2)}, u32[]{:S(2)}) collective-permute-start(bf16[128,512]{1,0:T(8,128)(2,1)S(1)} %collective-permute-done.8.rest_0_.ak), channel_id=1, source_target_pairs={{3,4},{4,5},{5,6},{6,7},{7,8},{8,9},{9,10},{10,11},{11,12},{12,13}... | collective-permute-start | bytes 393224 | tf_op jit(solution)/shard_map/ppermute | solution.py:261
  204.3 16.9 %collective-permute-start.13 = (bf16[128,512]{1,0:T(8,128)(2,1)S(1)}, bf16[128,512]{1,0:T(8,128)(2,1)S(1)}, u32[]{:S(2)}, u32[]{:S(2)}) collective-permute-start(bf16[128,512]{1,0:T(8,128)(2,1)S(1)} %collective-permute-done.9.rest_1_.av), channel_id=1, source_target_pairs={{3,4},{4,5},{5,6},{6,7},{7,8},{8,9},{9,10},{10,11},{11,12},{12,13}... | collective-permute-start | bytes 393224 | tf_op jit(solution)/shard_map/ppermute | solution.py:261
  205.0 16.9 %collective-permute-start.14 = (bf16[128,512]{1,0:T(8,128)(2,1)S(1)}, bf16[128,512]{1,0:T(8,128)(2,1)S(1)}, u32[]{:S(2)}, u32[]{:S(2)}) collective-permute-start(bf16[128,512]{1,0:T(8,128)(2,1)S(1)} %collective-permute-done.10.rest_2_.bk), channel_id=1, source_target_pairs={{12,11},{13,12},{14,13},{15,14},{0,15},{1,0},{2,1},{3,2},{19,20},{... | collective-permute-start | bytes 393224 | tf_op jit(solution)/shard_map/ppermute | solution.py:261
  209.4 17.7 %collective-permute-start.15 = (bf16[128,512]{1,0:T(8,128)(2,1)S(1)}, bf16[128,512]{1,0:T(8,128)(2,1)S(1)}, u32[]{:S(2)}, u32[]{:S(2)}) collective-permute-start(bf16[128,512]{1,0:T(8,128)(2,1)S(1)} %collective-permute-done.11.rest_3_.bv), channel_id=1, source_target_pairs={{12,11},{13,12},{14,13},{15,14},{0,15},{1,0},{2,1},{3,2},{19,20},{... | collective-permute-start | bytes 393224 | tf_op jit(solution)/shard_map/ppermute | solution.py:261
  220.5 12.4 %collective-permute-start.16 = (bf16[128,512]{1,0:T(8,128)(2,1)S(1)}, bf16[128,512]{1,0:T(8,128)(2,1)S(1)}, u32[]{:S(2)}, u32[]{:S(2)}) collective-permute-start(bf16[128,512]{1,0:T(8,128)(2,1)S(1)} %collective-permute-done.12.rest_4_.ak), channel_id=1, source_target_pairs={{4,5},{5,6},{6,7},{7,8},{8,9},{9,10},{10,11},{11,12},{12,13},{13,1... | collective-permute-start | bytes 393224 | tf_op jit(solution)/shard_map/ppermute | solution.py:261
  221.2 12.4 %collective-permute-start.17 = (bf16[128,512]{1,0:T(8,128)(2,1)S(1)}, bf16[128,512]{1,0:T(8,128)(2,1)S(1)}, u32[]{:S(2)}, u32[]{:S(2)}) collective-permute-start(bf16[128,512]{1,0:T(8,128)(2,1)S(1)} %collective-permute-done.13.rest_5_.av), channel_id=1, source_target_pairs={{4,5},{5,6},{6,7},{7,8},{8,9},{9,10},{10,11},{11,12},{12,13},{13,1... | collective-permute-start | bytes 393224 | tf_op jit(solution)/shard_map/ppermute | solution.py:261
  221.9 12.4 %collective-permute-start.18 = (bf16[128,512]{1,0:T(8,128)(2,1)S(1)}, bf16[128,512]{1,0:T(8,128)(2,1)S(1)}, u32[]{:S(2)}, u32[]{:S(2)}) collective-permute-start(bf16[128,512]{1,0:T(8,128)(2,1)S(1)} %collective-permute-done.14.rest_6_.bk), channel_id=1, source_target_pairs={{11,10},{12,11},{13,12},{14,13},{15,14},{0,15},{1,0},{2,1},{20,21}... | collective-permute-start | bytes 393224 | tf_op jit(solution)/shard_map/ppermute | solution.py:261
  227.1 12.4 %collective-permute-start.19 = (bf16[128,512]{1,0:T(8,128)(2,1)S(1)}, bf16[128,512]{1,0:T(8,128)(2,1)S(1)}, u32[]{:S(2)}, u32[]{:S(2)}) collective-permute-start(bf16[128,512]{1,0:T(8,128)(2,1)S(1)} %collective-permute-done.15.rest_7_.bv), channel_id=1, source_target_pairs={{11,10},{12,11},{13,12},{14,13},{15,14},{0,15},{1,0},{2,1},{20,21}... | collective-permute-start | bytes 393224 | tf_op jit(solution)/shard_map/ppermute | solution.py:261
  232.9 12.4 %collective-permute-start.20 = (bf16[128,512]{1,0:T(8,128)(2,1)S(1)}, bf16[128,512]{1,0:T(8,128)(2,1)S(1)}, u32[]{:S(2)}, u32[]{:S(2)}) collective-permute-start(bf16[128,512]{1,0:T(8,128)(2,1)S(1)} %collective-permute-done.16.rest_0_.ak), channel_id=1, source_target_pairs={{5,6},{6,7},{7,8},{8,9},{9,10},{10,11},{11,12},{12,13},{13,14},{14... | collective-permute-start | bytes 393224 | tf_op jit(solution)/shard_map/ppermute | solution.py:261
  233.6 12.4 %collective-permute-start.21 = (bf16[128,512]{1,0:T(8,128)(2,1)S(1)}, bf16[128,512]{1,0:T(8,128)(2,1)S(1)}, u32[]{:S(2)}, u32[]{:S(2)}) collective-permute-start(bf16[128,512]{1,0:T(8,128)(2,1)S(1)} %collective-permute-done.17.rest_1_.av), channel_id=1, source_target_pairs={{5,6},{6,7},{7,8},{8,9},{9,10},{10,11},{11,12},{12,13},{13,14},{14... | collective-permute-start | bytes 393224 | tf_op jit(solution)/shard_map/ppermute | solution.py:261
  234.3 12.4 %collective-permute-start.22 = (bf16[128,512]{1,0:T(8,128)(2,1)S(1)}, bf16[128,512]{1,0:T(8,128)(2,1)S(1)}, u32[]{:S(2)}, u32[]{:S(2)}) collective-permute-start(bf16[128,512]{1,0:T(8,128)(2,1)S(1)} %collective-permute-done.18.rest_2_.bk), channel_id=1, source_target_pairs={{10,9},{11,10},{12,11},{13,12},{14,13},{15,14},{0,15},{1,0},{21,22... | collective-permute-start | bytes 393224 | tf_op jit(solution)/shard_map/ppermute | solution.py:261
  239.5 18.1 %copy-start.8 = (bf16[128,512]{1,0:T(8,128)(2,1)}, bf16[128,512]{1,0:T(8,128)(2,1)S(1)}, u32[]{:S(2)}) copy-start(bf16[128,512]{1,0:T(8,128)(2,1)S(1)} %collective-permute-done.19.rest_3_.bv) | copy-start | bytes 393220
  239.5 12.9 %collective-permute-start.23 = (bf16[128,512]{1,0:T(8,128)(2,1)S(1)}, bf16[128,512]{1,0:T(8,128)(2,1)S(1)}, u32[]{:S(2)}, u32[]{:S(2)}) collective-permute-start(bf16[128,512]{1,0:T(8,128)(2,1)S(1)} %collective-permute-done.19.rest_3_.bv), channel_id=1, source_target_pairs={{10,9},{11,10},{12,11},{13,12},{14,13},{15,14},{0,15},{1,0},{21,22... | collective-permute-start | bytes 393224 | tf_op jit(solution)/shard_map/ppermute | solution.py:261
  245.4 12.9 %copy-start.10 = (bf16[128,512]{1,0:T(8,128)(2,1)}, bf16[128,512]{1,0:T(8,128)(2,1)S(1)}, u32[]{:S(2)}) copy-start(bf16[128,512]{1,0:T(8,128)(2,1)S(1)} %collective-permute-done.20.rest_4_.ak) | copy-start | bytes 393220
  245.4 12.9 %collective-permute-start.24 = (bf16[128,512]{1,0:T(8,128)(2,1)S(1)}, bf16[128,512]{1,0:T(8,128)(2,1)S(1)}, u32[]{:S(2)}, u32[]{:S(2)}) collective-permute-start(bf16[128,512]{1,0:T(8,128)(2,1)S(1)} %collective-permute-done.20.rest_4_.ak), channel_id=1, source_target_pairs={{6,7},{7,8},{8,9},{9,10},{10,11},{11,12},{12,13},{13,14},{14,15},{... | collective-permute-start | bytes 393224 | tf_op jit(solution)/shard_map/ppermute | solution.py:261
  246.1 12.2 %copy-start.12 = (bf16[128,512]{1,0:T(8,128)(2,1)}, bf16[128,512]{1,0:T(8,128)(2,1)S(1)}, u32[]{:S(2)}) copy-start(bf16[128,512]{1,0:T(8,128)(2,1)S(1)} %collective-permute-done.21.rest_5_.av) | copy-start | bytes 393220
  246.1 12.2 %collective-permute-start.25 = (bf16[128,512]{1,0:T(8,128)(2,1)S(1)}, bf16[128,512]{1,0:T(8,128)(2,1)S(1)}, u32[]{:S(2)}, u32[]{:S(2)}) collective-permute-start(bf16[128,512]{1,0:T(8,128)(2,1)S(1)} %collective-permute-done.21.rest_5_.av), channel_id=1, source_target_pairs={{6,7},{7,8},{8,9},{9,10},{10,11},{11,12},{12,13},{13,14},{14,15},{... | collective-permute-start | bytes 393224 | tf_op jit(solution)/shard_map/ppermute | solution.py:261
  246.8 11.5 %copy-start.14 = (bf16[128,512]{1,0:T(8,128)(2,1)}, bf16[128,512]{1,0:T(8,128)(2,1)S(1)}, u32[]{:S(2)}) copy-start(bf16[128,512]{1,0:T(8,128)(2,1)S(1)} %collective-permute-done.22.rest_6_.bk) | copy-start | bytes 393220
  246.8 11.6 %collective-permute-start.26 = (bf16[128,512]{1,0:T(8,128)(2,1)S(1)}, bf16[128,512]{1,0:T(8,128)(2,1)S(1)}, u32[]{:S(2)}, u32[]{:S(2)}) collective-permute-start(bf16[128,512]{1,0:T(8,128)(2,1)S(1)} %collective-permute-done.22.rest_6_.bk), channel_id=1, source_target_pairs={{9,8},{10,9},{11,10},{12,11},{13,12},{14,13},{15,14},{0,15},{22,23... | collective-permute-start | bytes 393224 | tf_op jit(solution)/shard_map/ppermute | solution.py:261
  252.4 5.9 %copy-start.16 = (bf16[128,512]{1,0:T(8,128)(2,1)}, bf16[128,512]{1,0:T(8,128)(2,1)S(1)}, u32[]{:S(2)}) copy-start(bf16[128,512]{1,0:T(8,128)(2,1)S(1)} %collective-permute-done.23.rest_7_.bv) | copy-start | bytes 393220
  252.4 7.7 %collective-permute-start.27 = (bf16[128,512]{1,0:T(8,128)(2,1)S(1)}, bf16[128,512]{1,0:T(8,128)(2,1)S(1)}, u32[]{:S(2)}, u32[]{:S(2)}) collective-permute-start(bf16[128,512]{1,0:T(8,128)(2,1)S(1)} %collective-permute-done.23.rest_7_.bv), channel_id=1, source_target_pairs={{9,8},{10,9},{11,10},{12,11},{13,12},{14,13},{15,14},{0,15},{22,23... | collective-permute-start | bytes 393224 | tf_op jit(solution)/shard_map/ppermute | solution.py:261
  260.1 9.4 %copy-start.1 = (bf16[128,2048]{1,0:T(8,128)(2,1)S(1)}, bf16[128,2048]{1,0:T(8,128)(2,1)}, u32[]{:S(2)}) copy-start(bf16[128,2048]{1,0:T(8,128)(2,1)} %q_ref.17) | copy-start | bytes 1572868
  265.6 11.8 %collective-permute-start.49 = (bf16[128,512]{1,0:T(8,128)(2,1)}, bf16[128,512]{1,0:T(8,128)(2,1)}, u32[]{:S(2)}, u32[]{:S(2)}) collective-permute-start(bf16[128,512]{1,0:T(8,128)(2,1)} %get-tuple-element.100), channel_id=1, source_target_pairs={{8,9},{9,10},{10,11},{11,12},{12,13},{13,14},{14,15},{15,0},{23,22... | collective-permute-start | bytes 393224 | tf_op jit(solution)/shard_map/ppermute | solution.py:261
  266.9 13.4 %collective-permute-start.28 = (bf16[128,512]{1,0:T(8,128)(2,1)}, bf16[128,512]{1,0:T(8,128)(2,1)S(1)}, u32[]{:S(2)}, u32[]{:S(2)}) collective-permute-start(bf16[128,512]{1,0:T(8,128)(2,1)} %copy-done.20), channel_id=1, source_target_pairs={{7,6},{8,7},{9,8},{10,9},{11,10},{12,11},{13,12},{14,13},{15,14},{... | collective-permute-start | bytes 393224 | tf_op jit(solution)/shard_map/ppermute | solution.py:261
  267.6 13.4 %collective-permute-start.42 = (bf16[128,512]{1,0:T(8,128)(2,1)}, bf16[128,512]{1,0:T(8,128)(2,1)S(1)}, u32[]{:S(2)}, u32[]{:S(2)}) collective-permute-start(bf16[128,512]{1,0:T(8,128)(2,1)} %copy-done.19), channel_id=1, source_target_pairs={{7,6},{8,7},{9,8},{10,9},{11,10},{12,11},{13,12},{14,13},{15,14},{... | collective-permute-start | bytes 393224 | tf_op jit(solution)/shard_map/ppermute | solution.py:261
  268.2 24.3 %collective-permute-start.35 = (bf16[128,512]{1,0:T(8,128)(2,1)}, bf16[128,512]{1,0:T(8,128)(2,1)S(1)}, u32[]{:S(2)}, u32[]{:S(2)}) collective-permute-start(bf16[128,512]{1,0:T(8,128)(2,1)} %copy-done.18), channel_id=1, source_target_pairs={{8,9},{9,10},{10,11},{11,12},{12,13},{13,14},{14,15},{15,0},{23,22... | collective-permute-start | bytes 393224 | tf_op jit(solution)/shard_map/ppermute | solution.py:261
  278.3 22.4 %collective-permute-start.50 = (bf16[128,512]{1,0:T(8,128)(2,1)S(1)}, bf16[128,512]{1,0:T(8,128)(2,1)S(1)}, u32[]{:S(2)}, u32[]{:S(2)}) collective-permute-start(bf16[128,512]{1,0:T(8,128)(2,1)S(1)} %add_convert_fusion.5), channel_id=1, source_target_pairs={{9,10},{10,11},{11,12},{12,13},{13,14},{14,15},{15,0},{0,1},{22,21... | collective-permute-start | bytes 393224 | tf_op jit(solution)/shard_map/ppermute | solution.py:261
  280.3 22.4 %collective-permute-start.29 = (bf16[128,512]{1,0:T(8,128)(2,1)S(1)}, bf16[128,512]{1,0:T(8,128)(2,1)S(1)}, u32[]{:S(2)}, u32[]{:S(2)}) collective-permute-start(bf16[128,512]{1,0:T(8,128)(2,1)S(1)} %add_convert_fusion.23), channel_id=1, source_target_pairs={{6,5},{7,6},{8,7},{9,8},{10,9},{11,10},{12,11},{13,12},{14,13},{15... | collective-permute-start | bytes 393224 | tf_op jit(solution)/shard_map/ppermute | solution.py:261
  281.0 22.4 %collective-permute-start.43 = (bf16[128,512]{1,0:T(8,128)(2,1)S(1)}, bf16[128,512]{1,0:T(8,128)(2,1)S(1)}, u32[]{:S(2)}, u32[]{:S(2)}) collective-permute-start(bf16[128,512]{1,0:T(8,128)(2,1)S(1)} %add_convert_fusion.11), channel_id=1, source_target_pairs={{6,5},{7,6},{8,7},{9,8},{10,9},{11,10},{12,11},{13,12},{14,13},{15... | collective-permute-start | bytes 393224 | tf_op jit(solution)/shard_map/ppermute | solution.py:261
  292.5 21.7 %collective-permute-start.36 = (bf16[128,512]{1,0:T(8,128)(2,1)S(1)}, bf16[128,512]{1,0:T(8,128)(2,1)S(1)}, u32[]{:S(2)}, u32[]{:S(2)}) collective-permute-start(bf16[128,512]{1,0:T(8,128)(2,1)S(1)} %add_convert_fusion.17), channel_id=1, source_target_pairs={{9,10},{10,11},{11,12},{12,13},{13,14},{14,15},{15,0},{0,1},{22,21... | collective-permute-start | bytes 393224 | tf_op jit(solution)/shard_map/ppermute | solution.py:261
  300.7 16.1 %collective-permute-start.51 = (bf16[128,512]{1,0:T(8,128)(2,1)S(1)}, bf16[128,512]{1,0:T(8,128)(2,1)S(1)}, u32[]{:S(2)}, u32[]{:S(2)}) collective-permute-start(bf16[128,512]{1,0:T(8,128)(2,1)S(1)} %add_convert_fusion.4), channel_id=1, source_target_pairs={{10,11},{11,12},{12,13},{13,14},{14,15},{15,0},{0,1},{1,2},{21,20}... | collective-permute-start | bytes 393224 | tf_op jit(solution)/shard_map/ppermute | solution.py:261
  302.7 16.1 %collective-permute-start.30 = (bf16[128,512]{1,0:T(8,128)(2,1)S(1)}, bf16[128,512]{1,0:T(8,128)(2,1)S(1)}, u32[]{:S(2)}, u32[]{:S(2)}) collective-permute-start(bf16[128,512]{1,0:T(8,128)(2,1)S(1)} %add_convert_fusion.22), channel_id=1, source_target_pairs={{5,4},{6,5},{7,6},{8,7},{9,8},{10,9},{11,10},{12,11},{13,12},{14,1... | collective-permute-start | bytes 393224 | tf_op jit(solution)/shard_map/ppermute | solution.py:261
  303.5 16.1 %collective-permute-start.44 = (bf16[128,512]{1,0:T(8,128)(2,1)S(1)}, bf16[128,512]{1,0:T(8,128)(2,1)S(1)}, u32[]{:S(2)}, u32[]{:S(2)}) collective-permute-start(bf16[128,512]{1,0:T(8,128)(2,1)S(1)} %add_convert_fusion.10), channel_id=1, source_target_pairs={{5,4},{6,5},{7,6},{8,7},{9,8},{10,9},{11,10},{12,11},{13,12},{14,1... | collective-permute-start | bytes 393224 | tf_op jit(solution)/shard_map/ppermute | solution.py:261
  314.3 15.0 %collective-permute-start.37 = (bf16[128,512]{1,0:T(8,128)(2,1)S(1)}, bf16[128,512]{1,0:T(8,128)(2,1)S(1)}, u32[]{:S(2)}, u32[]{:S(2)}) collective-permute-start(bf16[128,512]{1,0:T(8,128)(2,1)S(1)} %add_convert_fusion.16), channel_id=1, source_target_pairs={{10,11},{11,12},{12,13},{13,14},{14,15},{15,0},{0,1},{1,2},{21,20}... | collective-permute-start | bytes 393224 | tf_op jit(solution)/shard_map/ppermute | solution.py:261
  316.9 15.0 %collective-permute-start.52 = (bf16[128,512]{1,0:T(8,128)(2,1)S(1)}, bf16[128,512]{1,0:T(8,128)(2,1)S(1)}, u32[]{:S(2)}, u32[]{:S(2)}) collective-permute-start(bf16[128,512]{1,0:T(8,128)(2,1)S(1)} %add_convert_fusion.3), channel_id=1, source_target_pairs={{11,12},{12,13},{13,14},{14,15},{15,0},{0,1},{1,2},{2,3},{20,19},{... | collective-permute-start | bytes 393224 | tf_op jit(solution)/shard_map/ppermute | solution.py:261
  318.9 38.8 %collective-permute-start.31 = (bf16[128,512]{1,0:T(8,128)(2,1)S(1)}, bf16[128,512]{1,0:T(8,128)(2,1)S(1)}, u32[]{:S(2)}, u32[]{:S(2)}) collective-permute-start(bf16[128,512]{1,0:T(8,128)(2,1)S(1)} %add_convert_fusion.21), channel_id=1, source_target_pairs={{4,3},{5,4},{6,5},{7,6},{8,7},{9,8},{10,9},{11,10},{12,11},{13,12}... | collective-permute-start | bytes 393224 | tf_op jit(solution)/shard_map/ppermute | solution.py:261
  319.6 14.3 %collective-permute-start.45 = (bf16[128,512]{1,0:T(8,128)(2,1)S(1)}, bf16[128,512]{1,0:T(8,128)(2,1)S(1)}, u32[]{:S(2)}, u32[]{:S(2)}) collective-permute-start(bf16[128,512]{1,0:T(8,128)(2,1)S(1)} %add_convert_fusion.9), channel_id=1, source_target_pairs={{4,3},{5,4},{6,5},{7,6},{8,7},{9,8},{10,9},{11,10},{12,11},{13,12}... | collective-permute-start | bytes 393224 | tf_op jit(solution)/shard_map/ppermute | solution.py:261
  329.3 47.4 %collective-permute-start.38 = (bf16[128,512]{1,0:T(8,128)(2,1)S(1)}, bf16[128,512]{1,0:T(8,128)(2,1)S(1)}, u32[]{:S(2)}, u32[]{:S(2)}) collective-permute-start(bf16[128,512]{1,0:T(8,128)(2,1)S(1)} %add_convert_fusion.15), channel_id=1, source_target_pairs={{11,12},{12,13},{13,14},{14,15},{15,0},{0,1},{1,2},{2,3},{20,19},{... | collective-permute-start | bytes 393224 | tf_op jit(solution)/shard_map/ppermute | solution.py:261
  331.9 51.9 %collective-permute-start.53 = (bf16[128,512]{1,0:T(8,128)(2,1)S(1)}, bf16[128,512]{1,0:T(8,128)(2,1)S(1)}, u32[]{:S(2)}, u32[]{:S(2)}) collective-permute-start(bf16[128,512]{1,0:T(8,128)(2,1)S(1)} %add_convert_fusion.2), channel_id=1, source_target_pairs={{12,13},{13,14},{14,15},{15,0},{0,1},{1,2},{2,3},{3,4},{19,18},{20... | collective-permute-start | bytes 393224 | tf_op jit(solution)/shard_map/ppermute | solution.py:261
  333.9 49.9 %collective-permute-start.46 = (bf16[128,512]{1,0:T(8,128)(2,1)S(1)}, bf16[128,512]{1,0:T(8,128)(2,1)S(1)}, u32[]{:S(2)}, u32[]{:S(2)}) collective-permute-start(bf16[128,512]{1,0:T(8,128)(2,1)S(1)} %add_convert_fusion.8), channel_id=1, source_target_pairs={{3,2},{4,3},{5,4},{6,5},{7,6},{8,7},{9,8},{10,9},{11,10},{12,11},{... | collective-permute-start | bytes 393224 | tf_op jit(solution)/shard_map/ppermute | solution.py:261
  357.7 64.5 %collective-permute-start.32 = (bf16[128,512]{1,0:T(8,128)(2,1)S(1)}, bf16[128,512]{1,0:T(8,128)(2,1)S(1)}, u32[]{:S(2)}, u32[]{:S(2)}) collective-permute-start(bf16[128,512]{1,0:T(8,128)(2,1)S(1)} %add_convert_fusion.20), channel_id=1, source_target_pairs={{3,2},{4,3},{5,4},{6,5},{7,6},{8,7},{9,8},{10,9},{11,10},{12,11},{... | collective-permute-start | bytes 393224 | tf_op jit(solution)/shard_map/ppermute | solution.py:261
  376.8 4.1 copy-start.5
  376.8 45.4 %collective-permute-start.39 = (bf16[128,512]{1,0:T(8,128)(2,1)S(1)}, bf16[128,512]{1,0:T(8,128)(2,1)S(1)}, u32[]{:S(2)}, u32[]{:S(2)}) collective-permute-start(bf16[128,512]{1,0:T(8,128)(2,1)S(1)} %add_convert_fusion.14), channel_id=1, source_target_pairs={{12,13},{13,14},{14,15},{15,0},{0,1},{1,2},{2,3},{3,4},{19,18},{20... | collective-permute-start | bytes 393224 | tf_op jit(solution)/shard_map/ppermute | solution.py:261
  383.9 76.2 %collective-permute-start.47 = (bf16[128,512]{1,0:T(8,128)(2,1)S(1)}, bf16[128,512]{1,0:T(8,128)(2,1)S(1)}, u32[]{:S(2)}, u32[]{:S(2)}) collective-permute-start(bf16[128,512]{1,0:T(8,128)(2,1)S(1)} %get-tuple-element.108), channel_id=1, source_target_pairs={{2,1},{3,2},{4,3},{5,4},{6,5},{7,6},{8,7},{9,8},{10,9},{11,10},{12... | collective-permute-start | bytes 393224 | tf_op jit(solution)/shard_map/ppermute | solution.py:261
  402.6 57.5 %collective-permute-start.54 = (bf16[128,512]{1,0:T(8,128)(2,1)S(1)}, bf16[128,512]{1,0:T(8,128)(2,1)S(1)}, u32[]{:S(2)}, u32[]{:S(2)}) collective-permute-start(bf16[128,512]{1,0:T(8,128)(2,1)S(1)} %get-tuple-element.109), channel_id=1, source_target_pairs={{13,14},{14,15},{15,0},{0,1},{1,2},{2,3},{3,4},{4,5},{18,17},{19,1... | collective-permute-start | bytes 393224 | tf_op jit(solution)/shard_map/ppermute | solution.py:261
  422.3 75.7 %collective-permute-start.33 = (bf16[128,512]{1,0:T(8,128)(2,1)S(1)}, bf16[128,512]{1,0:T(8,128)(2,1)S(1)}, u32[]{:S(2)}, u32[]{:S(2)}) collective-permute-start(bf16[128,512]{1,0:T(8,128)(2,1)S(1)} %get-tuple-element.112), channel_id=1, source_target_pairs={{2,1},{3,2},{4,3},{5,4},{6,5},{7,6},{8,7},{9,8},{10,9},{11,10},{12... | collective-permute-start | bytes 393224 | tf_op jit(solution)/shard_map/ppermute | solution.py:261
  440.5 57.5 %collective-permute-start.40 = (bf16[128,512]{1,0:T(8,128)(2,1)S(1)}, bf16[128,512]{1,0:T(8,128)(2,1)S(1)}, u32[]{:S(2)}, u32[]{:S(2)}) collective-permute-start(bf16[128,512]{1,0:T(8,128)(2,1)S(1)} %get-tuple-element.113), channel_id=1, source_target_pairs={{13,14},{14,15},{15,0},{0,1},{1,2},{2,3},{3,4},{4,5},{18,17},{19,1... | collective-permute-start | bytes 393224 | tf_op jit(solution)/shard_map/ppermute | solution.py:261
  460.2 75.7 %collective-permute-start.48 = (bf16[128,512]{1,0:T(8,128)(2,1)S(1)}, bf16[128,512]{1,0:T(8,128)(2,1)S(1)}, u32[]{:S(2)}, u32[]{:S(2)}) collective-permute-start(bf16[128,512]{1,0:T(8,128)(2,1)S(1)} %get-tuple-element.106), channel_id=1, source_target_pairs={{1,0},{2,1},{3,2},{4,3},{5,4},{6,5},{7,6},{8,7},{9,8},{10,9},{11,1... | collective-permute-start | bytes 393224 | tf_op jit(solution)/shard_map/ppermute | solution.py:261
  478.3 57.6 %collective-permute-start.55 = (bf16[128,512]{1,0:T(8,128)(2,1)S(1)}, bf16[128,512]{1,0:T(8,128)(2,1)S(1)}, u32[]{:S(2)}, u32[]{:S(2)}) collective-permute-start(bf16[128,512]{1,0:T(8,128)(2,1)S(1)} %get-tuple-element.107), channel_id=1, source_target_pairs={{14,0},{15,1},{0,2},{1,3},{2,4},{3,5},{4,6},{5,7},{17,16},{18,17},... | collective-permute-start | bytes 393224 | tf_op jit(solution)/shard_map/ppermute | solution.py:261
  498.1 38.6 %collective-permute-start.34 = (bf16[128,512]{1,0:T(8,128)(2,1)S(1)}, bf16[128,512]{1,0:T(8,128)(2,1)S(1)}, u32[]{:S(2)}, u32[]{:S(2)}) collective-permute-start(bf16[128,512]{1,0:T(8,128)(2,1)S(1)} %get-tuple-element.110), channel_id=1, source_target_pairs={{1,0},{2,1},{3,2},{4,3},{5,4},{6,5},{7,6},{8,7},{9,8},{10,9},{11,1... | collective-permute-start | bytes 393224 | tf_op jit(solution)/shard_map/ppermute | solution.py:261
  516.2 30.0 %collective-permute-start.41 = (bf16[128,512]{1,0:T(8,128)(2,1)S(1)}, bf16[128,512]{1,0:T(8,128)(2,1)S(1)}, u32[]{:S(2)}, u32[]{:S(2)}) collective-permute-start(bf16[128,512]{1,0:T(8,128)(2,1)S(1)} %get-tuple-element.111), channel_id=1, source_target_pairs={{14,0},{15,1},{0,2},{1,3},{2,4},{3,5},{4,6},{5,7},{17,16},{18,17},... | collective-permute-start | bytes 393224 | tf_op jit(solution)/shard_map/ppermute | solution.py:261
  (18 other events, 23.6 us)

commit v5 on v3

--- a/solution.py
+++ b/solution.py
@@ -118,100 +118,136 @@
         return jnp.where(self.even, self.a[at], self.b[at])
 
 
-def first_kernel(scal, first_ref, q_ref, g_ref, own, a1, b1, a2, b2, top, total, acc, turned):
-    rows = q_ref.shape[0]
+def pack_kernel(k_ref, v_ref, out_ref, sems):
+    copies = [
+        pltpu.make_async_copy(k_ref, out_ref.at[:, pl.ds(0, WIDE)], sems.at[0]),
+        pltpu.make_async_copy(v_ref, out_ref.at[:, pl.ds(WIDE, WIDE)], sems.at[1]),
+    ]
+    for copy in copies:
+        copy.start()
+    for copy in copies:
+        copy.wait()
+
+
+def own_forward_kernel(scal, first_ref, q_ref, g_ref, own, top, total, acc, turned):
     top[...] = jnp.full(top.shape, neg_big, jnp.float32)
     total[...] = jnp.zeros(total.shape, jnp.float32)
     acc[...] = jnp.zeros(acc.shape, jnp.float32)
     forward_part(scal, first_ref, q_ref, [own], [0], top, total, acc)
-
-    @pl.when(scal[1] >= 1)
-    def _():
-        near = [Near(scal, a1, b1), Near(scal, a2, b2)]
-        forward_part(scal, first_ref, q_ref, near, [1, 2], top, total, acc)
-
     for g in range(KVH):
         turned[g] = heads_of(g_ref, g).astype(jnp.float32).T
 
 
-def more_kernel(steps, scal, first_ref, q_ref, top_in, total_in, acc_in, *rest):
-    blocks, (top, total, acc) = rest[: 2 * len(steps)], rest[2 * len(steps) :]
+def forward_kernel(groups, scal, first_ref, q_ref, top_in, total_in, acc_in, *rest):
+    blocks, (top, total, acc) = rest[:-3], rest[-3:]
     top[...] = top_in[...]
     total[...] = total_in[...]
     acc[...] = acc_in[...]
-    for i, step in enumerate(steps):
+    at = 0
+    for kind, step in groups:
+        count = {"near": 4, "pair": 2, "a": 1, "b": 1}[kind]
+        some = blocks[at : at + count]
+        at += count
 
         @pl.when(scal[1] >= step)
-        def _(i=i, step=step):
-            pair = blocks[2 * i : 2 * i + 2]
-            forward_part(scal, first_ref, q_ref, pair, backs_of(scal, step), top, total, acc)
+        def _(kind=kind, step=step, some=some):
+            if kind == "near":
+                use = [Near(scal, some[0], some[1]), Near(scal, some[2], some[3])]
+                backs = [1, 2]
+            else:
+                use, backs = list(some), backs_of(scal, step)
+                backs = {"pair": backs, "a": backs[:1], "b": backs[1:]}[kind]
+            forward_part(scal, first_ref, q_ref, use, backs, top, total, acc)
+
+
+def back_step(step, chosen, scal, first_ref, q_ref, g_ref, blocks, log_ref, inner_ref, acc, terms):
+    @pl.when(scal[1] >= step)
+    def _():
+        backs = backs_of(scal, step)[chosen]
+        backward_part(
+            scal, first_ref, q_ref, g_ref, blocks, backs, log_ref, inner_ref, acc, terms
+        )
+
+    @pl.when(scal[1] < step)
+    def _():
+        for term in terms:
+            term[...] = jnp.zeros(term.shape, term.dtype)
 
 
 def middle_kernel(
     scal, first_ref, q_ref, g_ref, turned, top_in, total_in, acc_in, a, b,
-    out_ref, log_ref, inner_ref, gq_acc, term_a, term_b, acc,
+    attended, log_ref, inner_ref, gq_acc, term_a,
 ):
     log_ref[...] = top_in[...]
     inner_ref[...] = total_in[...]
-    acc[...] = acc_in[...]
+    attended[...] = acc_in[...]
 
     @pl.when(scal[1] >= STEPS)
     def _():
-        backs = backs_of(scal, STEPS)
-        forward_part(scal, first_ref, q_ref, [a, b], backs, log_ref, inner_ref, acc)
+        backs = backs_of(scal, STEPS)[1:]
+        forward_part(scal, first_ref, q_ref, [b], backs, log_ref, inner_ref, attended)
 
     for g in range(KVH):
         total = inner_ref[g]
-        attended = acc[g] * (1.0 / total)
+        attended[g] = attended[g] * (1.0 / total)
         log_ref[g] = log_ref[g] + jnp.log2(total)
-        inner_ref[g] = jnp.sum(attended * turned[g], axis=0, keepdims=True)
-        put_heads(out_ref, g, attended)
+        inner_ref[g] = jnp.sum(attended[g] * turned[g], axis=0, keepdims=True)
     gq_acc[...] = jnp.zeros(gq_acc.shape, jnp.float32)
-    back_step(STEPS, scal, first_ref, q_ref, g_ref, a, b, log_ref, inner_ref, gq_acc, term_a, term_b)
-
-
-def back_step(step, scal, first_ref, q_ref, g_ref, a, b, log_ref, inner_ref, acc, term_a, term_b):
-    @pl.when(scal[1] >= step)
-    def _():
-        backs = backs_of(scal, step)
-        backward_part(
-            scal, first_ref, q_ref, g_ref, [a, b], backs, log_ref, inner_ref, acc, [term_a, term_b]
-        )
-
-    @pl.when(scal[1] < step)
-    def _():
-        term_a[...] = jnp.zeros(term_a.shape, term_a.dtype)
-        term_b[...] = jnp.zeros(term_b.shape, term_b.dtype)
+    back_step(
+        STEPS, slice(0, 1), scal, first_ref, q_ref, g_ref, [a], log_ref, inner_ref, gq_acc, [term_a]
+    )
+
+
+def second_kernel(
+    scal, first_ref, q_ref, g_ref, log_ref, inner_ref, acc_in, attended, b, acc, term_b, out_ref
+):
+    acc[...] = acc_in[...]
+    back_step(
+        STEPS, slice(1, 2), scal, first_ref, q_ref, g_ref, [b], log_ref, inner_ref, acc, [term_b]
+    )
+    for g in range(KVH):
+        put_heads(out_ref, g, attended[g])
 
 
 def back_kernel(
     step, scal, first_ref, q_ref, g_ref, log_ref, inner_ref, acc_in, a, b, acc, term_a, term_b
 ):
     acc[...] = acc_in[...]
-    back_step(step, scal, first_ref, q_ref, g_ref, a, b, log_ref, inner_ref, acc, term_a, term_b)
-
-
-def last_kernel(
-    scal, first_ref, q_ref, g_ref, log_ref, inner_ref, acc_in, own, a1, b1, a2, b2,
-    gq_ref, term_0, term_1, term_2, acc,
+    back_step(
+        step, slice(0, 2), scal, first_ref, q_ref, g_ref, [a, b], log_ref, inner_ref, acc,
+        [term_a, term_b],
+    )
+
+
+def near_back_kernel(
+    scal, first_ref, q_ref, g_ref, log_ref, inner_ref, acc_in, a1, b1, a2, b2,
+    acc, term_a1, term_b1, term_a2, term_b2,
+):
+    acc[...] = acc_in[...]
+    for term in (term_a1, term_b1, term_a2, term_b2):
+        term[...] = jnp.zeros(term.shape, term.dtype)
+
+    def run(blocks, terms):
+        backward_part(
+            scal, first_ref, q_ref, g_ref, blocks, [1, 2], log_ref, inner_ref, acc, terms
+        )
+
+    @pl.when((scal[1] >= 1) & (scal[2] == 0))
+    def _():
+        run([a1, a2], [term_a1, term_a2])
+
+    @pl.when((scal[1] >= 1) & (scal[2] == 1))
+    def _():
+        run([b1, b2], [term_b1, term_b2])
+
+
+def own_back_kernel(
+    scal, first_ref, q_ref, g_ref, log_ref, inner_ref, acc_in, own, gq_ref, term_0, acc
 ):
     acc[...] = acc_in[...]
     backward_part(
         scal, first_ref, q_ref, g_ref, [own], [0], log_ref, inner_ref, acc, [term_0]
     )
-
-    @pl.when(scal[1] >= 1)
-    def _():
-        near = [Near(scal, a1, b1), Near(scal, a2, b2)]
-        backward_part(
-            scal, first_ref, q_ref, g_ref, near, [1, 2], log_ref, inner_ref, acc, [term_1, term_2]
-        )
-
-    @pl.when(scal[1] < 1)
-    def _():
-        term_1[...] = jnp.zeros(term_1.shape, term_1.dtype)
-        term_2[...] = jnp.zeros(term_2.shape, term_2.dtype)
-
     for g in range(KVH):
         put_heads(gq_ref, g, acc[g] * SCALE)
 
@@ -235,6 +271,17 @@
     )(scal, *operands)
 
 
+def pack(keys, values):
+    rows = keys.shape[0]
+    return pl.pallas_call(
+        pack_kernel,
+        out_shape=jax.ShapeDtypeStruct((rows, 2 * WIDE), keys.dtype),
+        in_specs=[pl.BlockSpec(memory_space=pltpu.HBM)] * 2,
+        out_specs=pl.BlockSpec(memory_space=pltpu.VMEM),
+        scratch_shapes=[pltpu.SemaphoreType.DMA((2,))],
+    )(keys, values)
+
+
 def both_ways(x, near_pairs, far_pairs, flip):
     windows, count = lax.axis_size("dp"), lax.axis_size("ctx")
     pairs = []
@@ -269,62 +316,77 @@
     count = lax.axis_size("ctx")
     odd = lax.rem(lax.axis_index("dp"), 2)
     q_start = lax.axis_index("ctx") * rows
-    own = jnp.concatenate([keys, values], axis=1)
+    own = pack(keys, values)
     q_seg = lax.dynamic_slice_in_dim(segment_ids, q_start, rows, 0)
     first = jnp.sum((segment_ids[:, None] < q_seg[None, :]).astype(jnp.int32), axis=0, keepdims=True)
     scal = jnp.stack([q_start, (q_start - first[0, 0] + rows - 1) // rows, odd]).astype(jnp.int32)
 
     block = jax.ShapeDtypeStruct(own.shape, jnp.bfloat16)
+    exact = jax.ShapeDtypeStruct(own.shape, jnp.float32)
     wide = jax.ShapeDtypeStruct(queries.shape, jnp.bfloat16)
+    state = [ROW, ROW, TURNED]
+    top, total, acc, turned = call(
+        own_forward_kernel, state + [TURNED], 1.0, scal, first, queries, out_grad, own
+    )
+
+    def forward(groups, work, now, *blocks):
+        kernel = functools.partial(forward_kernel, groups)
+        return call(kernel, state, work, scal, first, queries, *now, *blocks)
+
+    now = (top, total, acc)
     a, b, tops = [own], [own], {}
     for step in range(1, STEPS + 1):
         pairs = gather_pairs(step, count)
-        to_a = a[-1]
+        to_a, to_b = a[-1], b[-1]
+        if step == 1:
+            to_b, _ = lax.optimization_barrier((to_b, top))
         if step in (5, 7):
             to_a, _ = lax.optimization_barrier((to_a, tops[step - 3]))
         a.append(both_ways(to_a, *pairs, 0))
-        b.append(both_ways(b[-1], *pairs, 1))
+        b.append(both_ways(to_b, *pairs, 1))
         if step == 2:
-            top, total, acc, turned = call(
-                first_kernel, [ROW, ROW, TURNED, TURNED], 0.8,
-                scal, first, queries, out_grad, own, a[1], b[1], a[2], b[2],
-            )
+            now = forward((("near", 1),), 0.8, now, a[1], b[1], a[2], b[2])
         elif step in (4, 6):
-            pairs = [x for i in (step - 1, step) for x in (a[i], b[i])]
-            top, total, acc = call(
-                functools.partial(more_kernel, (step - 1, step)), [ROW, ROW, TURNED], 1.0,
-                scal, first, queries, top, total, acc, *pairs,
-            )
-        tops[step] = top if step > 1 else None
-    attended, log_total, inner, acc, term_a, term_b = call(
-        middle_kernel, [wide, ROW, ROW, TURNED, block, block], 1.5,
-        scal, first, queries, out_grad, turned, top, total, acc, a[STEPS], b[STEPS],
-        scratch=[pltpu.VMEM((KVH, HD, LANES), jnp.float32)],
-    )
-
-    sum_a, sum_b = term_a, term_b
+            groups = (("pair", step - 1), ("pair", step))
+            now = forward(groups, 1.0, now, a[step - 1], b[step - 1], a[step], b[step])
+        tops[step] = now[0]
+    now = forward((("a", STEPS),), 0.5, now, a[STEPS])
+    attended_t, log_total, inner, acc, sum_a = call(
+        middle_kernel, [TURNED, ROW, ROW, TURNED, block], 1.5,
+        scal, first, queries, out_grad, turned, *now, a[STEPS], b[STEPS],
+    )
+
+    def backward(kernel, outs, work, *operands, scratch=()):
+        return call(
+            kernel, outs, work, scal, first, queries, out_grad, log_total, inner, acc, *operands,
+            scratch=scratch,
+        )
+
+    acc, sum_b, attended = backward(
+        second_kernel, [TURNED, block, wide], 1.0, attended_t, b[STEPS]
+    )
     for step in range(1, STEPS + 1):
         pairs = return_pairs(step, count)
         sum_a = both_ways(sum_a, *pairs, 0)
         sum_b = both_ways(sum_b, *pairs, 1)
         back = STEPS - step
         if back >= 3:
-            acc, term_a, term_b = call(
-                functools.partial(back_kernel, back), [TURNED, block, block], 1.2,
-                scal, first, queries, out_grad, log_total, inner, acc, a[back], b[back],
+            acc, term_a, term_b = backward(
+                functools.partial(back_kernel, back), [TURNED, block, block], 1.2, a[back], b[back]
             )
+        elif back == 2:
+            acc, *terms = backward(
+                near_back_kernel, [TURNED] + [block] * 4, 1.2, a[1], b[1], a[2], b[2]
+            )
+            term_a, term_b = terms[2:]
+        elif back == 1:
+            term_a, term_b = terms[:2]
+            acc, _ = lax.optimization_barrier((acc, sum_a))
+            grad_query, term_0 = backward(
+                own_back_kernel, [wide, exact], 1.0, own, scratch=[pltpu.VMEM(TURNED.shape, jnp.float32)]
+            )
+        if back >= 1:
             sum_a, sum_b = add_low(sum_a, term_a), add_low(sum_b, term_b)
-        elif back >= 1:
-            if back == 2:
-                grad_query, term_0, term_1, term_2 = call(
-                    last_kernel, [wide, jax.ShapeDtypeStruct(own.shape, jnp.float32), block, block], 2.0,
-                    scal, first, queries, out_grad, log_total, inner, acc, own, a[1], b[1], a[2], b[2],
-                    scratch=[pltpu.VMEM((KVH, HD, LANES), jnp.float32)],
-                )
-            term = term_2 if back == 2 else term_1
-            nothing = jnp.zeros_like(term)
-            sum_a = add_low(sum_a, jnp.where(odd == 0, term, nothing))
-            sum_b = add_low(sum_b, jnp.where(odd == 1, term, nothing))
     summed = sum_a.astype(jnp.float32) + sum_b.astype(jnp.float32) + term_0
     return (attended, grad_query, summed[:, :WIDE], summed[:, WIDE:])
 

time: 180 us -> 177 us (0.983)
  the two profiles are of different devices: /device:TPU:60 before, /device:TPU:18 now
where the time goes in v5:
time: 177 us; the launch traced here: 176 us
  waiting for transfers between devices  90.8 us (51%)
  starting transfers between devices  64 us (36%)
  Pallas kernels  15 us (8%)
  local copies, waits for them, and re-layouts  3.6 us (2%)
    ppermute x28, waiting for transfers between devices, both_ways(): return lax.ppermute(x, ('dp', 'ctx'), pairs)  90.8 us
    ppermute x28, starting transfers between devices, both_ways(): return lax.ppermute(x, ('dp', 'ctx'), pairs)  64 us
    pallas_call x13, Pallas kernels, call(): pl.pallas_call(kernel, out_shape=outs, in_specs=[pl.BlockSpec(memory_spac...  13.2 us
  transfers between devices with their start and end apart: 28, of which 14 were waited for; matrix products, arithmetic and copies ran while one was open for 1% of the time, Pallas kernels for 7%

profile of v5, /device:TPU:18, one launch (start us, length us, event | category | flops | bytes accessed | tf_op | source)
XLA Modules:
  0.0 176.0 jit_solution(1682058472586484948)
XLA Ops:
  0.6 1.7 shard_map.84.own
  2.4 3.8 %collective-permute-start = (bf16[128,1024]{1,0:T(8,128)(2,1)}, bf16[128,1024]{1,0:T(8,128)(2,1)S(1)}, u32[]{:S(2)}, u32[]{:S(2)}) collective-permute-start(bf16[128,1024]{1,0:T(8,128)(2,1)} %shard_map.84.own), channel_id=1, source_target_pairs={{0,1},{1,2},{2,3},{3,4},{4,5},{5,6},{6,7},{7,8},{8,9},{9,10},{10,1... | collective-permute-start | bytes 786440 | tf_op jit(solution)/shard_map/ppermute | solution.py:291
  6.3 0.7 copy-done.5
  6.9 0.1 dynamic_slice.3
  7.0 0.4 convert_reduce_fusion
  7.4 0.1 pad_add_fusion.scal
  7.5 1.0 copy-done
  8.5 1.0 copy-done.3
  9.5 1.8 %shard_map.85 = (f32[4,1,512]{2,1,0:T(1,128)S(1)}, f32[4,1,512]{2,1,0:T(1,128)S(1)}, f32[4,128,512]{2,1,0:T(8,128)S(1)}, f32[4,128,512]{2,1,0:T(8,128)S(1)}) custom-call(s32[3]{0:T(128)S(1)} %pad_add_fusion.scal, s32[1,128]{1,0:T(1,128)S(1)} %bitcast.7, bf16[128,2048]{1,0:T(8,128)(2,1)S(1)} %copy-done.2, bf16[128,2048]{1,0:T(8,128)(2,1)S(1)} %copy-done.3, ...), custom_call_target="tpu_custom_call" | custom-call | flops 1000000000 | bytes 4194304 | tf_op jit(solution)/shard_map/pallas_call | solution.py:261
  11.3 10.9 %collective-permute-start.1 = (bf16[128,1024]{1,0:T(8,128)(2,1)S(1)}, bf16[128,1024]{1,0:T(8,128)(2,1)S(1)}, u32[]{:S(2)}, u32[]{:S(2)}) collective-permute-start(bf16[128,1024]{1,0:T(8,128)(2,1)S(1)} %copy-done), channel_id=1, source_target_pairs={{0,14},{1,15},{2,0},{3,1},{4,2},{5,3},{6,4},{7,5},{16,17},{17,18},... | collective-permute-start | bytes 786440 | tf_op jit(solution)/shard_map/ppermute | solution.py:291
  22.3 0.7 collective-permute-start.2
  23.0 6.7 %collective-permute-done.1.rest_1_.b1 = bf16[128,1024]{1,0:T(8,128)(2,1)S(1)} collective-permute-done((bf16[128,1024]{1,0:T(8,128)(2,1)S(1)}, bf16[128,1024]{1,0:T(8,128)(2,1)S(1)}, u32[]{:S(2)}, u32[]{:S(2)}) %collective-permute-start.1) | collective-permute-done | bytes 262176 | tf_op jit(solution)/shard_map/ppermute | solution.py:291
  29.6 1.9 %collective-permute-start.3 = (bf16[128,1024]{1,0:T(8,128)(2,1)S(1)}, bf16[128,1024]{1,0:T(8,128)(2,1)S(1)}, u32[]{:S(2)}, u32[]{:S(2)}) collective-permute-start(bf16[128,1024]{1,0:T(8,128)(2,1)S(1)} %collective-permute-done.1.rest_1_.b1), channel_id=1, source_target_pairs={{14,13},{15,14},{0,15},{1,0},{2,1},{3,2},{4,3},{5,4},{17,18},{18,1... | collective-permute-start | bytes 786440 | tf_op jit(solution)/shard_map/ppermute | solution.py:291
  31.6 0.7 collective-permute-start.4
  32.2 8.4 %collective-permute-done.3.rest_3_.b2 = bf16[128,1024]{1,0:T(8,128)(2,1)S(1)} collective-permute-done((bf16[128,1024]{1,0:T(8,128)(2,1)S(1)}, bf16[128,1024]{1,0:T(8,128)(2,1)S(1)}, u32[]{:S(2)}, u32[]{:S(2)}) %collective-permute-start.3) | collective-permute-done | bytes 262176 | tf_op jit(solution)/shard_map/ppermute | solution.py:291
  40.6 3.3 %collective-permute-start.5 = (bf16[128,1024]{1,0:T(8,128)(2,1)S(1)}, bf16[128,1024]{1,0:T(8,128)(2,1)S(1)}, u32[]{:S(2)}, u32[]{:S(2)}) collective-permute-start(bf16[128,1024]{1,0:T(8,128)(2,1)S(1)} %collective-permute-done.3.rest_3_.b2), channel_id=1, source_target_pairs={{13,12},{14,13},{15,14},{0,15},{1,0},{2,1},{3,2},{4,3},{18,19},{19... | collective-permute-start | bytes 786440 | tf_op jit(solution)/shard_map/ppermute | solution.py:291
  43.9 0.7 collective-permute-start.6
  44.6 6.2 %collective-permute-done.5.rest_1_.b = bf16[128,1024]{1,0:T(8,128)(2,1)S(1)} collective-permute-done((bf16[128,1024]{1,0:T(8,128)(2,1)S(1)}, bf16[128,1024]{1,0:T(8,128)(2,1)S(1)}, u32[]{:S(2)}, u32[]{:S(2)}) %collective-permute-start.5) | collective-permute-done | bytes 262176 | tf_op jit(solution)/shard_map/ppermute | solution.py:291
  50.8 4.8 %collective-permute-start.7 = (bf16[128,1024]{1,0:T(8,128)(2,1)S(1)}, bf16[128,1024]{1,0:T(8,128)(2,1)S(1)}, u32[]{:S(2)}, u32[]{:S(2)}) collective-permute-start(bf16[128,1024]{1,0:T(8,128)(2,1)S(1)} %collective-permute-done.5.rest_1_.b), channel_id=1, source_target_pairs={{12,11},{13,12},{14,13},{15,14},{0,15},{1,0},{2,1},{3,2},{19,20},{... | collective-permute-start | bytes 786440 | tf_op jit(solution)/shard_map/ppermute | solution.py:291
  55.6 0.6 shard_map.86
  56.3 0.7 collective-permute-start.8
  56.9 4.0 %collective-permute-done.7.rest_3_.b = bf16[128,1024]{1,0:T(8,128)(2,1)S(1)} collective-permute-done((bf16[128,1024]{1,0:T(8,128)(2,1)S(1)}, bf16[128,1024]{1,0:T(8,128)(2,1)S(1)}, u32[]{:S(2)}, u32[]{:S(2)}) %collective-permute-start.7) | collective-permute-done | bytes 262176 | tf_op jit(solution)/shard_map/ppermute | solution.py:291
  61.0 5.6 %collective-permute-start.9 = (bf16[128,1024]{1,0:T(8,128)(2,1)S(1)}, bf16[128,1024]{1,0:T(8,128)(2,1)S(1)}, u32[]{:S(2)}, u32[]{:S(2)}) collective-permute-start(bf16[128,1024]{1,0:T(8,128)(2,1)S(1)} %collective-permute-done.7.rest_3_.b), channel_id=1, source_target_pairs={{11,10},{12,11},{13,12},{14,13},{15,14},{0,15},{1,0},{2,1},{20,21}... | collective-permute-start | bytes 786440 | tf_op jit(solution)/shard_map/ppermute | solution.py:291
  66.6 0.7 collective-permute-start.10
  67.3 3.8 %collective-permute-done.9.rest_1_.b = bf16[128,1024]{1,0:T(8,128)(2,1)S(1)} collective-permute-done((bf16[128,1024]{1,0:T(8,128)(2,1)S(1)}, bf16[128,1024]{1,0:T(8,128)(2,1)S(1)}, u32[]{:S(2)}, u32[]{:S(2)}) %collective-permute-start.9) | collective-permute-done | bytes 262176 | tf_op jit(solution)/shard_map/ppermute | solution.py:291
  71.0 5.6 %collective-permute-start.11 = (bf16[128,1024]{1,0:T(8,128)(2,1)S(1)}, bf16[128,1024]{1,0:T(8,128)(2,1)S(1)}, u32[]{:S(2)}, u32[]{:S(2)}) collective-permute-start(bf16[128,1024]{1,0:T(8,128)(2,1)S(1)} %collective-permute-done.9.rest_1_.b), channel_id=1, source_target_pairs={{10,9},{11,10},{12,11},{13,12},{14,13},{15,14},{0,15},{1,0},{21,22... | collective-permute-start | bytes 786440 | tf_op jit(solution)/shard_map/ppermute | solution.py:291
  76.6 0.6 shard_map.87
  77.2 0.7 collective-permute-start.12
  77.9 2.5 %collective-permute-done.11.rest_3_.b = bf16[128,1024]{1,0:T(8,128)(2,1)S(1)} collective-permute-done((bf16[128,1024]{1,0:T(8,128)(2,1)S(1)}, bf16[128,1024]{1,0:T(8,128)(2,1)S(1)}, u32[]{:S(2)}, u32[]{:S(2)}) %collective-permute-start.11) | collective-permute-done | bytes 262176 | tf_op jit(solution)/shard_map/ppermute | solution.py:291
  80.5 5.6 %collective-permute-start.13 = (bf16[128,1024]{1,0:T(8,128)(2,1)S(1)}, bf16[128,1024]{1,0:T(8,128)(2,1)S(1)}, u32[]{:S(2)}, u32[]{:S(2)}) collective-permute-start(bf16[128,1024]{1,0:T(8,128)(2,1)S(1)} %collective-permute-done.11.rest_3_.b), channel_id=1, source_target_pairs={{9,8},{10,9},{11,10},{12,11},{13,12},{14,13},{15,14},{0,15},{22,23... | collective-permute-start | bytes 786440 | tf_op jit(solution)/shard_map/ppermute | solution.py:291
  86.1 0.6 shard_map.88
  86.7 0.6 shard_map.89
  87.4 2.6 %collective-permute-done.13.b = bf16[128,1024]{1,0:T(8,128)(2,1)S(1)} collective-permute-done((bf16[128,1024]{1,0:T(8,128)(2,1)S(1)}, bf16[128,1024]{1,0:T(8,128)(2,1)S(1)}, u32[]{:S(2)}, u32[]{:S(2)}) %collective-permute-start.13) | collective-permute-done | bytes 262176 | tf_op jit(solution)/shard_map/ppermute | solution.py:291
  89.9 0.9 shard_map.90
  90.8 0.7 collective-permute-start.14
  91.5 1.8 %shard_map.91 = (f32[4,128,512]{2,1,0:T(8,128)S(1)}, bf16[128,1024]{1,0:T(8,128)(2,1)S(1)}, bf16[128,2048]{1,0:T(8,128)(2,1)}) custom-call(s32[3]{0:T(128)S(1)} %pad_add_fusion.scal, s32[1,128]{1,0:T(1,128)S(1)} %bitcast.13, bf16[128,2048]{1,0:T(8,128)(2,1)S(1)} %copy-done.2, bf16[128,2048]{1,0:T(8,128)(2,1)S(1)} %copy-done.4, ...), custom_call_target="tpu_custom_call" | custom-call | flops 1000000000 | bytes 4194304 | tf_op jit(solution)/shard_map/pallas_call | solution.py:261
  93.3 1.3 collective-permute-start.21
  94.6 0.6 shard_map.92
  95.4 0.7 collective-permute-start.15
  96.0 13.2 %collective-permute-done.21 = bf16[128,1024]{1,0:T(8,128)(2,1)S(1)} collective-permute-done((bf16[128,1024]{1,0:T(8,128)(2,1)S(1)}, bf16[128,1024]{1,0:T(8,128)(2,1)S(1)}, u32[]{:S(2)}, u32[]{:S(2)}) %collective-permute-start.21) | collective-permute-done | bytes 262176 | tf_op jit(solution)/shard_map/ppermute | solution.py:291
  109.3 1.9 %collective-permute-start.22 = (bf16[128,1024]{1,0:T(8,128)(2,1)S(1)}, bf16[128,1024]{1,0:T(8,128)(2,1)S(1)}, u32[]{:S(2)}, u32[]{:S(2)}) collective-permute-start(bf16[128,1024]{1,0:T(8,128)(2,1)S(1)} %add_convert_fusion.5), channel_id=1, source_target_pairs={{9,10},{10,11},{11,12},{12,13},{13,14},{14,15},{15,0},{0,1},{22,21... | collective-permute-start | bytes 786440 | tf_op jit(solution)/shard_map/ppermute | solution.py:291
  111.2 0.6 shard_map.93
  111.9 0.7 collective-permute-start.16
  112.6 8.7 %collective-permute-done.22 = bf16[128,1024]{1,0:T(8,128)(2,1)S(1)} collective-permute-done((bf16[128,1024]{1,0:T(8,128)(2,1)S(1)}, bf16[128,1024]{1,0:T(8,128)(2,1)S(1)}, u32[]{:S(2)}, u32[]{:S(2)}) %collective-permute-start.22) | collective-permute-done | bytes 262176 | tf_op jit(solution)/shard_map/ppermute | solution.py:291
  121.4 1.9 %collective-permute-start.23 = (bf16[128,1024]{1,0:T(8,128)(2,1)S(1)}, bf16[128,1024]{1,0:T(8,128)(2,1)S(1)}, u32[]{:S(2)}, u32[]{:S(2)}) collective-permute-start(bf16[128,1024]{1,0:T(8,128)(2,1)S(1)} %add_convert_fusion.4), channel_id=1, source_target_pairs={{10,11},{11,12},{12,13},{13,14},{14,15},{15,0},{0,1},{1,2},{21,20}... | collective-permute-start | bytes 786440 | tf_op jit(solution)/shard_map/ppermute | solution.py:291
  123.3 0.6 shard_map.94
  124.0 0.7 collective-permute-start.17
  124.7 8.1 %collective-permute-done.23 = bf16[128,1024]{1,0:T(8,128)(2,1)S(1)} collective-permute-done((bf16[128,1024]{1,0:T(8,128)(2,1)S(1)}, bf16[128,1024]{1,0:T(8,128)(2,1)S(1)}, u32[]{:S(2)}, u32[]{:S(2)}) %collective-permute-start.23) | collective-permute-done | bytes 262176 | tf_op jit(solution)/shard_map/ppermute | solution.py:291
  132.9 1.9 %collective-permute-start.24 = (bf16[128,1024]{1,0:T(8,128)(2,1)S(1)}, bf16[128,1024]{1,0:T(8,128)(2,1)S(1)}, u32[]{:S(2)}, u32[]{:S(2)}) collective-permute-start(bf16[128,1024]{1,0:T(8,128)(2,1)S(1)} %add_convert_fusion.3), channel_id=1, source_target_pairs={{11,12},{12,13},{13,14},{14,15},{15,0},{0,1},{1,2},{2,3},{20,19},{... | collective-permute-start | bytes 786440 | tf_op jit(solution)/shard_map/ppermute | solution.py:291
  134.8 0.6 shard_map.95
  135.5 0.7 collective-permute-start.18
  136.2 7.2 %collective-permute-done.24 = bf16[128,1024]{1,0:T(8,128)(2,1)S(1)} collective-permute-done((bf16[128,1024]{1,0:T(8,128)(2,1)S(1)}, bf16[128,1024]{1,0:T(8,128)(2,1)S(1)}, u32[]{:S(2)}, u32[]{:S(2)}) %collective-permute-start.24) | collective-permute-done | bytes 262176 | tf_op jit(solution)/shard_map/ppermute | solution.py:291
  143.5 1.9 %collective-permute-start.25 = (bf16[128,1024]{1,0:T(8,128)(2,1)S(1)}, bf16[128,1024]{1,0:T(8,128)(2,1)S(1)}, u32[]{:S(2)}, u32[]{:S(2)}) collective-permute-start(bf16[128,1024]{1,0:T(8,128)(2,1)S(1)} %add_convert_fusion.2), channel_id=1, source_target_pairs={{12,13},{13,14},{14,15},{15,0},{0,1},{1,2},{2,3},{3,4},{19,18},{20... | collective-permute-start | bytes 786440 | tf_op jit(solution)/shard_map/ppermute | solution.py:291
  145.5 0.9 shard_map.96
  146.5 0.7 collective-permute-start.19
  147.2 7.8 %collective-permute-done.25 = bf16[128,1024]{1,0:T(8,128)(2,1)S(1)} collective-permute-done((bf16[128,1024]{1,0:T(8,128)(2,1)S(1)}, bf16[128,1024]{1,0:T(8,128)(2,1)S(1)}, u32[]{:S(2)}, u32[]{:S(2)}) %collective-permute-start.25) | collective-permute-done | bytes 262176 | tf_op jit(solution)/shard_map/ppermute | solution.py:291
  155.0 2.1 %collective-permute-start.26 = (bf16[128,1024]{1,0:T(8,128)(2,1)S(1)}, bf16[128,1024]{1,0:T(8,128)(2,1)S(1)}, u32[]{:S(2)}, u32[]{:S(2)}) collective-permute-start(bf16[128,1024]{1,0:T(8,128)(2,1)S(1)} %add_convert_fusion.1), channel_id=1, source_target_pairs={{13,14},{14,15},{15,0},{0,1},{1,2},{2,3},{3,4},{4,5},{18,17},{19,1... | collective-permute-start | bytes 786440 | tf_op jit(solution)/shard_map/ppermute | solution.py:291
  157.2 1.3 collective-permute-start.20
  158.5 6.0 %collective-permute-done.26 = bf16[128,1024]{1,0:T(8,128)(2,1)S(1)} collective-permute-done((bf16[128,1024]{1,0:T(8,128)(2,1)S(1)}, bf16[128,1024]{1,0:T(8,128)(2,1)S(1)}, u32[]{:S(2)}, u32[]{:S(2)}) %collective-permute-start.26) | collective-permute-done | bytes 262176 | tf_op jit(solution)/shard_map/ppermute | solution.py:291
  164.6 1.9 %collective-permute-start.27 = (bf16[128,1024]{1,0:T(8,128)(2,1)S(1)}, bf16[128,1024]{1,0:T(8,128)(2,1)S(1)}, u32[]{:S(2)}, u32[]{:S(2)}) collective-permute-start(bf16[128,1024]{1,0:T(8,128)(2,1)S(1)} %add_convert_fusion), channel_id=1, source_target_pairs={{14,0},{15,1},{0,2},{1,3},{2,4},{3,5},{4,6},{5,7},{17,16},{18,17},... | collective-permute-start | bytes 786440 | tf_op jit(solution)/shard_map/ppermute | solution.py:291
  166.5 2.8 %shard_map.97 = (bf16[128,2048]{1,0:T(8,128)(2,1)}, f32[128,1024]{1,0:T(8,128)S(1)}) custom-call(s32[3]{0:T(128)S(1)} %pad_add_fusion.scal, s32[1,128]{1,0:T(1,128)S(1)} %bitcast.19, bf16[128,2048]{1,0:T(8,128)(2,1)S(1)} %copy-done.2, bf16[128,2048]{1,0:T(8,128)(2,1)S(1)} %copy-done.4, f32[4,1,512]{2,1,0:T(1,128)S(1)} %get-tuple-element.70.log_ref, ...), custom_call_target="tpu_custom_call" | custom-call | flops 1000000000 | bytes 4194304 | tf_op jit(solution)/shard_map/pallas_call | solution.py:261
  169.3 5.8 %collective-permute-done.27 = bf16[128,1024]{1,0:T(8,128)(2,1)S(1)} collective-permute-done((bf16[128,1024]{1,0:T(8,128)(2,1)S(1)}, bf16[128,1024]{1,0:T(8,128)(2,1)S(1)}, u32[]{:S(2)}, u32[]{:S(2)}) %collective-permute-start.27) | collective-permute-done | bytes 262176 | tf_op jit(solution)/shard_map/ppermute | solution.py:291
  175.0 0.1 add_add_fusion
  175.1 0.8 fusion
  (35 shorter events, 0.9 us)
Async XLA Ops:
  0.6 6.9 %copy-start.2 = (bf16[128,2048]{1,0:T(8,128)(2,1)S(1)}, bf16[128,2048]{1,0:T(8,128)(2,1)}, u32[]{:S(2)}) copy-start(bf16[128,2048]{1,0:T(8,128)(2,1)} %q_ref.25) | copy-start | bytes 1572868
  2.4 19.9 %collective-permute-start = (bf16[128,1024]{1,0:T(8,128)(2,1)}, bf16[128,1024]{1,0:T(8,128)(2,1)S(1)}, u32[]{:S(2)}, u32[]{:S(2)}) collective-permute-start(bf16[128,1024]{1,0:T(8,128)(2,1)} %shard_map.84.own), channel_id=1, source_target_pairs={{0,1},{1,2},{2,3},{3,4},{4,5},{5,6},{6,7},{7,8},{8,9},{9,10},{10,1... | collective-permute-start | bytes 786440 | tf_op jit(solution)/shard_map/ppermute | solution.py:291
  6.2 0.7 copy-start.5
  7.5 1.0 copy-start
  8.5 1.0 copy-start.3
  11.3 18.3 %collective-permute-start.1 = (bf16[128,1024]{1,0:T(8,128)(2,1)S(1)}, bf16[128,1024]{1,0:T(8,128)(2,1)S(1)}, u32[]{:S(2)}, u32[]{:S(2)}) collective-permute-start(bf16[128,1024]{1,0:T(8,128)(2,1)S(1)} %copy-done), channel_id=1, source_target_pairs={{0,14},{1,15},{2,0},{3,1},{4,2},{5,3},{6,4},{7,5},{16,17},{17,18},... | collective-permute-start | bytes 786440 | tf_op jit(solution)/shard_map/ppermute | solution.py:291
  22.3 9.3 %collective-permute-start.2 = (bf16[128,1024]{1,0:T(8,128)(2,1)S(1)}, bf16[128,1024]{1,0:T(8,128)(2,1)S(1)}, u32[]{:S(2)}, u32[]{:S(2)}) collective-permute-start(bf16[128,1024]{1,0:T(8,128)(2,1)S(1)} %collective-permute-done.rest_0_.a1), channel_id=1, source_target_pairs={{1,2},{2,3},{3,4},{4,5},{5,6},{6,7},{7,8},{8,9},{9,10},{10,11},{11... | collective-permute-start | bytes 786440 | tf_op jit(solution)/shard_map/ppermute | solution.py:291
  29.6 11.0 %collective-permute-start.3 = (bf16[128,1024]{1,0:T(8,128)(2,1)S(1)}, bf16[128,1024]{1,0:T(8,128)(2,1)S(1)}, u32[]{:S(2)}, u32[]{:S(2)}) collective-permute-start(bf16[128,1024]{1,0:T(8,128)(2,1)S(1)} %collective-permute-done.1.rest_1_.b1), channel_id=1, source_target_pairs={{14,13},{15,14},{0,15},{1,0},{2,1},{3,2},{4,3},{5,4},{17,18},{18,1... | collective-permute-start | bytes 786440 | tf_op jit(solution)/shard_map/ppermute | solution.py:291
  31.6 12.3 %collective-permute-start.4 = (bf16[128,1024]{1,0:T(8,128)(2,1)S(1)}, bf16[128,1024]{1,0:T(8,128)(2,1)S(1)}, u32[]{:S(2)}, u32[]{:S(2)}) collective-permute-start(bf16[128,1024]{1,0:T(8,128)(2,1)S(1)} %collective-permute-done.2.rest_2_.a2), channel_id=1, source_target_pairs={{2,3},{3,4},{4,5},{5,6},{6,7},{7,8},{8,9},{9,10},{10,11},{11,12},{... | collective-permute-start | bytes 786440 | tf_op jit(solution)/shard_map/ppermute | solution.py:291
  40.6 10.2 %collective-permute-start.5 = (bf16[128,1024]{1,0:T(8,128)(2,1)S(1)}, bf16[128,1024]{1,0:T(8,128)(2,1)S(1)}, u32[]{:S(2)}, u32[]{:S(2)}) collective-permute-start(bf16[128,1024]{1,0:T(8,128)(2,1)S(1)} %collective-permute-done.3.rest_3_.b2), channel_id=1, source_target_pairs={{13,12},{14,13},{15,14},{0,15},{1,0},{2,1},{3,2},{4,3},{18,19},{19... | collective-permute-start | bytes 786440 | tf_op jit(solution)/shard_map/ppermute | solution.py:291
  43.9 12.3 %collective-permute-start.6 = (bf16[128,1024]{1,0:T(8,128)(2,1)S(1)}, bf16[128,1024]{1,0:T(8,128)(2,1)S(1)}, u32[]{:S(2)}, u32[]{:S(2)}) collective-permute-start(bf16[128,1024]{1,0:T(8,128)(2,1)S(1)} %collective-permute-done.4.rest_0_.a), channel_id=1, source_target_pairs={{3,4},{4,5},{5,6},{6,7},{7,8},{8,9},{9,10},{10,11},{11,12},{12,13}... | collective-permute-start | bytes 786440 | tf_op jit(solution)/shard_map/ppermute | solution.py:291
  50.8 10.2 %collective-permute-start.7 = (bf16[128,1024]{1,0:T(8,128)(2,1)S(1)}, bf16[128,1024]{1,0:T(8,128)(2,1)S(1)}, u32[]{:S(2)}, u32[]{:S(2)}) collective-permute-start(bf16[128,1024]{1,0:T(8,128)(2,1)S(1)} %collective-permute-done.5.rest_1_.b), channel_id=1, source_target_pairs={{12,11},{13,12},{14,13},{15,14},{0,15},{1,0},{2,1},{3,2},{19,20},{... | collective-permute-start | bytes 786440 | tf_op jit(solution)/shard_map/ppermute | solution.py:291
  56.3 10.3 %collective-permute-start.8 = (bf16[128,1024]{1,0:T(8,128)(2,1)S(1)}, bf16[128,1024]{1,0:T(8,128)(2,1)S(1)}, u32[]{:S(2)}, u32[]{:S(2)}) collective-permute-start(bf16[128,1024]{1,0:T(8,128)(2,1)S(1)} %collective-permute-done.6.rest_2_.a), channel_id=1, source_target_pairs={{4,5},{5,6},{6,7},{7,8},{8,9},{9,10},{10,11},{11,12},{12,13},{13,1... | collective-permute-start | bytes 786440 | tf_op jit(solution)/shard_map/ppermute | solution.py:291
  61.0 10.0 %collective-permute-start.9 = (bf16[128,1024]{1,0:T(8,128)(2,1)S(1)}, bf16[128,1024]{1,0:T(8,128)(2,1)S(1)}, u32[]{:S(2)}, u32[]{:S(2)}) collective-permute-start(bf16[128,1024]{1,0:T(8,128)(2,1)S(1)} %collective-permute-done.7.rest_3_.b), channel_id=1, source_target_pairs={{11,10},{12,11},{13,12},{14,13},{15,14},{0,15},{1,0},{2,1},{20,21}... | collective-permute-start | bytes 786440 | tf_op jit(solution)/shard_map/ppermute | solution.py:291
  66.6 10.7 %collective-permute-start.10 = (bf16[128,1024]{1,0:T(8,128)(2,1)S(1)}, bf16[128,1024]{1,0:T(8,128)(2,1)S(1)}, u32[]{:S(2)}, u32[]{:S(2)}) collective-permute-start(bf16[128,1024]{1,0:T(8,128)(2,1)S(1)} %collective-permute-done.8.rest_0_.a), channel_id=1, source_target_pairs={{5,6},{6,7},{7,8},{8,9},{9,10},{10,11},{11,12},{12,13},{13,14},{14... | collective-permute-start | bytes 786440 | tf_op jit(solution)/shard_map/ppermute | solution.py:291
  71.0 9.5 %collective-permute-start.11 = (bf16[128,1024]{1,0:T(8,128)(2,1)S(1)}, bf16[128,1024]{1,0:T(8,128)(2,1)S(1)}, u32[]{:S(2)}, u32[]{:S(2)}) collective-permute-start(bf16[128,1024]{1,0:T(8,128)(2,1)S(1)} %collective-permute-done.9.rest_1_.b), channel_id=1, source_target_pairs={{10,9},{11,10},{12,11},{13,12},{14,13},{15,14},{0,15},{1,0},{21,22... | collective-permute-start | bytes 786440 | tf_op jit(solution)/shard_map/ppermute | solution.py:291
  77.2 9.5 %collective-permute-start.12 = (bf16[128,1024]{1,0:T(8,128)(2,1)S(1)}, bf16[128,1024]{1,0:T(8,128)(2,1)S(1)}, u32[]{:S(2)}, u32[]{:S(2)}) collective-permute-start(bf16[128,1024]{1,0:T(8,128)(2,1)S(1)} %collective-permute-done.10.rest_2_.a), channel_id=1, source_target_pairs={{6,7},{7,8},{8,9},{9,10},{10,11},{11,12},{12,13},{13,14},{14,15},{... | collective-permute-start | bytes 786440 | tf_op jit(solution)/shard_map/ppermute | solution.py:291
  80.5 9.5 %collective-permute-start.13 = (bf16[128,1024]{1,0:T(8,128)(2,1)S(1)}, bf16[128,1024]{1,0:T(8,128)(2,1)S(1)}, u32[]{:S(2)}, u32[]{:S(2)}) collective-permute-start(bf16[128,1024]{1,0:T(8,128)(2,1)S(1)} %collective-permute-done.11.rest_3_.b), channel_id=1, source_target_pairs={{9,8},{10,9},{11,10},{12,11},{13,12},{14,13},{15,14},{0,15},{22,23... | collective-permute-start | bytes 786440 | tf_op jit(solution)/shard_map/ppermute | solution.py:291
  86.7 3.2 %copy-start.4 = (bf16[128,2048]{1,0:T(8,128)(2,1)S(1)}, bf16[128,2048]{1,0:T(8,128)(2,1)}, u32[]{:S(2)}) copy-start(bf16[128,2048]{1,0:T(8,128)(2,1)} %g_ref.17) | copy-start | bytes 1572868
  90.8 4.4 %collective-permute-start.14 = (bf16[128,1024]{1,0:T(8,128)(2,1)S(1)}, bf16[128,1024]{1,0:T(8,128)(2,1)S(1)}, u32[]{:S(2)}, u32[]{:S(2)}) collective-permute-start(bf16[128,1024]{1,0:T(8,128)(2,1)S(1)} %get-tuple-element.81), channel_id=1, source_target_pairs={{7,6},{8,7},{9,8},{10,9},{11,10},{12,11},{13,12},{14,13},{15,14},{... | collective-permute-start | bytes 786440 | tf_op jit(solution)/shard_map/ppermute | solution.py:291
  93.3 15.9 %collective-permute-start.21 = (bf16[128,1024]{1,0:T(8,128)(2,1)S(1)}, bf16[128,1024]{1,0:T(8,128)(2,1)S(1)}, u32[]{:S(2)}, u32[]{:S(2)}) collective-permute-start(bf16[128,1024]{1,0:T(8,128)(2,1)S(1)} %get-tuple-element.90), channel_id=1, source_target_pairs={{8,9},{9,10},{10,11},{11,12},{12,13},{13,14},{14,15},{15,0},{23,22... | collective-permute-start | bytes 786440 | tf_op jit(solution)/shard_map/ppermute | solution.py:291
  95.4 16.5 %collective-permute-start.15 = (bf16[128,1024]{1,0:T(8,128)(2,1)S(1)}, bf16[128,1024]{1,0:T(8,128)(2,1)S(1)}, u32[]{:S(2)}, u32[]{:S(2)}) collective-permute-start(bf16[128,1024]{1,0:T(8,128)(2,1)S(1)} %add_convert_fusion.11), channel_id=1, source_target_pairs={{6,5},{7,6},{8,7},{9,8},{10,9},{11,10},{12,11},{13,12},{14,13},{15... | collective-permute-start | bytes 786440 | tf_op jit(solution)/shard_map/ppermute | solution.py:291
  109.3 12.0 %collective-permute-start.22 = (bf16[128,1024]{1,0:T(8,128)(2,1)S(1)}, bf16[128,1024]{1,0:T(8,128)(2,1)S(1)}, u32[]{:S(2)}, u32[]{:S(2)}) collective-permute-start(bf16[128,1024]{1,0:T(8,128)(2,1)S(1)} %add_convert_fusion.5), channel_id=1, source_target_pairs={{9,10},{10,11},{11,12},{12,13},{13,14},{14,15},{15,0},{0,1},{22,21... | collective-permute-start | bytes 786440 | tf_op jit(solution)/shard_map/ppermute | solution.py:291
  111.9 12.0 %collective-permute-start.16 = (bf16[128,1024]{1,0:T(8,128)(2,1)S(1)}, bf16[128,1024]{1,0:T(8,128)(2,1)S(1)}, u32[]{:S(2)}, u32[]{:S(2)}) collective-permute-start(bf16[128,1024]{1,0:T(8,128)(2,1)S(1)} %add_convert_fusion.10), channel_id=1, source_target_pairs={{5,4},{6,5},{7,6},{8,7},{9,8},{10,9},{11,10},{12,11},{13,12},{14,1... | collective-permute-start | bytes 786440 | tf_op jit(solution)/shard_map/ppermute | solution.py:291
  121.4 11.4 %collective-permute-start.23 = (bf16[128,1024]{1,0:T(8,128)(2,1)S(1)}, bf16[128,1024]{1,0:T(8,128)(2,1)S(1)}, u32[]{:S(2)}, u32[]{:S(2)}) collective-permute-start(bf16[128,1024]{1,0:T(8,128)(2,1)S(1)} %add_convert_fusion.4), channel_id=1, source_target_pairs={{10,11},{11,12},{12,13},{13,14},{14,15},{15,0},{0,1},{1,2},{21,20}... | collective-permute-start | bytes 786440 | tf_op jit(solution)/shard_map/ppermute | solution.py:291
  124.0 11.4 %collective-permute-start.17 = (bf16[128,1024]{1,0:T(8,128)(2,1)S(1)}, bf16[128,1024]{1,0:T(8,128)(2,1)S(1)}, u32[]{:S(2)}, u32[]{:S(2)}) collective-permute-start(bf16[128,1024]{1,0:T(8,128)(2,1)S(1)} %add_convert_fusion.9), channel_id=1, source_target_pairs={{4,3},{5,4},{6,5},{7,6},{8,7},{9,8},{10,9},{11,10},{12,11},{13,12}... | collective-permute-start | bytes 786440 | tf_op jit(solution)/shard_map/ppermute | solution.py:291
  132.9 10.6 %collective-permute-start.24 = (bf16[128,1024]{1,0:T(8,128)(2,1)S(1)}, bf16[128,1024]{1,0:T(8,128)(2,1)S(1)}, u32[]{:S(2)}, u32[]{:S(2)}) collective-permute-start(bf16[128,1024]{1,0:T(8,128)(2,1)S(1)} %add_convert_fusion.3), channel_id=1, source_target_pairs={{11,12},{12,13},{13,14},{14,15},{15,0},{0,1},{1,2},{2,3},{20,19},{... | collective-permute-start | bytes 786440 | tf_op jit(solution)/shard_map/ppermute | solution.py:291
  135.5 10.8 %collective-permute-start.18 = (bf16[128,1024]{1,0:T(8,128)(2,1)S(1)}, bf16[128,1024]{1,0:T(8,128)(2,1)S(1)}, u32[]{:S(2)}, u32[]{:S(2)}) collective-permute-start(bf16[128,1024]{1,0:T(8,128)(2,1)S(1)} %add_convert_fusion.8), channel_id=1, source_target_pairs={{3,2},{4,3},{5,4},{6,5},{7,6},{8,7},{9,8},{10,9},{11,10},{12,11},{... | collective-permute-start | bytes 786440 | tf_op jit(solution)/shard_map/ppermute | solution.py:291
  143.5 11.4 %collective-permute-start.25 = (bf16[128,1024]{1,0:T(8,128)(2,1)S(1)}, bf16[128,1024]{1,0:T(8,128)(2,1)S(1)}, u32[]{:S(2)}, u32[]{:S(2)}) collective-permute-start(bf16[128,1024]{1,0:T(8,128)(2,1)S(1)} %add_convert_fusion.2), channel_id=1, source_target_pairs={{12,13},{13,14},{14,15},{15,0},{0,1},{1,2},{2,3},{3,4},{19,18},{20... | collective-permute-start | bytes 786440 | tf_op jit(solution)/shard_map/ppermute | solution.py:291
  146.5 10.7 %collective-permute-start.19 = (bf16[128,1024]{1,0:T(8,128)(2,1)S(1)}, bf16[128,1024]{1,0:T(8,128)(2,1)S(1)}, u32[]{:S(2)}, u32[]{:S(2)}) collective-permute-start(bf16[128,1024]{1,0:T(8,128)(2,1)S(1)} %add_convert_fusion.7), channel_id=1, source_target_pairs={{2,1},{3,2},{4,3},{5,4},{6,5},{7,6},{8,7},{9,8},{10,9},{11,10},{12... | collective-permute-start | bytes 786440 | tf_op jit(solution)/shard_map/ppermute | solution.py:291
  155.0 9.5 %collective-permute-start.26 = (bf16[128,1024]{1,0:T(8,128)(2,1)S(1)}, bf16[128,1024]{1,0:T(8,128)(2,1)S(1)}, u32[]{:S(2)}, u32[]{:S(2)}) collective-permute-start(bf16[128,1024]{1,0:T(8,128)(2,1)S(1)} %add_convert_fusion.1), channel_id=1, source_target_pairs={{13,14},{14,15},{15,0},{0,1},{1,2},{2,3},{3,4},{4,5},{18,17},{19,1... | collective-permute-start | bytes 786440 | tf_op jit(solution)/shard_map/ppermute | solution.py:291
  157.2 12.0 %collective-permute-start.20 = (bf16[128,1024]{1,0:T(8,128)(2,1)S(1)}, bf16[128,1024]{1,0:T(8,128)(2,1)S(1)}, u32[]{:S(2)}, u32[]{:S(2)}) collective-permute-start(bf16[128,1024]{1,0:T(8,128)(2,1)S(1)} %add_convert_fusion.6), channel_id=1, source_target_pairs={{1,0},{2,1},{3,2},{4,3},{5,4},{6,5},{7,6},{8,7},{9,8},{10,9},{11,1... | collective-permute-start | bytes 786440 | tf_op jit(solution)/shard_map/ppermute | solution.py:291
  164.5 2.0 %copy-start.1 = (bf16[128,1024]{1,0:T(8,128)(2,1)S(1)}, bf16[128,1024]{1,0:T(8,128)(2,1)}, u32[]{:S(2)}) copy-start(bf16[128,1024]{1,0:T(8,128)(2,1)} %shard_map.84.own) | copy-start | bytes 786436
  164.6 10.5 %collective-permute-start.27 = (bf16[128,1024]{1,0:T(8,128)(2,1)S(1)}, bf16[128,1024]{1,0:T(8,128)(2,1)S(1)}, u32[]{:S(2)}, u32[]{:S(2)}) collective-permute-start(bf16[128,1024]{1,0:T(8,128)(2,1)S(1)} %add_convert_fusion), channel_id=1, source_target_pairs={{14,0},{15,1},{0,2},{1,3},{2,4},{3,5},{4,6},{5,7},{17,16},{18,17},... | collective-permute-start | bytes 786440 | tf_op jit(solution)/shard_map/ppermute | solution.py:291

commit v6 on v5

v6 whole, which is shorter than its diff:
```python
import functools
import math

import jax
import jax.numpy as jnp
from jax import lax
from jax.experimental import pallas as pl
from jax.experimental.pallas import tpu as pltpu
from jax.sharding import PartitionSpec as P

KVH = 4
HD = 128
GROUP = 4
WIDE = KVH * HD
FAR = 12
STEPS = 7
LANES = GROUP * 128
SCALE = 1.0 / math.sqrt(HD)
TO_TWO = SCALE / math.log(2.0)

neg_big = -1e30


def dot_nt(a, b):
    return lax.dot_general(a, b, (((1,), (1,)), ((), ())), preferred_element_type=jnp.float32)


def dot_nn(a, b):
    return lax.dot_general(a, b, (((1,), (0,)), ((), ())), preferred_element_type=jnp.float32)


def dot_tn(a, b):
    return lax.dot_general(a, b, (((0,), (0,)), ((), ())), preferred_element_type=jnp.float32)


def heads_of(ref, g):
    base = g * GROUP * HD
    return jnp.concatenate(
        [ref[:, base + r * HD : base + (r + 1) * HD] for r in range(GROUP)], axis=0
    )


def put_heads(ref, g, turned):
    flat = turned.T
    rows = ref.shape[0]
    for r in range(GROUP):
        cols = slice((g * GROUP + r) * HD, (g * GROUP + r + 1) * HD)
        ref[:, cols] = flat[r * rows : (r + 1) * rows].astype(ref.dtype)


def keys_of(blocks, g):
    return jnp.concatenate([b[:, g * HD : (g + 1) * HD] for b in blocks], axis=0)


def values_of(blocks, g):
    return jnp.concatenate([b[:, WIDE + g * HD : WIDE + (g + 1) * HD] for b in blocks], axis=0)


def allowed_keys(scal, first_ref, backs, rows):
    q_start = scal[0]
    first = jnp.concatenate([first_ref[...]] * GROUP, axis=1)
    within = lax.broadcasted_iota(jnp.int32, (rows, LANES), 0)
    parts = []
    for back in backs:
        place = (q_start - back * rows) + within
        seen = place >= first
        if isinstance(back, int) and back == 0:
            lanes = lax.broadcasted_iota(jnp.int32, (rows, LANES), 1)
            seen = seen & (within <= jnp.bitwise_and(lanes, rows - 1))
        parts.append(seen)
    return jnp.concatenate(parts, axis=0)


def forward_part(scal, first_ref, q_ref, g_ref, blocks, backs, top_ref, sum_ref, acc_ref, e_ref, gp_ref):
    allowed = allowed_keys(scal, first_ref, backs, q_ref.shape[0])
    for g in range(KVH):
        v = values_of(blocks, g)
        s = dot_nt(keys_of(blocks, g), heads_of(q_ref, g)) * TO_TWO
        s = jnp.where(allowed, s, neg_big)
        top = top_ref[g]
        new_top = jnp.maximum(top, jnp.max(s, axis=0, keepdims=True))
        e = jnp.exp2(s - new_top)
        shrink = jnp.exp2(top - new_top)
        e_low = e.astype(jnp.bfloat16)
        e_ref[g] = e_low
        gp_ref[g] = dot_nt(v, heads_of(g_ref, g)).astype(jnp.bfloat16)
        top_ref[g] = new_top
        sum_ref[g] = sum_ref[g] * shrink + jnp.sum(e, axis=0, keepdims=True)
        acc_ref[g] = acc_ref[g] * shrink + dot_tn(v, e_low)


def backward_part(q_ref, g_ref, blocks, factors, inner_ref, acc_ref, e_ref, gp_ref, outs):
    rows = q_ref.shape[0]
    for g in range(KVH):
        probs = e_ref[g].astype(jnp.float32) * factors[g]
        grad_scores = (probs * (gp_ref[g].astype(jnp.float32) - inner_ref[g])).astype(jnp.bfloat16)
        acc_ref[g] = acc_ref[g] + dot_tn(keys_of(blocks, g), grad_scores)
        grad_k = dot_nn(grad_scores, heads_of(q_ref, g)) * SCALE
        grad_v = dot_nn(probs.astype(jnp.bfloat16), heads_of(g_ref, g))
        for i, out in enumerate(outs):
            part = slice(i * rows, (i + 1) * rows)
            out[:, g * HD : (g + 1) * HD] = grad_k[part].astype(out.dtype)
            out[:, WIDE + g * HD : WIDE + (g + 1) * HD] = grad_v[part].astype(out.dtype)


def factors_of(top_ref, log_ref):
    return [jnp.exp2(top_ref[g] - log_ref[g]) for g in range(KVH)]


def clear(terms):
    for term in terms:
        term[...] = jnp.zeros(term.shape, term.dtype)


def backs_of(scal, step):
    near, far = step, 15 - step
    odd = scal[2] == 1
    return [jnp.where(odd, far, near), jnp.where(odd, near, far)]


class Near:
    def __init__(self, scal, a, b):
        self.even, self.a, self.b = scal[2] == 0, a, b

    def __getitem__(self, at):
        return jnp.where(self.even, self.a[at], self.b[at])


def pack_kernel(k_ref, v_ref, out_ref, sems):
    copies = [
        pltpu.make_async_copy(k_ref, out_ref.at[:, pl.ds(0, WIDE)], sems.at[0]),
        pltpu.make_async_copy(v_ref, out_ref.at[:, pl.ds(WIDE, WIDE)], sems.at[1]),
    ]
    for copy in copies:
        copy.start()
    for copy in copies:
        copy.wait()


def own_forward_kernel(scal, first_ref, q_ref, g_ref, own, top, total, acc, e, gp, turned):
    top[...] = jnp.full(top.shape, neg_big, jnp.float32)
    total[...] = jnp.zeros(total.shape, jnp.float32)
    acc[...] = jnp.zeros(acc.shape, jnp.float32)
    forward_part(scal, first_ref, q_ref, g_ref, [own], [0], top, total, acc, e, gp)
    for g in range(KVH):
        turned[g] = heads_of(g_ref, g).astype(jnp.float32).T


def forward_kernel(kind, step, scal, first_ref, q_ref, g_ref, top_in, total_in, acc_in, *rest):
    blocks, (top, total, acc, e, gp) = rest[:-5], rest[-5:]
    top[...] = top_in[...]
    total[...] = total_in[...]
    acc[...] = acc_in[...]

    @pl.when(scal[1] >= step)
    def _():
        if kind == "near":
            a1, b1, a2, b2 = blocks
            use, backs = [Near(scal, a1, b1), Near(scal, a2, b2)], [1, 2]
        else:
            use, backs = list(blocks), backs_of(scal, step)[: len(blocks)]
        forward_part(scal, first_ref, q_ref, g_ref, use, backs, top, total, acc, e, gp)


def middle_kernel(
    scal, first_ref, q_ref, g_ref, turned, top_in, total_in, acc_in, e_a, gp_a, a, b,
    attended, log_ref, inner_ref, gq_acc, term_a, term_b, e_b, gp_b,
):
    log_ref[...] = top_in[...]
    inner_ref[...] = total_in[...]
    attended[...] = acc_in[...]
    gq_acc[...] = jnp.zeros(gq_acc.shape, jnp.float32)

    @pl.when(scal[1] >= STEPS)
    def _():
        backs = backs_of(scal, STEPS)[1:]
        forward_part(
            scal, first_ref, q_ref, g_ref, [b], backs, log_ref, inner_ref, attended, e_b, gp_b
        )

    inverse = []
    for g in range(KVH):
        total = inner_ref[g]
        inverse.append(1.0 / total)
        attended[g] = attended[g] * inverse[g]
        log_ref[g] = log_ref[g] + jnp.log2(total)
        inner_ref[g] = jnp.sum(attended[g] * turned[g], axis=0, keepdims=True)

    @pl.when(scal[1] >= STEPS)
    def _():
        backward_part(
            q_ref, g_ref, [a], factors_of(top_in, log_ref), inner_ref, gq_acc, e_a, gp_a, [term_a]
        )
        backward_part(q_ref, g_ref, [b], inverse, inner_ref, gq_acc, e_b, gp_b, [term_b])

    @pl.when(scal[1] < STEPS)
    def _():
        clear([term_a, term_b])


def pair_back(step, scal, q_ref, g_ref, log_ref, inner_ref, top, e, gp, a, b, acc, term_a, term_b):
    @pl.when(scal[1] >= step)
    def _():
        backward_part(
            q_ref, g_ref, [a, b], factors_of(top, log_ref), inner_ref, acc, e, gp, [term_a, term_b]
        )

    @pl.when(scal[1] < step)
    def _():
        clear([term_a, term_b])


def back_kernel(
    step, scal, q_ref, g_ref, log_ref, inner_ref, acc_in, top, e, gp, a, b, acc, term_a, term_b
):
    acc[...] = acc_in[...]
    pair_back(step, scal, q_ref, g_ref, log_ref, inner_ref, top, e, gp, a, b, acc, term_a, term_b)


def second_kernel(
    step, scal, q_ref, g_ref, log_ref, inner_ref, acc_in, top, e, gp, a, b, attended,
    acc, term_a, term_b, out_ref,
):
    acc[...] = acc_in[...]
    pair_back(step, scal, q_ref, g_ref, log_ref, inner_ref, top, e, gp, a, b, acc, term_a, term_b)
    for g in range(KVH):
        put_heads(out_ref, g, attended[g])


def near_back_kernel(
    scal, q_ref, g_ref, log_ref, inner_ref, acc_in, top, e, gp, a1, b1, a2, b2,
    acc, term_a1, term_b1, term_a2, term_b2,
):
    acc[...] = acc_in[...]
    clear([term_a1, term_b1, term_a2, term_b2])

    def run(blocks, terms):
        backward_part(
            q_ref, g_ref, blocks, factors_of(top, log_ref), inner_ref, acc, e, gp, terms
        )

    @pl.when((scal[1] >= 1) & (scal[2] == 0))
    def _():
        run([a1, a2], [term_a1, term_a2])

    @pl.when((scal[1] >= 1) & (scal[2] == 1))
    def _():
        run([b1, b2], [term_b1, term_b2])


def own_back_kernel(
    scal, q_ref, g_ref, log_ref, inner_ref, acc_in, top, e, gp, own, gq_ref, term_0, acc
):
    acc[...] = acc_in[...]
    backward_part(
        q_ref, g_ref, [own], factors_of(top, log_ref), inner_ref, acc, e, gp, [term_0]
    )
    for g in range(KVH):
        put_heads(gq_ref, g, acc[g] * SCALE)


ROW = jax.ShapeDtypeStruct((KVH, 1, LANES), jnp.float32)
TURNED = jax.ShapeDtypeStruct((KVH, HD, LANES), jnp.float32)


def call(kernel, outs, work, scal, *operands, scratch=()):
    in_vmem = pl.BlockSpec(memory_space=pltpu.VMEM)
    return pl.pallas_call(
        kernel,
        out_shape=outs,
        in_specs=[pl.BlockSpec(memory_space=pltpu.SMEM)] + [in_vmem] * len(operands),
        out_specs=[in_vmem] * len(outs),
        scratch_shapes=list(scratch),
        compiler_params=pltpu.CompilerParams(vmem_limit_bytes=24 * 1024 * 1024),
        cost_estimate=pl.CostEstimate(
            flops=int(work * 1.0e9), bytes_accessed=4 * 1024 * 1024, transcendentals=1 << 20
        ),
    )(scal, *operands)


def pack(keys, values):
    rows = keys.shape[0]
    return pl.pallas_call(
        pack_kernel,
        out_shape=jax.ShapeDtypeStruct((rows, 2 * WIDE), keys.dtype),
        in_specs=[pl.BlockSpec(memory_space=pltpu.HBM)] * 2,
        out_specs=pl.BlockSpec(memory_space=pltpu.VMEM),
        scratch_shapes=[pltpu.SemaphoreType.DMA((2,))],
    )(keys, values)


def both_ways(x, near_pairs, far_pairs, flip):
    windows, count = lax.axis_size("dp"), lax.axis_size("ctx")
    pairs = []
    for window in range(windows):
        chosen = near_pairs if (window + flip) % 2 == 0 else far_pairs
        pairs += [(window * count + i, window * count + j) for i, j in chosen]
    return lax.ppermute(x, ("dp", "ctx"), pairs)


def gather_pairs(step, count):
    near = [(j, j + 1) for j in range(step - 1, count - 1)]
    blocks = range(count - STEPS - 1)
    start = 0 if step == 1 else step
    far = [((b - start) % count, (b - step - 1) % count) for b in blocks]
    return near, far


def return_pairs(step, count):
    near = [(j, j - 1) for j in range(STEPS + 1 - step, count)]
    blocks = range(count - STEPS - 1)
    end = STEPS + 1 + step if step < STEPS else count
    far = [((b + STEPS + step) % count, (b + end) % count) for b in blocks]
    return near, far


def add_low(a, b):
    return (a.astype(jnp.float32) + b.astype(jnp.float32)).astype(jnp.bfloat16)


def local(queries, keys, values, out_grad, segment_ids):
    rows = queries.shape[0]
    count = lax.axis_size("ctx")
    odd = lax.rem(lax.axis_index("dp"), 2)
    q_start = lax.axis_index("ctx") * rows
    own = pack(keys, values)
    q_seg = lax.dynamic_slice_in_dim(segment_ids, q_start, rows, 0)
    first = jnp.sum((segment_ids[:, None] < q_seg[None, :]).astype(jnp.int32), axis=0, keepdims=True)
    scal = jnp.stack([q_start, (q_start - first[0, 0] + rows - 1) // rows, odd]).astype(jnp.int32)

    block = jax.ShapeDtypeStruct(own.shape, jnp.bfloat16)
    exact = jax.ShapeDtypeStruct(own.shape, jnp.float32)
    wide = jax.ShapeDtypeStruct(queries.shape, jnp.bfloat16)
    state = [ROW, ROW, TURNED]
    one = [jax.ShapeDtypeStruct((KVH, rows, LANES), jnp.bfloat16)] * 2
    two = [jax.ShapeDtypeStruct((KVH, 2 * rows, LANES), jnp.bfloat16)] * 2
    *now, e, gp, turned = call(
        own_forward_kernel, state + one + [TURNED], 1.0, scal, first, queries, out_grad, own
    )
    kept = {0: (now[0], e, gp)}

    def forward(kind, step, *blocks):
        *state_now, e, gp = call(
            functools.partial(forward_kernel, kind, step), state + (one if kind == "a" else two), 1.0,
            scal, first, queries, out_grad, *now, *blocks,
        )
        kept[step] = (state_now[0], e, gp)
        return state_now

    a, b, tops = [own], [own], {1: now[0]}
    for step in range(1, STEPS + 1):
        pairs = gather_pairs(step, count)
        to_a = a[-1]
        if step >= 3:
            to_a, _ = lax.optimization_barrier((to_a, tops[step - 2]))
        a.append(both_ways(to_a, *pairs, 0))
        b.append(both_ways(b[-1], *pairs, 1))
        if step == 2:
            now = forward("near", 1, a[1], b[1], a[2], b[2])
        elif 3 <= step < STEPS:
            now = forward("pair", step, a[step], b[step])
        tops[step] = now[0]
    now = forward("a", STEPS, a[STEPS])
    part = pltpu.VMEM(one[0].shape, jnp.bfloat16)
    attended_t, log_total, inner, acc, sum_a, sum_b = call(
        middle_kernel, [TURNED, ROW, ROW, TURNED, block, block], 1.5,
        scal, first, queries, out_grad, turned, *now, *kept[STEPS][1:], a[STEPS], b[STEPS],
        scratch=[part, part],
    )

    def backward(kernel, outs, step, *operands, scratch=()):
        return call(
            kernel, outs, 1.0, scal, queries, out_grad, log_total, inner, acc, *kept[step], *operands,
            scratch=scratch,
        )

    for step in range(1, STEPS + 1):
        pairs = return_pairs(step, count)
        sum_a = both_ways(sum_a, *pairs, 0)
        sum_b = both_ways(sum_b, *pairs, 1)
        back = STEPS - step
        if back == 6:
            acc, term_a, term_b, attended = backward(
                functools.partial(second_kernel, back), [TURNED, block, block, wide], back,
                a[back], b[back], attended_t,
            )
        elif back >= 3:
            acc, term_a, term_b = backward(
                functools.partial(back_kernel, back), [TURNED, block, block], back, a[back], b[back]
            )
        elif back == 2:
            acc, *terms = backward(
                near_back_kernel, [TURNED] + [block] * 4, 1, a[1], b[1], a[2], b[2]
            )
            term_a, term_b = terms[2:]
        elif back == 1:
            term_a, term_b = terms[:2]
            acc, _ = lax.optimization_barrier((acc, sum_a))
            grad_query, term_0 = backward(
                own_back_kernel, [wide, exact], 0, own, scratch=[pltpu.VMEM(TURNED.shape, jnp.float32)]
            )
        if back >= 1:
            sum_a, sum_b = add_low(sum_a, term_a), add_low(sum_b, term_b)
    summed = sum_a.astype(jnp.float32) + sum_b.astype(jnp.float32) + term_0
    return (attended, grad_query, summed[:, :WIDE], summed[:, WIDE:])


def solution(mesh):
    placed = P(("dp", "ctx"), None)
    return jax.shard_map(
        local,
        mesh=mesh,
        in_specs=(placed, placed, placed, placed, P("dp")),
        out_specs=(placed, placed, placed, placed),
        check_vma=False,
    )
```

time: 177 us -> 172 us (0.972)
  the two profiles are of different devices: /device:TPU:18 before, /device:TPU:2 now
where the time goes in v6:
time: 172 us; the launch traced here: 171 us
  waiting for transfers between devices  84 us (49%)
  starting transfers between devices  66.7 us (39%)
  Pallas kernels  14.7 us (9%)
  local copies, waits for them, and re-layouts  2.91 us (2%)
    ppermute x28, waiting for transfers between devices, both_ways(): return lax.ppermute(x, ('dp', 'ctx'), pairs)  84 us
    ppermute x28, starting transfers between devices, both_ways(): return lax.ppermute(x, ('dp', 'ctx'), pairs)  66.7 us
    pallas_call x14, Pallas kernels, call(): pl.pallas_call(kernel, out_shape=outs, in_specs=[pl.BlockSpec(memory_spac...  12.9 us
  transfers between devices with their start and end apart: 28, of which 14 were waited for; matrix products, arithmetic and copies ran while one was open for 1% of the time, Pallas kernels for 7%

profile of v6, /device:TPU:2, one launch (start us, length us, event | category | flops | bytes accessed | tf_op | source)
XLA Modules:
  0.0 170.9 jit_solution(8339226498119965806)
XLA Ops:
  0.6 1.7 %shard_map.84.own = bf16[128,1024]{1,0:T(8,128)(2,1)} custom-call(bf16[128,512]{1,0:T(8,128)(2,1)} %k_ref.1, bf16[128,512]{1,0:T(8,128)(2,1)} %v_ref.1), custom_call_target="tpu_custom_call" | custom-call | tf_op jit(solution)/shard_map/pallas_call | solution.py:283
  2.4 3.8 %collective-permute-start = (bf16[128,1024]{1,0:T(8,128)(2,1)}, bf16[128,1024]{1,0:T(8,128)(2,1)S(1)}, u32[]{:S(2)}, u32[]{:S(2)}) collective-permute-start(bf16[128,1024]{1,0:T(8,128)(2,1)} %shard_map.84.own), channel_id=1, source_target_pairs={{0,1},{1,2},{2,3},{3,4},{4,5},{5,6},{6,7},{7,8},{8,9},{9,10},{10,1... | collective-permute-start | bytes 786440 | tf_op jit(solution)/shard_map/ppermute | solution.py:298
  6.2 10.9 %collective-permute-start.1 = (bf16[128,1024]{1,0:T(8,128)(2,1)}, bf16[128,1024]{1,0:T(8,128)(2,1)S(1)}, u32[]{:S(2)}, u32[]{:S(2)}) collective-permute-start(bf16[128,1024]{1,0:T(8,128)(2,1)} %shard_map.84.own), channel_id=1, source_target_pairs={{0,14},{1,15},{2,0},{3,1},{4,2},{5,3},{6,4},{7,5},{16,17},{17,18},... | collective-permute-start | bytes 786440 | tf_op jit(solution)/shard_map/ppermute | solution.py:298
  17.2 0.1 dynamic_slice.3
  17.3 0.7 collective-permute-start.2
  18.0 0.4 convert_reduce_fusion
  18.4 7.3 %collective-permute-done.1.rest_1_.b1 = bf16[128,1024]{1,0:T(8,128)(2,1)S(1)} collective-permute-done((bf16[128,1024]{1,0:T(8,128)(2,1)}, bf16[128,1024]{1,0:T(8,128)(2,1)S(1)}, u32[]{:S(2)}, u32[]{:S(2)}) %collective-permute-start.1) | collective-permute-done | bytes 262176 | tf_op jit(solution)/shard_map/ppermute | solution.py:298
  25.7 1.9 %collective-permute-start.3 = (bf16[128,1024]{1,0:T(8,128)(2,1)S(1)}, bf16[128,1024]{1,0:T(8,128)(2,1)S(1)}, u32[]{:S(2)}, u32[]{:S(2)}) collective-permute-start(bf16[128,1024]{1,0:T(8,128)(2,1)S(1)} %collective-permute-done.1.rest_1_.b1), channel_id=1, source_target_pairs={{14,13},{15,14},{0,15},{1,0},{2,1},{3,2},{4,3},{5,4},{17,18},{18,1... | collective-permute-start | bytes 786440 | tf_op jit(solution)/shard_map/ppermute | solution.py:298
  27.7 0.1 pad_add_fusion.scal
  27.7 1.0 copy-done.1
  28.8 0.9 copy-done.2
  29.7 1.8 %shard_map.85 = (f32[4,1,512]{2,1,0:T(1,128)S(1)}, f32[4,1,512]{2,1,0:T(1,128)S(1)}, f32[4,128,512]{2,1,0:T(8,128)S(1)}, bf16[4,128,512]{2,1,0:T(8,128)(2,1)S(1)...) custom-call(s32[3]{0:T(128)S(1)} %pad_add_fusion.scal, s32[1,128]{1,0:T(1,128)S(1)} %bitcast.7, ...), custom_call_target="tpu_custom_call" | custom-call | flops 1000000000 | bytes 4194304 | tf_op jit(solution)/shard_map/pallas_call | solution.py:268
  31.5 0.7 collective-permute-start.4
  32.2 2.1 %collective-permute-done.3.rest_3_.b2 = bf16[128,1024]{1,0:T(8,128)(2,1)S(1)} collective-permute-done((bf16[128,1024]{1,0:T(8,128)(2,1)S(1)}, bf16[128,1024]{1,0:T(8,128)(2,1)S(1)}, u32[]{:S(2)}, u32[]{:S(2)}) %collective-permute-start.3) | collective-permute-done | bytes 262176 | tf_op jit(solution)/shard_map/ppermute | solution.py:298
  34.4 5.4 %collective-permute-start.5 = (bf16[128,1024]{1,0:T(8,128)(2,1)S(1)}, bf16[128,1024]{1,0:T(8,128)(2,1)S(1)}, u32[]{:S(2)}, u32[]{:S(2)}) collective-permute-start(bf16[128,1024]{1,0:T(8,128)(2,1)S(1)} %collective-permute-done.3.rest_3_.b2), channel_id=1, source_target_pairs={{13,12},{14,13},{15,14},{0,15},{1,0},{2,1},{3,2},{4,3},{18,19},{19... | collective-permute-start | bytes 786440 | tf_op jit(solution)/shard_map/ppermute | solution.py:298
  39.8 0.6 shard_map.86
  40.4 0.7 collective-permute-start.6
  41.1 3.1 %collective-permute-done.5.rest_1_.b = bf16[128,1024]{1,0:T(8,128)(2,1)S(1)} collective-permute-done((bf16[128,1024]{1,0:T(8,128)(2,1)S(1)}, bf16[128,1024]{1,0:T(8,128)(2,1)S(1)}, u32[]{:S(2)}, u32[]{:S(2)}) %collective-permute-start.5) | collective-permute-done | bytes 262176 | tf_op jit(solution)/shard_map/ppermute | solution.py:298
  44.2 5.6 %collective-permute-start.7 = (bf16[128,1024]{1,0:T(8,128)(2,1)S(1)}, bf16[128,1024]{1,0:T(8,128)(2,1)S(1)}, u32[]{:S(2)}, u32[]{:S(2)}) collective-permute-start(bf16[128,1024]{1,0:T(8,128)(2,1)S(1)} %collective-permute-done.5.rest_1_.b), channel_id=1, source_target_pairs={{12,11},{13,12},{14,13},{15,14},{0,15},{1,0},{2,1},{3,2},{19,20},{... | collective-permute-start | bytes 786440 | tf_op jit(solution)/shard_map/ppermute | solution.py:298
  49.8 0.6 shard_map.87
  50.4 0.7 collective-permute-start.8
  51.1 2.5 %collective-permute-done.7.rest_1_.b = bf16[128,1024]{1,0:T(8,128)(2,1)S(1)} collective-permute-done((bf16[128,1024]{1,0:T(8,128)(2,1)S(1)}, bf16[128,1024]{1,0:T(8,128)(2,1)S(1)}, u32[]{:S(2)}, u32[]{:S(2)}) %collective-permute-start.7) | collective-permute-done | bytes 262176 | tf_op jit(solution)/shard_map/ppermute | solution.py:298
  53.7 5.6 %collective-permute-start.9 = (bf16[128,1024]{1,0:T(8,128)(2,1)S(1)}, bf16[128,1024]{1,0:T(8,128)(2,1)S(1)}, u32[]{:S(2)}, u32[]{:S(2)}) collective-permute-start(bf16[128,1024]{1,0:T(8,128)(2,1)S(1)} %collective-permute-done.7.rest_1_.b), channel_id=1, source_target_pairs={{11,10},{12,11},{13,12},{14,13},{15,14},{0,15},{1,0},{2,1},{20,21}... | collective-permute-start | bytes 786440 | tf_op jit(solution)/shard_map/ppermute | solution.py:298
  59.3 0.6 shard_map.88
  59.9 0.7 collective-permute-start.10
  60.6 2.5 %collective-permute-done.9.rest_1_.b = bf16[128,1024]{1,0:T(8,128)(2,1)S(1)} collective-permute-done((bf16[128,1024]{1,0:T(8,128)(2,1)S(1)}, bf16[128,1024]{1,0:T(8,128)(2,1)S(1)}, u32[]{:S(2)}, u32[]{:S(2)}) %collective-permute-start.9) | collective-permute-done | bytes 262176 | tf_op jit(solution)/shard_map/ppermute | solution.py:298
  63.1 5.6 %collective-permute-start.11 = (bf16[128,1024]{1,0:T(8,128)(2,1)S(1)}, bf16[128,1024]{1,0:T(8,128)(2,1)S(1)}, u32[]{:S(2)}, u32[]{:S(2)}) collective-permute-start(bf16[128,1024]{1,0:T(8,128)(2,1)S(1)} %collective-permute-done.9.rest_1_.b), channel_id=1, source_target_pairs={{10,9},{11,10},{12,11},{13,12},{14,13},{15,14},{0,15},{1,0},{21,22... | collective-permute-start | bytes 786440 | tf_op jit(solution)/shard_map/ppermute | solution.py:298
  68.7 0.6 shard_map.89
  69.4 0.7 collective-permute-start.12
  70.1 2.5 %collective-permute-done.11.rest_1_.b = bf16[128,1024]{1,0:T(8,128)(2,1)S(1)} collective-permute-done((bf16[128,1024]{1,0:T(8,128)(2,1)S(1)}, bf16[128,1024]{1,0:T(8,128)(2,1)S(1)}, u32[]{:S(2)}, u32[]{:S(2)}) %collective-permute-start.11) | collective-permute-done | bytes 262176 | tf_op jit(solution)/shard_map/ppermute | solution.py:298
  72.6 5.6 %collective-permute-start.13 = (bf16[128,1024]{1,0:T(8,128)(2,1)S(1)}, bf16[128,1024]{1,0:T(8,128)(2,1)S(1)}, u32[]{:S(2)}, u32[]{:S(2)}) collective-permute-start(bf16[128,1024]{1,0:T(8,128)(2,1)S(1)} %collective-permute-done.11.rest_1_.b), channel_id=1, source_target_pairs={{9,8},{10,9},{11,10},{12,11},{13,12},{14,13},{15,14},{0,15},{22,23... | collective-permute-start | bytes 786440 | tf_op jit(solution)/shard_map/ppermute | solution.py:298
  78.2 0.6 shard_map.90
  78.8 0.6 shard_map.91
  79.5 2.6 %collective-permute-done.13.b = bf16[128,1024]{1,0:T(8,128)(2,1)S(1)} collective-permute-done((bf16[128,1024]{1,0:T(8,128)(2,1)S(1)}, bf16[128,1024]{1,0:T(8,128)(2,1)S(1)}, u32[]{:S(2)}, u32[]{:S(2)}) %collective-permute-start.13) | collective-permute-done | bytes 262176 | tf_op jit(solution)/shard_map/ppermute | solution.py:298
  82.1 1.1 shard_map.92
  83.2 0.7 collective-permute-start.14
  83.8 1.3 collective-permute-start.21
  85.1 1.6 shard_map.93
  86.9 0.7 collective-permute-start.15
  87.6 10.4 %collective-permute-done.21 = bf16[128,1024]{1,0:T(8,128)(2,1)S(1)} collective-permute-done((bf16[128,1024]{1,0:T(8,128)(2,1)S(1)}, bf16[128,1024]{1,0:T(8,128)(2,1)S(1)}, u32[]{:S(2)}, u32[]{:S(2)}) %collective-permute-start.21) | collective-permute-done | bytes 262176 | tf_op jit(solution)/shard_map/ppermute | solution.py:298
  98.0 1.9 %collective-permute-start.22 = (bf16[128,1024]{1,0:T(8,128)(2,1)S(1)}, bf16[128,1024]{1,0:T(8,128)(2,1)S(1)}, u32[]{:S(2)}, u32[]{:S(2)}) collective-permute-start(bf16[128,1024]{1,0:T(8,128)(2,1)S(1)} %add_convert_fusion.5), channel_id=1, source_target_pairs={{9,10},{10,11},{11,12},{12,13},{13,14},{14,15},{15,0},{0,1},{22,21... | collective-permute-start | bytes 786440 | tf_op jit(solution)/shard_map/ppermute | solution.py:298
  100.0 0.7 shard_map.94
  100.7 0.7 collective-permute-start.16
  101.4 9.2 %collective-permute-done.22 = bf16[128,1024]{1,0:T(8,128)(2,1)S(1)} collective-permute-done((bf16[128,1024]{1,0:T(8,128)(2,1)S(1)}, bf16[128,1024]{1,0:T(8,128)(2,1)S(1)}, u32[]{:S(2)}, u32[]{:S(2)}) %collective-permute-start.22) | collective-permute-done | bytes 262176 | tf_op jit(solution)/shard_map/ppermute | solution.py:298
  110.6 1.9 %collective-permute-start.23 = (bf16[128,1024]{1,0:T(8,128)(2,1)S(1)}, bf16[128,1024]{1,0:T(8,128)(2,1)S(1)}, u32[]{:S(2)}, u32[]{:S(2)}) collective-permute-start(bf16[128,1024]{1,0:T(8,128)(2,1)S(1)} %add_convert_fusion.4), channel_id=1, source_target_pairs={{10,11},{11,12},{12,13},{13,14},{14,15},{15,0},{0,1},{1,2},{21,20}... | collective-permute-start | bytes 786440 | tf_op jit(solution)/shard_map/ppermute | solution.py:298
  112.6 0.7 shard_map.95
  113.3 0.7 collective-permute-start.17
  114.0 6.8 %collective-permute-done.23 = bf16[128,1024]{1,0:T(8,128)(2,1)S(1)} collective-permute-done((bf16[128,1024]{1,0:T(8,128)(2,1)S(1)}, bf16[128,1024]{1,0:T(8,128)(2,1)S(1)}, u32[]{:S(2)}, u32[]{:S(2)}) %collective-permute-start.23) | collective-permute-done | bytes 262176 | tf_op jit(solution)/shard_map/ppermute | solution.py:298
  120.9 1.9 %collective-permute-start.24 = (bf16[128,1024]{1,0:T(8,128)(2,1)S(1)}, bf16[128,1024]{1,0:T(8,128)(2,1)S(1)}, u32[]{:S(2)}, u32[]{:S(2)}) collective-permute-start(bf16[128,1024]{1,0:T(8,128)(2,1)S(1)} %add_convert_fusion.3), channel_id=1, source_target_pairs={{11,12},{12,13},{13,14},{14,15},{15,0},{0,1},{1,2},{2,3},{20,19},{... | collective-permute-start | bytes 786440 | tf_op jit(solution)/shard_map/ppermute | solution.py:298
  122.8 0.7 shard_map.96
  123.6 0.7 collective-permute-start.18
  124.2 8.1 %collective-permute-done.24 = bf16[128,1024]{1,0:T(8,128)(2,1)S(1)} collective-permute-done((bf16[128,1024]{1,0:T(8,128)(2,1)S(1)}, bf16[128,1024]{1,0:T(8,128)(2,1)S(1)}, u32[]{:S(2)}, u32[]{:S(2)}) %collective-permute-start.24) | collective-permute-done | bytes 262176 | tf_op jit(solution)/shard_map/ppermute | solution.py:298
  132.4 1.9 %collective-permute-start.25 = (bf16[128,1024]{1,0:T(8,128)(2,1)S(1)}, bf16[128,1024]{1,0:T(8,128)(2,1)S(1)}, u32[]{:S(2)}, u32[]{:S(2)}) collective-permute-start(bf16[128,1024]{1,0:T(8,128)(2,1)S(1)} %add_convert_fusion.2), channel_id=1, source_target_pairs={{12,13},{13,14},{14,15},{15,0},{0,1},{1,2},{2,3},{3,4},{19,18},{20... | collective-permute-start | bytes 786440 | tf_op jit(solution)/shard_map/ppermute | solution.py:298
  134.3 0.7 shard_map.97
  135.1 0.7 collective-permute-start.19
  135.8 14.1 %collective-permute-done.25 = bf16[128,1024]{1,0:T(8,128)(2,1)S(1)} collective-permute-done((bf16[128,1024]{1,0:T(8,128)(2,1)S(1)}, bf16[128,1024]{1,0:T(8,128)(2,1)S(1)}, u32[]{:S(2)}, u32[]{:S(2)}) %collective-permute-start.25) | collective-permute-done | bytes 262176 | tf_op jit(solution)/shard_map/ppermute | solution.py:298
  149.9 1.9 %collective-permute-start.26 = (bf16[128,1024]{1,0:T(8,128)(2,1)S(1)}, bf16[128,1024]{1,0:T(8,128)(2,1)S(1)}, u32[]{:S(2)}, u32[]{:S(2)}) collective-permute-start(bf16[128,1024]{1,0:T(8,128)(2,1)S(1)} %add_convert_fusion.1), channel_id=1, source_target_pairs={{13,14},{14,15},{15,0},{0,1},{1,2},{2,3},{3,4},{4,5},{18,17},{19,1... | collective-permute-start | bytes 786440 | tf_op jit(solution)/shard_map/ppermute | solution.py:298
  151.9 1.3 collective-permute-start.20
  153.2 6.2 %collective-permute-done.26 = bf16[128,1024]{1,0:T(8,128)(2,1)S(1)} collective-permute-done((bf16[128,1024]{1,0:T(8,128)(2,1)S(1)}, bf16[128,1024]{1,0:T(8,128)(2,1)S(1)}, u32[]{:S(2)}, u32[]{:S(2)}) %collective-permute-start.26) | collective-permute-done | bytes 262176 | tf_op jit(solution)/shard_map/ppermute | solution.py:298
  159.5 1.9 %collective-permute-start.27 = (bf16[128,1024]{1,0:T(8,128)(2,1)S(1)}, bf16[128,1024]{1,0:T(8,128)(2,1)S(1)}, u32[]{:S(2)}, u32[]{:S(2)}) collective-permute-start(bf16[128,1024]{1,0:T(8,128)(2,1)S(1)} %add_convert_fusion), channel_id=1, source_target_pairs={{14,0},{15,1},{0,2},{1,3},{2,4},{3,5},{4,6},{5,7},{17,16},{18,17},... | collective-permute-start | bytes 786440 | tf_op jit(solution)/shard_map/ppermute | solution.py:298
  161.4 2.1 %shard_map.98 = (bf16[128,2048]{1,0:T(8,128)(2,1)}, f32[128,1024]{1,0:T(8,128)S(1)}) custom-call(s32[3]{0:T(128)S(1)} %pad_add_fusion.scal, bf16[128,2048]{1,0:T(8,128)(2,1)S(1)} %copy-done, bf16[128,2048]{1,0:T(8,128)(2,1)S(1)} %copy-done.1, f32[4,1,512]{2,1,0:T(1,128)S(1)} %get-tuple-element.101.log_ref, f32[4,1,512]{2,1,0:T(1,128)S(1)} %get-tuple-element.102.inner_ref, ...), custom_call_target="tpu_custom_call" | custom-call | flops 1000000000 | bytes 4194304 | tf_op jit(solution)/shard_map/pallas_call | solution.py:268
  163.5 6.5 %collective-permute-done.27 = bf16[128,1024]{1,0:T(8,128)(2,1)S(1)} collective-permute-done((bf16[128,1024]{1,0:T(8,128)(2,1)S(1)}, bf16[128,1024]{1,0:T(8,128)(2,1)S(1)}, u32[]{:S(2)}, u32[]{:S(2)}) %collective-permute-start.27) | collective-permute-done | bytes 262176 | tf_op jit(solution)/shard_map/ppermute | solution.py:298
  169.9 0.1 add_add_fusion
  170.1 0.8 fusion
  (34 shorter events, 0.9 us)
Async XLA Ops:
  0.6 27.1 %copy-start = (bf16[128,2048]{1,0:T(8,128)(2,1)S(1)}, bf16[128,2048]{1,0:T(8,128)(2,1)}, u32[]{:S(2)}) copy-start(bf16[128,2048]{1,0:T(8,128)(2,1)} %q_ref.27) | copy-start | bytes 1572868
  2.4 14.8 %copy-start.4 = (s32[2048]{0:T(1024)S(1)}, s32[2048]{0:T(1024)}, u32[]{:S(2)}) copy-start(s32[2048]{0:T(1024)} %param.9) | copy-start | bytes 24580
  2.4 14.9 %collective-permute-start = (bf16[128,1024]{1,0:T(8,128)(2,1)}, bf16[128,1024]{1,0:T(8,128)(2,1)S(1)}, u32[]{:S(2)}, u32[]{:S(2)}) collective-permute-start(bf16[128,1024]{1,0:T(8,128)(2,1)} %shard_map.84.own), channel_id=1, source_target_pairs={{0,1},{1,2},{2,3},{3,4},{4,5},{5,6},{6,7},{7,8},{8,9},{9,10},{10,1... | collective-permute-start | bytes 786440 | tf_op jit(solution)/shard_map/ppermute | solution.py:298
  6.2 19.5 %collective-permute-start.1 = (bf16[128,1024]{1,0:T(8,128)(2,1)}, bf16[128,1024]{1,0:T(8,128)(2,1)S(1)}, u32[]{:S(2)}, u32[]{:S(2)}) collective-permute-start(bf16[128,1024]{1,0:T(8,128)(2,1)} %shard_map.84.own), channel_id=1, source_target_pairs={{0,14},{1,15},{2,0},{3,1},{4,2},{5,3},{6,4},{7,5},{16,17},{17,18},... | collective-permute-start | bytes 786440 | tf_op jit(solution)/shard_map/ppermute | solution.py:298
  17.3 14.2 %collective-permute-start.2 = (bf16[128,1024]{1,0:T(8,128)(2,1)S(1)}, bf16[128,1024]{1,0:T(8,128)(2,1)S(1)}, u32[]{:S(2)}, u32[]{:S(2)}) collective-permute-start(bf16[128,1024]{1,0:T(8,128)(2,1)S(1)} %collective-permute-done.rest_0_.a1), channel_id=1, source_target_pairs={{1,2},{2,3},{3,4},{4,5},{5,6},{6,7},{7,8},{8,9},{9,10},{10,11},{11... | collective-permute-start | bytes 786440 | tf_op jit(solution)/shard_map/ppermute | solution.py:298
  25.7 8.6 %collective-permute-start.3 = (bf16[128,1024]{1,0:T(8,128)(2,1)S(1)}, bf16[128,1024]{1,0:T(8,128)(2,1)S(1)}, u32[]{:S(2)}, u32[]{:S(2)}) collective-permute-start(bf16[128,1024]{1,0:T(8,128)(2,1)S(1)} %collective-permute-done.1.rest_1_.b1), channel_id=1, source_target_pairs={{14,13},{15,14},{0,15},{1,0},{2,1},{3,2},{4,3},{5,4},{17,18},{18,1... | collective-permute-start | bytes 786440 | tf_op jit(solution)/shard_map/ppermute | solution.py:298
  27.7 1.0 copy-start.1
  28.8 0.9 copy-start.2
  31.5 8.9 %collective-permute-start.4 = (bf16[128,1024]{1,0:T(8,128)(2,1)S(1)}, bf16[128,1024]{1,0:T(8,128)(2,1)S(1)}, u32[]{:S(2)}, u32[]{:S(2)}) collective-permute-start(bf16[128,1024]{1,0:T(8,128)(2,1)S(1)} %collective-permute-done.2.rest_2_.a2), channel_id=1, source_target_pairs={{2,3},{3,4},{4,5},{5,6},{6,7},{7,8},{8,9},{9,10},{10,11},{11,12},{... | collective-permute-start | bytes 786440 | tf_op jit(solution)/shard_map/ppermute | solution.py:298
  34.4 9.8 %collective-permute-start.5 = (bf16[128,1024]{1,0:T(8,128)(2,1)S(1)}, bf16[128,1024]{1,0:T(8,128)(2,1)S(1)}, u32[]{:S(2)}, u32[]{:S(2)}) collective-permute-start(bf16[128,1024]{1,0:T(8,128)(2,1)S(1)} %collective-permute-done.3.rest_3_.b2), channel_id=1, source_target_pairs={{13,12},{14,13},{15,14},{0,15},{1,0},{2,1},{3,2},{4,3},{18,19},{19... | collective-permute-start | bytes 786440 | tf_op jit(solution)/shard_map/ppermute | solution.py:298
  40.4 10.0 %collective-permute-start.6 = (bf16[128,1024]{1,0:T(8,128)(2,1)S(1)}, bf16[128,1024]{1,0:T(8,128)(2,1)S(1)}, u32[]{:S(2)}, u32[]{:S(2)}) collective-permute-start(bf16[128,1024]{1,0:T(8,128)(2,1)S(1)} %collective-permute-done.4.rest_0_.a), channel_id=1, source_target_pairs={{3,4},{4,5},{5,6},{6,7},{7,8},{8,9},{9,10},{10,11},{11,12},{12,13}... | collective-permute-start | bytes 786440 | tf_op jit(solution)/shard_map/ppermute | solution.py:298
  44.2 9.5 %collective-permute-start.7 = (bf16[128,1024]{1,0:T(8,128)(2,1)S(1)}, bf16[128,1024]{1,0:T(8,128)(2,1)S(1)}, u32[]{:S(2)}, u32[]{:S(2)}) collective-permute-start(bf16[128,1024]{1,0:T(8,128)(2,1)S(1)} %collective-permute-done.5.rest_1_.b), channel_id=1, source_target_pairs={{12,11},{13,12},{14,13},{15,14},{0,15},{1,0},{2,1},{3,2},{19,20},{... | collective-permute-start | bytes 786440 | tf_op jit(solution)/shard_map/ppermute | solution.py:298
  50.4 9.5 %collective-permute-start.8 = (bf16[128,1024]{1,0:T(8,128)(2,1)S(1)}, bf16[128,1024]{1,0:T(8,128)(2,1)S(1)}, u32[]{:S(2)}, u32[]{:S(2)}) collective-permute-start(bf16[128,1024]{1,0:T(8,128)(2,1)S(1)} %collective-permute-done.6.rest_0_.a), channel_id=1, source_target_pairs={{4,5},{5,6},{6,7},{7,8},{8,9},{9,10},{10,11},{11,12},{12,13},{13,1... | collective-permute-start | bytes 786440 | tf_op jit(solution)/shard_map/ppermute | solution.py:298
  53.7 9.5 %collective-permute-start.9 = (bf16[128,1024]{1,0:T(8,128)(2,1)S(1)}, bf16[128,1024]{1,0:T(8,128)(2,1)S(1)}, u32[]{:S(2)}, u32[]{:S(2)}) collective-permute-start(bf16[128,1024]{1,0:T(8,128)(2,1)S(1)} %collective-permute-done.7.rest_1_.b), channel_id=1, source_target_pairs={{11,10},{12,11},{13,12},{14,13},{15,14},{0,15},{1,0},{2,1},{20,21}... | collective-permute-start | bytes 786440 | tf_op jit(solution)/shard_map/ppermute | solution.py:298
  59.9 9.5 %collective-permute-start.10 = (bf16[128,1024]{1,0:T(8,128)(2,1)S(1)}, bf16[128,1024]{1,0:T(8,128)(2,1)S(1)}, u32[]{:S(2)}, u32[]{:S(2)}) collective-permute-start(bf16[128,1024]{1,0:T(8,128)(2,1)S(1)} %collective-permute-done.8.rest_0_.a), channel_id=1, source_target_pairs={{5,6},{6,7},{7,8},{8,9},{9,10},{10,11},{11,12},{12,13},{13,14},{14... | collective-permute-start | bytes 786440 | tf_op jit(solution)/shard_map/ppermute | solution.py:298
  63.1 9.5 %collective-permute-start.11 = (bf16[128,1024]{1,0:T(8,128)(2,1)S(1)}, bf16[128,1024]{1,0:T(8,128)(2,1)S(1)}, u32[]{:S(2)}, u32[]{:S(2)}) collective-permute-start(bf16[128,1024]{1,0:T(8,128)(2,1)S(1)} %collective-permute-done.9.rest_1_.b), channel_id=1, source_target_pairs={{10,9},{11,10},{12,11},{13,12},{14,13},{15,14},{0,15},{1,0},{21,22... | collective-permute-start | bytes 786440 | tf_op jit(solution)/shard_map/ppermute | solution.py:298
  69.4 9.5 %collective-permute-start.12 = (bf16[128,1024]{1,0:T(8,128)(2,1)S(1)}, bf16[128,1024]{1,0:T(8,128)(2,1)S(1)}, u32[]{:S(2)}, u32[]{:S(2)}) collective-permute-start(bf16[128,1024]{1,0:T(8,128)(2,1)S(1)} %collective-permute-done.10.rest_0_.a), channel_id=1, source_target_pairs={{6,7},{7,8},{8,9},{9,10},{10,11},{11,12},{12,13},{13,14},{14,15},{... | collective-permute-start | bytes 786440 | tf_op jit(solution)/shard_map/ppermute | solution.py:298
  72.6 9.5 %collective-permute-start.13 = (bf16[128,1024]{1,0:T(8,128)(2,1)S(1)}, bf16[128,1024]{1,0:T(8,128)(2,1)S(1)}, u32[]{:S(2)}, u32[]{:S(2)}) collective-permute-start(bf16[128,1024]{1,0:T(8,128)(2,1)S(1)} %collective-permute-done.11.rest_1_.b), channel_id=1, source_target_pairs={{9,8},{10,9},{11,10},{12,11},{13,12},{14,13},{15,14},{0,15},{22,23... | collective-permute-start | bytes 786440 | tf_op jit(solution)/shard_map/ppermute | solution.py:298
  83.2 3.6 %collective-permute-start.14 = (bf16[128,1024]{1,0:T(8,128)(2,1)S(1)}, bf16[128,1024]{1,0:T(8,128)(2,1)S(1)}, u32[]{:S(2)}, u32[]{:S(2)}) collective-permute-start(bf16[128,1024]{1,0:T(8,128)(2,1)S(1)} %get-tuple-element.121), channel_id=1, source_target_pairs={{7,6},{8,7},{9,8},{10,9},{11,10},{12,11},{13,12},{14,13},{15,14},{... | collective-permute-start | bytes 786440 | tf_op jit(solution)/shard_map/ppermute | solution.py:298
  83.8 14.1 %collective-permute-start.21 = (bf16[128,1024]{1,0:T(8,128)(2,1)S(1)}, bf16[128,1024]{1,0:T(8,128)(2,1)S(1)}, u32[]{:S(2)}, u32[]{:S(2)}) collective-permute-start(bf16[128,1024]{1,0:T(8,128)(2,1)S(1)} %get-tuple-element.132), channel_id=1, source_target_pairs={{8,9},{9,10},{10,11},{11,12},{12,13},{13,14},{14,15},{15,0},{23,22... | collective-permute-start | bytes 786440 | tf_op jit(solution)/shard_map/ppermute | solution.py:298
  86.9 13.8 %collective-permute-start.15 = (bf16[128,1024]{1,0:T(8,128)(2,1)S(1)}, bf16[128,1024]{1,0:T(8,128)(2,1)S(1)}, u32[]{:S(2)}, u32[]{:S(2)}) collective-permute-start(bf16[128,1024]{1,0:T(8,128)(2,1)S(1)} %add_convert_fusion.11), channel_id=1, source_target_pairs={{6,5},{7,6},{8,7},{9,8},{10,9},{11,10},{12,11},{13,12},{14,13},{15... | collective-permute-start | bytes 786440 | tf_op jit(solution)/shard_map/ppermute | solution.py:298
  98.0 12.5 %collective-permute-start.22 = (bf16[128,1024]{1,0:T(8,128)(2,1)S(1)}, bf16[128,1024]{1,0:T(8,128)(2,1)S(1)}, u32[]{:S(2)}, u32[]{:S(2)}) collective-permute-start(bf16[128,1024]{1,0:T(8,128)(2,1)S(1)} %add_convert_fusion.5), channel_id=1, source_target_pairs={{9,10},{10,11},{11,12},{12,13},{13,14},{14,15},{15,0},{0,1},{22,21... | collective-permute-start | bytes 786440 | tf_op jit(solution)/shard_map/ppermute | solution.py:298
  100.7 12.5 %collective-permute-start.16 = (bf16[128,1024]{1,0:T(8,128)(2,1)S(1)}, bf16[128,1024]{1,0:T(8,128)(2,1)S(1)}, u32[]{:S(2)}, u32[]{:S(2)}) collective-permute-start(bf16[128,1024]{1,0:T(8,128)(2,1)S(1)} %add_convert_fusion.10), channel_id=1, source_target_pairs={{5,4},{6,5},{7,6},{8,7},{9,8},{10,9},{11,10},{12,11},{13,12},{14,1... | collective-permute-start | bytes 786440 | tf_op jit(solution)/shard_map/ppermute | solution.py:298
  110.6 10.2 %collective-permute-start.23 = (bf16[128,1024]{1,0:T(8,128)(2,1)S(1)}, bf16[128,1024]{1,0:T(8,128)(2,1)S(1)}, u32[]{:S(2)}, u32[]{:S(2)}) collective-permute-start(bf16[128,1024]{1,0:T(8,128)(2,1)S(1)} %add_convert_fusion.4), channel_id=1, source_target_pairs={{10,11},{11,12},{12,13},{13,14},{14,15},{15,0},{0,1},{1,2},{21,20}... | collective-permute-start | bytes 786440 | tf_op jit(solution)/shard_map/ppermute | solution.py:298
  113.3 10.2 %collective-permute-start.17 = (bf16[128,1024]{1,0:T(8,128)(2,1)S(1)}, bf16[128,1024]{1,0:T(8,128)(2,1)S(1)}, u32[]{:S(2)}, u32[]{:S(2)}) collective-permute-start(bf16[128,1024]{1,0:T(8,128)(2,1)S(1)} %add_convert_fusion.9), channel_id=1, source_target_pairs={{4,3},{5,4},{6,5},{7,6},{8,7},{9,8},{10,9},{11,10},{12,11},{13,12}... | collective-permute-start | bytes 786440 | tf_op jit(solution)/shard_map/ppermute | solution.py:298
  120.9 11.4 %collective-permute-start.24 = (bf16[128,1024]{1,0:T(8,128)(2,1)S(1)}, bf16[128,1024]{1,0:T(8,128)(2,1)S(1)}, u32[]{:S(2)}, u32[]{:S(2)}) collective-permute-start(bf16[128,1024]{1,0:T(8,128)(2,1)S(1)} %add_convert_fusion.3), channel_id=1, source_target_pairs={{11,12},{12,13},{13,14},{14,15},{15,0},{0,1},{1,2},{2,3},{20,19},{... | collective-permute-start | bytes 786440 | tf_op jit(solution)/shard_map/ppermute | solution.py:298
  123.6 11.5 %collective-permute-start.18 = (bf16[128,1024]{1,0:T(8,128)(2,1)S(1)}, bf16[128,1024]{1,0:T(8,128)(2,1)S(1)}, u32[]{:S(2)}, u32[]{:S(2)}) collective-permute-start(bf16[128,1024]{1,0:T(8,128)(2,1)S(1)} %add_convert_fusion.8), channel_id=1, source_target_pairs={{3,2},{4,3},{5,4},{6,5},{7,6},{8,7},{9,8},{10,9},{11,10},{12,11},{... | collective-permute-start | bytes 786440 | tf_op jit(solution)/shard_map/ppermute | solution.py:298
  132.4 17.5 %collective-permute-start.25 = (bf16[128,1024]{1,0:T(8,128)(2,1)S(1)}, bf16[128,1024]{1,0:T(8,128)(2,1)S(1)}, u32[]{:S(2)}, u32[]{:S(2)}) collective-permute-start(bf16[128,1024]{1,0:T(8,128)(2,1)S(1)} %add_convert_fusion.2), channel_id=1, source_target_pairs={{12,13},{13,14},{14,15},{15,0},{0,1},{1,2},{2,3},{3,4},{19,18},{20... | collective-permute-start | bytes 786440 | tf_op jit(solution)/shard_map/ppermute | solution.py:298
  135.1 16.7 %collective-permute-start.19 = (bf16[128,1024]{1,0:T(8,128)(2,1)S(1)}, bf16[128,1024]{1,0:T(8,128)(2,1)S(1)}, u32[]{:S(2)}, u32[]{:S(2)}) collective-permute-start(bf16[128,1024]{1,0:T(8,128)(2,1)S(1)} %add_convert_fusion.7), channel_id=1, source_target_pairs={{2,1},{3,2},{4,3},{5,4},{6,5},{7,6},{8,7},{9,8},{10,9},{11,10},{12... | collective-permute-start | bytes 786440 | tf_op jit(solution)/shard_map/ppermute | solution.py:298
  149.9 9.5 %collective-permute-start.26 = (bf16[128,1024]{1,0:T(8,128)(2,1)S(1)}, bf16[128,1024]{1,0:T(8,128)(2,1)S(1)}, u32[]{:S(2)}, u32[]{:S(2)}) collective-permute-start(bf16[128,1024]{1,0:T(8,128)(2,1)S(1)} %add_convert_fusion.1), channel_id=1, source_target_pairs={{13,14},{14,15},{15,0},{0,1},{1,2},{2,3},{3,4},{4,5},{18,17},{19,1... | collective-permute-start | bytes 786440 | tf_op jit(solution)/shard_map/ppermute | solution.py:298
  151.9 11.5 %collective-permute-start.20 = (bf16[128,1024]{1,0:T(8,128)(2,1)S(1)}, bf16[128,1024]{1,0:T(8,128)(2,1)S(1)}, u32[]{:S(2)}, u32[]{:S(2)}) collective-permute-start(bf16[128,1024]{1,0:T(8,128)(2,1)S(1)} %add_convert_fusion.6), channel_id=1, source_target_pairs={{1,0},{2,1},{3,2},{4,3},{5,4},{6,5},{7,6},{8,7},{9,8},{10,9},{11,1... | collective-permute-start | bytes 786440 | tf_op jit(solution)/shard_map/ppermute | solution.py:298
  159.4 2.0 %copy-start.3 = (bf16[128,1024]{1,0:T(8,128)(2,1)S(1)}, bf16[128,1024]{1,0:T(8,128)(2,1)}, u32[]{:S(2)}) copy-start(bf16[128,1024]{1,0:T(8,128)(2,1)} %shard_map.84.own) | copy-start | bytes 786436
  159.5 10.5 %collective-permute-start.27 = (bf16[128,1024]{1,0:T(8,128)(2,1)S(1)}, bf16[128,1024]{1,0:T(8,128)(2,1)S(1)}, u32[]{:S(2)}, u32[]{:S(2)}) collective-permute-start(bf16[128,1024]{1,0:T(8,128)(2,1)S(1)} %add_convert_fusion), channel_id=1, source_target_pairs={{14,0},{15,1},{0,2},{1,3},{2,4},{3,5},{4,6},{5,7},{17,16},{18,17},... | collective-permute-start | bytes 786440 | tf_op jit(solution)/shard_map/ppermute | solution.py:298

commit v7 on v6

--- a/solution.py
+++ b/solution.py
@@ -293,7 +293,7 @@
     windows, count = lax.axis_size("dp"), lax.axis_size("ctx")
     pairs = []
     for window in range(windows):
-        chosen = near_pairs if (window + flip) % 2 == 0 else far_pairs
+        chosen = near_pairs if flip else far_pairs
         pairs += [(window * count + i, window * count + j) for i, j in chosen]
     return lax.ppermute(x, ("dp", "ctx"), pairs)
 
@@ -321,7 +321,7 @@
 def local(queries, keys, values, out_grad, segment_ids):
     rows = queries.shape[0]
     count = lax.axis_size("ctx")
-    odd = lax.rem(lax.axis_index("dp"), 2)
+    odd = jnp.ones((), jnp.int32)
     q_start = lax.axis_index("ctx") * rows
     own = pack(keys, values)
     q_seg = lax.dynamic_slice_in_dim(segment_ids, q_start, rows, 0)

time: 172 us -> 167 us (0.971)
  the two profiles are of different devices: /device:TPU:2 before, /device:TPU:60 now
where the time goes in v7:
time: 167 us; the launch traced here: 166 us
  waiting for transfers between devices  78.7 us (47%)
  starting transfers between devices  64.5 us (39%)
  Pallas kernels  17.4 us (10%)
  local copies, waits for them, and re-layouts  2.92 us (2%)
    ppermute x28, waiting for transfers between devices, both_ways(): return lax.ppermute(x, ('dp', 'ctx'), pairs)  78.7 us
    ppermute x28, starting transfers between devices, both_ways(): return lax.ppermute(x, ('dp', 'ctx'), pairs)  64.5 us
    pallas_call x14, Pallas kernels, call(): pl.pallas_call(kernel, out_shape=outs, in_specs=[pl.BlockSpec(memory_spac...  15.7 us
  transfers between devices with their start and end apart: 28, of which 11 were waited for; matrix products, arithmetic and copies ran while one was open for 1% of the time, Pallas kernels for 9%

profile of v7, /device:TPU:60, one launch (start us, length us, event | category | flops | bytes accessed | tf_op | source)
XLA Modules:
  0.0 166.1 jit_solution(16091554886841959852)
XLA Ops:
  0.6 1.7 %shard_map.84.own = bf16[128,1024]{1,0:T(8,128)(2,1)} custom-call(bf16[128,512]{1,0:T(8,128)(2,1)} %k_ref.1, bf16[128,512]{1,0:T(8,128)(2,1)} %v_ref.1), custom_call_target="tpu_custom_call" | custom-call | tf_op jit(solution)/shard_map/pallas_call | solution.py:283
  2.4 10.9 %collective-permute-start = (bf16[128,1024]{1,0:T(8,128)(2,1)}, bf16[128,1024]{1,0:T(8,128)(2,1)S(1)}, u32[]{:S(2)}, u32[]{:S(2)}) collective-permute-start(bf16[128,1024]{1,0:T(8,128)(2,1)} %shard_map.84.own), channel_id=1, source_target_pairs={{0,14},{1,15},{2,0},{3,1},{4,2},{5,3},{6,4},{7,5},{16,30},{17,31},... | collective-permute-start | bytes 786440 | tf_op jit(solution)/shard_map/ppermute | solution.py:298
  13.4 1.9 %collective-permute-start.1 = (bf16[128,1024]{1,0:T(8,128)(2,1)}, bf16[128,1024]{1,0:T(8,128)(2,1)S(1)}, u32[]{:S(2)}, u32[]{:S(2)}) collective-permute-start(bf16[128,1024]{1,0:T(8,128)(2,1)} %shard_map.84.own), channel_id=1, source_target_pairs={{0,1},{1,2},{2,3},{3,4},{4,5},{5,6},{6,7},{7,8},{8,9},{9,10},{10,1... | collective-permute-start | bytes 786440 | tf_op jit(solution)/shard_map/ppermute | solution.py:298
  15.3 0.1 dynamic_slice.3
  15.4 5.6 %collective-permute-done.rest_0_.a1 = bf16[128,1024]{1,0:T(8,128)(2,1)S(1)} collective-permute-done((bf16[128,1024]{1,0:T(8,128)(2,1)}, bf16[128,1024]{1,0:T(8,128)(2,1)S(1)}, u32[]{:S(2)}, u32[]{:S(2)}) %collective-permute-start) | collective-permute-done | bytes 262176 | tf_op jit(solution)/shard_map/ppermute | solution.py:298
  21.0 6.8 %collective-permute-start.2 = (bf16[128,1024]{1,0:T(8,128)(2,1)S(1)}, bf16[128,1024]{1,0:T(8,128)(2,1)S(1)}, u32[]{:S(2)}, u32[]{:S(2)}) collective-permute-start(bf16[128,1024]{1,0:T(8,128)(2,1)S(1)} %collective-permute-done.rest_0_.a1), channel_id=1, source_target_pairs={{14,13},{15,14},{0,15},{1,0},{2,1},{3,2},{4,3},{5,4},{30,29},{31,3... | collective-permute-start | bytes 786440 | tf_op jit(solution)/shard_map/ppermute | solution.py:298
  27.7 0.4 convert_reduce_fusion
  28.2 1.3 collective-permute-start.3
  29.5 0.1 pad_add_fusion.scal
  29.6 1.0 copy-done.1
  30.6 0.9 copy-done.2
  31.6 1.8 %shard_map.85 = (f32[4,1,512]{2,1,0:T(1,128)S(1)}, f32[4,1,512]{2,1,0:T(1,128)S(1)}, f32[4,128,512]{2,1,0:T(8,128)S(1)}, bf16[4,128,512]{2,1,0:T(8,128)(2,1)S(1)...) custom-call(s32[3]{0:T(128)S(1)} %pad_add_fusion.scal, s32[1,128]{1,0:T(1,128)S(1)} %bitcast.6, ...), custom_call_target="tpu_custom_call" | custom-call | flops 1000000000 | bytes 4194304 | tf_op jit(solution)/shard_map/pallas_call | solution.py:268
  33.4 3.6 %collective-permute-start.4 = (bf16[128,1024]{1,0:T(8,128)(2,1)S(1)}, bf16[128,1024]{1,0:T(8,128)(2,1)S(1)}, u32[]{:S(2)}, u32[]{:S(2)}) collective-permute-start(bf16[128,1024]{1,0:T(8,128)(2,1)S(1)} %collective-permute-done.2.rest_2_.a2), channel_id=1, source_target_pairs={{13,12},{14,13},{15,14},{0,15},{1,0},{2,1},{3,2},{4,3},{29,28},{30... | collective-permute-start | bytes 786440 | tf_op jit(solution)/shard_map/ppermute | solution.py:298
  37.0 0.7 collective-permute-start.5
  37.7 2.3 %shard_map.86 = (f32[4,1,512]{2,1,0:T(1,128)S(1)}, f32[4,1,512]{2,1,0:T(1,128)S(1)}, f32[4,128,512]{2,1,0:T(8,128)S(1)}, bf16[4,256,512]{2,1,0:T(8,128)(2,1)S(1)}, bf16[4,256,512]{2,1,0:T(8,128)(2,1)S(1)}) custom-call(s32[3]{0:T(128)S(1)} %pad_add_fusion.scal, s32[1,128]{1,0:T(1,128)S(1)} %bitcast.7, bf16[128,2048]{1,0:T(8,128)(2,1)S(1)} %copy-done, ...), custom_call_target="tpu_custom_call" | custom-call | flops 1000000000 | bytes 4194304 | tf_op jit(solution)/shard_map/pallas_call | solution.py:268
  39.9 2.4 %collective-permute-done.4.rest_0_.a = bf16[128,1024]{1,0:T(8,128)(2,1)S(1)} collective-permute-done((bf16[128,1024]{1,0:T(8,128)(2,1)S(1)}, bf16[128,1024]{1,0:T(8,128)(2,1)S(1)}, u32[]{:S(2)}, u32[]{:S(2)}) %collective-permute-start.4) | collective-permute-done | bytes 262176 | tf_op jit(solution)/shard_map/ppermute | solution.py:298
  42.3 4.4 %collective-permute-start.6 = (bf16[128,1024]{1,0:T(8,128)(2,1)S(1)}, bf16[128,1024]{1,0:T(8,128)(2,1)S(1)}, u32[]{:S(2)}, u32[]{:S(2)}) collective-permute-start(bf16[128,1024]{1,0:T(8,128)(2,1)S(1)} %collective-permute-done.4.rest_0_.a), channel_id=1, source_target_pairs={{12,11},{13,12},{14,13},{15,14},{0,15},{1,0},{2,1},{3,2},{28,27},{... | collective-permute-start | bytes 786440 | tf_op jit(solution)/shard_map/ppermute | solution.py:298
  46.8 0.7 collective-permute-start.7
  47.5 0.6 shard_map.87
  48.1 2.5 %collective-permute-done.6.rest_0_.a = bf16[128,1024]{1,0:T(8,128)(2,1)S(1)} collective-permute-done((bf16[128,1024]{1,0:T(8,128)(2,1)S(1)}, bf16[128,1024]{1,0:T(8,128)(2,1)S(1)}, u32[]{:S(2)}, u32[]{:S(2)}) %collective-permute-start.6) | collective-permute-done | bytes 262176 | tf_op jit(solution)/shard_map/ppermute | solution.py:298
  50.7 5.6 %collective-permute-start.8 = (bf16[128,1024]{1,0:T(8,128)(2,1)S(1)}, bf16[128,1024]{1,0:T(8,128)(2,1)S(1)}, u32[]{:S(2)}, u32[]{:S(2)}) collective-permute-start(bf16[128,1024]{1,0:T(8,128)(2,1)S(1)} %collective-permute-done.6.rest_0_.a), channel_id=1, source_target_pairs={{11,10},{12,11},{13,12},{14,13},{15,14},{0,15},{1,0},{2,1},{27,26}... | collective-permute-start | bytes 786440 | tf_op jit(solution)/shard_map/ppermute | solution.py:298
  56.3 0.7 collective-permute-start.9
  57.0 0.6 shard_map.88
  57.6 2.5 %collective-permute-done.8.rest_0_.a = bf16[128,1024]{1,0:T(8,128)(2,1)S(1)} collective-permute-done((bf16[128,1024]{1,0:T(8,128)(2,1)S(1)}, bf16[128,1024]{1,0:T(8,128)(2,1)S(1)}, u32[]{:S(2)}, u32[]{:S(2)}) %collective-permute-start.8) | collective-permute-done | bytes 262176 | tf_op jit(solution)/shard_map/ppermute | solution.py:298
  60.1 5.6 %collective-permute-start.10 = (bf16[128,1024]{1,0:T(8,128)(2,1)S(1)}, bf16[128,1024]{1,0:T(8,128)(2,1)S(1)}, u32[]{:S(2)}, u32[]{:S(2)}) collective-permute-start(bf16[128,1024]{1,0:T(8,128)(2,1)S(1)} %collective-permute-done.8.rest_0_.a), channel_id=1, source_target_pairs={{10,9},{11,10},{12,11},{13,12},{14,13},{15,14},{0,15},{1,0},{26,25... | collective-permute-start | bytes 786440 | tf_op jit(solution)/shard_map/ppermute | solution.py:298
  65.8 0.7 collective-permute-start.11
  66.4 0.6 shard_map.89
  67.1 2.5 %collective-permute-done.10.rest_0_.a = bf16[128,1024]{1,0:T(8,128)(2,1)S(1)} collective-permute-done((bf16[128,1024]{1,0:T(8,128)(2,1)S(1)}, bf16[128,1024]{1,0:T(8,128)(2,1)S(1)}, u32[]{:S(2)}, u32[]{:S(2)}) %collective-permute-start.10) | collective-permute-done | bytes 262176 | tf_op jit(solution)/shard_map/ppermute | solution.py:298
  69.6 0.7 collective-permute-start.12
  70.3 0.7 collective-permute-start.13
  71.0 0.6 shard_map.90
  71.6 0.6 shard_map.91
  72.2 1.1 shard_map.92
  73.3 0.7 collective-permute-start.14
  74.0 0.7 collective-permute-start.21
  74.7 1.6 shard_map.93
  76.4 1.3 collective-permute-start.15
  77.8 0.7 collective-permute-start.22
  78.5 0.7 shard_map.94
  79.2 29.7 %collective-permute-done.15 = bf16[128,1024]{1,0:T(8,128)(2,1)S(1)} collective-permute-done((bf16[128,1024]{1,0:T(8,128)(2,1)S(1)}, bf16[128,1024]{1,0:T(8,128)(2,1)S(1)}, u32[]{:S(2)}, u32[]{:S(2)}) %collective-permute-start.15) | collective-permute-done | bytes 262176 | tf_op jit(solution)/shard_map/ppermute | solution.py:298
  108.9 1.9 %collective-permute-start.16 = (bf16[128,1024]{1,0:T(8,128)(2,1)S(1)}, bf16[128,1024]{1,0:T(8,128)(2,1)S(1)}, u32[]{:S(2)}, u32[]{:S(2)}) collective-permute-start(bf16[128,1024]{1,0:T(8,128)(2,1)S(1)} %add_convert_fusion.10), channel_id=1, source_target_pairs={{10,11},{11,12},{12,13},{13,14},{14,15},{15,0},{0,1},{1,2},{26,27}... | collective-permute-start | bytes 786440 | tf_op jit(solution)/shard_map/ppermute | solution.py:298
  110.9 0.7 collective-permute-start.23
  111.6 0.7 shard_map.95
  112.3 8.3 %collective-permute-done.16 = bf16[128,1024]{1,0:T(8,128)(2,1)S(1)} collective-permute-done((bf16[128,1024]{1,0:T(8,128)(2,1)S(1)}, bf16[128,1024]{1,0:T(8,128)(2,1)S(1)}, u32[]{:S(2)}, u32[]{:S(2)}) %collective-permute-start.16) | collective-permute-done | bytes 262176 | tf_op jit(solution)/shard_map/ppermute | solution.py:298
  120.6 1.9 %collective-permute-start.17 = (bf16[128,1024]{1,0:T(8,128)(2,1)S(1)}, bf16[128,1024]{1,0:T(8,128)(2,1)S(1)}, u32[]{:S(2)}, u32[]{:S(2)}) collective-permute-start(bf16[128,1024]{1,0:T(8,128)(2,1)S(1)} %add_convert_fusion.9), channel_id=1, source_target_pairs={{11,12},{12,13},{13,14},{14,15},{15,0},{0,1},{1,2},{2,3},{27,28},{... | collective-permute-start | bytes 786440 | tf_op jit(solution)/shard_map/ppermute | solution.py:298
  122.6 0.1 add_convert_fusion.3
  122.7 0.7 collective-permute-start.24
  123.3 0.7 shard_map.96
  124.0 7.1 %collective-permute-done.17 = bf16[128,1024]{1,0:T(8,128)(2,1)S(1)} collective-permute-done((bf16[128,1024]{1,0:T(8,128)(2,1)S(1)}, bf16[128,1024]{1,0:T(8,128)(2,1)S(1)}, u32[]{:S(2)}, u32[]{:S(2)}) %collective-permute-start.17) | collective-permute-done | bytes 262176 | tf_op jit(solution)/shard_map/ppermute | solution.py:298
  131.2 1.9 %collective-permute-start.18 = (bf16[128,1024]{1,0:T(8,128)(2,1)S(1)}, bf16[128,1024]{1,0:T(8,128)(2,1)S(1)}, u32[]{:S(2)}, u32[]{:S(2)}) collective-permute-start(bf16[128,1024]{1,0:T(8,128)(2,1)S(1)} %add_convert_fusion.8), channel_id=1, source_target_pairs={{12,13},{13,14},{14,15},{15,0},{0,1},{1,2},{2,3},{3,4},{28,29},{29... | collective-permute-start | bytes 786440 | tf_op jit(solution)/shard_map/ppermute | solution.py:298
  133.1 0.1 add_convert_fusion.2
  133.2 0.7 collective-permute-start.25
  133.9 1.8 %shard_map.97 = (f32[4,128,512]{2,1,0:T(8,128)S(1)}, bf16[128,1024]{1,0:T(8,128)(2,1)S(1)}, bf16[128,1024]{1,0:T(8,128)(2,1)S(1)}, bf16[128,1024]{1,0:T(8,128)(2,1)S(1)}, bf16[128,1024]{1,0:T(8,128)(2,1)S(1)}) custom-call(s32[3]{0:T(128)S(1)} %pad_add_fusion.scal, bf16[128,2048]{1,0:T(8,128)(2,1)S(1)} %copy-done, bf16[128,2048]{1,0:T(8,128)(2,1)S(1)} %copy-done.1, ...), custom_call_target="tpu_custom_call" | custom-call | flops 1000000000 | bytes 4194304 | tf_op jit(solution)/shard_map/pallas_call | solution.py:268
  135.6 5.1 %collective-permute-done.18 = bf16[128,1024]{1,0:T(8,128)(2,1)S(1)} collective-permute-done((bf16[128,1024]{1,0:T(8,128)(2,1)S(1)}, bf16[128,1024]{1,0:T(8,128)(2,1)S(1)}, u32[]{:S(2)}, u32[]{:S(2)}) %collective-permute-start.18) | collective-permute-done | bytes 262176 | tf_op jit(solution)/shard_map/ppermute | solution.py:298
  140.8 1.9 %collective-permute-start.19 = (bf16[128,1024]{1,0:T(8,128)(2,1)S(1)}, bf16[128,1024]{1,0:T(8,128)(2,1)S(1)}, u32[]{:S(2)}, u32[]{:S(2)}) collective-permute-start(bf16[128,1024]{1,0:T(8,128)(2,1)S(1)} %add_convert_fusion.7), channel_id=1, source_target_pairs={{13,14},{14,15},{15,0},{0,1},{1,2},{2,3},{3,4},{4,5},{29,30},{30,3... | collective-permute-start | bytes 786440 | tf_op jit(solution)/shard_map/ppermute | solution.py:298
  142.8 1.3 collective-permute-start.26
  144.1 7.9 %collective-permute-done.19 = bf16[128,1024]{1,0:T(8,128)(2,1)S(1)} collective-permute-done((bf16[128,1024]{1,0:T(8,128)(2,1)S(1)}, bf16[128,1024]{1,0:T(8,128)(2,1)S(1)}, u32[]{:S(2)}, u32[]{:S(2)}) %collective-permute-start.19) | collective-permute-done | bytes 262176 | tf_op jit(solution)/shard_map/ppermute | solution.py:298
  152.0 1.9 %collective-permute-start.20 = (bf16[128,1024]{1,0:T(8,128)(2,1)S(1)}, bf16[128,1024]{1,0:T(8,128)(2,1)S(1)}, u32[]{:S(2)}, u32[]{:S(2)}) collective-permute-start(bf16[128,1024]{1,0:T(8,128)(2,1)S(1)} %add_convert_fusion.6), channel_id=1, source_target_pairs={{14,0},{15,1},{0,2},{1,3},{2,4},{3,5},{4,6},{5,7},{30,16},{31,17},... | collective-permute-start | bytes 786440 | tf_op jit(solution)/shard_map/ppermute | solution.py:298
  154.0 0.1 add_convert_fusion
  154.1 4.0 %collective-permute-start.27 = (bf16[128,1024]{1,0:T(8,128)(2,1)S(1)}, bf16[128,1024]{1,0:T(8,128)(2,1)S(1)}, u32[]{:S(2)}, u32[]{:S(2)}) collective-permute-start(bf16[128,1024]{1,0:T(8,128)(2,1)S(1)} %add_convert_fusion), channel_id=1, source_target_pairs={{1,0},{2,1},{3,2},{4,3},{5,4},{6,5},{7,6},{8,7},{9,8},{10,9},{11,1... | collective-permute-start | bytes 786440 | tf_op jit(solution)/shard_map/ppermute | solution.py:298
  158.1 2.1 %shard_map.98 = (bf16[128,2048]{1,0:T(8,128)(2,1)}, f32[128,1024]{1,0:T(8,128)S(1)}) custom-call(s32[3]{0:T(128)S(1)} %pad_add_fusion.scal, bf16[128,2048]{1,0:T(8,128)(2,1)S(1)} %copy-done, bf16[128,2048]{1,0:T(8,128)(2,1)S(1)} %copy-done.1, f32[4,1,512]{2,1,0:T(1,128)S(1)} %get-tuple-element.101.log_ref, f32[4,1,512]{2,1,0:T(1,128)S(1)} %get-tuple-element.102.inner_ref, ...), custom_call_target="tpu_custom_call" | custom-call | flops 1000000000 | bytes 4194304 | tf_op jit(solution)/shard_map/pallas_call | solution.py:268
  160.2 5.0 %collective-permute-done.20 = bf16[128,1024]{1,0:T(8,128)(2,1)S(1)} collective-permute-done((bf16[128,1024]{1,0:T(8,128)(2,1)S(1)}, bf16[128,1024]{1,0:T(8,128)(2,1)S(1)}, u32[]{:S(2)}, u32[]{:S(2)}) %collective-permute-start.20) | collective-permute-done | bytes 262176 | tf_op jit(solution)/shard_map/ppermute | solution.py:298
  165.2 0.1 add_add_fusion
  165.3 0.8 fusion
  (34 shorter events, 0.7 us)
Async XLA Ops:
  0.6 28.9 %copy-start = (bf16[128,2048]{1,0:T(8,128)(2,1)S(1)}, bf16[128,2048]{1,0:T(8,128)(2,1)}, u32[]{:S(2)}) copy-start(bf16[128,2048]{1,0:T(8,128)(2,1)} %q_ref.27) | copy-start | bytes 1572868
  2.4 12.9 %copy-start.4 = (s32[2048]{0:T(1024)S(1)}, s32[2048]{0:T(1024)}, u32[]{:S(2)}) copy-start(s32[2048]{0:T(1024)} %param.9) | copy-start | bytes 24580
  2.4 18.6 %collective-permute-start = (bf16[128,1024]{1,0:T(8,128)(2,1)}, bf16[128,1024]{1,0:T(8,128)(2,1)S(1)}, u32[]{:S(2)}, u32[]{:S(2)}) collective-permute-start(bf16[128,1024]{1,0:T(8,128)(2,1)} %shard_map.84.own), channel_id=1, source_target_pairs={{0,14},{1,15},{2,0},{3,1},{4,2},{5,3},{6,4},{7,5},{16,30},{17,31},... | collective-permute-start | bytes 786440 | tf_op jit(solution)/shard_map/ppermute | solution.py:298
  13.4 14.8 %collective-permute-start.1 = (bf16[128,1024]{1,0:T(8,128)(2,1)}, bf16[128,1024]{1,0:T(8,128)(2,1)S(1)}, u32[]{:S(2)}, u32[]{:S(2)}) collective-permute-start(bf16[128,1024]{1,0:T(8,128)(2,1)} %shard_map.84.own), channel_id=1, source_target_pairs={{0,1},{1,2},{2,3},{3,4},{4,5},{5,6},{6,7},{7,8},{8,9},{9,10},{10,1... | collective-permute-start | bytes 786440 | tf_op jit(solution)/shard_map/ppermute | solution.py:298
  21.0 12.4 %collective-permute-start.2 = (bf16[128,1024]{1,0:T(8,128)(2,1)S(1)}, bf16[128,1024]{1,0:T(8,128)(2,1)S(1)}, u32[]{:S(2)}, u32[]{:S(2)}) collective-permute-start(bf16[128,1024]{1,0:T(8,128)(2,1)S(1)} %collective-permute-done.rest_0_.a1), channel_id=1, source_target_pairs={{14,13},{15,14},{0,15},{1,0},{2,1},{3,2},{4,3},{5,4},{30,29},{31,3... | collective-permute-start | bytes 786440 | tf_op jit(solution)/shard_map/ppermute | solution.py:298
  28.2 8.8 %collective-permute-start.3 = (bf16[128,1024]{1,0:T(8,128)(2,1)S(1)}, bf16[128,1024]{1,0:T(8,128)(2,1)S(1)}, u32[]{:S(2)}, u32[]{:S(2)}) collective-permute-start(bf16[128,1024]{1,0:T(8,128)(2,1)S(1)} %collective-permute-done.1.rest_1_.b1), channel_id=1, source_target_pairs={{1,2},{2,3},{3,4},{4,5},{5,6},{6,7},{7,8},{8,9},{9,10},{10,11},{11... | collective-permute-start | bytes 786440 | tf_op jit(solution)/shard_map/ppermute | solution.py:298
  29.6 1.0 copy-start.1
  30.6 0.9 copy-start.2
  33.4 8.9 %collective-permute-start.4 = (bf16[128,1024]{1,0:T(8,128)(2,1)S(1)}, bf16[128,1024]{1,0:T(8,128)(2,1)S(1)}, u32[]{:S(2)}, u32[]{:S(2)}) collective-permute-start(bf16[128,1024]{1,0:T(8,128)(2,1)S(1)} %collective-permute-done.2.rest_2_.a2), channel_id=1, source_target_pairs={{13,12},{14,13},{15,14},{0,15},{1,0},{2,1},{3,2},{4,3},{29,28},{30... | collective-permute-start | bytes 786440 | tf_op jit(solution)/shard_map/ppermute | solution.py:298
  37.0 9.8 %collective-permute-start.5 = (bf16[128,1024]{1,0:T(8,128)(2,1)S(1)}, bf16[128,1024]{1,0:T(8,128)(2,1)S(1)}, u32[]{:S(2)}, u32[]{:S(2)}) collective-permute-start(bf16[128,1024]{1,0:T(8,128)(2,1)S(1)} %collective-permute-done.3.rest_3_.b2), channel_id=1, source_target_pairs={{2,3},{3,4},{4,5},{5,6},{6,7},{7,8},{8,9},{9,10},{10,11},{11,12},{... | collective-permute-start | bytes 786440 | tf_op jit(solution)/shard_map/ppermute | solution.py:298
  42.3 8.3 %collective-permute-start.6 = (bf16[128,1024]{1,0:T(8,128)(2,1)S(1)}, bf16[128,1024]{1,0:T(8,128)(2,1)S(1)}, u32[]{:S(2)}, u32[]{:S(2)}) collective-permute-start(bf16[128,1024]{1,0:T(8,128)(2,1)S(1)} %collective-permute-done.4.rest_0_.a), channel_id=1, source_target_pairs={{12,11},{13,12},{14,13},{15,14},{0,15},{1,0},{2,1},{3,2},{28,27},{... | collective-permute-start | bytes 786440 | tf_op jit(solution)/shard_map/ppermute | solution.py:298
  46.8 9.5 %collective-permute-start.7 = (bf16[128,1024]{1,0:T(8,128)(2,1)S(1)}, bf16[128,1024]{1,0:T(8,128)(2,1)S(1)}, u32[]{:S(2)}, u32[]{:S(2)}) collective-permute-start(bf16[128,1024]{1,0:T(8,128)(2,1)S(1)} %collective-permute-done.5.rest_1_.b), channel_id=1, source_target_pairs={{3,4},{4,5},{5,6},{6,7},{7,8},{8,9},{9,10},{10,11},{11,12},{12,13}... | collective-permute-start | bytes 786440 | tf_op jit(solution)/shard_map/ppermute | solution.py:298
  50.7 9.5 %collective-permute-start.8 = (bf16[128,1024]{1,0:T(8,128)(2,1)S(1)}, bf16[128,1024]{1,0:T(8,128)(2,1)S(1)}, u32[]{:S(2)}, u32[]{:S(2)}) collective-permute-start(bf16[128,1024]{1,0:T(8,128)(2,1)S(1)} %collective-permute-done.6.rest_0_.a), channel_id=1, source_target_pairs={{11,10},{12,11},{13,12},{14,13},{15,14},{0,15},{1,0},{2,1},{27,26}... | collective-permute-start | bytes 786440 | tf_op jit(solution)/shard_map/ppermute | solution.py:298
  56.3 9.5 %collective-permute-start.9 = (bf16[128,1024]{1,0:T(8,128)(2,1)S(1)}, bf16[128,1024]{1,0:T(8,128)(2,1)S(1)}, u32[]{:S(2)}, u32[]{:S(2)}) collective-permute-start(bf16[128,1024]{1,0:T(8,128)(2,1)S(1)} %collective-permute-done.7.rest_1_.b), channel_id=1, source_target_pairs={{4,5},{5,6},{6,7},{7,8},{8,9},{9,10},{10,11},{11,12},{12,13},{13,1... | collective-permute-start | bytes 786440 | tf_op jit(solution)/shard_map/ppermute | solution.py:298
  60.1 9.5 %collective-permute-start.10 = (bf16[128,1024]{1,0:T(8,128)(2,1)S(1)}, bf16[128,1024]{1,0:T(8,128)(2,1)S(1)}, u32[]{:S(2)}, u32[]{:S(2)}) collective-permute-start(bf16[128,1024]{1,0:T(8,128)(2,1)S(1)} %collective-permute-done.8.rest_0_.a), channel_id=1, source_target_pairs={{10,9},{11,10},{12,11},{13,12},{14,13},{15,14},{0,15},{1,0},{26,25... | collective-permute-start | bytes 786440 | tf_op jit(solution)/shard_map/ppermute | solution.py:298
  65.8 4.5 %collective-permute-start.11 = (bf16[128,1024]{1,0:T(8,128)(2,1)S(1)}, bf16[128,1024]{1,0:T(8,128)(2,1)S(1)}, u32[]{:S(2)}, u32[]{:S(2)}) collective-permute-start(bf16[128,1024]{1,0:T(8,128)(2,1)S(1)} %collective-permute-done.9.rest_1_.b), channel_id=1, source_target_pairs={{5,6},{6,7},{7,8},{8,9},{9,10},{10,11},{11,12},{12,13},{13,14},{14... | collective-permute-start | bytes 786440 | tf_op jit(solution)/shard_map/ppermute | solution.py:298
  69.6 2.0 %collective-permute-start.12 = (bf16[128,1024]{1,0:T(8,128)(2,1)S(1)}, bf16[128,1024]{1,0:T(8,128)(2,1)S(1)}, u32[]{:S(2)}, u32[]{:S(2)}) collective-permute-start(bf16[128,1024]{1,0:T(8,128)(2,1)S(1)} %collective-permute-done.10.rest_0_.a), channel_id=1, source_target_pairs={{9,8},{10,9},{11,10},{12,11},{13,12},{14,13},{15,14},{0,15},{25,24... | collective-permute-start | bytes 786440 | tf_op jit(solution)/shard_map/ppermute | solution.py:298
  70.3 1.9 %collective-permute-start.13 = (bf16[128,1024]{1,0:T(8,128)(2,1)S(1)}, bf16[128,1024]{1,0:T(8,128)(2,1)S(1)}, u32[]{:S(2)}, u32[]{:S(2)}) collective-permute-start(bf16[128,1024]{1,0:T(8,128)(2,1)S(1)} %collective-permute-done.11.rest_1_.b), channel_id=1, source_target_pairs={{6,7},{7,8},{8,9},{9,10},{10,11},{11,12},{12,13},{13,14},{14,15},{... | collective-permute-start | bytes 786440 | tf_op jit(solution)/shard_map/ppermute | solution.py:298
  73.3 3.0 %collective-permute-start.14 = (bf16[128,1024]{1,0:T(8,128)(2,1)S(1)}, bf16[128,1024]{1,0:T(8,128)(2,1)S(1)}, u32[]{:S(2)}, u32[]{:S(2)}) collective-permute-start(bf16[128,1024]{1,0:T(8,128)(2,1)S(1)} %get-tuple-element.121), channel_id=1, source_target_pairs={{8,9},{9,10},{10,11},{11,12},{12,13},{13,14},{14,15},{15,0},{24,25... | collective-permute-start | bytes 786440 | tf_op jit(solution)/shard_map/ppermute | solution.py:298
  74.0 3.7 %collective-permute-start.21 = (bf16[128,1024]{1,0:T(8,128)(2,1)S(1)}, bf16[128,1024]{1,0:T(8,128)(2,1)S(1)}, u32[]{:S(2)}, u32[]{:S(2)}) collective-permute-start(bf16[128,1024]{1,0:T(8,128)(2,1)S(1)} %get-tuple-element.132), channel_id=1, source_target_pairs={{7,6},{8,7},{9,8},{10,9},{11,10},{12,11},{13,12},{14,13},{15,14},{... | collective-permute-start | bytes 786440 | tf_op jit(solution)/shard_map/ppermute | solution.py:298
  76.4 32.4 %collective-permute-start.15 = (bf16[128,1024]{1,0:T(8,128)(2,1)S(1)}, bf16[128,1024]{1,0:T(8,128)(2,1)S(1)}, u32[]{:S(2)}, u32[]{:S(2)}) collective-permute-start(bf16[128,1024]{1,0:T(8,128)(2,1)S(1)} %add_convert_fusion.11), channel_id=1, source_target_pairs={{9,10},{10,11},{11,12},{12,13},{13,14},{14,15},{15,0},{0,1},{25,26... | collective-permute-start | bytes 786440 | tf_op jit(solution)/shard_map/ppermute | solution.py:298
  77.8 33.0 %collective-permute-start.22 = (bf16[128,1024]{1,0:T(8,128)(2,1)S(1)}, bf16[128,1024]{1,0:T(8,128)(2,1)S(1)}, u32[]{:S(2)}, u32[]{:S(2)}) collective-permute-start(bf16[128,1024]{1,0:T(8,128)(2,1)S(1)} %add_convert_fusion.5), channel_id=1, source_target_pairs={{6,5},{7,6},{8,7},{9,8},{10,9},{11,10},{12,11},{13,12},{14,13},{15... | collective-permute-start | bytes 786440 | tf_op jit(solution)/shard_map/ppermute | solution.py:298
  108.9 11.7 %collective-permute-start.16 = (bf16[128,1024]{1,0:T(8,128)(2,1)S(1)}, bf16[128,1024]{1,0:T(8,128)(2,1)S(1)}, u32[]{:S(2)}, u32[]{:S(2)}) collective-permute-start(bf16[128,1024]{1,0:T(8,128)(2,1)S(1)} %add_convert_fusion.10), channel_id=1, source_target_pairs={{10,11},{11,12},{12,13},{13,14},{14,15},{15,0},{0,1},{1,2},{26,27}... | collective-permute-start | bytes 786440 | tf_op jit(solution)/shard_map/ppermute | solution.py:298
  110.9 11.6 %collective-permute-start.23 = (bf16[128,1024]{1,0:T(8,128)(2,1)S(1)}, bf16[128,1024]{1,0:T(8,128)(2,1)S(1)}, u32[]{:S(2)}, u32[]{:S(2)}) collective-permute-start(bf16[128,1024]{1,0:T(8,128)(2,1)S(1)} %add_convert_fusion.4), channel_id=1, source_target_pairs={{5,4},{6,5},{7,6},{8,7},{9,8},{10,9},{11,10},{12,11},{13,12},{14,1... | collective-permute-start | bytes 786440 | tf_op jit(solution)/shard_map/ppermute | solution.py:298
  120.6 10.5 %collective-permute-start.17 = (bf16[128,1024]{1,0:T(8,128)(2,1)S(1)}, bf16[128,1024]{1,0:T(8,128)(2,1)S(1)}, u32[]{:S(2)}, u32[]{:S(2)}) collective-permute-start(bf16[128,1024]{1,0:T(8,128)(2,1)S(1)} %add_convert_fusion.9), channel_id=1, source_target_pairs={{11,12},{12,13},{13,14},{14,15},{15,0},{0,1},{1,2},{2,3},{27,28},{... | collective-permute-start | bytes 786440 | tf_op jit(solution)/shard_map/ppermute | solution.py:298
  122.7 10.5 %collective-permute-start.24 = (bf16[128,1024]{1,0:T(8,128)(2,1)S(1)}, bf16[128,1024]{1,0:T(8,128)(2,1)S(1)}, u32[]{:S(2)}, u32[]{:S(2)}) collective-permute-start(bf16[128,1024]{1,0:T(8,128)(2,1)S(1)} %add_convert_fusion.3), channel_id=1, source_target_pairs={{4,3},{5,4},{6,5},{7,6},{8,7},{9,8},{10,9},{11,10},{12,11},{13,12}... | collective-permute-start | bytes 786440 | tf_op jit(solution)/shard_map/ppermute | solution.py:298
  131.2 9.5 %collective-permute-start.18 = (bf16[128,1024]{1,0:T(8,128)(2,1)S(1)}, bf16[128,1024]{1,0:T(8,128)(2,1)S(1)}, u32[]{:S(2)}, u32[]{:S(2)}) collective-permute-start(bf16[128,1024]{1,0:T(8,128)(2,1)S(1)} %add_convert_fusion.8), channel_id=1, source_target_pairs={{12,13},{13,14},{14,15},{15,0},{0,1},{1,2},{2,3},{3,4},{28,29},{29... | collective-permute-start | bytes 786440 | tf_op jit(solution)/shard_map/ppermute | solution.py:298
  133.2 9.5 %collective-permute-start.25 = (bf16[128,1024]{1,0:T(8,128)(2,1)S(1)}, bf16[128,1024]{1,0:T(8,128)(2,1)S(1)}, u32[]{:S(2)}, u32[]{:S(2)}) collective-permute-start(bf16[128,1024]{1,0:T(8,128)(2,1)S(1)} %add_convert_fusion.2), channel_id=1, source_target_pairs={{3,2},{4,3},{5,4},{6,5},{7,6},{8,7},{9,8},{10,9},{11,10},{12,11},{... | collective-permute-start | bytes 786440 | tf_op jit(solution)/shard_map/ppermute | solution.py:298
  140.8 11.2 %collective-permute-start.19 = (bf16[128,1024]{1,0:T(8,128)(2,1)S(1)}, bf16[128,1024]{1,0:T(8,128)(2,1)S(1)}, u32[]{:S(2)}, u32[]{:S(2)}) collective-permute-start(bf16[128,1024]{1,0:T(8,128)(2,1)S(1)} %add_convert_fusion.7), channel_id=1, source_target_pairs={{13,14},{14,15},{15,0},{0,1},{1,2},{2,3},{3,4},{4,5},{29,30},{30,3... | collective-permute-start | bytes 786440 | tf_op jit(solution)/shard_map/ppermute | solution.py:298
  142.8 11.2 %collective-permute-start.26 = (bf16[128,1024]{1,0:T(8,128)(2,1)S(1)}, bf16[128,1024]{1,0:T(8,128)(2,1)S(1)}, u32[]{:S(2)}, u32[]{:S(2)}) collective-permute-start(bf16[128,1024]{1,0:T(8,128)(2,1)S(1)} %add_convert_fusion.1), channel_id=1, source_target_pairs={{2,1},{3,2},{4,3},{5,4},{6,5},{7,6},{8,7},{9,8},{10,9},{11,10},{12... | collective-permute-start | bytes 786440 | tf_op jit(solution)/shard_map/ppermute | solution.py:298
  152.0 13.2 %collective-permute-start.20 = (bf16[128,1024]{1,0:T(8,128)(2,1)S(1)}, bf16[128,1024]{1,0:T(8,128)(2,1)S(1)}, u32[]{:S(2)}, u32[]{:S(2)}) collective-permute-start(bf16[128,1024]{1,0:T(8,128)(2,1)S(1)} %add_convert_fusion.6), channel_id=1, source_target_pairs={{14,0},{15,1},{0,2},{1,3},{2,4},{3,5},{4,6},{5,7},{30,16},{31,17},... | collective-permute-start | bytes 786440 | tf_op jit(solution)/shard_map/ppermute | solution.py:298
  154.0 4.1 %copy-start.3 = (bf16[128,1024]{1,0:T(8,128)(2,1)S(1)}, bf16[128,1024]{1,0:T(8,128)(2,1)}, u32[]{:S(2)}) copy-start(bf16[128,1024]{1,0:T(8,128)(2,1)} %shard_map.84.own) | copy-start | bytes 786436
  154.1 11.2 %collective-permute-start.27 = (bf16[128,1024]{1,0:T(8,128)(2,1)S(1)}, bf16[128,1024]{1,0:T(8,128)(2,1)S(1)}, u32[]{:S(2)}, u32[]{:S(2)}) collective-permute-start(bf16[128,1024]{1,0:T(8,128)(2,1)S(1)} %add_convert_fusion), channel_id=1, source_target_pairs={{1,0},{2,1},{3,2},{4,3},{5,4},{6,5},{7,6},{8,7},{9,8},{10,9},{11,1... | collective-permute-start | bytes 786440 | tf_op jit(solution)/shard_map/ppermute | solution.py:298

commit v8 on v7

--- a/solution.py
+++ b/solution.py
@@ -126,15 +126,9 @@
         return jnp.where(self.even, self.a[at], self.b[at])
 
 
-def pack_kernel(k_ref, v_ref, out_ref, sems):
-    copies = [
-        pltpu.make_async_copy(k_ref, out_ref.at[:, pl.ds(0, WIDE)], sems.at[0]),
-        pltpu.make_async_copy(v_ref, out_ref.at[:, pl.ds(WIDE, WIDE)], sems.at[1]),
-    ]
-    for copy in copies:
-        copy.start()
-    for copy in copies:
-        copy.wait()
+def pack_kernel(k_ref, v_ref, out_ref):
+    out_ref[:, :WIDE] = k_ref[...]
+    out_ref[:, WIDE:] = v_ref[...]
 
 
 def own_forward_kernel(scal, first_ref, q_ref, g_ref, own, top, total, acc, e, gp, turned):
@@ -283,9 +277,8 @@
     return pl.pallas_call(
         pack_kernel,
         out_shape=jax.ShapeDtypeStruct((rows, 2 * WIDE), keys.dtype),
-        in_specs=[pl.BlockSpec(memory_space=pltpu.HBM)] * 2,
+        in_specs=[pl.BlockSpec(memory_space=pltpu.VMEM)] * 2,
         out_specs=pl.BlockSpec(memory_space=pltpu.VMEM),
-        scratch_shapes=[pltpu.SemaphoreType.DMA((2,))],
     )(keys, values)
 
 
@@ -315,7 +308,7 @@
 
 
 def add_low(a, b):
-    return (a.astype(jnp.float32) + b.astype(jnp.float32)).astype(jnp.bfloat16)
+    return a + b
 
 
 def local(queries, keys, values, out_grad, segment_ids):
@@ -351,8 +344,8 @@
     for step in range(1, STEPS + 1):
         pairs = gather_pairs(step, count)
         to_a = a[-1]
-        if step >= 3:
-            to_a, _ = lax.optimization_barrier((to_a, tops[step - 2]))
+        if step == 2 or step >= 4:
+            to_a, _ = lax.optimization_barrier((to_a, tops[max(step - 2, 1)]))
         a.append(both_ways(to_a, *pairs, 0))
         b.append(both_ways(b[-1], *pairs, 1))
         if step == 2:

time: 167 us -> 167 us (level)
  the two profiles are of different devices: /device:TPU:60 before, /device:TPU:38 now
where the time goes in v8:
time: 167 us; the launch traced here: 166 us
  waiting for transfers between devices  78.2 us (47%)
  starting transfers between devices  64.8 us (39%)
  Pallas kernels  17.4 us (10%)
  local copies, waits for them, and re-layouts  2.91 us (2%)
    ppermute x28, waiting for transfers between devices, both_ways(): return lax.ppermute(x, ('dp', 'ctx'), pairs)  78.2 us
    ppermute x28, starting transfers between devices, both_ways(): return lax.ppermute(x, ('dp', 'ctx'), pairs)  64.8 us
    pallas_call x14, Pallas kernels, call(): pl.pallas_call(kernel, out_shape=outs, in_specs=[pl.BlockSpec(memory_spac...  15.7 us
  transfers between devices with their start and end apart: 28, of which 12 were waited for; matrix products, arithmetic and copies ran while one was open for 1% of the time, Pallas kernels for 9%

profile of v8, /device:TPU:38, one launch (start us, length us, event | category | flops | bytes accessed | tf_op | source)
XLA Modules:
  0.0 165.9 jit_solution(12859079586078090647)
XLA Ops:
  0.6 1.7 %shard_map.84.own = bf16[128,1024]{1,0:T(8,128)(2,1)} custom-call(bf16[128,512]{1,0:T(8,128)(2,1)} %k_ref.1, bf16[128,512]{1,0:T(8,128)(2,1)} %v_ref.1), custom_call_target="tpu_custom_call" | custom-call | tf_op jit(solution)/shard_map/pallas_call | solution.py:277
  2.4 3.9 %collective-permute-start.1 = (bf16[128,1024]{1,0:T(8,128)(2,1)}, bf16[128,1024]{1,0:T(8,128)(2,1)S(1)}, u32[]{:S(2)}, u32[]{:S(2)}) collective-permute-start(bf16[128,1024]{1,0:T(8,128)(2,1)} %shard_map.84.own), channel_id=1, source_target_pairs={{0,1},{1,2},{2,3},{3,4},{4,5},{5,6},{6,7},{7,8},{8,9},{9,10},{10,1... | collective-permute-start | bytes 786440 | tf_op jit(solution)/shard_map/ppermute | solution.py:291
  6.3 8.4 %collective-permute-start = (bf16[128,1024]{1,0:T(8,128)(2,1)}, bf16[128,1024]{1,0:T(8,128)(2,1)S(1)}, u32[]{:S(2)}, u32[]{:S(2)}) collective-permute-start(bf16[128,1024]{1,0:T(8,128)(2,1)} %shard_map.84.own), channel_id=1, source_target_pairs={{0,14},{1,15},{2,0},{3,1},{4,2},{5,3},{6,4},{7,5},{16,30},{17,31},... | collective-permute-start | bytes 786440 | tf_op jit(solution)/shard_map/ppermute | solution.py:291
  14.8 0.1 dynamic_slice.3
  14.9 0.4 convert_reduce_fusion
  15.3 0.1 pad_add_fusion.scal
  15.4 1.0 copy-done.1
  16.4 0.9 copy-done.2
  17.4 1.8 %shard_map.85 = (f32[4,1,512]{2,1,0:T(1,128)S(1)}, f32[4,1,512]{2,1,0:T(1,128)S(1)}, f32[4,128,512]{2,1,0:T(8,128)S(1)}, bf16[4,128,512]{2,1,0:T(8,128)(2,1)S(1)...) custom-call(s32[3]{0:T(128)S(1)} %pad_add_fusion.scal, s32[1,128]{1,0:T(1,128)S(1)} %bitcast.6, ...), custom_call_target="tpu_custom_call" | custom-call | flops 1000000000 | bytes 4194304 | tf_op jit(solution)/shard_map/pallas_call | solution.py:262
  19.2 4.5 %collective-permute-done.rest_0_.a1 = bf16[128,1024]{1,0:T(8,128)(2,1)S(1)} collective-permute-done((bf16[128,1024]{1,0:T(8,128)(2,1)}, bf16[128,1024]{1,0:T(8,128)(2,1)S(1)}, u32[]{:S(2)}, u32[]{:S(2)}) %collective-permute-start) | collective-permute-done | bytes 262176 | tf_op jit(solution)/shard_map/ppermute | solution.py:291
  23.7 6.8 %collective-permute-start.2 = (bf16[128,1024]{1,0:T(8,128)(2,1)S(1)}, bf16[128,1024]{1,0:T(8,128)(2,1)S(1)}, u32[]{:S(2)}, u32[]{:S(2)}) collective-permute-start(bf16[128,1024]{1,0:T(8,128)(2,1)S(1)} %collective-permute-done.rest_0_.a1), channel_id=1, source_target_pairs={{14,13},{15,14},{0,15},{1,0},{2,1},{3,2},{4,3},{5,4},{30,29},{31,3... | collective-permute-start | bytes 786440 | tf_op jit(solution)/shard_map/ppermute | solution.py:291
  30.4 1.3 collective-permute-start.3
  31.7 3.4 %collective-permute-done.2.rest_2_.a2 = bf16[128,1024]{1,0:T(8,128)(2,1)S(1)} collective-permute-done((bf16[128,1024]{1,0:T(8,128)(2,1)S(1)}, bf16[128,1024]{1,0:T(8,128)(2,1)S(1)}, u32[]{:S(2)}, u32[]{:S(2)}) %collective-permute-start.2) | collective-permute-done | bytes 262176 | tf_op jit(solution)/shard_map/ppermute | solution.py:291
  35.1 4.4 %collective-permute-start.4 = (bf16[128,1024]{1,0:T(8,128)(2,1)S(1)}, bf16[128,1024]{1,0:T(8,128)(2,1)S(1)}, u32[]{:S(2)}, u32[]{:S(2)}) collective-permute-start(bf16[128,1024]{1,0:T(8,128)(2,1)S(1)} %collective-permute-done.2.rest_2_.a2), channel_id=1, source_target_pairs={{13,12},{14,13},{15,14},{0,15},{1,0},{2,1},{3,2},{4,3},{29,28},{30... | collective-permute-start | bytes 786440 | tf_op jit(solution)/shard_map/ppermute | solution.py:291
  39.5 0.7 collective-permute-start.5
  40.2 2.3 %shard_map.86 = (f32[4,1,512]{2,1,0:T(1,128)S(1)}, f32[4,1,512]{2,1,0:T(1,128)S(1)}, f32[4,128,512]{2,1,0:T(8,128)S(1)}, bf16[4,256,512]{2,1,0:T(8,128)(2,1)S(1)}, bf16[4,256,512]{2,1,0:T(8,128)(2,1)S(1)}) custom-call(s32[3]{0:T(128)S(1)} %pad_add_fusion.scal, s32[1,128]{1,0:T(1,128)S(1)} %bitcast.7, bf16[128,2048]{1,0:T(8,128)(2,1)S(1)} %copy-done, ...), custom_call_target="tpu_custom_call" | custom-call | flops 1000000000 | bytes 4194304 | tf_op jit(solution)/shard_map/pallas_call | solution.py:262
  42.5 0.9 collective-permute-done.4.rest_0_.a
  43.4 4.5 %collective-permute-start.6 = (bf16[128,1024]{1,0:T(8,128)(2,1)S(1)}, bf16[128,1024]{1,0:T(8,128)(2,1)S(1)}, u32[]{:S(2)}, u32[]{:S(2)}) collective-permute-start(bf16[128,1024]{1,0:T(8,128)(2,1)S(1)} %collective-permute-done.4.rest_0_.a), channel_id=1, source_target_pairs={{12,11},{13,12},{14,13},{15,14},{0,15},{1,0},{2,1},{3,2},{28,27},{... | collective-permute-start | bytes 786440 | tf_op jit(solution)/shard_map/ppermute | solution.py:291
  47.8 0.7 collective-permute-start.7
  48.5 0.6 shard_map.87
  49.1 2.5 %collective-permute-done.6.rest_0_.a = bf16[128,1024]{1,0:T(8,128)(2,1)S(1)} collective-permute-done((bf16[128,1024]{1,0:T(8,128)(2,1)S(1)}, bf16[128,1024]{1,0:T(8,128)(2,1)S(1)}, u32[]{:S(2)}, u32[]{:S(2)}) %collective-permute-start.6) | collective-permute-done | bytes 262176 | tf_op jit(solution)/shard_map/ppermute | solution.py:291
  51.7 5.6 %collective-permute-start.8 = (bf16[128,1024]{1,0:T(8,128)(2,1)S(1)}, bf16[128,1024]{1,0:T(8,128)(2,1)S(1)}, u32[]{:S(2)}, u32[]{:S(2)}) collective-permute-start(bf16[128,1024]{1,0:T(8,128)(2,1)S(1)} %collective-permute-done.6.rest_0_.a), channel_id=1, source_target_pairs={{11,10},{12,11},{13,12},{14,13},{15,14},{0,15},{1,0},{2,1},{27,26}... | collective-permute-start | bytes 786440 | tf_op jit(solution)/shard_map/ppermute | solution.py:291
  57.3 0.7 collective-permute-start.9
  58.0 0.6 shard_map.88
  58.6 2.5 %collective-permute-done.8.rest_0_.a = bf16[128,1024]{1,0:T(8,128)(2,1)S(1)} collective-permute-done((bf16[128,1024]{1,0:T(8,128)(2,1)S(1)}, bf16[128,1024]{1,0:T(8,128)(2,1)S(1)}, u32[]{:S(2)}, u32[]{:S(2)}) %collective-permute-start.8) | collective-permute-done | bytes 262176 | tf_op jit(solution)/shard_map/ppermute | solution.py:291
  61.2 5.6 %collective-permute-start.10 = (bf16[128,1024]{1,0:T(8,128)(2,1)S(1)}, bf16[128,1024]{1,0:T(8,128)(2,1)S(1)}, u32[]{:S(2)}, u32[]{:S(2)}) collective-permute-start(bf16[128,1024]{1,0:T(8,128)(2,1)S(1)} %collective-permute-done.8.rest_0_.a), channel_id=1, source_target_pairs={{10,9},{11,10},{12,11},{13,12},{14,13},{15,14},{0,15},{1,0},{26,25... | collective-permute-start | bytes 786440 | tf_op jit(solution)/shard_map/ppermute | solution.py:291
  66.8 0.7 collective-permute-start.11
  67.5 0.6 shard_map.89
  68.1 2.5 %collective-permute-done.10.rest_0_.a = bf16[128,1024]{1,0:T(8,128)(2,1)S(1)} collective-permute-done((bf16[128,1024]{1,0:T(8,128)(2,1)S(1)}, bf16[128,1024]{1,0:T(8,128)(2,1)S(1)}, u32[]{:S(2)}, u32[]{:S(2)}) %collective-permute-start.10) | collective-permute-done | bytes 262176 | tf_op jit(solution)/shard_map/ppermute | solution.py:291
  70.6 0.7 collective-permute-start.12
  71.3 0.7 collective-permute-start.13
  72.0 0.6 shard_map.90
  72.6 0.6 shard_map.91
  73.3 1.1 shard_map.92
  74.4 0.7 collective-permute-start.14
  75.1 0.7 collective-permute-start.21
  75.8 1.6 shard_map.93
  77.5 1.3 collective-permute-start.15
  78.9 0.7 collective-permute-start.22
  79.5 0.7 shard_map.94
  80.2 31.0 %collective-permute-done.15 = bf16[128,1024]{1,0:T(8,128)(2,1)S(1)} collective-permute-done((bf16[128,1024]{1,0:T(8,128)(2,1)S(1)}, bf16[128,1024]{1,0:T(8,128)(2,1)S(1)}, u32[]{:S(2)}, u32[]{:S(2)}) %collective-permute-start.15) | collective-permute-done | bytes 262176 | tf_op jit(solution)/shard_map/ppermute | solution.py:291
  111.3 1.9 %collective-permute-start.16 = (bf16[128,1024]{1,0:T(8,128)(2,1)S(1)}, bf16[128,1024]{1,0:T(8,128)(2,1)S(1)}, u32[]{:S(2)}, u32[]{:S(2)}) collective-permute-start(bf16[128,1024]{1,0:T(8,128)(2,1)S(1)} %add.52), channel_id=1, source_target_pairs={{10,11},{11,12},{12,13},{13,14},{14,15},{15,0},{0,1},{1,2},{26,27}... | collective-permute-start | bytes 786440 | tf_op jit(solution)/shard_map/ppermute | solution.py:291
  113.3 0.7 collective-permute-start.23
  114.0 0.7 shard_map.95
  114.6 7.2 %collective-permute-done.16 = bf16[128,1024]{1,0:T(8,128)(2,1)S(1)} collective-permute-done((bf16[128,1024]{1,0:T(8,128)(2,1)S(1)}, bf16[128,1024]{1,0:T(8,128)(2,1)S(1)}, u32[]{:S(2)}, u32[]{:S(2)}) %collective-permute-start.16) | collective-permute-done | bytes 262176 | tf_op jit(solution)/shard_map/ppermute | solution.py:291
  121.9 1.9 %collective-permute-start.17 = (bf16[128,1024]{1,0:T(8,128)(2,1)S(1)}, bf16[128,1024]{1,0:T(8,128)(2,1)S(1)}, u32[]{:S(2)}, u32[]{:S(2)}) collective-permute-start(bf16[128,1024]{1,0:T(8,128)(2,1)S(1)} %add.53), channel_id=1, source_target_pairs={{11,12},{12,13},{13,14},{14,15},{15,0},{0,1},{1,2},{2,3},{27,28},{... | collective-permute-start | bytes 786440 | tf_op jit(solution)/shard_map/ppermute | solution.py:291
  123.9 0.1 add.59
  124.0 0.7 collective-permute-start.24
  124.6 0.7 shard_map.96
  125.3 6.3 %collective-permute-done.17 = bf16[128,1024]{1,0:T(8,128)(2,1)S(1)} collective-permute-done((bf16[128,1024]{1,0:T(8,128)(2,1)S(1)}, bf16[128,1024]{1,0:T(8,128)(2,1)S(1)}, u32[]{:S(2)}, u32[]{:S(2)}) %collective-permute-start.17) | collective-permute-done | bytes 262176 | tf_op jit(solution)/shard_map/ppermute | solution.py:291
  131.7 1.9 %collective-permute-start.18 = (bf16[128,1024]{1,0:T(8,128)(2,1)S(1)}, bf16[128,1024]{1,0:T(8,128)(2,1)S(1)}, u32[]{:S(2)}, u32[]{:S(2)}) collective-permute-start(bf16[128,1024]{1,0:T(8,128)(2,1)S(1)} %add.54), channel_id=1, source_target_pairs={{12,13},{13,14},{14,15},{15,0},{0,1},{1,2},{2,3},{3,4},{28,29},{29... | collective-permute-start | bytes 786440 | tf_op jit(solution)/shard_map/ppermute | solution.py:291
  133.6 0.1 add.60
  133.7 0.7 collective-permute-start.25
  134.4 1.8 %shard_map.97 = (f32[4,128,512]{2,1,0:T(8,128)S(1)}, bf16[128,1024]{1,0:T(8,128)(2,1)S(1)}, bf16[128,1024]{1,0:T(8,128)(2,1)S(1)}, bf16[128,1024]{1,0:T(8,128)(2,1)S(1)}, bf16[128,1024]{1,0:T(8,128)(2,1)S(1)}) custom-call(s32[3]{0:T(128)S(1)} %pad_add_fusion.scal, bf16[128,2048]{1,0:T(8,128)(2,1)S(1)} %copy-done, bf16[128,2048]{1,0:T(8,128)(2,1)S(1)} %copy-done.1, ...), custom_call_target="tpu_custom_call" | custom-call | flops 1000000000 | bytes 4194304 | tf_op jit(solution)/shard_map/pallas_call | solution.py:262
  136.2 4.7 %collective-permute-done.18 = bf16[128,1024]{1,0:T(8,128)(2,1)S(1)} collective-permute-done((bf16[128,1024]{1,0:T(8,128)(2,1)S(1)}, bf16[128,1024]{1,0:T(8,128)(2,1)S(1)}, u32[]{:S(2)}, u32[]{:S(2)}) %collective-permute-start.18) | collective-permute-done | bytes 262176 | tf_op jit(solution)/shard_map/ppermute | solution.py:291
  141.0 1.9 %collective-permute-start.19 = (bf16[128,1024]{1,0:T(8,128)(2,1)S(1)}, bf16[128,1024]{1,0:T(8,128)(2,1)S(1)}, u32[]{:S(2)}, u32[]{:S(2)}) collective-permute-start(bf16[128,1024]{1,0:T(8,128)(2,1)S(1)} %add.55), channel_id=1, source_target_pairs={{13,14},{14,15},{15,0},{0,1},{1,2},{2,3},{3,4},{4,5},{29,30},{30,3... | collective-permute-start | bytes 786440 | tf_op jit(solution)/shard_map/ppermute | solution.py:291
  143.0 1.3 collective-permute-start.26
  144.3 7.4 %collective-permute-done.19 = bf16[128,1024]{1,0:T(8,128)(2,1)S(1)} collective-permute-done((bf16[128,1024]{1,0:T(8,128)(2,1)S(1)}, bf16[128,1024]{1,0:T(8,128)(2,1)S(1)}, u32[]{:S(2)}, u32[]{:S(2)}) %collective-permute-start.19) | collective-permute-done | bytes 262176 | tf_op jit(solution)/shard_map/ppermute | solution.py:291
  151.8 1.9 %collective-permute-start.20 = (bf16[128,1024]{1,0:T(8,128)(2,1)S(1)}, bf16[128,1024]{1,0:T(8,128)(2,1)S(1)}, u32[]{:S(2)}, u32[]{:S(2)}) collective-permute-start(bf16[128,1024]{1,0:T(8,128)(2,1)S(1)} %add.56), channel_id=1, source_target_pairs={{14,0},{15,1},{0,2},{1,3},{2,4},{3,5},{4,6},{5,7},{30,16},{31,17},... | collective-permute-start | bytes 786440 | tf_op jit(solution)/shard_map/ppermute | solution.py:291
  153.8 4.0 %collective-permute-start.27 = (bf16[128,1024]{1,0:T(8,128)(2,1)S(1)}, bf16[128,1024]{1,0:T(8,128)(2,1)S(1)}, u32[]{:S(2)}, u32[]{:S(2)}) collective-permute-start(bf16[128,1024]{1,0:T(8,128)(2,1)S(1)} %add.62), channel_id=1, source_target_pairs={{1,0},{2,1},{3,2},{4,3},{5,4},{6,5},{7,6},{8,7},{9,8},{10,9},{11,1... | collective-permute-start | bytes 786440 | tf_op jit(solution)/shard_map/ppermute | solution.py:291
  157.8 2.1 %shard_map.98 = (bf16[128,2048]{1,0:T(8,128)(2,1)}, f32[128,1024]{1,0:T(8,128)S(1)}) custom-call(s32[3]{0:T(128)S(1)} %pad_add_fusion.scal, bf16[128,2048]{1,0:T(8,128)(2,1)S(1)} %copy-done, bf16[128,2048]{1,0:T(8,128)(2,1)S(1)} %copy-done.1, f32[4,1,512]{2,1,0:T(1,128)S(1)} %get-tuple-element.101.log_ref, f32[4,1,512]{2,1,0:T(1,128)S(1)} %get-tuple-element.102.inner_ref, ...), custom_call_target="tpu_custom_call" | custom-call | flops 1000000000 | bytes 4194304 | tf_op jit(solution)/shard_map/pallas_call | solution.py:262
  159.9 5.0 %collective-permute-done.20 = bf16[128,1024]{1,0:T(8,128)(2,1)S(1)} collective-permute-done((bf16[128,1024]{1,0:T(8,128)(2,1)S(1)}, bf16[128,1024]{1,0:T(8,128)(2,1)S(1)}, u32[]{:S(2)}, u32[]{:S(2)}) %collective-permute-start.20) | collective-permute-done | bytes 262176 | tf_op jit(solution)/shard_map/ppermute | solution.py:291
  165.0 0.1 add_add_fusion
  165.0 0.8 fusion
  (34 shorter events, 0.7 us)
Async XLA Ops:
  0.6 14.7 %copy-start = (bf16[128,2048]{1,0:T(8,128)(2,1)S(1)}, bf16[128,2048]{1,0:T(8,128)(2,1)}, u32[]{:S(2)}) copy-start(bf16[128,2048]{1,0:T(8,128)(2,1)} %q_ref.27) | copy-start | bytes 1572868
  2.4 12.4 %copy-start.4 = (s32[2048]{0:T(1024)S(1)}, s32[2048]{0:T(1024)}, u32[]{:S(2)}) copy-start(s32[2048]{0:T(1024)} %param.9) | copy-start | bytes 24580
  2.4 28.0 %collective-permute-start.1 = (bf16[128,1024]{1,0:T(8,128)(2,1)}, bf16[128,1024]{1,0:T(8,128)(2,1)S(1)}, u32[]{:S(2)}, u32[]{:S(2)}) collective-permute-start(bf16[128,1024]{1,0:T(8,128)(2,1)} %shard_map.84.own), channel_id=1, source_target_pairs={{0,1},{1,2},{2,3},{3,4},{4,5},{5,6},{6,7},{7,8},{8,9},{9,10},{10,1... | collective-permute-start | bytes 786440 | tf_op jit(solution)/shard_map/ppermute | solution.py:291
  6.3 17.3 %collective-permute-start = (bf16[128,1024]{1,0:T(8,128)(2,1)}, bf16[128,1024]{1,0:T(8,128)(2,1)S(1)}, u32[]{:S(2)}, u32[]{:S(2)}) collective-permute-start(bf16[128,1024]{1,0:T(8,128)(2,1)} %shard_map.84.own), channel_id=1, source_target_pairs={{0,14},{1,15},{2,0},{3,1},{4,2},{5,3},{6,4},{7,5},{16,30},{17,31},... | collective-permute-start | bytes 786440 | tf_op jit(solution)/shard_map/ppermute | solution.py:291
  15.4 1.0 copy-start.1
  16.4 0.9 copy-start.2
  23.7 11.5 %collective-permute-start.2 = (bf16[128,1024]{1,0:T(8,128)(2,1)S(1)}, bf16[128,1024]{1,0:T(8,128)(2,1)S(1)}, u32[]{:S(2)}, u32[]{:S(2)}) collective-permute-start(bf16[128,1024]{1,0:T(8,128)(2,1)S(1)} %collective-permute-done.rest_0_.a1), channel_id=1, source_target_pairs={{14,13},{15,14},{0,15},{1,0},{2,1},{3,2},{4,3},{5,4},{30,29},{31,3... | collective-permute-start | bytes 786440 | tf_op jit(solution)/shard_map/ppermute | solution.py:291
  30.4 9.1 %collective-permute-start.3 = (bf16[128,1024]{1,0:T(8,128)(2,1)S(1)}, bf16[128,1024]{1,0:T(8,128)(2,1)S(1)}, u32[]{:S(2)}, u32[]{:S(2)}) collective-permute-start(bf16[128,1024]{1,0:T(8,128)(2,1)S(1)} %collective-permute-done.1.rest_1_.b1), channel_id=1, source_target_pairs={{1,2},{2,3},{3,4},{4,5},{5,6},{6,7},{7,8},{8,9},{9,10},{10,11},{11... | collective-permute-start | bytes 786440 | tf_op jit(solution)/shard_map/ppermute | solution.py:291
  35.1 8.3 %collective-permute-start.4 = (bf16[128,1024]{1,0:T(8,128)(2,1)S(1)}, bf16[128,1024]{1,0:T(8,128)(2,1)S(1)}, u32[]{:S(2)}, u32[]{:S(2)}) collective-permute-start(bf16[128,1024]{1,0:T(8,128)(2,1)S(1)} %collective-permute-done.2.rest_2_.a2), channel_id=1, source_target_pairs={{13,12},{14,13},{15,14},{0,15},{1,0},{2,1},{3,2},{4,3},{29,28},{30... | collective-permute-start | bytes 786440 | tf_op jit(solution)/shard_map/ppermute | solution.py:291
  39.5 8.3 %collective-permute-start.5 = (bf16[128,1024]{1,0:T(8,128)(2,1)S(1)}, bf16[128,1024]{1,0:T(8,128)(2,1)S(1)}, u32[]{:S(2)}, u32[]{:S(2)}) collective-permute-start(bf16[128,1024]{1,0:T(8,128)(2,1)S(1)} %collective-permute-done.3.rest_3_.b2), channel_id=1, source_target_pairs={{2,3},{3,4},{4,5},{5,6},{6,7},{7,8},{8,9},{9,10},{10,11},{11,12},{... | collective-permute-start | bytes 786440 | tf_op jit(solution)/shard_map/ppermute | solution.py:291
  43.4 8.3 %collective-permute-start.6 = (bf16[128,1024]{1,0:T(8,128)(2,1)S(1)}, bf16[128,1024]{1,0:T(8,128)(2,1)S(1)}, u32[]{:S(2)}, u32[]{:S(2)}) collective-permute-start(bf16[128,1024]{1,0:T(8,128)(2,1)S(1)} %collective-permute-done.4.rest_0_.a), channel_id=1, source_target_pairs={{12,11},{13,12},{14,13},{15,14},{0,15},{1,0},{2,1},{3,2},{28,27},{... | collective-permute-start | bytes 786440 | tf_op jit(solution)/shard_map/ppermute | solution.py:291
  47.8 9.5 %collective-permute-start.7 = (bf16[128,1024]{1,0:T(8,128)(2,1)S(1)}, bf16[128,1024]{1,0:T(8,128)(2,1)S(1)}, u32[]{:S(2)}, u32[]{:S(2)}) collective-permute-start(bf16[128,1024]{1,0:T(8,128)(2,1)S(1)} %collective-permute-done.5.rest_1_.b), channel_id=1, source_target_pairs={{3,4},{4,5},{5,6},{6,7},{7,8},{8,9},{9,10},{10,11},{11,12},{12,13}... | collective-permute-start | bytes 786440 | tf_op jit(solution)/shard_map/ppermute | solution.py:291
  51.7 9.5 %collective-permute-start.8 = (bf16[128,1024]{1,0:T(8,128)(2,1)S(1)}, bf16[128,1024]{1,0:T(8,128)(2,1)S(1)}, u32[]{:S(2)}, u32[]{:S(2)}) collective-permute-start(bf16[128,1024]{1,0:T(8,128)(2,1)S(1)} %collective-permute-done.6.rest_0_.a), channel_id=1, source_target_pairs={{11,10},{12,11},{13,12},{14,13},{15,14},{0,15},{1,0},{2,1},{27,26}... | collective-permute-start | bytes 786440 | tf_op jit(solution)/shard_map/ppermute | solution.py:291
  57.3 9.5 %collective-permute-start.9 = (bf16[128,1024]{1,0:T(8,128)(2,1)S(1)}, bf16[128,1024]{1,0:T(8,128)(2,1)S(1)}, u32[]{:S(2)}, u32[]{:S(2)}) collective-permute-start(bf16[128,1024]{1,0:T(8,128)(2,1)S(1)} %collective-permute-done.7.rest_1_.b), channel_id=1, source_target_pairs={{4,5},{5,6},{6,7},{7,8},{8,9},{9,10},{10,11},{11,12},{12,13},{13,1... | collective-permute-start | bytes 786440 | tf_op jit(solution)/shard_map/ppermute | solution.py:291
  61.2 9.5 %collective-permute-start.10 = (bf16[128,1024]{1,0:T(8,128)(2,1)S(1)}, bf16[128,1024]{1,0:T(8,128)(2,1)S(1)}, u32[]{:S(2)}, u32[]{:S(2)}) collective-permute-start(bf16[128,1024]{1,0:T(8,128)(2,1)S(1)} %collective-permute-done.8.rest_0_.a), channel_id=1, source_target_pairs={{10,9},{11,10},{12,11},{13,12},{14,13},{15,14},{0,15},{1,0},{26,25... | collective-permute-start | bytes 786440 | tf_op jit(solution)/shard_map/ppermute | solution.py:291
  66.8 4.5 %collective-permute-start.11 = (bf16[128,1024]{1,0:T(8,128)(2,1)S(1)}, bf16[128,1024]{1,0:T(8,128)(2,1)S(1)}, u32[]{:S(2)}, u32[]{:S(2)}) collective-permute-start(bf16[128,1024]{1,0:T(8,128)(2,1)S(1)} %collective-permute-done.9.rest_1_.b), channel_id=1, source_target_pairs={{5,6},{6,7},{7,8},{8,9},{9,10},{10,11},{11,12},{12,13},{13,14},{14... | collective-permute-start | bytes 786440 | tf_op jit(solution)/shard_map/ppermute | solution.py:291
  70.6 2.0 %collective-permute-start.12 = (bf16[128,1024]{1,0:T(8,128)(2,1)S(1)}, bf16[128,1024]{1,0:T(8,128)(2,1)S(1)}, u32[]{:S(2)}, u32[]{:S(2)}) collective-permute-start(bf16[128,1024]{1,0:T(8,128)(2,1)S(1)} %collective-permute-done.10.rest_0_.a), channel_id=1, source_target_pairs={{9,8},{10,9},{11,10},{12,11},{13,12},{14,13},{15,14},{0,15},{25,24... | collective-permute-start | bytes 786440 | tf_op jit(solution)/shard_map/ppermute | solution.py:291
  71.3 1.9 %collective-permute-start.13 = (bf16[128,1024]{1,0:T(8,128)(2,1)S(1)}, bf16[128,1024]{1,0:T(8,128)(2,1)S(1)}, u32[]{:S(2)}, u32[]{:S(2)}) collective-permute-start(bf16[128,1024]{1,0:T(8,128)(2,1)S(1)} %collective-permute-done.11.rest_1_.b), channel_id=1, source_target_pairs={{6,7},{7,8},{8,9},{9,10},{10,11},{11,12},{12,13},{13,14},{14,15},{... | collective-permute-start | bytes 786440 | tf_op jit(solution)/shard_map/ppermute | solution.py:291
  74.4 3.0 %collective-permute-start.14 = (bf16[128,1024]{1,0:T(8,128)(2,1)S(1)}, bf16[128,1024]{1,0:T(8,128)(2,1)S(1)}, u32[]{:S(2)}, u32[]{:S(2)}) collective-permute-start(bf16[128,1024]{1,0:T(8,128)(2,1)S(1)} %get-tuple-element.121), channel_id=1, source_target_pairs={{8,9},{9,10},{10,11},{11,12},{12,13},{13,14},{14,15},{15,0},{24,25... | collective-permute-start | bytes 786440 | tf_op jit(solution)/shard_map/ppermute | solution.py:291
  75.1 3.7 %collective-permute-start.21 = (bf16[128,1024]{1,0:T(8,128)(2,1)S(1)}, bf16[128,1024]{1,0:T(8,128)(2,1)S(1)}, u32[]{:S(2)}, u32[]{:S(2)}) collective-permute-start(bf16[128,1024]{1,0:T(8,128)(2,1)S(1)} %get-tuple-element.132), channel_id=1, source_target_pairs={{7,6},{8,7},{9,8},{10,9},{11,10},{12,11},{13,12},{14,13},{15,14},{... | collective-permute-start | bytes 786440 | tf_op jit(solution)/shard_map/ppermute | solution.py:291
  77.5 33.7 %collective-permute-start.15 = (bf16[128,1024]{1,0:T(8,128)(2,1)S(1)}, bf16[128,1024]{1,0:T(8,128)(2,1)S(1)}, u32[]{:S(2)}, u32[]{:S(2)}) collective-permute-start(bf16[128,1024]{1,0:T(8,128)(2,1)S(1)} %add.51), channel_id=1, source_target_pairs={{9,10},{10,11},{11,12},{12,13},{13,14},{14,15},{15,0},{0,1},{25,26... | collective-permute-start | bytes 786440 | tf_op jit(solution)/shard_map/ppermute | solution.py:291
  78.9 34.3 %collective-permute-start.22 = (bf16[128,1024]{1,0:T(8,128)(2,1)S(1)}, bf16[128,1024]{1,0:T(8,128)(2,1)S(1)}, u32[]{:S(2)}, u32[]{:S(2)}) collective-permute-start(bf16[128,1024]{1,0:T(8,128)(2,1)S(1)} %add.57), channel_id=1, source_target_pairs={{6,5},{7,6},{8,7},{9,8},{10,9},{11,10},{12,11},{13,12},{14,13},{15... | collective-permute-start | bytes 786440 | tf_op jit(solution)/shard_map/ppermute | solution.py:291
  111.3 10.6 %collective-permute-start.16 = (bf16[128,1024]{1,0:T(8,128)(2,1)S(1)}, bf16[128,1024]{1,0:T(8,128)(2,1)S(1)}, u32[]{:S(2)}, u32[]{:S(2)}) collective-permute-start(bf16[128,1024]{1,0:T(8,128)(2,1)S(1)} %add.52), channel_id=1, source_target_pairs={{10,11},{11,12},{12,13},{13,14},{14,15},{15,0},{0,1},{1,2},{26,27}... | collective-permute-start | bytes 786440 | tf_op jit(solution)/shard_map/ppermute | solution.py:291
  113.3 10.6 %collective-permute-start.23 = (bf16[128,1024]{1,0:T(8,128)(2,1)S(1)}, bf16[128,1024]{1,0:T(8,128)(2,1)S(1)}, u32[]{:S(2)}, u32[]{:S(2)}) collective-permute-start(bf16[128,1024]{1,0:T(8,128)(2,1)S(1)} %add.58), channel_id=1, source_target_pairs={{5,4},{6,5},{7,6},{8,7},{9,8},{10,9},{11,10},{12,11},{13,12},{14,1... | collective-permute-start | bytes 786440 | tf_op jit(solution)/shard_map/ppermute | solution.py:291
  121.9 9.7 %collective-permute-start.17 = (bf16[128,1024]{1,0:T(8,128)(2,1)S(1)}, bf16[128,1024]{1,0:T(8,128)(2,1)S(1)}, u32[]{:S(2)}, u32[]{:S(2)}) collective-permute-start(bf16[128,1024]{1,0:T(8,128)(2,1)S(1)} %add.53), channel_id=1, source_target_pairs={{11,12},{12,13},{13,14},{14,15},{15,0},{0,1},{1,2},{2,3},{27,28},{... | collective-permute-start | bytes 786440 | tf_op jit(solution)/shard_map/ppermute | solution.py:291
  124.0 9.7 %collective-permute-start.24 = (bf16[128,1024]{1,0:T(8,128)(2,1)S(1)}, bf16[128,1024]{1,0:T(8,128)(2,1)S(1)}, u32[]{:S(2)}, u32[]{:S(2)}) collective-permute-start(bf16[128,1024]{1,0:T(8,128)(2,1)S(1)} %add.59), channel_id=1, source_target_pairs={{4,3},{5,4},{6,5},{7,6},{8,7},{9,8},{10,9},{11,10},{12,11},{13,12}... | collective-permute-start | bytes 786440 | tf_op jit(solution)/shard_map/ppermute | solution.py:291
  131.7 9.2 %collective-permute-start.18 = (bf16[128,1024]{1,0:T(8,128)(2,1)S(1)}, bf16[128,1024]{1,0:T(8,128)(2,1)S(1)}, u32[]{:S(2)}, u32[]{:S(2)}) collective-permute-start(bf16[128,1024]{1,0:T(8,128)(2,1)S(1)} %add.54), channel_id=1, source_target_pairs={{12,13},{13,14},{14,15},{15,0},{0,1},{1,2},{2,3},{3,4},{28,29},{29... | collective-permute-start | bytes 786440 | tf_op jit(solution)/shard_map/ppermute | solution.py:291
  133.7 9.2 %collective-permute-start.25 = (bf16[128,1024]{1,0:T(8,128)(2,1)S(1)}, bf16[128,1024]{1,0:T(8,128)(2,1)S(1)}, u32[]{:S(2)}, u32[]{:S(2)}) collective-permute-start(bf16[128,1024]{1,0:T(8,128)(2,1)S(1)} %add.60), channel_id=1, source_target_pairs={{3,2},{4,3},{5,4},{6,5},{7,6},{8,7},{9,8},{10,9},{11,10},{12,11},{... | collective-permute-start | bytes 786440 | tf_op jit(solution)/shard_map/ppermute | solution.py:291
  141.0 10.7 %collective-permute-start.19 = (bf16[128,1024]{1,0:T(8,128)(2,1)S(1)}, bf16[128,1024]{1,0:T(8,128)(2,1)S(1)}, u32[]{:S(2)}, u32[]{:S(2)}) collective-permute-start(bf16[128,1024]{1,0:T(8,128)(2,1)S(1)} %add.55), channel_id=1, source_target_pairs={{13,14},{14,15},{15,0},{0,1},{1,2},{2,3},{3,4},{4,5},{29,30},{30,3... | collective-permute-start | bytes 786440 | tf_op jit(solution)/shard_map/ppermute | solution.py:291
  143.0 10.7 %collective-permute-start.26 = (bf16[128,1024]{1,0:T(8,128)(2,1)S(1)}, bf16[128,1024]{1,0:T(8,128)(2,1)S(1)}, u32[]{:S(2)}, u32[]{:S(2)}) collective-permute-start(bf16[128,1024]{1,0:T(8,128)(2,1)S(1)} %add.61), channel_id=1, source_target_pairs={{2,1},{3,2},{4,3},{5,4},{6,5},{7,6},{8,7},{9,8},{10,9},{11,10},{12... | collective-permute-start | bytes 786440 | tf_op jit(solution)/shard_map/ppermute | solution.py:291
  151.8 13.2 %collective-permute-start.20 = (bf16[128,1024]{1,0:T(8,128)(2,1)S(1)}, bf16[128,1024]{1,0:T(8,128)(2,1)S(1)}, u32[]{:S(2)}, u32[]{:S(2)}) collective-permute-start(bf16[128,1024]{1,0:T(8,128)(2,1)S(1)} %add.56), channel_id=1, source_target_pairs={{14,0},{15,1},{0,2},{1,3},{2,4},{3,5},{4,6},{5,7},{30,16},{31,17},... | collective-permute-start | bytes 786440 | tf_op jit(solution)/shard_map/ppermute | solution.py:291
  153.7 4.1 %copy-start.3 = (bf16[128,1024]{1,0:T(8,128)(2,1)S(1)}, bf16[128,1024]{1,0:T(8,128)(2,1)}, u32[]{:S(2)}) copy-start(bf16[128,1024]{1,0:T(8,128)(2,1)} %shard_map.84.own) | copy-start | bytes 786436
  153.8 11.2 %collective-permute-start.27 = (bf16[128,1024]{1,0:T(8,128)(2,1)S(1)}, bf16[128,1024]{1,0:T(8,128)(2,1)S(1)}, u32[]{:S(2)}, u32[]{:S(2)}) collective-permute-start(bf16[128,1024]{1,0:T(8,128)(2,1)S(1)} %add.62), channel_id=1, source_target_pairs={{1,0},{2,1},{3,2},{4,3},{5,4},{6,5},{7,6},{8,7},{9,8},{10,9},{11,1... | collective-permute-start | bytes 786440 | tf_op jit(solution)/shard_map/ppermute | solution.py:291

commit v9 on v8

--- a/solution.py
+++ b/solution.py
@@ -301,9 +301,12 @@
 
 def return_pairs(step, count):
     near = [(j, j - 1) for j in range(STEPS + 1 - step, count)]
-    blocks = range(count - STEPS - 1)
-    end = STEPS + 1 + step if step < STEPS else count
-    far = [((b + STEPS + step) % count, (b + end) % count) for b in blocks]
+    if step <= FAR - STEPS - 1:
+        far = [(z, z + 1) for z in range(STEPS + step, count - 1)]
+        far.append((count - 1, count - 1 - STEPS - step))
+    else:
+        begin, end = {5: (0, 2), 6: (2, 3), 7: (3, 4)}[step]
+        far = [((b + FAR + begin) % count, (b + FAR + end) % count) for b in range(count - FAR)]
     return near, far
 
 
@@ -367,11 +370,14 @@
             scratch=scratch,
         )
 
+    early = []
     for step in range(1, STEPS + 1):
         pairs = return_pairs(step, count)
         sum_a = both_ways(sum_a, *pairs, 0)
         sum_b = both_ways(sum_b, *pairs, 1)
         back = STEPS - step
+        if back >= 3:
+            early.append(sum_a.astype(jnp.float32))
         if back == 6:
             acc, term_a, term_b, attended = backward(
                 functools.partial(second_kernel, back), [TURNED, block, block, wide], back,
@@ -395,6 +401,7 @@
         if back >= 1:
             sum_a, sum_b = add_low(sum_a, term_a), add_low(sum_b, term_b)
     summed = sum_a.astype(jnp.float32) + sum_b.astype(jnp.float32) + term_0
+    summed = summed + jnp.where(q_start <= STEPS * rows, sum(early), 0.0)
     return (attended, grad_query, summed[:, :WIDE], summed[:, WIDE:])
 
 

time: 167 us -> 175 us (1.048)
  the two profiles are of different devices: /device:TPU:38 before, /device:TPU:24 now
where the time goes in v9:
time: 175 us; the launch traced here: 172 us
  waiting for transfers between devices  83.3 us (48%)
  starting transfers between devices  63.4 us (36%)
  Pallas kernels  14.7 us (8%)
  local copies, waits for them, and re-layouts  5.42 us (3%)
  other arithmetic  3.96 us (2%)
    ppermute x28, waiting for transfers between devices, both_ways(): return lax.ppermute(x, ('dp', 'ctx'), pairs)  83.3 us
    ppermute x28, starting transfers between devices, both_ways(): return lax.ppermute(x, ('dp', 'ctx'), pairs)  63.4 us
    pallas_call x14, Pallas kernels, call(): pl.pallas_call(kernel, out_shape=outs, in_specs=[pl.BlockSpec(memory_spac...  13 us
    unnamed x28, local copies, waits for them, and re-layouts  4.52 us
  transfers between devices with their start and end apart: 28, of which 11 were waited for; matrix products, arithmetic and copies ran while one was open for 2% of the time, Pallas kernels for 7%

profile of v9, /device:TPU:24, one launch (start us, length us, event | category | flops | bytes accessed | tf_op | source)
XLA Modules:
  0.0 172.1 jit_solution(8778688000845850665)
XLA Ops:
  0.6 1.7 %shard_map.84.own = bf16[128,1024]{1,0:T(8,128)(2,1)} custom-call(bf16[128,512]{1,0:T(8,128)(2,1)} %k_ref.1, bf16[128,512]{1,0:T(8,128)(2,1)} %v_ref.1), custom_call_target="tpu_custom_call" | custom-call | tf_op jit(solution)/shard_map/pallas_call | solution.py:277
  2.4 4.0 %collective-permute-start.1 = (bf16[128,1024]{1,0:T(8,128)(2,1)}, bf16[128,1024]{1,0:T(8,128)(2,1)S(1)}, u32[]{:S(2)}, u32[]{:S(2)}) collective-permute-start(bf16[128,1024]{1,0:T(8,128)(2,1)} %shard_map.84.own), channel_id=1, source_target_pairs={{0,1},{1,2},{2,3},{3,4},{4,5},{5,6},{6,7},{7,8},{8,9},{9,10},{10,1... | collective-permute-start | bytes 786440 | tf_op jit(solution)/shard_map/ppermute | solution.py:291
  6.4 10.9 %collective-permute-start = (bf16[128,1024]{1,0:T(8,128)(2,1)}, bf16[128,1024]{1,0:T(8,128)(2,1)S(1)}, u32[]{:S(2)}, u32[]{:S(2)}) collective-permute-start(bf16[128,1024]{1,0:T(8,128)(2,1)} %shard_map.84.own), channel_id=1, source_target_pairs={{0,14},{1,15},{2,0},{3,1},{4,2},{5,3},{6,4},{7,5},{16,30},{17,31},... | collective-permute-start | bytes 786440 | tf_op jit(solution)/shard_map/ppermute | solution.py:291
  17.9 1.0 copy-done.1
  18.9 0.9 copy-done.3
  19.9 1.8 %shard_map.85 = (f32[4,1,512]{2,1,0:T(1,128)S(1)}, f32[4,1,512]{2,1,0:T(1,128)S(1)}, f32[4,128,512]{2,1,0:T(8,128)S(1)}, bf16[4,128,512]{2,1,0:T(8,128)(2,1)S(1)...) custom-call(s32[3]{0:T(128)S(1)} %pad_add_fusion.scal, s32[1,128]{1,0:T(1,128)S(1)} %bitcast.6, ...), custom_call_target="tpu_custom_call" | custom-call | flops 1000000000 | bytes 4194304 | tf_op jit(solution)/shard_map/pallas_call | solution.py:262
  21.7 6.7 %collective-permute-done.rest_0_.a1 = bf16[128,1024]{1,0:T(8,128)(2,1)S(1)} collective-permute-done((bf16[128,1024]{1,0:T(8,128)(2,1)}, bf16[128,1024]{1,0:T(8,128)(2,1)S(1)}, u32[]{:S(2)}, u32[]{:S(2)}) %collective-permute-start) | collective-permute-done | bytes 262176 | tf_op jit(solution)/shard_map/ppermute | solution.py:291
  28.4 1.9 %collective-permute-start.2 = (bf16[128,1024]{1,0:T(8,128)(2,1)S(1)}, bf16[128,1024]{1,0:T(8,128)(2,1)S(1)}, u32[]{:S(2)}, u32[]{:S(2)}) collective-permute-start(bf16[128,1024]{1,0:T(8,128)(2,1)S(1)} %collective-permute-done.rest_0_.a1), channel_id=1, source_target_pairs={{14,13},{15,14},{0,15},{1,0},{2,1},{3,2},{4,3},{5,4},{30,29},{31,3... | collective-permute-start | bytes 786440 | tf_op jit(solution)/shard_map/ppermute | solution.py:291
  30.3 0.7 collective-permute-start.3
  31.0 6.5 %collective-permute-done.2.rest_2_.a2 = bf16[128,1024]{1,0:T(8,128)(2,1)S(1)} collective-permute-done((bf16[128,1024]{1,0:T(8,128)(2,1)S(1)}, bf16[128,1024]{1,0:T(8,128)(2,1)S(1)}, u32[]{:S(2)}, u32[]{:S(2)}) %collective-permute-start.2) | collective-permute-done | bytes 262176 | tf_op jit(solution)/shard_map/ppermute | solution.py:291
  37.5 4.5 %collective-permute-start.4 = (bf16[128,1024]{1,0:T(8,128)(2,1)S(1)}, bf16[128,1024]{1,0:T(8,128)(2,1)S(1)}, u32[]{:S(2)}, u32[]{:S(2)}) collective-permute-start(bf16[128,1024]{1,0:T(8,128)(2,1)S(1)} %collective-permute-done.2.rest_2_.a2), channel_id=1, source_target_pairs={{13,12},{14,13},{15,14},{0,15},{1,0},{2,1},{3,2},{4,3},{29,28},{30... | collective-permute-start | bytes 786440 | tf_op jit(solution)/shard_map/ppermute | solution.py:291
  42.0 0.7 collective-permute-start.5
  42.6 0.6 shard_map.86
  43.3 2.5 %collective-permute-done.4.rest_0_.a = bf16[128,1024]{1,0:T(8,128)(2,1)S(1)} collective-permute-done((bf16[128,1024]{1,0:T(8,128)(2,1)S(1)}, bf16[128,1024]{1,0:T(8,128)(2,1)S(1)}, u32[]{:S(2)}, u32[]{:S(2)}) %collective-permute-start.4) | collective-permute-done | bytes 262176 | tf_op jit(solution)/shard_map/ppermute | solution.py:291
  45.8 5.6 %collective-permute-start.6 = (bf16[128,1024]{1,0:T(8,128)(2,1)S(1)}, bf16[128,1024]{1,0:T(8,128)(2,1)S(1)}, u32[]{:S(2)}, u32[]{:S(2)}) collective-permute-start(bf16[128,1024]{1,0:T(8,128)(2,1)S(1)} %collective-permute-done.4.rest_0_.a), channel_id=1, source_target_pairs={{12,11},{13,12},{14,13},{15,14},{0,15},{1,0},{2,1},{3,2},{28,27},{... | collective-permute-start | bytes 786440 | tf_op jit(solution)/shard_map/ppermute | solution.py:291
  51.4 0.7 collective-permute-start.7
  52.1 0.6 shard_map.87
  52.7 2.5 %collective-permute-done.6.rest_0_.a = bf16[128,1024]{1,0:T(8,128)(2,1)S(1)} collective-permute-done((bf16[128,1024]{1,0:T(8,128)(2,1)S(1)}, bf16[128,1024]{1,0:T(8,128)(2,1)S(1)}, u32[]{:S(2)}, u32[]{:S(2)}) %collective-permute-start.6) | collective-permute-done | bytes 262176 | tf_op jit(solution)/shard_map/ppermute | solution.py:291
  55.3 5.6 %collective-permute-start.8 = (bf16[128,1024]{1,0:T(8,128)(2,1)S(1)}, bf16[128,1024]{1,0:T(8,128)(2,1)S(1)}, u32[]{:S(2)}, u32[]{:S(2)}) collective-permute-start(bf16[128,1024]{1,0:T(8,128)(2,1)S(1)} %collective-permute-done.6.rest_0_.a), channel_id=1, source_target_pairs={{11,10},{12,11},{13,12},{14,13},{15,14},{0,15},{1,0},{2,1},{27,26}... | collective-permute-start | bytes 786440 | tf_op jit(solution)/shard_map/ppermute | solution.py:291
  60.9 0.7 collective-permute-start.9
  61.6 0.6 shard_map.88
  62.2 2.5 %collective-permute-done.8.rest_0_.a = bf16[128,1024]{1,0:T(8,128)(2,1)S(1)} collective-permute-done((bf16[128,1024]{1,0:T(8,128)(2,1)S(1)}, bf16[128,1024]{1,0:T(8,128)(2,1)S(1)}, u32[]{:S(2)}, u32[]{:S(2)}) %collective-permute-start.8) | collective-permute-done | bytes 262176 | tf_op jit(solution)/shard_map/ppermute | solution.py:291
  64.7 5.6 %collective-permute-start.10 = (bf16[128,1024]{1,0:T(8,128)(2,1)S(1)}, bf16[128,1024]{1,0:T(8,128)(2,1)S(1)}, u32[]{:S(2)}, u32[]{:S(2)}) collective-permute-start(bf16[128,1024]{1,0:T(8,128)(2,1)S(1)} %collective-permute-done.8.rest_0_.a), channel_id=1, source_target_pairs={{10,9},{11,10},{12,11},{13,12},{14,13},{15,14},{0,15},{1,0},{26,25... | collective-permute-start | bytes 786440 | tf_op jit(solution)/shard_map/ppermute | solution.py:291
  70.4 0.7 collective-permute-start.11
  71.0 0.6 shard_map.89
  71.7 3.3 %collective-permute-done.10.rest_0_.a = bf16[128,1024]{1,0:T(8,128)(2,1)S(1)} collective-permute-done((bf16[128,1024]{1,0:T(8,128)(2,1)S(1)}, bf16[128,1024]{1,0:T(8,128)(2,1)S(1)}, u32[]{:S(2)}, u32[]{:S(2)}) %collective-permute-start.10) | collective-permute-done | bytes 262176 | tf_op jit(solution)/shard_map/ppermute | solution.py:291
  75.0 5.6 %collective-permute-start.12 = (bf16[128,1024]{1,0:T(8,128)(2,1)S(1)}, bf16[128,1024]{1,0:T(8,128)(2,1)S(1)}, u32[]{:S(2)}, u32[]{:S(2)}) collective-permute-start(bf16[128,1024]{1,0:T(8,128)(2,1)S(1)} %collective-permute-done.10.rest_0_.a), channel_id=1, source_target_pairs={{9,8},{10,9},{11,10},{12,11},{13,12},{14,13},{15,14},{0,15},{25,24... | collective-permute-start | bytes 786440 | tf_op jit(solution)/shard_map/ppermute | solution.py:291
  80.6 0.7 collective-permute-start.13
  81.3 0.6 shard_map.90
  81.9 2.5 %collective-permute-done.12.rest_0_.a = bf16[128,1024]{1,0:T(8,128)(2,1)S(1)} collective-permute-done((bf16[128,1024]{1,0:T(8,128)(2,1)S(1)}, bf16[128,1024]{1,0:T(8,128)(2,1)S(1)}, u32[]{:S(2)}, u32[]{:S(2)}) %collective-permute-start.12) | collective-permute-done | bytes 262176 | tf_op jit(solution)/shard_map/ppermute | solution.py:291
  84.5 0.6 shard_map.91
  85.1 1.1 shard_map.92
  86.2 0.7 collective-permute-start.14
  86.9 0.7 collective-permute-start.21
  87.6 1.6 shard_map.93
  89.3 0.6 copy-done.5
  89.9 0.7 collective-permute-start.15
  90.7 0.7 collective-permute-start.22
  91.4 0.7 shard_map.94
  92.1 0.6 copy-done.7
  92.7 0.7 collective-permute-start.16
  93.5 0.7 collective-permute-start.23
  94.2 0.7 shard_map.95
  94.9 0.6 copy-done.9
  95.6 0.7 collective-permute-start.17
  96.3 0.7 collective-permute-start.24
  97.0 0.7 shard_map.96
  97.8 0.6 copy-done.11
  98.4 1.3 collective-permute-start.18
  99.8 0.7 collective-permute-start.25
  100.4 0.7 shard_map.97
  101.1 45.6 %collective-permute-done.18 = bf16[128,1024]{1,0:T(8,128)(2,1)S(1)} collective-permute-done((bf16[128,1024]{1,0:T(8,128)(2,1)S(1)}, bf16[128,1024]{1,0:T(8,128)(2,1)S(1)}, u32[]{:S(2)}, u32[]{:S(2)}) %collective-permute-start.18) | collective-permute-done | bytes 262176 | tf_op jit(solution)/shard_map/ppermute | solution.py:291
  146.8 4.3 %collective-permute-start.19 = (bf16[128,1024]{1,0:T(8,128)(2,1)S(1)}, bf16[128,1024]{1,0:T(8,128)(2,1)S(1)}, u32[]{:S(2)}, u32[]{:S(2)}) collective-permute-start(bf16[128,1024]{1,0:T(8,128)(2,1)S(1)} %add.67), channel_id=1, source_target_pairs={{14,15},{15,0},{0,1},{1,2},{30,31},{31,16},{16,17},{17,18},{46,47}... | collective-permute-start | bytes 786440 | tf_op jit(solution)/shard_map/ppermute | solution.py:291
  151.2 0.7 collective-permute-start.26
  151.9 5.8 %collective-permute-done.19 = bf16[128,1024]{1,0:T(8,128)(2,1)S(1)} collective-permute-done((bf16[128,1024]{1,0:T(8,128)(2,1)S(1)}, bf16[128,1024]{1,0:T(8,128)(2,1)S(1)}, u32[]{:S(2)}, u32[]{:S(2)}) %collective-permute-start.19) | collective-permute-done | bytes 262176 | tf_op jit(solution)/shard_map/ppermute | solution.py:291
  157.7 0.8 add.68
  158.5 2.0 %collective-permute-start.20 = (bf16[128,1024]{1,0:T(8,128)(2,1)}, bf16[128,1024]{1,0:T(8,128)(2,1)}, u32[]{:S(2)}, u32[]{:S(2)}) collective-permute-start(bf16[128,1024]{1,0:T(8,128)(2,1)} %add.68), channel_id=1, source_target_pairs={{15,0},{0,1},{1,2},{2,3},{31,16},{16,17},{17,18},{18,19},{47,32},{... | collective-permute-start | bytes 786440 | tf_op jit(solution)/shard_map/ppermute | solution.py:291
  160.6 0.8 add.74
  161.4 1.3 collective-permute-start.27
  162.7 2.1 %shard_map.98 = (bf16[128,2048]{1,0:T(8,128)(2,1)}, f32[128,1024]{1,0:T(8,128)S(1)}) custom-call(s32[3]{0:T(128)S(1)} %pad_add_fusion.scal, bf16[128,2048]{1,0:T(8,128)(2,1)S(1)} %copy-done, bf16[128,2048]{1,0:T(8,128)(2,1)S(1)} %copy-done.2, f32[4,1,512]{2,1,0:T(1,128)S(1)} %get-tuple-element.101.log_ref, f32[4,1,512]{2,1,0:T(1,128)S(1)} %get-tuple-element.102.inner_ref, ...), custom_call_target="tpu_custom_call" | custom-call | flops 1000000000 | bytes 4194304 | tf_op jit(solution)/shard_map/pallas_call | solution.py:262
  164.8 3.6 %collective-permute-done.20 = bf16[128,1024]{1,0:T(8,128)(2,1)} collective-permute-done((bf16[128,1024]{1,0:T(8,128)(2,1)}, bf16[128,1024]{1,0:T(8,128)(2,1)}, u32[]{:S(2)}, u32[]{:S(2)}) %collective-permute-start.20) | collective-permute-done | bytes 262176 | tf_op jit(solution)/shard_map/ppermute | solution.py:291
  168.4 1.5 collective-permute-done.27
  169.9 1.3 select_add_fusion
  171.3 0.8 fusion
  (52 shorter events, 1.3 us)
Async XLA Ops:
  0.6 17.3 %copy-start = (bf16[128,2048]{1,0:T(8,128)(2,1)S(1)}, bf16[128,2048]{1,0:T(8,128)(2,1)}, u32[]{:S(2)}) copy-start(bf16[128,2048]{1,0:T(8,128)(2,1)} %q_ref.27) | copy-start | bytes 1572868
  2.4 14.9 %copy-start.13 = (s32[2048]{0:T(1024)S(1)}, s32[2048]{0:T(1024)}, u32[]{:S(2)}) copy-start(s32[2048]{0:T(1024)} %param.9) | copy-start | bytes 24580
  2.4 27.9 %collective-permute-start.1 = (bf16[128,1024]{1,0:T(8,128)(2,1)}, bf16[128,1024]{1,0:T(8,128)(2,1)S(1)}, u32[]{:S(2)}, u32[]{:S(2)}) collective-permute-start(bf16[128,1024]{1,0:T(8,128)(2,1)} %shard_map.84.own), channel_id=1, source_target_pairs={{0,1},{1,2},{2,3},{3,4},{4,5},{5,6},{6,7},{7,8},{8,9},{9,10},{10,1... | collective-permute-start | bytes 786440 | tf_op jit(solution)/shard_map/ppermute | solution.py:291
  6.4 22.1 %collective-permute-start = (bf16[128,1024]{1,0:T(8,128)(2,1)}, bf16[128,1024]{1,0:T(8,128)(2,1)S(1)}, u32[]{:S(2)}, u32[]{:S(2)}) collective-permute-start(bf16[128,1024]{1,0:T(8,128)(2,1)} %shard_map.84.own), channel_id=1, source_target_pairs={{0,14},{1,15},{2,0},{3,1},{4,2},{5,3},{6,4},{7,5},{16,30},{17,31},... | collective-permute-start | bytes 786440 | tf_op jit(solution)/shard_map/ppermute | solution.py:291
  17.9 1.0 copy-start.1
  18.9 0.9 copy-start.3
  28.4 9.1 %collective-permute-start.2 = (bf16[128,1024]{1,0:T(8,128)(2,1)S(1)}, bf16[128,1024]{1,0:T(8,128)(2,1)S(1)}, u32[]{:S(2)}, u32[]{:S(2)}) collective-permute-start(bf16[128,1024]{1,0:T(8,128)(2,1)S(1)} %collective-permute-done.rest_0_.a1), channel_id=1, source_target_pairs={{14,13},{15,14},{0,15},{1,0},{2,1},{3,2},{4,3},{5,4},{30,29},{31,3... | collective-permute-start | bytes 786440 | tf_op jit(solution)/shard_map/ppermute | solution.py:291
  30.3 11.6 %collective-permute-start.3 = (bf16[128,1024]{1,0:T(8,128)(2,1)S(1)}, bf16[128,1024]{1,0:T(8,128)(2,1)S(1)}, u32[]{:S(2)}, u32[]{:S(2)}) collective-permute-start(bf16[128,1024]{1,0:T(8,128)(2,1)S(1)} %collective-permute-done.1.rest_1_.b1), channel_id=1, source_target_pairs={{1,2},{2,3},{3,4},{4,5},{5,6},{6,7},{7,8},{8,9},{9,10},{10,11},{11... | collective-permute-start | bytes 786440 | tf_op jit(solution)/shard_map/ppermute | solution.py:291
  37.5 8.3 %collective-permute-start.4 = (bf16[128,1024]{1,0:T(8,128)(2,1)S(1)}, bf16[128,1024]{1,0:T(8,128)(2,1)S(1)}, u32[]{:S(2)}, u32[]{:S(2)}) collective-permute-start(bf16[128,1024]{1,0:T(8,128)(2,1)S(1)} %collective-permute-done.2.rest_2_.a2), channel_id=1, source_target_pairs={{13,12},{14,13},{15,14},{0,15},{1,0},{2,1},{3,2},{4,3},{29,28},{30... | collective-permute-start | bytes 786440 | tf_op jit(solution)/shard_map/ppermute | solution.py:291
  42.0 9.5 %collective-permute-start.5 = (bf16[128,1024]{1,0:T(8,128)(2,1)S(1)}, bf16[128,1024]{1,0:T(8,128)(2,1)S(1)}, u32[]{:S(2)}, u32[]{:S(2)}) collective-permute-start(bf16[128,1024]{1,0:T(8,128)(2,1)S(1)} %collective-permute-done.3.rest_3_.b2), channel_id=1, source_target_pairs={{2,3},{3,4},{4,5},{5,6},{6,7},{7,8},{8,9},{9,10},{10,11},{11,12},{... | collective-permute-start | bytes 786440 | tf_op jit(solution)/shard_map/ppermute | solution.py:291
  45.8 9.5 %collective-permute-start.6 = (bf16[128,1024]{1,0:T(8,128)(2,1)S(1)}, bf16[128,1024]{1,0:T(8,128)(2,1)S(1)}, u32[]{:S(2)}, u32[]{:S(2)}) collective-permute-start(bf16[128,1024]{1,0:T(8,128)(2,1)S(1)} %collective-permute-done.4.rest_0_.a), channel_id=1, source_target_pairs={{12,11},{13,12},{14,13},{15,14},{0,15},{1,0},{2,1},{3,2},{28,27},{... | collective-permute-start | bytes 786440 | tf_op jit(solution)/shard_map/ppermute | solution.py:291
  51.4 9.5 %collective-permute-start.7 = (bf16[128,1024]{1,0:T(8,128)(2,1)S(1)}, bf16[128,1024]{1,0:T(8,128)(2,1)S(1)}, u32[]{:S(2)}, u32[]{:S(2)}) collective-permute-start(bf16[128,1024]{1,0:T(8,128)(2,1)S(1)} %collective-permute-done.5.rest_1_.b), channel_id=1, source_target_pairs={{3,4},{4,5},{5,6},{6,7},{7,8},{8,9},{9,10},{10,11},{11,12},{12,13}... | collective-permute-start | bytes 786440 | tf_op jit(solution)/shard_map/ppermute | solution.py:291
  55.3 9.5 %collective-permute-start.8 = (bf16[128,1024]{1,0:T(8,128)(2,1)S(1)}, bf16[128,1024]{1,0:T(8,128)(2,1)S(1)}, u32[]{:S(2)}, u32[]{:S(2)}) collective-permute-start(bf16[128,1024]{1,0:T(8,128)(2,1)S(1)} %collective-permute-done.6.rest_0_.a), channel_id=1, source_target_pairs={{11,10},{12,11},{13,12},{14,13},{15,14},{0,15},{1,0},{2,1},{27,26}... | collective-permute-start | bytes 786440 | tf_op jit(solution)/shard_map/ppermute | solution.py:291
  60.9 9.5 %collective-permute-start.9 = (bf16[128,1024]{1,0:T(8,128)(2,1)S(1)}, bf16[128,1024]{1,0:T(8,128)(2,1)S(1)}, u32[]{:S(2)}, u32[]{:S(2)}) collective-permute-start(bf16[128,1024]{1,0:T(8,128)(2,1)S(1)} %collective-permute-done.7.rest_1_.b), channel_id=1, source_target_pairs={{4,5},{5,6},{6,7},{7,8},{8,9},{9,10},{10,11},{11,12},{12,13},{13,1... | collective-permute-start | bytes 786440 | tf_op jit(solution)/shard_map/ppermute | solution.py:291
  64.7 10.2 %collective-permute-start.10 = (bf16[128,1024]{1,0:T(8,128)(2,1)S(1)}, bf16[128,1024]{1,0:T(8,128)(2,1)S(1)}, u32[]{:S(2)}, u32[]{:S(2)}) collective-permute-start(bf16[128,1024]{1,0:T(8,128)(2,1)S(1)} %collective-permute-done.8.rest_0_.a), channel_id=1, source_target_pairs={{10,9},{11,10},{12,11},{13,12},{14,13},{15,14},{0,15},{1,0},{26,25... | collective-permute-start | bytes 786440 | tf_op jit(solution)/shard_map/ppermute | solution.py:291
  70.4 10.3 %collective-permute-start.11 = (bf16[128,1024]{1,0:T(8,128)(2,1)S(1)}, bf16[128,1024]{1,0:T(8,128)(2,1)S(1)}, u32[]{:S(2)}, u32[]{:S(2)}) collective-permute-start(bf16[128,1024]{1,0:T(8,128)(2,1)S(1)} %collective-permute-done.9.rest_1_.b), channel_id=1, source_target_pairs={{5,6},{6,7},{7,8},{8,9},{9,10},{10,11},{11,12},{12,13},{13,14},{14... | collective-permute-start | bytes 786440 | tf_op jit(solution)/shard_map/ppermute | solution.py:291
  75.0 9.5 %collective-permute-start.12 = (bf16[128,1024]{1,0:T(8,128)(2,1)S(1)}, bf16[128,1024]{1,0:T(8,128)(2,1)S(1)}, u32[]{:S(2)}, u32[]{:S(2)}) collective-permute-start(bf16[128,1024]{1,0:T(8,128)(2,1)S(1)} %collective-permute-done.10.rest_0_.a), channel_id=1, source_target_pairs={{9,8},{10,9},{11,10},{12,11},{13,12},{14,13},{15,14},{0,15},{25,24... | collective-permute-start | bytes 786440 | tf_op jit(solution)/shard_map/ppermute | solution.py:291
  80.6 4.5 %collective-permute-start.13 = (bf16[128,1024]{1,0:T(8,128)(2,1)S(1)}, bf16[128,1024]{1,0:T(8,128)(2,1)S(1)}, u32[]{:S(2)}, u32[]{:S(2)}) collective-permute-start(bf16[128,1024]{1,0:T(8,128)(2,1)S(1)} %collective-permute-done.11.rest_1_.b), channel_id=1, source_target_pairs={{6,7},{7,8},{8,9},{9,10},{10,11},{11,12},{12,13},{13,14},{14,15},{... | collective-permute-start | bytes 786440 | tf_op jit(solution)/shard_map/ppermute | solution.py:291
  86.2 3.0 %collective-permute-start.14 = (bf16[128,1024]{1,0:T(8,128)(2,1)S(1)}, bf16[128,1024]{1,0:T(8,128)(2,1)S(1)}, u32[]{:S(2)}, u32[]{:S(2)}) collective-permute-start(bf16[128,1024]{1,0:T(8,128)(2,1)S(1)} %get-tuple-element.121), channel_id=1, source_target_pairs={{8,9},{9,10},{10,11},{11,12},{12,13},{13,14},{14,15},{15,7},{24,25... | collective-permute-start | bytes 786440 | tf_op jit(solution)/shard_map/ppermute | solution.py:291
  86.9 3.7 %collective-permute-start.21 = (bf16[128,1024]{1,0:T(8,128)(2,1)S(1)}, bf16[128,1024]{1,0:T(8,128)(2,1)S(1)}, u32[]{:S(2)}, u32[]{:S(2)}) collective-permute-start(bf16[128,1024]{1,0:T(8,128)(2,1)S(1)} %get-tuple-element.132), channel_id=1, source_target_pairs={{7,6},{8,7},{9,8},{10,9},{11,10},{12,11},{13,12},{14,13},{15,14},{... | collective-permute-start | bytes 786440 | tf_op jit(solution)/shard_map/ppermute | solution.py:291
  89.2 0.7 copy-start.5
  89.9 2.1 %collective-permute-start.15 = (bf16[128,1024]{1,0:T(8,128)(2,1)S(1)}, bf16[128,1024]{1,0:T(8,128)(2,1)S(1)}, u32[]{:S(2)}, u32[]{:S(2)}) collective-permute-start(bf16[128,1024]{1,0:T(8,128)(2,1)S(1)} %add.63), channel_id=1, source_target_pairs={{9,10},{10,11},{11,12},{12,13},{13,14},{14,15},{15,6},{25,26},{26,... | collective-permute-start | bytes 786440 | tf_op jit(solution)/shard_map/ppermute | solution.py:291
  90.7 2.7 %collective-permute-start.22 = (bf16[128,1024]{1,0:T(8,128)(2,1)S(1)}, bf16[128,1024]{1,0:T(8,128)(2,1)S(1)}, u32[]{:S(2)}, u32[]{:S(2)}) collective-permute-start(bf16[128,1024]{1,0:T(8,128)(2,1)S(1)} %add.69), channel_id=1, source_target_pairs={{6,5},{7,6},{8,7},{9,8},{10,9},{11,10},{12,11},{13,12},{14,13},{15... | collective-permute-start | bytes 786440 | tf_op jit(solution)/shard_map/ppermute | solution.py:291
  92.0 0.7 copy-start.7
  92.7 2.1 %collective-permute-start.16 = (bf16[128,1024]{1,0:T(8,128)(2,1)S(1)}, bf16[128,1024]{1,0:T(8,128)(2,1)S(1)}, u32[]{:S(2)}, u32[]{:S(2)}) collective-permute-start(bf16[128,1024]{1,0:T(8,128)(2,1)S(1)} %add.64), channel_id=1, source_target_pairs={{10,11},{11,12},{12,13},{13,14},{14,15},{15,5},{26,27},{27,28},{28... | collective-permute-start | bytes 786440 | tf_op jit(solution)/shard_map/ppermute | solution.py:291
  93.5 2.7 %collective-permute-start.23 = (bf16[128,1024]{1,0:T(8,128)(2,1)S(1)}, bf16[128,1024]{1,0:T(8,128)(2,1)S(1)}, u32[]{:S(2)}, u32[]{:S(2)}) collective-permute-start(bf16[128,1024]{1,0:T(8,128)(2,1)S(1)} %add.70), channel_id=1, source_target_pairs={{5,4},{6,5},{7,6},{8,7},{9,8},{10,9},{11,10},{12,11},{13,12},{14,1... | collective-permute-start | bytes 786440 | tf_op jit(solution)/shard_map/ppermute | solution.py:291
  94.9 0.7 copy-start.9
  95.6 2.1 %collective-permute-start.17 = (bf16[128,1024]{1,0:T(8,128)(2,1)S(1)}, bf16[128,1024]{1,0:T(8,128)(2,1)S(1)}, u32[]{:S(2)}, u32[]{:S(2)}) collective-permute-start(bf16[128,1024]{1,0:T(8,128)(2,1)S(1)} %add.65), channel_id=1, source_target_pairs={{11,12},{12,13},{13,14},{14,15},{15,4},{27,28},{28,29},{29,30},{30... | collective-permute-start | bytes 786440 | tf_op jit(solution)/shard_map/ppermute | solution.py:291
  96.3 3.4 %collective-permute-start.24 = (bf16[128,1024]{1,0:T(8,128)(2,1)S(1)}, bf16[128,1024]{1,0:T(8,128)(2,1)S(1)}, u32[]{:S(2)}, u32[]{:S(2)}) collective-permute-start(bf16[128,1024]{1,0:T(8,128)(2,1)S(1)} %add.71), channel_id=1, source_target_pairs={{4,3},{5,4},{6,5},{7,6},{8,7},{9,8},{10,9},{11,10},{12,11},{13,12}... | collective-permute-start | bytes 786440 | tf_op jit(solution)/shard_map/ppermute | solution.py:291
  97.7 0.7 copy-start.11
  98.4 48.4 %collective-permute-start.18 = (bf16[128,1024]{1,0:T(8,128)(2,1)S(1)}, bf16[128,1024]{1,0:T(8,128)(2,1)S(1)}, u32[]{:S(2)}, u32[]{:S(2)}) collective-permute-start(bf16[128,1024]{1,0:T(8,128)(2,1)S(1)} %add.66), channel_id=1, source_target_pairs={{12,14},{13,15},{14,0},{15,1},{28,30},{29,31},{30,16},{31,17},{44,... | collective-permute-start | bytes 786440 | tf_op jit(solution)/shard_map/ppermute | solution.py:291
  99.8 51.4 %collective-permute-start.25 = (bf16[128,1024]{1,0:T(8,128)(2,1)S(1)}, bf16[128,1024]{1,0:T(8,128)(2,1)S(1)}, u32[]{:S(2)}, u32[]{:S(2)}) collective-permute-start(bf16[128,1024]{1,0:T(8,128)(2,1)S(1)} %add.72), channel_id=1, source_target_pairs={{3,2},{4,3},{5,4},{6,5},{7,6},{8,7},{9,8},{10,9},{11,10},{12,11},{... | collective-permute-start | bytes 786440 | tf_op jit(solution)/shard_map/ppermute | solution.py:291
  146.8 10.9 %collective-permute-start.19 = (bf16[128,1024]{1,0:T(8,128)(2,1)S(1)}, bf16[128,1024]{1,0:T(8,128)(2,1)S(1)}, u32[]{:S(2)}, u32[]{:S(2)}) collective-permute-start(bf16[128,1024]{1,0:T(8,128)(2,1)S(1)} %add.67), channel_id=1, source_target_pairs={{14,15},{15,0},{0,1},{1,2},{30,31},{31,16},{16,17},{17,18},{46,47}... | collective-permute-start | bytes 786440 | tf_op jit(solution)/shard_map/ppermute | solution.py:291
  151.2 9.3 %collective-permute-start.26 = (bf16[128,1024]{1,0:T(8,128)(2,1)S(1)}, bf16[128,1024]{1,0:T(8,128)(2,1)S(1)}, u32[]{:S(2)}, u32[]{:S(2)}) collective-permute-start(bf16[128,1024]{1,0:T(8,128)(2,1)S(1)} %add.73), channel_id=1, source_target_pairs={{2,1},{3,2},{4,3},{5,4},{6,5},{7,6},{8,7},{9,8},{10,9},{11,10},{12... | collective-permute-start | bytes 786440 | tf_op jit(solution)/shard_map/ppermute | solution.py:291
  158.5 4.1 %copy-start.2 = (bf16[128,2048]{1,0:T(8,128)(2,1)S(1)}, bf16[128,2048]{1,0:T(8,128)(2,1)}, u32[]{:S(2)}) copy-start(bf16[128,2048]{1,0:T(8,128)(2,1)} %g_ref.27) | copy-start | bytes 1572868
  158.5 9.9 %collective-permute-start.20 = (bf16[128,1024]{1,0:T(8,128)(2,1)}, bf16[128,1024]{1,0:T(8,128)(2,1)}, u32[]{:S(2)}, u32[]{:S(2)}) collective-permute-start(bf16[128,1024]{1,0:T(8,128)(2,1)} %add.68), channel_id=1, source_target_pairs={{15,0},{0,1},{1,2},{2,3},{31,16},{16,17},{17,18},{18,19},{47,32},{... | collective-permute-start | bytes 786440 | tf_op jit(solution)/shard_map/ppermute | solution.py:291
  160.6 2.1 %copy-start.4 = (bf16[128,1024]{1,0:T(8,128)(2,1)S(1)}, bf16[128,1024]{1,0:T(8,128)(2,1)}, u32[]{:S(2)}) copy-start(bf16[128,1024]{1,0:T(8,128)(2,1)} %shard_map.84.own) | copy-start | bytes 786436
  161.4 8.6 %collective-permute-start.27 = (bf16[128,1024]{1,0:T(8,128)(2,1)}, bf16[128,1024]{1,0:T(8,128)(2,1)}, u32[]{:S(2)}, u32[]{:S(2)}) collective-permute-start(bf16[128,1024]{1,0:T(8,128)(2,1)} %add.74), channel_id=1, source_target_pairs={{1,0},{2,1},{3,2},{4,3},{5,4},{6,5},{7,6},{8,7},{9,8},{10,9},{11,1... | collective-permute-start | bytes 786440 | tf_op jit(solution)/shard_map/ppermute | solution.py:291
  162.7 7.3 %copy-start.6 = (bf16[128,1024]{1,0:T(8,128)(2,1)S(1)}, bf16[128,1024]{1,0:T(8,128)(2,1)}, u32[]{:S(2)}) copy-start(bf16[128,1024]{1,0:T(8,128)(2,1)} %copy-done.5) | copy-start | bytes 786436
  162.7 7.3 %copy-start.8 = (bf16[128,1024]{1,0:T(8,128)(2,1)S(1)}, bf16[128,1024]{1,0:T(8,128)(2,1)}, u32[]{:S(2)}) copy-start(bf16[128,1024]{1,0:T(8,128)(2,1)} %copy-done.7) | copy-start | bytes 786436
  162.7 7.2 %copy-start.10 = (bf16[128,1024]{1,0:T(8,128)(2,1)S(1)}, bf16[128,1024]{1,0:T(8,128)(2,1)}, u32[]{:S(2)}) copy-start(bf16[128,1024]{1,0:T(8,128)(2,1)} %copy-done.9) | copy-start | bytes 786436
  162.7 7.2 %copy-start.12 = (bf16[128,1024]{1,0:T(8,128)(2,1)S(1)}, bf16[128,1024]{1,0:T(8,128)(2,1)}, u32[]{:S(2)}) copy-start(bf16[128,1024]{1,0:T(8,128)(2,1)} %copy-done.11) | copy-start | bytes 786436
